TPU v7x, 256 devices: a whole 4x4x8 slice. The times are simulated.
256 devices in a mesh: space: 64 (over y, x, z_hi), rep: 4 (over z_lo, core).
Axes of the slice: x: 4, y: 4, z: 8 (z_hi: 4, z_lo: 2; z = z_hi * 2 + z_lo), core: 2. Of those that a mesh axis runs over, the one named last changes fastest.
Arguments:
- leaf_density: bfloat16 [888, 65536], P(None, 'space'), may hold values from -6 to 6
- upward_ops: bfloat16 [8, 888, 888], P(None, 'rep'), may hold values from -0.0625 to 0.0625
- far_ops: bfloat16 [12, 888, 888], P('rep'), may hold values from -0.0625 to 0.0625
- downward_ops: bfloat16 [8, 888, 888], P(None, 'rep'), may hold values from -0.1875 to 0.1875
- fine_lists: int32 [12, 65536], P('rep', 'space'), may hold values from 0 to 3071
- coarse_lists: int32 [12, 8192], P('rep', 'space'), may hold values from 0 to 383
Outputs:
- local_check: bfloat16 [888, 65536], P('rep', 'space')
Inputs may be any that keep to these rules, and one draw needn't show every extreme that they name: `fine_lists`: entry k of box g names a box of the previous subtree (below 1024), of its own (below 2048) or of the next one; indices outside the grid of subtrees read zeros. `coarse_lists`: entry k of coarse box p names a coarse box of the previous coarse subtree (below 128), of its own (below 256) or of the next one; indices outside the grid read zeros.
All inputs are finite; a program needn't handle non-finite values.
Results may differ from a plain program's by a relative error of at most 0.013.
Values may be sent and summed in bfloat16 or wider, within the bound.
No kernel may reach another device: no remote copies, remote signals or barrier semaphores. Data moves between devices by JAX's collectives and lax.ppermute only.
A program may use at most 128 MiB of HBM per device.

v0:
```python
import jax
import jax.numpy as jnp
from jax import lax
from jax.sharding import PartitionSpec as P

coarse_scale = 0.5


def extended(x, sides, width):
    for axis, dim in sides:
        peers, length = (lax.axis_size(axis), x.shape[dim])
        up = [(i, (i + 1) % peers) for i in range(peers - 1)]
        down = [(j, i) for i, j in up]
        last = lax.slice_in_dim(x, length - width, length, axis=dim)
        initial = lax.slice_in_dim(x, 0, width, axis=dim)
        before = lax.ppermute(last, axis, up)
        after = lax.ppermute(initial, axis, down)
        x = jnp.concatenate([before, x, after], axis=dim)
    return x


def sent_to_all(x, axis):
    peers = lax.axis_size(axis)
    return lax.all_to_all(jnp.broadcast_to(x[None], (peers, *x.shape)), axis, 0, 0, tiled=True)


def laid_out(blocks, dim):
    lengths = list(blocks.shape[1:])
    lengths[dim] *= blocks.shape[0]
    return jnp.moveaxis(blocks, 0, dim).reshape(lengths)


def gather_directly(x, axis, dim):
    blocks = sent_to_all(x, axis)
    return laid_out(blocks, dim)


def split_up(x, dim, peers):
    before, after = (x.shape[:dim], x.shape[dim + 1 :])
    return jnp.moveaxis(x.reshape(*before, peers, -1, *after), dim, 0)


def sum_at_owner(x, axis, dim):
    blocks = split_up(x, dim, lax.axis_size(axis))
    arrived = lax.all_to_all(blocks, axis, split_axis=0, concat_axis=0, tiled=True)
    return arrived.astype(jnp.float32).sum(axis=0)


def of_everyone(x, axis):
    everything = sent_to_all(x, axis)
    return jnp.sum(everything.astype(jnp.float32), axis=0)


def parent_rows(leaf_density, upward_ops):
    density_rows, box_count = leaf_density.shape
    children = leaf_density.reshape(density_rows, box_count // 8, 8)
    parents = jnp.einsum("crq,qpc->rp", upward_ops, children, preferred_element_type=jnp.float32)
    return parents.astype(jnp.bfloat16)


def translate(operators, sources, lists):
    summed = jnp.zeros((operators.shape[1], lists.shape[1]), jnp.float32)
    for offset in range(operators.shape[0]):
        picked = jnp.take(sources, lists[offset], axis=1)
        summed = summed + jnp.dot(operators[offset], picked, preferred_element_type=jnp.float32)
    return summed


def local(leaf_density, upward_ops, far_ops, downward_ops, fine_lists, coarse_lists):
    up_rows = parent_rows(leaf_density, upward_ops)
    coarse_width = up_rows.shape[1]
    rim_rows = extended(up_rows, (("space", 1),), coarse_width)
    coarse_window = gather_directly(rim_rows, "rep", 0)
    window = extended(leaf_density, (("space", 1),), leaf_density.shape[1])
    fine_partial = translate(far_ops, window, fine_lists)
    coarse_partial = coarse_scale * translate(far_ops, coarse_window, coarse_lists)
    fine_check = sum_at_owner(fine_partial.astype(jnp.bfloat16), "rep", 0)
    coarse_check = (
        of_everyone(coarse_partial.astype(jnp.bfloat16), "rep")
        .astype(jnp.float32)
        .astype(jnp.bfloat16)
    )
    parents_here = coarse_check.shape[1]
    spread = jnp.einsum(
        "crq,qp->rpc", downward_ops, coarse_check, preferred_element_type=jnp.float32
    )
    return (fine_check + spread.reshape(spread.shape[0], parents_here * 8)).astype(jnp.bfloat16)


def solution(mesh):
    return jax.shard_map(
        local,
        mesh=mesh,
        in_specs=(
            P(None, "space"),
            P(None, "rep", None),
            P("rep", None, None),
            P(None, "rep", None),
            P("rep", "space"),
            P("rep", "space"),
        ),
        out_specs=P("rep", "space"),
        check_vma=False,
    )
```

profile of v0, /device:TPU:24, one launch (start us, length us, event | category | flops | bytes accessed | tf_op | source)
XLA Modules:
  0.0 222.4 jit_solution(7378458492255734014)
XLA Ops:
  0.0 5.4 %collective-permute-start = (bf16[888,1024]{1,0:T(8,128)(2,1)}, bf16[888,1024]{1,0:T(8,128)(2,1)}, u32[]{:S(2)}, u32[]{:S(2)}) collective-permute-start(bf16[888,1024]{1,0:T(8,128)(2,1)} %param.10), channel_id=1, source_target_pairs={{0,4},{4,8},{8,12},{12,16},{16,20},{20,24},{24,28},{28,32},{32,36}... | collective-permute-start | bytes 5455880 | tf_op jit(solution)/shard_map/ppermute | solution.py:16
  5.4 7.3 %collective-permute-start.1 = (bf16[888,1024]{1,0:T(8,128)(2,1)}, bf16[888,1024]{1,0:T(8,128)(2,1)}, u32[]{:S(2)}, u32[]{:S(2)}) collective-permute-start(bf16[888,1024]{1,0:T(8,128)(2,1)} %param.10), channel_id=1, source_target_pairs={{4,0},{8,4},{12,8},{16,12},{20,16},{24,20},{28,24},{32,28},{36,32}... | collective-permute-start | bytes 5455880 | tf_op jit(solution)/shard_map/ppermute | solution.py:17
  12.8 3.8 %copy.41 = bf16[888,1024]{0,1:T(8,128)(2,1)} copy(bf16[888,1024]{1,0:T(8,128)(2,1)} %param.10) | data formatting | bytes 3637248 | tf_op args[0]
  16.6 3.5 %fusion.60 = bf16[222,128]{1,0:T(8,128)(2,1)S(1)} fusion(bf16[888,128,8]{0,2,1:T(8,128)(2,1)} %bitcast.74, bf16[8,222,888]{2,0,1:T(8,128)(2,1)} %param.11), kind=kOutput, calls=%fused_computation.49 | convolution fusion | flops 403762944 | bytes 5029632 | tf_op jit(solution)/shard_map/crq,qpc->rp/dot_general | solution.py:57
  20.1 4.8 %collective-permute-start.3 = (bf16[222,128]{1,0:T(8,128)(2,1)S(1)}, bf16[222,128]{1,0:T(8,128)(2,1)S(1)}, u32[]{:S(2)}, u32[]{:S(2)}) collective-permute-start(bf16[222,128]{1,0:T(8,128)(2,1)S(1)} %fusion.60), channel_id=1, source_target_pairs={{4,0},{8,4},{12,8},{16,12},{20,16},{24,20},{28,24},{32,28},{36,32}... | collective-permute-start | bytes 170504 | tf_op jit(solution)/shard_map/ppermute | solution.py:17
  26.9 66.2 %collective-permute-done.3 = bf16[222,128]{1,0:T(8,128)(2,1)S(1)} collective-permute-done((bf16[222,128]{1,0:T(8,128)(2,1)S(1)}, bf16[222,128]{1,0:T(8,128)(2,1)S(1)}, u32[]{:S(2)}, u32[]{:S(2)}) %collective-permute-start.3) | collective-permute-done | bytes 56864 | tf_op jit(solution)/shard_map/ppermute | solution.py:17
  94.1 4.2 %all-to-all-start.1 = ((bf16[4,222,384]{2,1,0:T(8,128)(2,1)}), bf16[4,222,384]{2,1,0:T(8,128)(2,1)}, u32[]{:S(2)}, u32[]{:S(2)}) async-start(bf16[4,222,384]{2,1,0:T(8,128)(2,1)} %broadcast_in_dim.30), calls=%async_computation.1 | async-start | bytes 1376256 | tf_op jit(solution)/shard_map/all_to_all | solution.py:24
  98.4 10.6 %all-to-all-done.1 = bf16[4,222,384]{2,1,0:T(8,128)(2,1)} async-done(((bf16[4,222,384]{2,1,0:T(8,128)(2,1)}), bf16[4,222,384]{2,1,0:T(8,128)(2,1)}, u32[]{:S(2)}, u32[]{:S(2)}) %all-to-all-start.1) | async-done | bytes 682016 | tf_op jit(solution)/shard_map/all_to_all | solution.py:24
  109.0 2.1 reshape.26
  111.1 2.2 copy.46
  113.3 2.9 %gather_fusion.5 = bf16[128,888]{1,0:T(8,128)(2,1)} fusion(bf16[888,384]{0,1:T(8,128)(2,1)} %copy.46, s32[1024]{0:T(1024)S(1)} %get-tuple-element.20), kind=kCustom, calls=%fused_computation.5.clone | custom fusion | bytes 455168 | tf_op jit(solution)/shard_map/jit(_take)/gather | solution.py:64
  116.2 2.9 %gather_fusion.4 = bf16[128,888]{1,0:T(8,128)(2,1)} fusion(bf16[888,384]{0,1:T(8,128)(2,1)} %copy.46, s32[1024]{0:T(1024)S(1)} %get-tuple-element.21), kind=kCustom, calls=%fused_computation.4.clone | custom fusion | bytes 455168 | tf_op jit(solution)/shard_map/jit(_take)/gather | solution.py:64
  119.1 2.2 gather_fusion.3
  121.3 2.3 %fusion.18 = f32[128,888]{0,1:T(8,128)S(1)} fusion(bf16[3,888,888]{2,1,0:T(8,128)(2,1)} %param.12, bf16[128,888]{1,0:T(8,128)(2,1)} %gather_fusion.5, pred[128]{0:T(512)(128)(4,1)S(1)} %get-tuple-element.16), kind=kOutput, calls=%fused_computation.27 | convolution fusion | flops 201980928 | bytes 2275456 | tf_op jit(solution)/shard_map/dot_general | solution.py:65
  123.6 2.1 fusion.21
  125.8 2.2 fusion.52
  129.0 4.4 %all-to-all-start.2 = ((bf16[4,888,128]{2,1,0:T(8,128)(2,1)}), bf16[4,888,128]{2,1,0:T(8,128)(2,1)}, u32[]{:S(2)}, u32[]{:S(2)}) async-start(bf16[4,888,128]{2,1,0:T(8,128)(2,1)} %broadcast_in_dim.31), calls=%async_computation.2 | async-start | bytes 1818624 | tf_op jit(solution)/shard_map/all_to_all | solution.py:24
  133.4 3.9 %copy.40 = bf16[888,1024]{0,1:T(8,128)(2,1)} copy(bf16[888,1024]{1,0:T(8,128)(2,1)} %collective-permute-done) | data formatting | bytes 3637248 | tf_op jit(solution)/shard_map/ppermute | solution.py:16
  137.2 3.8 %copy.42 = bf16[888,1024]{0,1:T(8,128)(2,1)} copy(bf16[888,1024]{1,0:T(8,128)(2,1)} %collective-permute-done.1) | data formatting | bytes 3637248 | tf_op jit(solution)/shard_map/ppermute | solution.py:17
  141.0 5.5 %pad_maximum_fusion = bf16[888,3072]{0,1:T(8,128)(2,1)} fusion(bf16[888,1024]{0,1:T(8,128)(2,1)} %copy.42, bf16[888,1024]{0,1:T(8,128)(2,1)} %copy.41, bf16[888,1024]{0,1:T(8,128)(2,1)} %copy.40), kind=kLoop, calls=%fused_computation.6 | loop fusion | flops 16367616 | bytes 10911744 | tf_op jit(solution)/shard_map/concatenate | solution.py:18
  146.5 9.0 %gather_fusion = bf16[1024,888]{1,0:T(8,128)(2,1)} fusion(bf16[888,3072]{0,1:T(8,128)(2,1)} %pad_maximum_fusion, s32[1024]{0:T(1024)S(1)} %fusion.81), kind=kCustom, calls=%fused_computation.clone | custom fusion | bytes 3641344 | tf_op jit(solution)/shard_map/jit(_take)/gather | solution.py:64
  155.6 6.0 %fusion.8 = f32[1024,888]{0,1:T(8,128)} fusion(bf16[1024,888]{1,0:T(8,128)(2,1)} %gather_fusion, pred[1024]{0:T(1024)(128)(4,1)S(1)} %compare_and_fusion.2, bf16[3,888,888]{2,1,0:T(8,128)(2,1)} %param.12), kind=kOutput, calls=%fused_computation.17 | convolution fusion | flops 1615847424 | bytes 7064576 | tf_op jit(solution)/shard_map/dot_general | solution.py:65
  161.6 9.0 %gather_fusion.2 = bf16[1024,888]{1,0:T(8,128)(2,1)} fusion(bf16[888,3072]{0,1:T(8,128)(2,1)} %pad_maximum_fusion, s32[1024]{0:T(1024)S(1)} %fusion.83), kind=kCustom, calls=%fused_computation.3.clone | custom fusion | bytes 3641344 | tf_op jit(solution)/shard_map/jit(_take)/gather | solution.py:64
  170.6 9.0 %gather_fusion.1 = bf16[1024,888]{1,0:T(8,128)(2,1)} fusion(bf16[888,3072]{0,1:T(8,128)(2,1)} %pad_maximum_fusion, s32[1024]{0:T(1024)S(1)} %fusion.82), kind=kCustom, calls=%fused_computation.2.clone | custom fusion | bytes 3641344 | tf_op jit(solution)/shard_map/jit(_take)/gather | solution.py:64
  179.6 4.3 %fusion.6 = f32[1024,888]{0,1:T(8,128)S(1)} fusion(bf16[1024,888]{1,0:T(8,128)(2,1)} %gather_fusion.1, pred[1024]{0:T(1024)(128)(4,1)S(1)} %compare_and_fusion.1, bf16[3,888,888]{2,1,0:T(8,128)(2,1)} %param.12), kind=kOutput, calls=%fused_computation.15 | convolution fusion | flops 1615847424 | bytes 7064576 | tf_op jit(solution)/shard_map/dot_general | solution.py:65
  184.0 4.9 %fusion.17 = bf16[888,1024]{1,0:T(8,128)(2,1)} fusion(f32[1024,888]{0,1:T(8,128)S(1)} %copy-done.6, f32[1024,888]{0,1:T(8,128)S(1)} %fusion.6, bf16[3,888,888]{2,1,0:T(8,128)(2,1)} %param.12, bf16[1024,888]{1,0:T(8,128)(2,1)S(1)} %copy-done.2, pred[1024]{0:T(1024)(128)(4,1)S(1)} %compare_and_fusion), kind=kOutput, calls=%fused_computation.26 | convolution fusion | flops 1618575360 | bytes 12504064 | tf_op jit(solution)/shard_map/dot_general | solution.py:65
  188.9 3.2 %reshape.24 = bf16[4,222,1024]{2,1,0:T(8,128)(2,1)} reshape(bf16[888,1024]{1,0:T(8,128)(2,1)} %fusion.17) | data formatting | bytes 3637248 | tf_op jit(solution)/shard_map/reshape | solution.py:40
  192.1 4.4 %all-to-all-start = ((bf16[4,222,1024]{2,1,0:T(8,128)(2,1)}), bf16[4,222,1024]{2,1,0:T(8,128)(2,1)}, u32[]{:S(2)}, u32[]{:S(2)}) async-start(bf16[4,222,1024]{2,1,0:T(8,128)(2,1)} %reshape.24), calls=%async_computation | async-start | bytes 3670016 | tf_op jit(solution)/shard_map/all_to_all | solution.py:45
  199.9 2.6 %copy.50 = f32[222,128,8]{0,2,1:T(8,128)} copy(f32[222,128,8]{1,0,2:T(8,128)} %fusion.37) | data formatting | bytes 1818624 | tf_op jit(solution)/shard_map/crq,qp->rpc/transpose | solution.py:84
  202.5 2.5 %copy.51 = f32[222,1024]{1,0:T(8,128)} copy(f32[222,1024]{0,1:T(8,128)} %bitcast.75) | data formatting | bytes 1818624 | tf_op jit(solution)/shard_map/reshape | solution.py:87
  205.0 14.5 %all-to-all-done = bf16[4,222,1024]{2,1,0:T(8,128)(2,1)} async-done(((bf16[4,222,1024]{2,1,0:T(8,128)(2,1)}), bf16[4,222,1024]{2,1,0:T(8,128)(2,1)}, u32[]{:S(2)}, u32[]{:S(2)}) %all-to-all-start) | async-done | bytes 1818656 | tf_op jit(solution)/shard_map/all_to_all | solution.py:45
  219.5 2.0 convert_reduce_fusion
  (35 shorter events, 8.3 us)
Async XLA Ops:
  0.0 197.9 %copy-start = (bf16[8,222,888]{2,0,1:T(8,128)(2,1)S(1)}, bf16[8,222,888]{2,0,1:T(8,128)(2,1)}, u32[]{:S(2)}) copy-start(bf16[8,222,888]{2,0,1:T(8,128)(2,1)} %param.13) | copy-start | bytes 9462532
  0.0 133.4 %collective-permute-start = (bf16[888,1024]{1,0:T(8,128)(2,1)}, bf16[888,1024]{1,0:T(8,128)(2,1)}, u32[]{:S(2)}, u32[]{:S(2)}) collective-permute-start(bf16[888,1024]{1,0:T(8,128)(2,1)} %param.10), channel_id=1, source_target_pairs={{0,4},{4,8},{8,12},{12,16},{16,20},{20,24},{24,28},{28,32},{32,36}... | collective-permute-start | bytes 5455880 | tf_op jit(solution)/shard_map/ppermute | solution.py:16
  5.4 131.8 %collective-permute-start.1 = (bf16[888,1024]{1,0:T(8,128)(2,1)}, bf16[888,1024]{1,0:T(8,128)(2,1)}, u32[]{:S(2)}, u32[]{:S(2)}) collective-permute-start(bf16[888,1024]{1,0:T(8,128)(2,1)} %param.10), channel_id=1, source_target_pairs={{4,0},{8,4},{12,8},{16,12},{20,16},{24,20},{28,24},{32,28},{36,32}... | collective-permute-start | bytes 5455880 | tf_op jit(solution)/shard_map/ppermute | solution.py:17
  16.6 10.3 %copy-start.5 = (s32[3,128]{1,0:T(4,128)S(1)}, s32[3,128]{1,0:T(4,128)}, u32[]{:S(2)}) copy-start(s32[3,128]{1,0:T(4,128)} %param.15) | copy-start | bytes 4612
  16.6 10.3 %copy-start.4 = (s32[3,1024]{1,0:T(4,128)S(1)}, s32[3,1024]{1,0:T(4,128)}, u32[]{:S(2)}) copy-start(s32[3,1024]{1,0:T(4,128)} %param.14) | copy-start | bytes 36868
  20.1 73.1 %collective-permute-start.3 = (bf16[222,128]{1,0:T(8,128)(2,1)S(1)}, bf16[222,128]{1,0:T(8,128)(2,1)S(1)}, u32[]{:S(2)}, u32[]{:S(2)}) collective-permute-start(bf16[222,128]{1,0:T(8,128)(2,1)S(1)} %fusion.60), channel_id=1, source_target_pairs={{4,0},{8,4},{12,8},{16,12},{20,16},{24,20},{28,24},{32,28},{36,32}... | collective-permute-start | bytes 170504 | tf_op jit(solution)/shard_map/ppermute | solution.py:17
  24.9 68.3 %collective-permute-start.2 = (bf16[222,128]{1,0:T(8,128)(2,1)S(1)}, bf16[222,128]{1,0:T(8,128)(2,1)S(1)}, u32[]{:S(2)}, u32[]{:S(2)}) collective-permute-start(bf16[222,128]{1,0:T(8,128)(2,1)S(1)} %fusion.60), channel_id=1, source_target_pairs={{0,4},{4,8},{8,12},{12,16},{16,20},{20,24},{24,28},{28,32},{32,36}... | collective-permute-start | bytes 170504 | tf_op jit(solution)/shard_map/ppermute | solution.py:16
  94.1 14.8 %all-to-all-start.1 = ((bf16[4,222,384]{2,1,0:T(8,128)(2,1)}), bf16[4,222,384]{2,1,0:T(8,128)(2,1)}, u32[]{:S(2)}, u32[]{:S(2)}) async-start(bf16[4,222,384]{2,1,0:T(8,128)(2,1)} %broadcast_in_dim.30), calls=%async_computation.1 | async-start | bytes 1376256 | tf_op jit(solution)/shard_map/all_to_all | solution.py:24
  121.3 2.3 %copy-start.3 = (bf16[128,888]{1,0:T(8,128)(2,1)S(1)}, bf16[128,888]{1,0:T(8,128)(2,1)}, u32[]{:S(2)}) copy-start(bf16[128,888]{1,0:T(8,128)(2,1)} %gather_fusion.4) | copy-start | bytes 681988
  129.0 63.2 %all-to-all-start.2 = ((bf16[4,888,128]{2,1,0:T(8,128)(2,1)}), bf16[4,888,128]{2,1,0:T(8,128)(2,1)}, u32[]{:S(2)}, u32[]{:S(2)}) async-start(bf16[4,888,128]{2,1,0:T(8,128)(2,1)} %broadcast_in_dim.31), calls=%async_computation.2 | async-start | bytes 1818624 | tf_op jit(solution)/shard_map/all_to_all | solution.py:24
  179.6 4.3 %copy-start.2 = (bf16[1024,888]{1,0:T(8,128)(2,1)S(1)}, bf16[1024,888]{1,0:T(8,128)(2,1)}, u32[]{:S(2)}) copy-start(bf16[1024,888]{1,0:T(8,128)(2,1)} %gather_fusion.2) | copy-start | bytes 5455876
  179.6 4.3 %copy-start.6 = (f32[1024,888]{0,1:T(8,128)S(1)}, f32[1024,888]{0,1:T(8,128)}, u32[]{:S(2)}) copy-start(f32[1024,888]{0,1:T(8,128)} %fusion.8) | copy-start | bytes 10911748
  192.1 27.4 %all-to-all-start = ((bf16[4,222,1024]{2,1,0:T(8,128)(2,1)}), bf16[4,222,1024]{2,1,0:T(8,128)(2,1)}, u32[]{:S(2)}, u32[]{:S(2)}) async-start(bf16[4,222,1024]{2,1,0:T(8,128)(2,1)} %reshape.24), calls=%async_computation | async-start | bytes 3670016 | tf_op jit(solution)/shard_map/all_to_all | solution.py:45
  219.5 2.0 copy-start.1
where the time goes:
time: 224 us; the launch traced here: 222 us
  waiting for transfers between devices  91.3 us (41%)
  local copies, waits for them, and re-layouts  61.3 us (27%)
  starting transfers between devices  32.5 us (15%)
  matrix products  27.2 us (12%)
  other arithmetic  9.82 us (4%)
    ppermute x2, waiting for transfers between devices, extended(): after = lax.ppermute(initial, axis, down)  66.2 us
    gather x6, local copies, waits for them, and re-layouts, translate(): picked = jnp.take(sources, lists[offset], axis=1)  35.1 us
    dot_general x6, matrix products, translate(): jnp.dot(operators[offset], picked, preferred_element_type=jnp.float32)  21.8 us
    all_to_all x1, waiting for transfers between devices, sum_at_owner(): lax.all_to_all(blocks, axis, split_axis=0, concat_axis=0, tiled=True)  14.5 us
    ppermute x2, starting transfers between devices, extended(): after = lax.ppermute(initial, axis, down)  12.1 us
    all_to_all x2, waiting for transfers between devices, sent_to_all(): lax.all_to_all(jnp.broadcast_to(x[None], (peers, *x.shape)), axis, 0, 0,...  10.6 us
    all_to_all x2, starting transfers between devices, sent_to_all(): lax.all_to_all(jnp.broadcast_to(x[None], (peers, *x.shape)), axis, 0, 0,...  8.56 us
    ppermute x2, starting transfers between devices, extended(): before = lax.ppermute(last, axis, up)  7.35 us
  transfers between devices with their start and end apart: 7, of which 3 were waited for; matrix products, arithmetic and copies ran while one was open for 43% of the time, Pallas kernels for 0%

commit v1 on v0

v1 whole, which is shorter than its diff:
```python
import functools

import jax
import jax.numpy as jnp
from jax import lax
from jax.experimental import pallas as pl
from jax.experimental.pallas import tpu as pltpu
from jax.sharding import PartitionSpec as P

bf16, f32 = jnp.bfloat16, jnp.float32
both = ("space", "rep")
coarse_scale = 0.5
rows, wide, tiles = 888, 896, 7
boxes, half = 1024, 512
parents = 128
share = 222
chunks = 2
chunk = half // chunks
window = 6 * half
vmem = pltpu.CompilerParams(vmem_limit_bytes=56 << 20)


def one_hop(groups):
    up = [(4 * s + 2 + c, 4 * (s + 1) + c) for s in range(groups - 1) for c in (0, 1)]
    return up + [(j, i) for i, j in up]


def across(groups, flip):
    return [(4 * s + r, 4 * s + (r ^ flip)) for s in range(groups) for r in range(4)]


def call(kernel, scalars, args, in_specs, out_specs, out_shape, grid=(1,), scratch=(), cost=0):
    moved = sum(a.size * a.dtype.itemsize for a in args)
    return pl.pallas_call(
        kernel,
        grid_spec=pltpu.PrefetchScalarGridSpec(
            num_scalar_prefetch=1,
            grid=grid,
            in_specs=in_specs,
            out_specs=out_specs,
            scratch_shapes=scratch,
        ),
        out_shape=out_shape,
        compiler_params=vmem,
        cost_estimate=pl.CostEstimate(flops=cost, bytes_accessed=moved, transcendentals=0),
    )(scalars, *args)


def whole(a):
    zeros = (0,) * a.ndim
    return pl.BlockSpec(a.shape, lambda *_: zeros)


def turn_kernel(first, x_ref, o_ref):
    width = x_ref.shape[1]
    tall = jnp.concatenate([x_ref[...].astype(f32), jnp.zeros((wide - rows, width), f32)], 0)
    o_ref[...] = tall.T.astype(bf16)


def turned(x, first, count, width):
    return call(
        turn_kernel,
        first,
        (x,),
        [pl.BlockSpec((rows, width), lambda i, s: (0, s[0] + i))],
        pl.BlockSpec((width, wide), lambda i, s: (i, 0)),
        jax.ShapeDtypeStruct((count * width, wide), bf16),
        grid=(count,),
        cost=count * width * 4000000,
    )


def to_planes(src, dst, height):
    for s in range(tiles - 1):
        dst[pl.ds(s * height, height), :] = src[:, s * 128 : (s + 1) * 128].astype(f32)
    last = src[:, (tiles - 1) * 128 :].astype(f32)
    if last.shape[1] < 128:
        last = jnp.concatenate([last, jnp.zeros((height, 128 - last.shape[1]), f32)], 1)
    dst[pl.ds((tiles - 1) * height, height), :] = last


def every_eighth(planes, height, child, count):
    parts = [planes[pl.ds(s * height + child, count, stride=8), :] for s in range(tiles)]
    return jnp.concatenate(parts, 1).astype(bf16)


def up_kernel(sc, ops, other, *refs):
    mine, o_ref, op_planes, box_planes = refs[:-3], refs[-3], refs[-2], refs[-1]
    to_planes(ops, op_planes, 8 * share)
    for s in range(tiles):
        lanes = slice(s * 128, (s + 1) * 128)
        for i, part in enumerate(mine):
            at = pl.multiple_of(s * boxes + sc[0] * half + i * chunk, chunk)
            box_planes[pl.ds(at, chunk), :] = part[:, lanes].astype(f32)
        at = pl.multiple_of(s * boxes + (1 - sc[0]) * half, half)
        box_planes[pl.ds(at, half), :] = other[:, lanes].astype(f32)
    total = None
    for child in range(8):
        left = every_eighth(op_planes, 8 * share, child, share)
        right = every_eighth(box_planes, boxes, child, parents)
        term = lax.dot_general(left, right, (((1,), (1,)), ((), ())), preferred_element_type=f32)
        total = term if total is None else total + term
    o_ref[...] = total.astype(bf16)


def parent_rows(sc, ops, mine, other):
    args = (ops, other, *mine)
    return call(
        up_kernel,
        sc,
        args,
        [whole(a) for a in args],
        pl.BlockSpec((share, parents), lambda *_: (0, 0)),
        jax.ShapeDtypeStruct((share, parents), bf16),
        scratch=[
            pltpu.VMEM((tiles * 8 * share, 128), f32),
            pltpu.VMEM((tiles * boxes, 128), f32),
        ],
        cost=4000000000,
    )


def coarse_kernel(sc, lists, far, own, a, b, own_o, ab_o, send, keep, picked, result):
    c, l = sc[0], sc[1]
    wanted = lists[...]
    count = wanted.shape[1]
    near = jnp.where(l == 0, 0, 2 * parents)
    spot = lax.broadcasted_iota(jnp.int32, (parents, count), 0)
    hot = jnp.concatenate(
        [
            (spot == wanted - base).astype(f32).astype(bf16)
            for base in (parents, near, 2 * parents - near)
        ],
        0,
    )

    def pick(*parts):
        return jnp.dot(jnp.concatenate(parts, 1), hot, preferred_element_type=f32)

    lo, hi = slice(0, parents), slice(parents, 2 * parents)
    a_o, b_o = ab_o[:, : 2 * parents], ab_o[:, 2 * parents :]
    found = (
        (pick(own[:, lo], a[:, hi], b[:, lo]), pick(own[:, hi], a[:, lo], b[:, hi])),
        (pick(own_o[:, lo], a_o[:, hi], b_o[:, lo]), pick(own_o[:, hi], a_o[:, lo], b_o[:, hi])),
    )
    for j in range(4):
        x, y = j // 2, j % 2
        mine = jnp.where(l == x, found[0][0], found[0][1])
        theirs = jnp.where(l == x, found[1][0], found[1][1])
        picked[pl.ds(share * j, share), :] = jnp.where(c == y, mine, theirs)
    sources = picked[...].astype(bf16)
    total = None
    for k in range(3):
        term = jnp.dot(
            far[k], sources[:, k * parents : (k + 1) * parents], preferred_element_type=f32
        )
        total = term if total is None else total + term
    result[pl.ds(0, rows), :] = total * coarse_scale
    result[pl.ds(rows, wide - rows), :] = jnp.zeros((wide - rows, parents), f32)
    part = wide // 2
    keep[...] = result[pl.ds(pl.multiple_of(c * part, part), part), :]
    send[...] = result[pl.ds(pl.multiple_of((1 - c) * part, part), part), :].astype(bf16)


def coarse_partial(sc, lists, far, own, a, b, own_o, ab_o):
    args = (lists, far, own, a, b, own_o, ab_o)
    shape = (wide // 2, parents)
    spec = pl.BlockSpec(shape, lambda *_: (0, 0))
    return call(
        coarse_kernel,
        sc,
        args,
        [whole(x) for x in args],
        [spec, spec],
        [jax.ShapeDtypeStruct(shape, bf16), jax.ShapeDtypeStruct(shape, f32)],
        scratch=[pltpu.VMEM((rows, 3 * parents), f32), pltpu.VMEM((wide, parents), f32)],
        cost=3000000000,
    )


def down_kernel(sc, ops, mine, other, o_ref, op_planes, check, turned_rows):
    c, part = sc[0], wide // 2
    to_planes(ops, op_planes, 8 * share)
    check[pl.ds(pl.multiple_of(c * part, part), part), :] = mine[...]
    check[pl.ds(pl.multiple_of((1 - c) * part, part), part), :] = other[...]
    whole_check = check[...]
    for child in range(8):
        left = every_eighth(op_planes, 8 * share, child, share)
        z = jnp.dot(left, whole_check, preferred_element_type=f32)
        z = jnp.concatenate([z, jnp.zeros((256 - share, parents), f32)], 0).T
        for t in (0, 1):
            turned_rows[pl.ds(t * boxes + child, parents, stride=8), :] = z[
                :, t * 128 : (t + 1) * 128
            ]
    o_ref[pl.ds(0, 128), :] = turned_rows[pl.ds(0, boxes), :].T
    o_ref[pl.ds(128, share - 128), :] = turned_rows[pl.ds(boxes, boxes), :].T[: share - 128]


def downward(sc, ops, mine, other):
    args = (ops, mine, other)
    return call(
        down_kernel,
        sc,
        args,
        [whole(x) for x in args],
        pl.BlockSpec((share, boxes), lambda *_: (0, 0)),
        jax.ShapeDtypeStruct((share, boxes), f32),
        scratch=[
            pltpu.VMEM((tiles * 8 * share, 128), f32),
            pltpu.VMEM((wide, parents), bf16),
            pltpu.VMEM((2 * boxes, 128), f32),
        ],
        cost=3000000000,
    )


pitch, step_boxes, unroll = window + 8, 512, 32


def gather_kernel(spots, *refs):
    pieces, o_ref, planes, got = refs[:-3], refs[-3], refs[-2], refs[-1]
    step = pl.program_id(0)
    depth = step_boxes + 8

    @pl.when(step == 0)
    def _():
        at = 0
        for piece in pieces:
            count = piece.shape[0]
            for s in range(tiles):
                planes[pl.ds(s * pitch + at, count), :] = piece[
                    :, s * 128 : (s + 1) * 128
                ].astype(f32)
            at += count

    def body(i, carry):
        found = [
            planes[pl.ds(spots[step * step_boxes + i * unroll + u], 8, stride=pitch), :]
            for u in range(unroll)
        ]
        for u in range(unroll):
            got[pl.ds(i * unroll + u, 8, stride=depth), :] = found[u]
        return carry

    lax.fori_loop(0, step_boxes // unroll, body, 0)
    for s in range(tiles):
        o_ref[0, :, s * 128 : (s + 1) * 128] = got[pl.ds(s * depth, step_boxes), :].astype(bf16)


def gathered(spots, pieces):
    steps = boxes // step_boxes
    return call(
        gather_kernel,
        spots,
        tuple(pieces),
        [whole(p) for p in pieces],
        pl.BlockSpec((1, step_boxes, wide), lambda i, s: (i // steps, i % steps, 0)),
        jax.ShapeDtypeStruct((3, boxes, wide), bf16),
        grid=(3 * steps,),
        scratch=[
            pltpu.VMEM((8 * pitch, 128), f32),
            pltpu.VMEM((8 * (step_boxes + 8), 128), f32),
        ],
        cost=8000000000,
    )


def far_kernel(sc, far, sources, send, keep, result):
    c = sc[0]
    total = None
    for k in range(3):
        term = lax.dot_general(
            far[k], sources[k][:, :rows], (((1,), (1,)), ((), ())), preferred_element_type=f32
        )
        total = term if total is None else total + term
    result[...] = total
    for x in (0, 1):
        first = result[pl.ds(share * 2 * x, share), :]
        second = result[pl.ds(share * (2 * x + 1), share), :]
        keep[x] = jnp.where(c == 0, first, second)
        send[x] = jnp.where(c == 0, second, first).astype(bf16)


def far_partial(sc, far, sources, start, count, width=256):
    shape = (2, share, count)
    spec = pl.BlockSpec((2, share, width), lambda i, s: (0, 0, i))
    skip = start // width
    return call(
        far_kernel,
        sc,
        (far, sources),
        [whole(far), pl.BlockSpec((3, width, wide), lambda i, s: (0, skip + i, 0))],
        [spec, spec],
        [jax.ShapeDtypeStruct(shape, bf16), jax.ShapeDtypeStruct(shape, f32)],
        grid=(count // width,),
        scratch=[pltpu.VMEM((rows, width), f32)],
        cost=3 * 2 * rows * rows * count,
    )


def local(leaf_density, upward_ops, far_ops, downward_ops, fine_lists, coarse_lists):
    groups = lax.axis_size("space")
    rep = lax.axis_index("rep")
    l, c = rep // 2, rep % 2
    sc = jnp.stack([c, l]).astype(jnp.int32)
    hop = functools.partial(lax.ppermute, axis_name=both, perm=one_hop(groups))
    zswap = functools.partial(lax.ppermute, axis_name=both, perm=across(groups, 2))
    cswap = functools.partial(lax.ppermute, axis_name=both, perm=across(groups, 1))

    def at(i):
        return jnp.reshape(i, (1,)).astype(jnp.int32)

    mine = [turned(leaf_density, at(c * chunks + i), 1, chunk) for i in range(chunks)]
    other = turned(leaf_density, at((1 - c) * 2), 2, 256)
    a = [hop(m) for m in mine]
    b = [zswap(x) for x in a]
    a_o = [cswap(x) for x in a]
    b_o = [cswap(x) for x in b]

    up_ops = jnp.transpose(upward_ops, (1, 0, 2)).reshape(8 * share, rows)
    down_ops = jnp.transpose(downward_ops, (1, 0, 2)).reshape(8 * share, rows)
    up = parent_rows(sc, up_ops, mine, other)
    own = jnp.concatenate([up, zswap(up)], 1)
    ca = hop(own)
    cb = zswap(ca)
    own_o = cswap(own)
    cab_o = cswap(jnp.concatenate([ca, cb], 1))
    send, keep = coarse_partial(
        sc, coarse_lists.reshape(1, 3 * parents), far_ops, own, ca, cb, own_o, cab_o
    )
    part = keep + cswap(send).astype(f32)
    check = (part + zswap(part.astype(bf16)).astype(f32)).astype(bf16)
    spread = downward(sc, down_ops, check, cswap(check))

    which, side, offset = fine_lists >> 10, (fine_lists >> 9) & 1, fine_lists & (half - 1)
    base = jnp.where(which == 1, 0, jnp.where((which == 0) == (l == 0), 2, 4))
    spots = (base + jnp.where(side == c, 0, 1)) * half + offset
    picked = gathered(spots.reshape(-1), [*mine, other, *a, *a_o, *b, *b_o])

    outs = []
    for start in (0, half):
        send, keep = far_partial(sc, far_ops, picked, start, half)
        part = keep + cswap(send).astype(f32)
        away = lax.dynamic_index_in_dim(part, 1 - l, 0, keepdims=False).astype(bf16)
        here = lax.dynamic_index_in_dim(part, l, 0, keepdims=False)
        outs.append(
            here + zswap(away).astype(f32) + lax.slice_in_dim(spread, start, start + half, axis=1)
        )
    return jnp.concatenate(outs, 1).astype(bf16)


def solution(mesh):
    return jax.shard_map(
        local,
        mesh=mesh,
        in_specs=(
            P(None, "space"),
            P(None, "rep", None),
            P("rep", None, None),
            P(None, "rep", None),
            P("rep", "space"),
            P("rep", "space"),
        ),
        out_specs=P("rep", "space"),
        check_vma=False,
    )
```

time: 224 us -> 121 us (0.54)
  waiting for transfers between devices: 91.3 us -> 31.8 us
  local copies, waits for them, and re-layouts: 61.3 us -> 3.4 us
  Pallas kernels: 0 us -> 51.2 us
  matrix products: 27.2 us -> 0 us
  other arithmetic: 9.82 us -> 5.01 us
  starting transfers between devices: 32.5 us -> 28.7 us
    pallas_call x0 -> x9, Pallas kernels: none -> 51.2 us  [call(): pl.pallas_call(kernel, grid_spec=pltpu.PrefetchScalarGridSpec(num_scalar_...]
    gather x6 -> x0, local copies, waits for them, and re-layouts: 35.1 us -> none  [translate(): picked = jnp.take(sources, lists[offset], axis=1)]
    ppermute x4 -> x20, waiting for transfers between devices: 66.2 us -> 31.8 us  [the longest x2 12.2 us: local(): b = [zswap(x) for x in a]]
    dot_general x8 -> x0, matrix products: 27.2 us -> none  [the longest x6 21.8 us: translate(): jnp.dot(operators[offset], picked, preferred_element_type=jnp.float32)]
    all_to_all x3 -> x0, waiting for transfers between devices: 25.1 us -> none  [the longest x1 14.5 us: sum_at_owner(): lax.all_to_all(blocks, axis, split_axis=0, concat_axis=0, tiled=True)]
    all_to_all x3 -> x0, starting transfers between devices: 13 us -> none  [the longest x2 8.56 us: sent_to_all(): lax.all_to_all(jnp.broadcast_to(x[None], (peers, *x.shape)), axis, 0, 0,...]
    reshape x4 -> x1, local copies, waits for them, and re-layouts: 10.1 us -> 0.69 us  [local(): picked = gathered(spots.reshape(-1), [*mine, other, *a, *a_o, *b, *b_o])]
    ppermute x4 -> x20, starting transfers between devices: 19.5 us -> 28.7 us  [the longest x2 11.1 us: local(): a = [hop(m) for m in mine]]
  transfers between devices with their start and end apart: 7 -> 20, of which waited for: 3 -> 6; matrix products, arithmetic and copies ran while one was open for 43% -> 3% of each run, Pallas kernels for 0% -> 32%
where the time goes in v1:
time: 121 us; the launch traced here: 120 us
  Pallas kernels  51.2 us (42%)
  waiting for transfers between devices  31.8 us (26%)
  starting transfers between devices  28.7 us (24%)
  other arithmetic  5.01 us (4%)
  local copies, waits for them, and re-layouts  3.4 us (3%)
    pallas_call x9, Pallas kernels, call(): pl.pallas_call(kernel, grid_spec=pltpu.PrefetchScalarGridSpec(num_scalar_...  51.2 us
    ppermute x2, waiting for transfers between devices, local(): b = [zswap(x) for x in a]  12.2 us
    ppermute x1, waiting for transfers between devices, local(): ca = hop(own)  11.6 us
    ppermute x2, starting transfers between devices, local(): a = [hop(m) for m in mine]  11.1 us
    ppermute x1, starting transfers between devices, local(): ca = hop(own)  8.14 us
    ppermute x1, waiting for transfers between devices, local(): cb = zswap(ca)  4.79 us
    ppermute x2, starting transfers between devices, local(): zswap(away).astype(f32)  2.98 us
    ppermute x2, waiting for transfers between devices, local(): zswap(away).astype(f32)  2.93 us
  transfers between devices with their start and end apart: 20, of which 6 were waited for; matrix products, arithmetic and copies ran while one was open for 3% of the time, Pallas kernels for 32%

profile of v1, /device:TPU:24, one launch (start us, length us, event | category | flops | bytes accessed | tf_op | source)
XLA Modules:
  0.0 120.3 jit_solution(13522142738480445870)
XLA Ops:
  0.0 2.0 %shard_map.65.refs_1_ = bf16[256,896]{1,0:T(8,128)(2,1)} custom-call(s32[1]{0:T(128)} %bitcast.3.first, bf16[888,1024]{1,0:T(8,128)(2,1)} %x_ref.5), custom_call_target="tpu_custom_call" | custom-call | flops 1024000000 | bytes 1818624 | tf_op jit(solution)/shard_map/pallas_call | solution.py:34
  2.0 2.0 %shard_map.64.refs_0_ = bf16[256,896]{1,0:T(8,128)(2,1)} custom-call(s32[1]{0:T(128)} %bitcast.2.first, bf16[888,1024]{1,0:T(8,128)(2,1)} %x_ref.5), custom_call_target="tpu_custom_call" | custom-call | flops 1024000000 | bytes 1818624 | tf_op jit(solution)/shard_map/pallas_call | solution.py:34
  4.0 2.2 %shard_map.66.refs_2_.other = bf16[512,896]{1,0:T(8,128)(2,1)} custom-call(s32[1]{0:T(128)} %bitcast.4.first, bf16[888,1024]{1,0:T(8,128)(2,1)} %x_ref.5), custom_call_target="tpu_custom_call" | custom-call | flops 2048000000 | bytes 1818624 | tf_op jit(solution)/shard_map/pallas_call | solution.py:34
  6.2 0.6 pad_add_fusion.sc
  6.8 6.1 %shard_map.69 = bf16[222,128]{1,0:T(8,128)(2,1)} custom-call(s32[2]{0:T(128)} %pad_add_fusion.sc, bf16[1776,888]{1,0:T(8,128)(2,1)} %bitcast.30, bf16[512,896]{1,0:T(8,128)(2,1)} %shard_map.66.refs_2_.other, bf16[256,896]{1,0:T(8,128)(2,1)} %shard_map.64.refs_0_, bf16[256,896]{1,0:T(8,128)(2,1)} %shard_map.65.refs_1_), custom_call_target="tpu_custom_call" | custom-call | flops 4000000000 | bytes 4989184 | tf_op jit(solution)/shard_map/pallas_call | solution.py:34
  13.0 1.9 %collective-permute-start.10 = (bf16[222,128]{1,0:T(8,128)(2,1)}, bf16[222,128]{1,0:T(8,128)(2,1)S(1)}, u32[]{:S(2)}, u32[]{:S(2)}) collective-permute-start(bf16[222,128]{1,0:T(8,128)(2,1)} %shard_map.69), channel_id=1, source_target_pairs={{0,2},{1,3},{2,0},{3,1},{4,6},{5,7},{6,4},{7,5},{8,10},{9,11},{10,... | collective-permute-start | bytes 170504 | tf_op jit(solution)/shard_map/ppermute | solution.py:323
  14.9 9.2 %collective-permute-start.1 = (bf16[256,896]{1,0:T(8,128)(2,1)S(1)}, bf16[256,896]{1,0:T(8,128)(2,1)S(1)}, u32[]{:S(2)}, u32[]{:S(2)}) collective-permute-start(bf16[256,896]{1,0:T(8,128)(2,1)S(1)} %copy-done.9), channel_id=1, source_target_pairs={{2,4},{3,5},{6,8},{7,9},{10,12},{11,13},{14,16},{15,17},{18,20},{1... | collective-permute-start | bytes 1376264 | tf_op jit(solution)/shard_map/ppermute | solution.py:315
  24.1 1.9 %collective-permute-start = (bf16[256,896]{1,0:T(8,128)(2,1)S(1)}, bf16[256,896]{1,0:T(8,128)(2,1)S(1)}, u32[]{:S(2)}, u32[]{:S(2)}) collective-permute-start(bf16[256,896]{1,0:T(8,128)(2,1)S(1)} %copy-done.10), channel_id=1, source_target_pairs={{2,4},{3,5},{6,8},{7,9},{10,12},{11,13},{14,16},{15,17},{18,20},{1... | collective-permute-start | bytes 1376264 | tf_op jit(solution)/shard_map/ppermute | solution.py:315
  26.0 0.8 pad_maximum_fusion.2.own
  26.9 8.1 %collective-permute-start.11 = (bf16[222,256]{1,0:T(8,128)(2,1)S(1)}, bf16[222,256]{1,0:T(8,128)(2,1)S(1)}, u32[]{:S(2)}, u32[]{:S(2)}) collective-permute-start(bf16[222,256]{1,0:T(8,128)(2,1)S(1)} %pad_maximum_fusion.2.own), channel_id=1, source_target_pairs={{2,4},{3,5},{6,8},{7,9},{10,12},{11,13},{14,16},{15,17},{18,20},{1... | collective-permute-start | bytes 341000 | tf_op jit(solution)/shard_map/ppermute | solution.py:324
  35.0 11.6 %collective-permute-done.11.a = bf16[222,256]{1,0:T(8,128)(2,1)S(1)} collective-permute-done((bf16[222,256]{1,0:T(8,128)(2,1)S(1)}, bf16[222,256]{1,0:T(8,128)(2,1)S(1)}, u32[]{:S(2)}, u32[]{:S(2)}) %collective-permute-start.11) | collective-permute-done | bytes 113696 | tf_op jit(solution)/shard_map/ppermute | solution.py:324
  46.6 4.8 %collective-permute-done.12.b = bf16[222,256]{1,0:T(8,128)(2,1)S(1)} collective-permute-done((bf16[222,256]{1,0:T(8,128)(2,1)S(1)}, bf16[222,256]{1,0:T(8,128)(2,1)S(1)}, u32[]{:S(2)}, u32[]{:S(2)}) %collective-permute-start.12) | collective-permute-done | bytes 113696 | tf_op jit(solution)/shard_map/ppermute | solution.py:325
  51.7 2.0 %collective-permute-start.4 = (bf16[256,896]{1,0:T(8,128)(2,1)S(1)}, bf16[256,896]{1,0:T(8,128)(2,1)S(1)}, u32[]{:S(2)}, u32[]{:S(2)}) collective-permute-start(bf16[256,896]{1,0:T(8,128)(2,1)S(1)} %collective-permute-done.refs_3_), channel_id=1, source_target_pairs={{0,2},{1,3},{2,0},{3,1},{4,6},{5,7},{6,4},{7,5},{8,10},{9,11},{10,... | collective-permute-start | bytes 1376264 | tf_op jit(solution)/shard_map/ppermute | solution.py:316
  53.7 0.6 copy.9
  54.3 0.5 collective-permute-start.3
  55.7 6.2 %shard_map.70 = (bf16[448,128]{1,0:T(8,128)(2,1)}, f32[448,128]{1,0:T(8,128)}) custom-call(s32[2]{0:T(128)} %pad_add_fusion.sc, s32[1,384]{1,0:T(1,128)} %bitcast.29, bf16[3,888,888]{2,1,0:T(8,128)(2,1)} %far.5, bf16[222,256]{1,0:T(8,128)(2,1)} %copy-done.5, bf16[222,256]{1,0:T(8,128)(2,1)} %copy-done.3, bf16[222,256]{1,0:T(8,128)(2,1)} %copy-done.4, ...), custom_call_target="tpu_custom_call" | custom-call | flops 3000000000 | bytes 5414784 | tf_op jit(solution)/shard_map/pallas_call | solution.py:34
  62.1 2.9 %collective-permute-done.5.refs_8_ = bf16[256,896]{1,0:T(8,128)(2,1)S(1)} collective-permute-done((bf16[256,896]{1,0:T(8,128)(2,1)S(1)}, bf16[256,896]{1,0:T(8,128)(2,1)S(1)}, u32[]{:S(2)}, u32[]{:S(2)}) %collective-permute-start.5) | collective-permute-done | bytes 458784 | tf_op jit(solution)/shard_map/ppermute | solution.py:316
  65.0 9.3 %collective-permute-done.4.refs_7_ = bf16[256,896]{1,0:T(8,128)(2,1)S(1)} collective-permute-done((bf16[256,896]{1,0:T(8,128)(2,1)S(1)}, bf16[256,896]{1,0:T(8,128)(2,1)S(1)}, u32[]{:S(2)}, u32[]{:S(2)}) %collective-permute-start.4) | collective-permute-done | bytes 458784 | tf_op jit(solution)/shard_map/ppermute | solution.py:316
  74.3 0.7 reshape.23.spots
  75.0 1.0 fusion.4
  76.0 0.6 collective-permute-start.16
  76.6 0.7 copy-done.15
  77.5 11.3 %shard_map.67.sources = bf16[3,1024,896]{2,1,0:T(8,128)(2,1)} custom-call(s32[3072]{0:T(1024)} %reshape.23.spots, bf16[256,896]{1,0:T(8,128)(2,1)} %shard_map.64.refs_0_, bf16[256,896]{1,0:T(8,128)(2,1)} %shard_map.65.refs_1_, bf16[512,896]{1,0:T(8,128)(2,1)} %shard_map.66.refs_2_.other, bf16[256,896]{1,0:T(8,128)(2,1)} %copy-done.12, ...), custom_call_target="tpu_custom_call" | custom-call | flops 8000000000 | bytes 5505024 | tf_op jit(solution)/shard_map/pallas_call | solution.py:34
  88.8 7.7 %shard_map.72 = (bf16[2,222,512]{2,1,0:T(8,128)(2,1)}, f32[2,222,512]{2,1,0:T(8,128)}) custom-call(s32[2]{0:T(128)} %pad_add_fusion.sc, bf16[3,888,888]{2,1,0:T(8,128)(2,1)} %far.5, bf16[3,1024,896]{2,1,0:T(8,128)(2,1)} %shard_map.67.sources), custom_call_target="tpu_custom_call" | custom-call | flops 2422407168 | bytes 10236288 | tf_op jit(solution)/shard_map/pallas_call | solution.py:34
  96.7 7.7 %shard_map.68 = (bf16[2,222,512]{2,1,0:T(8,128)(2,1)}, f32[2,222,512]{2,1,0:T(8,128)}) custom-call(s32[2]{0:T(128)} %pad_add_fusion.sc, bf16[3,888,888]{2,1,0:T(8,128)(2,1)} %far.5, bf16[3,1024,896]{2,1,0:T(8,128)(2,1)} %shard_map.67.sources), custom_call_target="tpu_custom_call" | custom-call | flops 2422407168 | bytes 10236288 | tf_op jit(solution)/shard_map/pallas_call | solution.py:34
  105.3 1.8 %collective-permute-start.19 = (bf16[222,512]{1,0:T(8,128)(2,1)S(1)}, bf16[222,512]{1,0:T(8,128)(2,1)S(1)}, u32[]{:S(2)}, u32[]{:S(2)}) collective-permute-start(bf16[222,512]{1,0:T(8,128)(2,1)S(1)} %fusion.3), channel_id=1, source_target_pairs={{0,2},{1,3},{2,0},{3,1},{4,6},{5,7},{6,4},{7,5},{8,10},{9,11},{10,... | collective-permute-start | bytes 681992 | tf_op jit(solution)/shard_map/ppermute | solution.py:347
  107.3 1.2 collective-permute-start.9
  108.5 0.6 copy-done.17
  109.1 6.0 %shard_map.71 = f32[222,1024]{1,0:T(8,128)} custom-call(s32[2]{0:T(128)} %pad_add_fusion.sc, bf16[1776,888]{1,0:T(8,128)(2,1)} %bitcast.31, bf16[448,128]{1,0:T(8,128)(2,1)} %copy-done.6, bf16[448,128]{1,0:T(8,128)(2,1)} %copy-done.17), custom_call_target="tpu_custom_call" | custom-call | flops 3000000000 | bytes 3383552 | tf_op jit(solution)/shard_map/pallas_call | solution.py:34
  115.1 2.9 %collective-permute-done.9 = bf16[222,512]{1,0:T(8,128)(2,1)S(1)} collective-permute-done((bf16[222,512]{1,0:T(8,128)(2,1)S(1)}, bf16[222,512]{1,0:T(8,128)(2,1)S(1)}, u32[]{:S(2)}, u32[]{:S(2)}) %collective-permute-start.9) | collective-permute-done | bytes 227360 | tf_op jit(solution)/shard_map/ppermute | solution.py:347
  118.0 1.4 %fusion.1 = (bf16[222,512]{1,0:T(8,128)(2,1)S(1)}, bf16[222,512]{1,0:T(8,128)(2,1)S(1)}) fusion(f32[222,1024]{1,0:T(8,128)} %shard_map.71, bf16[222,512]{1,0:T(8,128)(2,1)S(1)} %collective-permute-done.9, f32[2,222,512]{2,1,0:T(8,128)S(1)} %convert_add_fusion.1, s32[]{:T(128)S(6)} %select_n.36, bf16[222,512]{1,0:T(8,128)(2,1)S(1)} %collective-permute-done.19, ...), kind=kLoop, calls=%fused_computation.5 | loop fusion | flops 909312 | bytes 2727940 | tf_op jit(solution)/shard_map/convert
  119.4 0.8 pad_maximum_fusion
  (69 shorter events, 2.8 us)
Async XLA Ops:
  6.8 8.1 %copy-start.9 = (bf16[256,896]{1,0:T(8,128)(2,1)S(1)}, bf16[256,896]{1,0:T(8,128)(2,1)}, u32[]{:S(2)}) copy-start(bf16[256,896]{1,0:T(8,128)(2,1)} %shard_map.65.refs_1_) | copy-start | bytes 1376260
  6.8 17.3 %copy-start.10 = (bf16[256,896]{1,0:T(8,128)(2,1)S(1)}, bf16[256,896]{1,0:T(8,128)(2,1)}, u32[]{:S(2)}) copy-start(bf16[256,896]{1,0:T(8,128)(2,1)} %shard_map.64.refs_0_) | copy-start | bytes 1376260
  6.8 46.9 %copy-start.8 = (s32[3,128]{1,0:T(4,128)S(1)}, s32[3,128]{1,0:T(4,128)}, u32[]{:S(2)}) copy-start(s32[3,128]{1,0:T(4,128)} %param.11) | copy-start | bytes 4612
  13.0 13.1 %collective-permute-start.10 = (bf16[222,128]{1,0:T(8,128)(2,1)}, bf16[222,128]{1,0:T(8,128)(2,1)S(1)}, u32[]{:S(2)}, u32[]{:S(2)}) collective-permute-start(bf16[222,128]{1,0:T(8,128)(2,1)} %shard_map.69), channel_id=1, source_target_pairs={{0,2},{1,3},{2,0},{3,1},{4,6},{5,7},{6,4},{7,5},{8,10},{9,11},{10,... | collective-permute-start | bytes 170504 | tf_op jit(solution)/shard_map/ppermute | solution.py:323
  14.9 36.7 %collective-permute-start.1 = (bf16[256,896]{1,0:T(8,128)(2,1)S(1)}, bf16[256,896]{1,0:T(8,128)(2,1)S(1)}, u32[]{:S(2)}, u32[]{:S(2)}) collective-permute-start(bf16[256,896]{1,0:T(8,128)(2,1)S(1)} %copy-done.9), channel_id=1, source_target_pairs={{2,4},{3,5},{6,8},{7,9},{10,12},{11,13},{14,16},{15,17},{18,20},{1... | collective-permute-start | bytes 1376264 | tf_op jit(solution)/shard_map/ppermute | solution.py:315
  24.1 27.6 %collective-permute-start = (bf16[256,896]{1,0:T(8,128)(2,1)S(1)}, bf16[256,896]{1,0:T(8,128)(2,1)S(1)}, u32[]{:S(2)}, u32[]{:S(2)}) collective-permute-start(bf16[256,896]{1,0:T(8,128)(2,1)S(1)} %copy-done.10), channel_id=1, source_target_pairs={{2,4},{3,5},{6,8},{7,9},{10,12},{11,13},{14,16},{15,17},{18,20},{1... | collective-permute-start | bytes 1376264 | tf_op jit(solution)/shard_map/ppermute | solution.py:315
  26.9 28.3 %copy-start.5 = (bf16[222,256]{1,0:T(8,128)(2,1)}, bf16[222,256]{1,0:T(8,128)(2,1)S(1)}, u32[]{:S(2)}) copy-start(bf16[222,256]{1,0:T(8,128)(2,1)S(1)} %pad_maximum_fusion.2.own) | copy-start | bytes 340996
  26.9 19.7 %collective-permute-start.11 = (bf16[222,256]{1,0:T(8,128)(2,1)S(1)}, bf16[222,256]{1,0:T(8,128)(2,1)S(1)}, u32[]{:S(2)}, u32[]{:S(2)}) collective-permute-start(bf16[222,256]{1,0:T(8,128)(2,1)S(1)} %pad_maximum_fusion.2.own), channel_id=1, source_target_pairs={{2,4},{3,5},{6,8},{7,9},{10,12},{11,13},{14,16},{15,17},{18,20},{1... | collective-permute-start | bytes 341000 | tf_op jit(solution)/shard_map/ppermute | solution.py:324
  46.6 8.6 %copy-start.3 = (bf16[222,256]{1,0:T(8,128)(2,1)}, bf16[222,256]{1,0:T(8,128)(2,1)S(1)}, u32[]{:S(2)}) copy-start(bf16[222,256]{1,0:T(8,128)(2,1)S(1)} %collective-permute-done.11.a) | copy-start | bytes 340996
  46.6 4.8 %collective-permute-start.12 = (bf16[222,256]{1,0:T(8,128)(2,1)S(1)}, bf16[222,256]{1,0:T(8,128)(2,1)S(1)}, u32[]{:S(2)}, u32[]{:S(2)}) collective-permute-start(bf16[222,256]{1,0:T(8,128)(2,1)S(1)} %collective-permute-done.11.a), channel_id=1, source_target_pairs={{0,2},{1,3},{2,0},{3,1},{4,6},{5,7},{6,4},{7,5},{8,10},{9,11},{10,... | collective-permute-start | bytes 341000 | tf_op jit(solution)/shard_map/ppermute | solution.py:325
  51.4 3.8 %copy-start.4 = (bf16[222,256]{1,0:T(8,128)(2,1)}, bf16[222,256]{1,0:T(8,128)(2,1)S(1)}, u32[]{:S(2)}) copy-start(bf16[222,256]{1,0:T(8,128)(2,1)S(1)} %collective-permute-done.12.b) | copy-start | bytes 340996
  51.4 3.8 %collective-permute-start.14 = (bf16[222,512]{1,0:T(8,128)(2,1)S(1)}, bf16[222,512]{1,0:T(8,128)(2,1)}, u32[]{:S(2)}, u32[]{:S(2)}) collective-permute-start(bf16[222,512]{1,0:T(8,128)(2,1)S(1)} %pad_maximum_fusion.1), channel_id=1, source_target_pairs={{0,1},{1,0},{2,3},{3,2},{4,5},{5,4},{6,7},{7,6},{8,9},{9,8},{10,11... | collective-permute-start | bytes 681992 | tf_op jit(solution)/shard_map/ppermute | solution.py:327
  51.5 10.3 %copy-start.11 = (bf16[256,896]{1,0:T(8,128)(2,1)}, bf16[256,896]{1,0:T(8,128)(2,1)S(1)}, u32[]{:S(2)}) copy-start(bf16[256,896]{1,0:T(8,128)(2,1)S(1)} %collective-permute-done.1.refs_4_) | copy-start | bytes 1376260
  51.6 13.5 %collective-permute-start.5 = (bf16[256,896]{1,0:T(8,128)(2,1)S(1)}, bf16[256,896]{1,0:T(8,128)(2,1)S(1)}, u32[]{:S(2)}, u32[]{:S(2)}) collective-permute-start(bf16[256,896]{1,0:T(8,128)(2,1)S(1)} %collective-permute-done.1.refs_4_), channel_id=1, source_target_pairs={{0,2},{1,3},{2,0},{3,1},{4,6},{5,7},{6,4},{7,5},{8,10},{9,11},{10,... | collective-permute-start | bytes 1376264 | tf_op jit(solution)/shard_map/ppermute | solution.py:316
  51.7 10.2 %copy-start.12 = (bf16[256,896]{1,0:T(8,128)(2,1)}, bf16[256,896]{1,0:T(8,128)(2,1)S(1)}, u32[]{:S(2)}) copy-start(bf16[256,896]{1,0:T(8,128)(2,1)S(1)} %collective-permute-done.refs_3_) | copy-start | bytes 1376260
  51.7 22.6 %collective-permute-start.4 = (bf16[256,896]{1,0:T(8,128)(2,1)S(1)}, bf16[256,896]{1,0:T(8,128)(2,1)S(1)}, u32[]{:S(2)}, u32[]{:S(2)}) collective-permute-start(bf16[256,896]{1,0:T(8,128)(2,1)S(1)} %collective-permute-done.refs_3_), channel_id=1, source_target_pairs={{0,2},{1,3},{2,0},{3,1},{4,6},{5,7},{6,4},{7,5},{8,10},{9,11},{10,... | collective-permute-start | bytes 1376264 | tf_op jit(solution)/shard_map/ppermute | solution.py:316
  53.7 1.3 %collective-permute-start.13 = (bf16[222,256]{1,0:T(8,128)(2,1)S(1)}, bf16[222,256]{1,0:T(8,128)(2,1)S(1)}, u32[]{:S(2)}, u32[]{:S(2)}) collective-permute-start(bf16[222,256]{1,0:T(8,128)(2,1)S(1)} %pad_maximum_fusion.2.own), channel_id=1, source_target_pairs={{0,1},{1,0},{2,3},{3,2},{4,5},{5,4},{6,7},{7,6},{8,9},{9,8},{10,11... | collective-permute-start | bytes 341000 | tf_op jit(solution)/shard_map/ppermute | solution.py:326
  54.3 22.2 %collective-permute-start.3 = (bf16[256,896]{1,0:T(8,128)(2,1)S(1)}, bf16[256,896]{1,0:T(8,128)(2,1)S(1)}, u32[]{:S(2)}, u32[]{:S(2)}) collective-permute-start(bf16[256,896]{1,0:T(8,128)(2,1)S(1)} %collective-permute-done.1.refs_4_), channel_id=1, source_target_pairs={{0,1},{1,0},{2,3},{3,2},{4,5},{5,4},{6,7},{7,6},{8,9},{9,8},{10,11... | collective-permute-start | bytes 1376264 | tf_op jit(solution)/shard_map/ppermute | solution.py:317
  55.0 21.5 %collective-permute-start.2 = (bf16[256,896]{1,0:T(8,128)(2,1)S(1)}, bf16[256,896]{1,0:T(8,128)(2,1)S(1)}, u32[]{:S(2)}, u32[]{:S(2)}) collective-permute-start(bf16[256,896]{1,0:T(8,128)(2,1)S(1)} %collective-permute-done.refs_3_), channel_id=1, source_target_pairs={{0,1},{1,0},{2,3},{3,2},{4,5},{5,4},{6,7},{7,6},{8,9},{9,8},{10,11... | collective-permute-start | bytes 1376264 | tf_op jit(solution)/shard_map/ppermute | solution.py:317
  55.7 18.6 %copy-start.7 = (s32[3,1024]{1,0:T(4,128)S(1)}, s32[3,1024]{1,0:T(4,128)}, u32[]{:S(2)}) copy-start(s32[3,1024]{1,0:T(4,128)} %param.10) | copy-start | bytes 36868
  61.8 13.2 %collective-permute-start.15 = (bf16[448,128]{1,0:T(8,128)(2,1)}, bf16[448,128]{1,0:T(8,128)(2,1)S(1)}, u32[]{:S(2)}, u32[]{:S(2)}) collective-permute-start(bf16[448,128]{1,0:T(8,128)(2,1)} %get-tuple-element.14), channel_id=1, source_target_pairs={{0,1},{1,0},{2,3},{3,2},{4,5},{5,4},{6,7},{7,6},{8,9},{9,8},{10,11... | collective-permute-start | bytes 344072 | tf_op jit(solution)/shard_map/ppermute | solution.py:331
  65.0 11.6 %copy-start.13 = (bf16[256,896]{1,0:T(8,128)(2,1)}, bf16[256,896]{1,0:T(8,128)(2,1)S(1)}, u32[]{:S(2)}) copy-start(bf16[256,896]{1,0:T(8,128)(2,1)S(1)} %collective-permute-done.5.refs_8_) | copy-start | bytes 1376260
  65.0 11.6 %collective-permute-start.7 = (bf16[256,896]{1,0:T(8,128)(2,1)S(1)}, bf16[256,896]{1,0:T(8,128)(2,1)}, u32[]{:S(2)}, u32[]{:S(2)}) collective-permute-start(bf16[256,896]{1,0:T(8,128)(2,1)S(1)} %collective-permute-done.5.refs_8_), channel_id=1, source_target_pairs={{0,1},{1,0},{2,3},{3,2},{4,5},{5,4},{6,7},{7,6},{8,9},{9,8},{10,11... | collective-permute-start | bytes 1376264 | tf_op jit(solution)/shard_map/ppermute | solution.py:318
  74.3 2.3 %collective-permute-start.6 = (bf16[256,896]{1,0:T(8,128)(2,1)S(1)}, bf16[256,896]{1,0:T(8,128)(2,1)}, u32[]{:S(2)}, u32[]{:S(2)}) collective-permute-start(bf16[256,896]{1,0:T(8,128)(2,1)S(1)} %collective-permute-done.4.refs_7_), channel_id=1, source_target_pairs={{0,1},{1,0},{2,3},{3,2},{4,5},{5,4},{6,7},{7,6},{8,9},{9,8},{10,11... | collective-permute-start | bytes 1376264 | tf_op jit(solution)/shard_map/ppermute | solution.py:318
  76.0 28.7 %collective-permute-start.16 = (bf16[448,128]{1,0:T(8,128)(2,1)S(1)}, bf16[448,128]{1,0:T(8,128)(2,1)S(1)}, u32[]{:S(2)}, u32[]{:S(2)}) collective-permute-start(bf16[448,128]{1,0:T(8,128)(2,1)S(1)} %fusion.4), channel_id=1, source_target_pairs={{0,2},{1,3},{2,0},{3,1},{4,6},{5,7},{6,4},{7,5},{8,10},{9,11},{10,... | collective-permute-start | bytes 344072 | tf_op jit(solution)/shard_map/ppermute | solution.py:332
  96.4 8.2 %copy-start.2 = (f32[448,128]{1,0:T(8,128)S(1)}, f32[448,128]{1,0:T(8,128)}, u32[]{:S(2)}) copy-start(f32[448,128]{1,0:T(8,128)} %get-tuple-element.13) | copy-start | bytes 688132
  96.4 8.6 %copy-start.1 = (f32[2,222,512]{2,1,0:T(8,128)S(1)}, f32[2,222,512]{2,1,0:T(8,128)}, u32[]{:S(2)}) copy-start(f32[2,222,512]{2,1,0:T(8,128)} %get-tuple-element.15) | copy-start | bytes 2727940
  96.4 8.6 %collective-permute-start.18 = (bf16[2,222,512]{2,1,0:T(8,128)(2,1)}, bf16[2,222,512]{2,1,0:T(8,128)(2,1)S(1)}, u32[]{:S(2)}, u32[]{:S(2)}) collective-permute-start(bf16[2,222,512]{2,1,0:T(8,128)(2,1)} %get-tuple-element.16), channel_id=1, source_target_pairs={{0,1},{1,0},{2,3},{3,2},{4,5},{5,4},{6,7},{7,6},{8,9},{9,8},{10,11... | collective-permute-start | bytes 1363976 | tf_op jit(solution)/shard_map/ppermute | solution.py:343
  104.4 2.7 %collective-permute-start.8 = (bf16[2,222,512]{2,1,0:T(8,128)(2,1)}, bf16[2,222,512]{2,1,0:T(8,128)(2,1)S(1)}, u32[]{:S(2)}, u32[]{:S(2)}) collective-permute-start(bf16[2,222,512]{2,1,0:T(8,128)(2,1)} %get-tuple-element.12), channel_id=1, source_target_pairs={{0,1},{1,0},{2,3},{3,2},{4,5},{5,4},{6,7},{7,6},{8,9},{9,8},{10,11... | collective-permute-start | bytes 1363976 | tf_op jit(solution)/shard_map/ppermute | solution.py:343
  104.7 3.8 %collective-permute-start.17 = (bf16[448,128]{1,0:T(8,128)(2,1)S(1)}, bf16[448,128]{1,0:T(8,128)(2,1)S(1)}, u32[]{:S(2)}, u32[]{:S(2)}) collective-permute-start(bf16[448,128]{1,0:T(8,128)(2,1)S(1)} %add_convert_fusion.mine), channel_id=1, source_target_pairs={{0,1},{1,0},{2,3},{3,2},{4,5},{5,4},{6,7},{7,6},{8,9},{9,8},{10,11... | collective-permute-start | bytes 344072 | tf_op jit(solution)/shard_map/ppermute | solution.py:333
  105.3 9.8 %collective-permute-start.19 = (bf16[222,512]{1,0:T(8,128)(2,1)S(1)}, bf16[222,512]{1,0:T(8,128)(2,1)S(1)}, u32[]{:S(2)}, u32[]{:S(2)}) collective-permute-start(bf16[222,512]{1,0:T(8,128)(2,1)S(1)} %fusion.3), channel_id=1, source_target_pairs={{0,2},{1,3},{2,0},{3,1},{4,6},{5,7},{6,4},{7,5},{8,10},{9,11},{10,... | collective-permute-start | bytes 681992 | tf_op jit(solution)/shard_map/ppermute | solution.py:347
  107.3 10.7 %collective-permute-start.9 = (bf16[222,512]{1,0:T(8,128)(2,1)S(1)}, bf16[222,512]{1,0:T(8,128)(2,1)S(1)}, u32[]{:S(2)}, u32[]{:S(2)}) collective-permute-start(bf16[222,512]{1,0:T(8,128)(2,1)S(1)} %fusion.2), channel_id=1, source_target_pairs={{0,2},{1,3},{2,0},{3,1},{4,6},{5,7},{6,4},{7,5},{8,10},{9,11},{10,... | collective-permute-start | bytes 681992 | tf_op jit(solution)/shard_map/ppermute | solution.py:347
  (7 other events, 11.8 us)

commit v2 on v1

--- a/solution.py
+++ b/solution.py
@@ -16,12 +16,12 @@
 share = 222
 chunks = 2
 chunk = half // chunks
-window = 6 * half
-vmem = pltpu.CompilerParams(vmem_limit_bytes=56 << 20)
+early = 6 * half - 2 * chunk
+vmem = pltpu.CompilerParams(vmem_limit_bytes=24 << 20)
 
 
 def one_hop(groups):
-    up = [(4 * s + 2 + c, 4 * (s + 1) + c) for s in range(groups - 1) for c in (0, 1)]
+    up = [(4 * s + 2 + c, 4 * ((s + 1) % groups) + c) for s in range(groups) for c in (0, 1)]
     return up + [(j, i) for i, j in up]
 
 
@@ -29,8 +29,7 @@
     return [(4 * s + r, 4 * s + (r ^ flip)) for s in range(groups) for r in range(4)]
 
 
-def call(kernel, scalars, args, in_specs, out_specs, out_shape, grid=(1,), scratch=(), cost=0):
-    moved = sum(a.size * a.dtype.itemsize for a in args)
+def call(kernel, scalars, args, in_specs, out_specs, out_shape, grid=(1,), scratch=()):
     return pl.pallas_call(
         kernel,
         grid_spec=pltpu.PrefetchScalarGridSpec(
@@ -42,13 +41,12 @@
         ),
         out_shape=out_shape,
         compiler_params=vmem,
-        cost_estimate=pl.CostEstimate(flops=cost, bytes_accessed=moved, transcendentals=0),
+        cost_estimate=pl.CostEstimate(flops=0, bytes_accessed=0, transcendentals=0),
     )(scalars, *args)
 
 
 def whole(a):
-    zeros = (0,) * a.ndim
-    return pl.BlockSpec(a.shape, lambda *_: zeros)
+    return pl.BlockSpec(memory_space=pltpu.VMEM)
 
 
 def turn_kernel(first, x_ref, o_ref):
@@ -66,7 +64,6 @@
         pl.BlockSpec((width, wide), lambda i, s: (i, 0)),
         jax.ShapeDtypeStruct((count * width, wide), bf16),
         grid=(count,),
-        cost=count * width * 4000000,
     )
 
 
@@ -116,7 +113,6 @@
             pltpu.VMEM((tiles * 8 * share, 128), f32),
             pltpu.VMEM((tiles * boxes, 128), f32),
         ],
-        cost=4000000000,
     )
 
 
@@ -124,12 +120,11 @@
     c, l = sc[0], sc[1]
     wanted = lists[...]
     count = wanted.shape[1]
-    near = jnp.where(l == 0, 0, 2 * parents)
     spot = lax.broadcasted_iota(jnp.int32, (parents, count), 0)
     hot = jnp.concatenate(
         [
             (spot == wanted - base).astype(f32).astype(bf16)
-            for base in (parents, near, 2 * parents - near)
+            for base in (parents, sc[2], sc[3])
         ],
         0,
     )
@@ -174,7 +169,6 @@
         [spec, spec],
         [jax.ShapeDtypeStruct(shape, bf16), jax.ShapeDtypeStruct(shape, f32)],
         scratch=[pltpu.VMEM((rows, 3 * parents), f32), pltpu.VMEM((wide, parents), f32)],
-        cost=3000000000,
     )
 
 
@@ -210,11 +204,10 @@
             pltpu.VMEM((wide, parents), bf16),
             pltpu.VMEM((2 * boxes, 128), f32),
         ],
-        cost=3000000000,
-    )
-
-
-pitch, step_boxes, unroll = window + 8, 512, 32
+    )
+
+
+pitch, step_boxes, unroll = early + 8, 512, 32
 
 
 def gather_kernel(spots, *refs):
@@ -232,6 +225,8 @@
                     :, s * 128 : (s + 1) * 128
                 ].astype(f32)
             at += count
+        for s in range(tiles):
+            planes[pl.ds(s * pitch + early, 8), :] = jnp.zeros((8, 128), f32)
 
     def body(i, carry):
         found = [
@@ -261,16 +256,30 @@
             pltpu.VMEM((8 * pitch, 128), f32),
             pltpu.VMEM((8 * (step_boxes + 8), 128), f32),
         ],
-        cost=8000000000,
-    )
-
-
-def far_kernel(sc, far, sources, send, keep, result):
+    )
+
+
+def far_kernel(sc, far, sources, lists, late, late_o, send, keep, result):
     c = sc[0]
+    width = sources.shape[1]
+    spot = lax.broadcasted_iota(jnp.int32, (width, 128), 1).astype(f32)
+    late_boxes = jnp.concatenate([late[...], late_o[...]], 0)
     total = None
     for k in range(3):
+        wanted = jnp.broadcast_to(lists[k].astype(f32), (128, width)).T
+        hot = jnp.concatenate(
+            [
+                (wanted == spot + float(base)).astype(f32).astype(bf16)
+                for base in range(0, 2 * chunk, 128)
+            ],
+            1,
+        )
+        found = jnp.dot(hot, late_boxes, preferred_element_type=f32) + sources[k].astype(f32)
         term = lax.dot_general(
-            far[k], sources[k][:, :rows], (((1,), (1,)), ((), ())), preferred_element_type=f32
+            far[k],
+            found.astype(bf16)[:, :rows],
+            (((1,), (1,)), ((), ())),
+            preferred_element_type=f32,
         )
         total = term if total is None else total + term
     result[...] = total
@@ -281,28 +290,48 @@
         send[x] = jnp.where(c == 0, second, first).astype(bf16)
 
 
-def far_partial(sc, far, sources, start, count, width=256):
+def far_partial(sc, far, sources, lists, late, late_o, start, count, width=256):
     shape = (2, share, count)
     spec = pl.BlockSpec((2, share, width), lambda i, s: (0, 0, i))
     skip = start // width
     return call(
         far_kernel,
         sc,
-        (far, sources),
-        [whole(far), pl.BlockSpec((3, width, wide), lambda i, s: (0, skip + i, 0))],
+        (far, sources, lists, late, late_o),
+        [
+            whole(far),
+            pl.BlockSpec((3, width, wide), lambda i, s: (0, skip + i, 0)),
+            pl.BlockSpec((3, 1, width), lambda i, s: (0, 0, skip + i)),
+            whole(late),
+            whole(late_o),
+        ],
         [spec, spec],
         [jax.ShapeDtypeStruct(shape, bf16), jax.ShapeDtypeStruct(shape, f32)],
         grid=(count // width,),
         scratch=[pltpu.VMEM((rows, width), f32)],
-        cost=3 * 2 * rows * rows * count,
-    )
+    )
+
+
+def after(x, *others):
+    return lax.optimization_barrier((x, *others))[0]
 
 
 def local(leaf_density, upward_ops, far_ops, downward_ops, fine_lists, coarse_lists):
     groups = lax.axis_size("space")
-    rep = lax.axis_index("rep")
-    l, c = rep // 2, rep % 2
-    sc = jnp.stack([c, l]).astype(jnp.int32)
+    group, rep = lax.axis_index("space"), lax.axis_index("rep")
+    l, c = rep >> 1, rep & 1
+    no_previous, no_next = group == 0, group == groups - 1
+    nowhere = -16384
+    base_previous = jnp.where(no_previous, nowhere, 0)
+    base_next = jnp.where(no_next, nowhere, 2 * parents)
+    sc = jnp.stack(
+        [
+            c,
+            l,
+            jnp.where(l == 0, base_previous, base_next),
+            jnp.where(l == 0, base_next, base_previous),
+        ]
+    ).astype(jnp.int32)
     hop = functools.partial(lax.ppermute, axis_name=both, perm=one_hop(groups))
     zswap = functools.partial(lax.ppermute, axis_name=both, perm=across(groups, 2))
     cswap = functools.partial(lax.ppermute, axis_name=both, perm=across(groups, 1))
@@ -310,43 +339,65 @@
     def at(i):
         return jnp.reshape(i, (1,)).astype(jnp.int32)
 
-    mine = [turned(leaf_density, at(c * chunks + i), 1, chunk) for i in range(chunks)]
-    other = turned(leaf_density, at((1 - c) * 2), 2, 256)
-    a = [hop(m) for m in mine]
-    b = [zswap(x) for x in a]
-    a_o = [cswap(x) for x in a]
-    b_o = [cswap(x) for x in b]
-
     up_ops = jnp.transpose(upward_ops, (1, 0, 2)).reshape(8 * share, rows)
     down_ops = jnp.transpose(downward_ops, (1, 0, 2)).reshape(8 * share, rows)
+
+    mine = [turned(leaf_density, at(c * chunks + i), 1, chunk) for i in range(chunks)]
+    a = [hop(m) for m in mine]
+    other = turned(leaf_density, at((1 - c) * 2), 2, 256)
     up = parent_rows(sc, up_ops, mine, other)
+    first = after(a[0], up)
+    b = [zswap(first)]
+    a_o = [cswap(first)]
     own = jnp.concatenate([up, zswap(up)], 1)
     ca = hop(own)
+    own_o = cswap(own)
+    second = after(a[1], own)
+    b.append(zswap(second))
+    a_o.append(cswap(second))
     cb = zswap(ca)
-    own_o = cswap(own)
+    b_o = [cswap(x) for x in b]
     cab_o = cswap(jnp.concatenate([ca, cb], 1))
-    send, keep = coarse_partial(
-        sc, coarse_lists.reshape(1, 3 * parents), far_ops, own, ca, cb, own_o, cab_o
-    )
-    part = keep + cswap(send).astype(f32)
-    check = (part + zswap(part.astype(bf16)).astype(f32)).astype(bf16)
-    spread = downward(sc, down_ops, check, cswap(check))
 
     which, side, offset = fine_lists >> 10, (fine_lists >> 9) & 1, fine_lists & (half - 1)
-    base = jnp.where(which == 1, 0, jnp.where((which == 0) == (l == 0), 2, 4))
-    spots = (base + jnp.where(side == c, 0, 1)) * half + offset
-    picked = gathered(spots.reshape(-1), [*mine, other, *a, *a_o, *b, *b_o])
-
-    outs = []
-    for start in (0, half):
-        send, keep = far_partial(sc, far_ops, picked, start, half)
+    outside = ((which == 0) & no_previous) | ((which == 2) & no_next)
+    direct = (which == 0) == (l == 0)
+    theirs = (side != c).astype(jnp.int32)
+    is_late = (which != 1) & ~direct & (offset >= half - chunk)
+    spots = jnp.where(
+        which == 1,
+        theirs * half + offset,
+        jnp.where(
+            direct,
+            2 * half + theirs * half + offset,
+            4 * half + theirs * (half - chunk) + offset,
+        ),
+    )
+    spots = jnp.where(outside | is_late, early, spots)
+    late_lists = jnp.where(is_late & ~outside, theirs * chunk + offset - (half - chunk), -1)
+    late_lists = late_lists.reshape(3, 1, boxes)
+    picked = gathered(spots.reshape(-1), [*mine, other, *a, *a_o, b[0], b_o[0]])
+
+    def summed(send, keep):
         part = keep + cswap(send).astype(f32)
         away = lax.dynamic_index_in_dim(part, 1 - l, 0, keepdims=False).astype(bf16)
         here = lax.dynamic_index_in_dim(part, l, 0, keepdims=False)
-        outs.append(
-            here + zswap(away).astype(f32) + lax.slice_in_dim(spread, start, start + half, axis=1)
-        )
-    return jnp.concatenate(outs, 1).astype(bf16)
+        return here, zswap(away), away
+
+    late = (b[1], b_o[1])
+    send, keep = far_partial(sc, far_ops, picked, late_lists, *late, 0, half)
+    left = summed(send, keep)
+    send, keep = coarse_partial(
+        after(sc, send), coarse_lists.reshape(1, 3 * parents), far_ops, own, ca, cb, own_o, cab_o
+    )
+    part = keep + cswap(send).astype(f32)
+    send, keep = far_partial(after(sc, part, left[2]), far_ops, picked, late_lists, *late, half, half)
+    right = summed(send, keep)
+    check = (part + zswap(part.astype(bf16)).astype(f32)).astype(bf16)
+    spread = downward(sc, down_ops, check, cswap(check))
+
+    fine = jnp.concatenate([here + there.astype(f32) for here, there, _ in (left, right)], 1)
+    return (fine + spread).astype(bf16)
 
 
 def solution(mesh):

time: 121 us -> 122 us (level)
  the two profiles are of different devices: /device:TPU:24 before, /device:TPU:1 now
where the time goes in v2:
time: 122 us; the launch traced here: 121 us
  Pallas kernels  36.4 us (30%)
  waiting for transfers between devices  35.3 us (29%)
  starting transfers between devices  31.9 us (26%)
  local copies, waits for them, and re-layouts  14.4 us (12%)
  other arithmetic  3.3 us (3%)
    pallas_call x9, Pallas kernels, call(): pl.pallas_call(kernel, grid_spec=pltpu.PrefetchScalarGridSpec(num_scalar_...  36.4 us
    unnamed x45, local copies, waits for them, and re-layouts  13.5 us
    ppermute x2, starting transfers between devices, local(): a = [hop(m) for m in mine]  11.2 us
    ppermute x2, waiting for transfers between devices, local(): a = [hop(m) for m in mine]  9.18 us
    ppermute x2, waiting for transfers between devices, summed(): return (here, zswap(away), away)  8.92 us
    ppermute x1, starting transfers between devices, local(): ca = hop(own)  6.89 us
    ppermute x2, starting transfers between devices, local(): b_o = [cswap(x) for x in b]  6.05 us
    ppermute x1, waiting for transfers between devices, local(): b.append(zswap(second))  5.93 us
  transfers between devices with their start and end apart: 20, of which 9 were waited for; matrix products, arithmetic and copies ran while one was open for 3% of the time, Pallas kernels for 30%

profile of v2, /device:TPU:1, one launch (start us, length us, event | category | flops | bytes accessed | tf_op | source)
XLA Modules:
  0.0 121.5 jit_solution(18099125665694381999)
XLA Ops:
  0.0 1.5 %copy-done.3 = bf16[888,1024]{1,0:T(8,128)(2,1)S(1)} copy-done((bf16[888,1024]{1,0:T(8,128)(2,1)S(1)}, bf16[888,1024]{1,0:T(8,128)(2,1)}, u32[]{:S(2)}) %copy-start.3) | copy-done | bytes 1818648
  1.7 11.1 %collective-permute-start.1 = (bf16[256,896]{1,0:T(8,128)(2,1)S(1)}, bf16[256,896]{1,0:T(8,128)(2,1)}, u32[]{:S(2)}, u32[]{:S(2)}) collective-permute-start(bf16[256,896]{1,0:T(8,128)(2,1)S(1)} %shard_map.65.refs_1_), channel_id=1, source_target_pairs={{2,4},{3,5},{6,8},{7,9},{10,12},{11,13},{14,16},{15,17},{18,20},{1... | collective-permute-start | bytes 1376264 | tf_op jit(solution)/shard_map/ppermute | solution.py:346
  12.8 1.0 shard_map.64.refs_0_
  14.5 1.9 %copy-done.5 = bf16[8,222,888]{2,0,1:T(8,128)(2,1)S(1)} copy-done((bf16[8,222,888]{2,0,1:T(8,128)(2,1)S(1)}, bf16[8,222,888]{2,0,1:T(8,128)(2,1)}, u32[]{:S(2)}) %copy-start.5) | copy-done | bytes 3154200
  16.4 3.9 %shard_map.67 = bf16[222,128]{1,0:T(8,128)(2,1)S(1)} custom-call(s32[4]{0:T(128)S(1)} %pad_add_fusion.sc, bf16[1776,888]{1,0:T(8,128)(2,1)S(1)} %bitcast.28, bf16[512,896]{1,0:T(8,128)(2,1)S(1)} %shard_map.66.other.refs_2_, bf16[256,896]{1,0:T(8,128)(2,1)} %shard_map.64.refs_0_, bf16[256,896]{1,0:T(8,128)(2,1)S(1)} %shard_map.65.refs_1_), custom_call_target="tpu_custom_call" | custom-call | tf_op jit(solution)/shard_map/pallas_call | solution.py:33
  20.4 3.4 %collective-permute-done.3 = bf16[222,128]{1,0:T(8,128)(2,1)S(1)} collective-permute-done((bf16[222,128]{1,0:T(8,128)(2,1)S(1)}, bf16[222,128]{1,0:T(8,128)(2,1)S(1)}, u32[]{:S(2)}, u32[]{:S(2)}) %collective-permute-start.3) | collective-permute-done | bytes 56864 | tf_op jit(solution)/shard_map/ppermute | solution.py:352
  23.8 9.2 %collective-permute-done.refs_3_ = bf16[256,896]{1,0:T(8,128)(2,1)} collective-permute-done((bf16[256,896]{1,0:T(8,128)(2,1)}, bf16[256,896]{1,0:T(8,128)(2,1)}, u32[]{:S(2)}, u32[]{:S(2)}) %collective-permute-start) | collective-permute-done | bytes 458784 | tf_op jit(solution)/shard_map/ppermute | solution.py:346
  33.0 1.5 %collective-permute-start.7 = (bf16[256,896]{1,0:T(8,128)(2,1)}, bf16[256,896]{1,0:T(8,128)(2,1)S(1)}, u32[]{:S(2)}, u32[]{:S(2)}) collective-permute-start(bf16[256,896]{1,0:T(8,128)(2,1)} %collective-permute-done.1.refs_4_), channel_id=1, source_target_pairs={{0,2},{1,3},{2,0},{3,1},{4,6},{5,7},{6,4},{7,5},{8,10},{9,11},{10,... | collective-permute-start | bytes 1376264 | tf_op jit(solution)/shard_map/ppermute | solution.py:356
  34.5 1.8 %collective-permute-start.4 = (bf16[256,896]{1,0:T(8,128)(2,1)}, bf16[256,896]{1,0:T(8,128)(2,1)S(1)}, u32[]{:S(2)}, u32[]{:S(2)}) collective-permute-start(bf16[256,896]{1,0:T(8,128)(2,1)} %collective-permute-done.1.refs_4_), channel_id=1, source_target_pairs={{0,1},{1,0},{2,3},{3,2},{4,5},{5,4},{6,7},{7,6},{8,9},{9,8},{10,11... | collective-permute-start | bytes 1376264 | tf_op jit(solution)/shard_map/ppermute | solution.py:357
  36.3 6.9 %collective-permute-start.11 = (bf16[222,256]{1,0:T(8,128)(2,1)S(1)}, bf16[222,256]{1,0:T(8,128)(2,1)S(1)}, u32[]{:S(2)}, u32[]{:S(2)}) collective-permute-start(bf16[222,256]{1,0:T(8,128)(2,1)S(1)} %pad_maximum_fusion.1.own), channel_id=1, source_target_pairs={{2,4},{3,5},{6,8},{7,9},{10,12},{11,13},{14,16},{15,17},{18,20},{1... | collective-permute-start | bytes 341000 | tf_op jit(solution)/shard_map/ppermute | solution.py:353
  44.0 3.9 %collective-permute-start.6 = (bf16[256,896]{1,0:T(8,128)(2,1)S(1)}, bf16[256,896]{1,0:T(8,128)(2,1)}, u32[]{:S(2)}, u32[]{:S(2)}) collective-permute-start(bf16[256,896]{1,0:T(8,128)(2,1)S(1)} %collective-permute-done.5.refs_7_), channel_id=1, source_target_pairs={{0,1},{1,0},{2,3},{3,2},{4,5},{5,4},{6,7},{7,6},{8,9},{9,8},{10,11... | collective-permute-start | bytes 1376264 | tf_op jit(solution)/shard_map/ppermute | solution.py:359
  47.9 5.9 %collective-permute-done.7.late = bf16[256,896]{1,0:T(8,128)(2,1)S(1)} collective-permute-done((bf16[256,896]{1,0:T(8,128)(2,1)}, bf16[256,896]{1,0:T(8,128)(2,1)S(1)}, u32[]{:S(2)}, u32[]{:S(2)}) %collective-permute-start.7) | collective-permute-done | bytes 458784 | tf_op jit(solution)/shard_map/ppermute | solution.py:356
  53.9 2.1 %collective-permute-start.8 = (bf16[256,896]{1,0:T(8,128)(2,1)S(1)}, bf16[256,896]{1,0:T(8,128)(2,1)S(1)}, u32[]{:S(2)}, u32[]{:S(2)}) collective-permute-start(bf16[256,896]{1,0:T(8,128)(2,1)S(1)} %collective-permute-done.7.late), channel_id=1, source_target_pairs={{0,1},{1,0},{2,3},{3,2},{4,5},{5,4},{6,7},{7,6},{8,9},{9,8},{10,11... | collective-permute-start | bytes 1376264 | tf_op jit(solution)/shard_map/ppermute | solution.py:359
  56.0 4.7 %collective-permute-done.12.b = bf16[222,256]{1,0:T(8,128)(2,1)S(1)} collective-permute-done((bf16[222,256]{1,0:T(8,128)(2,1)S(1)}, bf16[222,256]{1,0:T(8,128)(2,1)S(1)}, u32[]{:S(2)}, u32[]{:S(2)}) %collective-permute-start.12) | collective-permute-done | bytes 113696 | tf_op jit(solution)/shard_map/ppermute | solution.py:358
  63.2 1.2 copy-done.14
  64.4 8.9 %shard_map.68.sources = bf16[3,1024,896]{2,1,0:T(8,128)(2,1)S(1)} custom-call(s32[3072]{0:T(1024)S(1)} %reshape.26.spots, bf16[256,896]{1,0:T(8,128)(2,1)} %shard_map.64.refs_0_, bf16[256,896]{1,0:T(8,128)(2,1)S(1)} %shard_map.65.refs_1_, bf16[512,896]{1,0:T(8,128)(2,1)S(1)} %shard_map.66.other.refs_2_, bf16[256,896]{1,0:T(8,128)(2,1)} %collective-permute-done.refs_3_, ...), custom_call_target="tpu_custom_call" | custom-call | tf_op jit(solution)/shard_map/pallas_call | solution.py:33
  73.4 7.3 %shard_map.69 = (bf16[2,222,512]{2,1,0:T(8,128)(2,1)S(1)}, f32[2,222,512]{2,1,0:T(8,128)S(1)}) custom-call(s32[4]{0:T(128)S(1)} %pad_add_fusion.sc, bf16[3,888,888]{2,1,0:T(8,128)(2,1)S(1)} %bitcast.27, bf16[3,1024,896]{2,1,0:T(8,128)(2,1)S(1)} %shard_map.68.sources, s32[3,1,1024]{2,1,0:T(1,128)S(1)} %reshape.31.lists, ...), custom_call_target="tpu_custom_call" | custom-call | tf_op jit(solution)/shard_map/pallas_call | solution.py:33
  81.3 3.7 %shard_map.70 = (bf16[448,128]{1,0:T(8,128)(2,1)S(1)}, f32[448,128]{1,0:T(8,128)S(1)}) custom-call(s32[4]{0:T(128)S(1)} %pad_add_fusion.sc, s32[1,384]{1,0:T(1,128)S(1)} %bitcast.30, bf16[3,888,888]{2,1,0:T(8,128)(2,1)S(1)} %bitcast.27, bf16[222,256]{1,0:T(8,128)(2,1)S(1)} %pad_maximum_fusion.1.own, bf16[222,256]{1,0:T(8,128)(2,1)S(1)} %collective-permute-done.11.a, ...), custom_call_target="tpu_custom_call" | custom-call | tf_op jit(solution)/shard_map/pallas_call | solution.py:33
  85.2 1.3 %collective-permute-done.15 = bf16[448,128]{1,0:T(8,128)(2,1)S(1)} collective-permute-done((bf16[448,128]{1,0:T(8,128)(2,1)S(1)}, bf16[448,128]{1,0:T(8,128)(2,1)S(1)}, u32[]{:S(2)}, u32[]{:S(2)}) %collective-permute-start.15) | collective-permute-done | bytes 114720 | tf_op jit(solution)/shard_map/ppermute | solution.py:393
  87.8 2.6 %copy-done.1 = bf16[3,1024,896]{2,1,0:T(8,128)(2,1)S(1)} copy-done((bf16[3,1024,896]{2,1,0:T(8,128)(2,1)S(1)}, bf16[3,1024,896]{2,1,0:T(8,128)(2,1)}, u32[]{:S(2)}) %copy-start.1) | copy-done | bytes 5505048
  90.4 2.4 %copy-done.2 = bf16[3,888,888]{2,1,0:T(8,128)(2,1)S(1)} copy-done((bf16[3,888,888]{2,1,0:T(8,128)(2,1)S(1)}, bf16[3,888,888]{2,1,0:T(8,128)(2,1)}, u32[]{:S(2)}) %copy-start.2) | copy-done | bytes 4731288
  92.7 1.0 copy-done.8
  93.7 1.0 copy-done.10
  94.8 7.9 %shard_map.71 = (bf16[2,222,512]{2,1,0:T(8,128)(2,1)}, f32[2,222,512]{2,1,0:T(8,128)S(1)}) custom-call(s32[4]{0:T(128)S(1)} %pad_add_fusion.sc, bf16[3,888,888]{2,1,0:T(8,128)(2,1)S(1)} %copy-done.2, bf16[3,1024,896]{2,1,0:T(8,128)(2,1)S(1)} %copy-done.1, s32[3,1,1024]{2,1,0:T(1,128)S(1)} %reshape.31.lists, bf16[256,896]{1,0:T(8,128)(2,1)S(1)} %copy-done.8, ...), custom_call_target="tpu_custom_call" | custom-call | tf_op jit(solution)/shard_map/pallas_call | solution.py:33
  102.6 0.9 copy-done.11
  104.4 1.2 %collective-permute-done.19.other = bf16[448,128]{1,0:T(8,128)(2,1)S(1)} collective-permute-done((bf16[448,128]{1,0:T(8,128)(2,1)S(1)}, bf16[448,128]{1,0:T(8,128)(2,1)S(1)}, u32[]{:S(2)}, u32[]{:S(2)}) %collective-permute-start.19) | collective-permute-done | bytes 114720 | tf_op jit(solution)/shard_map/ppermute | solution.py:397
  105.7 2.9 %shard_map.72 = f32[222,1024]{1,0:T(8,128)S(1)} custom-call(s32[4]{0:T(128)S(1)} %pad_add_fusion.sc, bf16[1776,888]{1,0:T(8,128)(2,1)S(1)} %bitcast.29, bf16[448,128]{1,0:T(8,128)(2,1)S(1)} %add_convert_fusion.mine, bf16[448,128]{1,0:T(8,128)(2,1)S(1)} %collective-permute-done.19.other), custom_call_target="tpu_custom_call" | custom-call | tf_op jit(solution)/shard_map/pallas_call | solution.py:33
  108.6 1.6 %collective-permute-start.10 = (bf16[222,512]{1,0:T(8,128)(2,1)S(1)}, bf16[222,512]{1,0:T(8,128)(2,1)S(1)}, u32[]{:S(2)}, u32[]{:S(2)}) collective-permute-start(bf16[222,512]{1,0:T(8,128)(2,1)S(1)} %copy-done.17), channel_id=1, source_target_pairs={{0,2},{1,3},{2,0},{3,1},{4,6},{5,7},{6,4},{7,5},{8,10},{9,11},{10,... | collective-permute-start | bytes 681992 | tf_op jit(solution)/shard_map/ppermute | solution.py:385
  110.2 1.2 convert_add_fusion
  111.5 4.1 %collective-permute-done.10 = bf16[222,512]{1,0:T(8,128)(2,1)S(1)} collective-permute-done((bf16[222,512]{1,0:T(8,128)(2,1)S(1)}, bf16[222,512]{1,0:T(8,128)(2,1)S(1)}, u32[]{:S(2)}, u32[]{:S(2)}) %collective-permute-start.10) | collective-permute-done | bytes 227360 | tf_op jit(solution)/shard_map/ppermute | solution.py:385
  115.7 4.8 %collective-permute-done.17 = bf16[222,512]{1,0:T(8,128)(2,1)S(1)} collective-permute-done((bf16[222,512]{1,0:T(8,128)(2,1)S(1)}, bf16[222,512]{1,0:T(8,128)(2,1)S(1)}, u32[]{:S(2)}, u32[]{:S(2)}) %collective-permute-start.17) | collective-permute-done | bytes 227360 | tf_op jit(solution)/shard_map/ppermute | solution.py:385
  120.6 0.9 fusion
  (78 shorter events, 7.5 us)
Async XLA Ops:
  1.5 12.3 %copy-start.4 = (bf16[888,1024]{1,0:T(8,128)(2,1)S(1)}, bf16[888,1024]{1,0:T(8,128)(2,1)}, u32[]{:S(2)}) copy-start(bf16[888,1024]{1,0:T(8,128)(2,1)} %x_ref.5) | copy-start | bytes 5455876
  1.7 22.1 %collective-permute-start.1 = (bf16[256,896]{1,0:T(8,128)(2,1)S(1)}, bf16[256,896]{1,0:T(8,128)(2,1)}, u32[]{:S(2)}, u32[]{:S(2)}) collective-permute-start(bf16[256,896]{1,0:T(8,128)(2,1)S(1)} %shard_map.65.refs_1_), channel_id=1, source_target_pairs={{2,4},{3,5},{6,8},{7,9},{10,12},{11,13},{14,16},{15,17},{18,20},{1... | collective-permute-start | bytes 1376264 | tf_op jit(solution)/shard_map/ppermute | solution.py:346
  13.8 19.2 %collective-permute-start = (bf16[256,896]{1,0:T(8,128)(2,1)}, bf16[256,896]{1,0:T(8,128)(2,1)}, u32[]{:S(2)}, u32[]{:S(2)}) collective-permute-start(bf16[256,896]{1,0:T(8,128)(2,1)} %shard_map.64.refs_0_), channel_id=1, source_target_pairs={{2,4},{3,5},{6,8},{7,9},{10,12},{11,13},{14,16},{15,17},{18,20},{1... | collective-permute-start | bytes 1376264 | tf_op jit(solution)/shard_map/ppermute | solution.py:346
  13.8 49.3 %copy-start.18 = (s32[3,1024]{1,0:T(4,128)S(1)}, s32[3,1024]{1,0:T(4,128)}, u32[]{:S(2)}) copy-start(s32[3,1024]{1,0:T(4,128)} %param.10) | copy-start | bytes 36868
  20.3 3.5 %collective-permute-start.3 = (bf16[222,128]{1,0:T(8,128)(2,1)S(1)}, bf16[222,128]{1,0:T(8,128)(2,1)S(1)}, u32[]{:S(2)}, u32[]{:S(2)}) collective-permute-start(bf16[222,128]{1,0:T(8,128)(2,1)S(1)} %shard_map.67), channel_id=1, source_target_pairs={{0,2},{1,3},{2,0},{3,1},{4,6},{5,7},{6,4},{7,5},{8,10},{9,11},{10,... | collective-permute-start | bytes 170504 | tf_op jit(solution)/shard_map/ppermute | solution.py:352
  33.0 11.0 %collective-permute-start.5 = (bf16[256,896]{1,0:T(8,128)(2,1)}, bf16[256,896]{1,0:T(8,128)(2,1)S(1)}, u32[]{:S(2)}, u32[]{:S(2)}) collective-permute-start(bf16[256,896]{1,0:T(8,128)(2,1)} %collective-permute-done.refs_3_), channel_id=1, source_target_pairs={{0,2},{1,3},{2,0},{3,1},{4,6},{5,7},{6,4},{7,5},{8,10},{9,11},{10,... | collective-permute-start | bytes 1376264 | tf_op jit(solution)/shard_map/ppermute | solution.py:350
  33.0 20.8 %collective-permute-start.7 = (bf16[256,896]{1,0:T(8,128)(2,1)}, bf16[256,896]{1,0:T(8,128)(2,1)S(1)}, u32[]{:S(2)}, u32[]{:S(2)}) collective-permute-start(bf16[256,896]{1,0:T(8,128)(2,1)} %collective-permute-done.1.refs_4_), channel_id=1, source_target_pairs={{0,2},{1,3},{2,0},{3,1},{4,6},{5,7},{6,4},{7,5},{8,10},{9,11},{10,... | collective-permute-start | bytes 1376264 | tf_op jit(solution)/shard_map/ppermute | solution.py:356
  34.5 27.8 %collective-permute-start.4 = (bf16[256,896]{1,0:T(8,128)(2,1)}, bf16[256,896]{1,0:T(8,128)(2,1)S(1)}, u32[]{:S(2)}, u32[]{:S(2)}) collective-permute-start(bf16[256,896]{1,0:T(8,128)(2,1)} %collective-permute-done.1.refs_4_), channel_id=1, source_target_pairs={{0,1},{1,0},{2,3},{3,2},{4,5},{5,4},{6,7},{7,6},{8,9},{9,8},{10,11... | collective-permute-start | bytes 1376264 | tf_op jit(solution)/shard_map/ppermute | solution.py:357
  36.3 19.7 %collective-permute-start.11 = (bf16[222,256]{1,0:T(8,128)(2,1)S(1)}, bf16[222,256]{1,0:T(8,128)(2,1)S(1)}, u32[]{:S(2)}, u32[]{:S(2)}) collective-permute-start(bf16[222,256]{1,0:T(8,128)(2,1)S(1)} %pad_maximum_fusion.1.own), channel_id=1, source_target_pairs={{2,4},{3,5},{6,8},{7,9},{10,12},{11,13},{14,16},{15,17},{18,20},{1... | collective-permute-start | bytes 341000 | tf_op jit(solution)/shard_map/ppermute | solution.py:353
  43.2 20.0 %collective-permute-start.2 = (bf16[256,896]{1,0:T(8,128)(2,1)}, bf16[256,896]{1,0:T(8,128)(2,1)}, u32[]{:S(2)}, u32[]{:S(2)}) collective-permute-start(bf16[256,896]{1,0:T(8,128)(2,1)} %collective-permute-done.refs_3_), channel_id=1, source_target_pairs={{0,1},{1,0},{2,3},{3,2},{4,5},{5,4},{6,7},{7,6},{8,9},{9,8},{10,11... | collective-permute-start | bytes 1376264 | tf_op jit(solution)/shard_map/ppermute | solution.py:351
  44.0 19.2 %collective-permute-start.6 = (bf16[256,896]{1,0:T(8,128)(2,1)S(1)}, bf16[256,896]{1,0:T(8,128)(2,1)}, u32[]{:S(2)}, u32[]{:S(2)}) collective-permute-start(bf16[256,896]{1,0:T(8,128)(2,1)S(1)} %collective-permute-done.5.refs_7_), channel_id=1, source_target_pairs={{0,1},{1,0},{2,3},{3,2},{4,5},{5,4},{6,7},{7,6},{8,9},{9,8},{10,11... | collective-permute-start | bytes 1376264 | tf_op jit(solution)/shard_map/ppermute | solution.py:359
  53.8 19.5 %copy-start.7 = (bf16[256,896]{1,0:T(8,128)(2,1)}, bf16[256,896]{1,0:T(8,128)(2,1)S(1)}, u32[]{:S(2)}) copy-start(bf16[256,896]{1,0:T(8,128)(2,1)S(1)} %collective-permute-done.7.late) | copy-start | bytes 1376260
  53.9 19.5 %collective-permute-start.8 = (bf16[256,896]{1,0:T(8,128)(2,1)S(1)}, bf16[256,896]{1,0:T(8,128)(2,1)S(1)}, u32[]{:S(2)}, u32[]{:S(2)}) collective-permute-start(bf16[256,896]{1,0:T(8,128)(2,1)S(1)} %collective-permute-done.7.late), channel_id=1, source_target_pairs={{0,1},{1,0},{2,3},{3,2},{4,5},{5,4},{6,7},{7,6},{8,9},{9,8},{10,11... | collective-permute-start | bytes 1376264 | tf_op jit(solution)/shard_map/ppermute | solution.py:359
  56.0 4.7 %collective-permute-start.12 = (bf16[222,256]{1,0:T(8,128)(2,1)S(1)}, bf16[222,256]{1,0:T(8,128)(2,1)S(1)}, u32[]{:S(2)}, u32[]{:S(2)}) collective-permute-start(bf16[222,256]{1,0:T(8,128)(2,1)S(1)} %collective-permute-done.11.a), channel_id=1, source_target_pairs={{0,2},{1,3},{2,0},{3,1},{4,6},{5,7},{6,4},{7,5},{8,10},{9,11},{10,... | collective-permute-start | bytes 341000 | tf_op jit(solution)/shard_map/ppermute | solution.py:358
  60.7 20.6 %collective-permute-start.13 = (bf16[222,256]{1,0:T(8,128)(2,1)S(1)}, bf16[222,256]{1,0:T(8,128)(2,1)}, u32[]{:S(2)}, u32[]{:S(2)}) collective-permute-start(bf16[222,256]{1,0:T(8,128)(2,1)S(1)} %pad_maximum_fusion.1.own), channel_id=1, source_target_pairs={{0,1},{1,0},{2,3},{3,2},{4,5},{5,4},{6,7},{7,6},{8,9},{9,8},{10,11... | collective-permute-start | bytes 341000 | tf_op jit(solution)/shard_map/ppermute | solution.py:354
  63.1 18.2 %collective-permute-start.14 = (bf16[222,512]{1,0:T(8,128)(2,1)}, bf16[222,512]{1,0:T(8,128)(2,1)}, u32[]{:S(2)}, u32[]{:S(2)}) collective-permute-start(bf16[222,512]{1,0:T(8,128)(2,1)} %pad_maximum_fusion), channel_id=1, source_target_pairs={{0,1},{1,0},{2,3},{3,2},{4,5},{5,4},{6,7},{7,6},{8,9},{9,8},{10,11... | collective-permute-start | bytes 681992 | tf_op jit(solution)/shard_map/ppermute | solution.py:360
  63.2 10.2 %slice-start = ((s8[4773888]{0:T(1024)(128)(4,1)}), s8[4194304]{0:T(1024)(128)(4,1)S(1)}, s32[]{:S(2)}) async-start(s8[4773888]{0:T(1024)(128)(4,1)} %bitcast.26), calls=%async_computation | async-start | bytes 8388608
  63.2 10.2 %slice-start.1 = ((s8[4773888]{0:T(1024)(128)(4,1)}), s8[579584]{0:T(1024)(128)(4,1)S(1)}, s32[]{:S(2)}) async-start(s8[4773888]{0:T(1024)(128)(4,1)} %bitcast.26), calls=%async_computation.1 | async-start | bytes 1159168
  73.3 7.4 %copy-start = (bf16[3,1024,896]{2,1,0:T(8,128)(2,1)}, bf16[3,1024,896]{2,1,0:T(8,128)(2,1)S(1)}, u32[]{:S(2)}) copy-start(bf16[3,1024,896]{2,1,0:T(8,128)(2,1)S(1)} %shard_map.68.sources) | copy-start | bytes 16515076
  73.3 8.0 %copy-start.19 = (s32[3,128]{1,0:T(4,128)S(1)}, s32[3,128]{1,0:T(4,128)}, u32[]{:S(2)}) copy-start(s32[3,128]{1,0:T(4,128)} %param.11) | copy-start | bytes 4612
  73.4 7.3 %copy-start.9 = (bf16[256,896]{1,0:T(8,128)(2,1)}, bf16[256,896]{1,0:T(8,128)(2,1)S(1)}, u32[]{:S(2)}) copy-start(bf16[256,896]{1,0:T(8,128)(2,1)S(1)} %collective-permute-done.8.late_o) | copy-start | bytes 1376260
  80.7 5.9 %collective-permute-start.9 = (bf16[2,222,512]{2,1,0:T(8,128)(2,1)S(1)}, bf16[2,222,512]{2,1,0:T(8,128)(2,1)S(1)}, u32[]{:S(2)}, u32[]{:S(2)}) collective-permute-start(bf16[2,222,512]{2,1,0:T(8,128)(2,1)S(1)} %get-tuple-element.18), channel_id=1, source_target_pairs={{0,1},{1,0},{2,3},{3,2},{4,5},{5,4},{6,7},{7,6},{8,9},{9,8},{10,11... | collective-permute-start | bytes 1363976 | tf_op jit(solution)/shard_map/ppermute | solution.py:382
  85.1 1.4 %collective-permute-start.15 = (bf16[448,128]{1,0:T(8,128)(2,1)S(1)}, bf16[448,128]{1,0:T(8,128)(2,1)S(1)}, u32[]{:S(2)}, u32[]{:S(2)}) collective-permute-start(bf16[448,128]{1,0:T(8,128)(2,1)S(1)} %get-tuple-element.21), channel_id=1, source_target_pairs={{0,1},{1,0},{2,3},{3,2},{4,5},{5,4},{6,7},{7,6},{8,9},{9,8},{10,11... | collective-permute-start | bytes 344072 | tf_op jit(solution)/shard_map/ppermute | solution.py:393
  86.5 17.5 %collective-permute-start.18 = (bf16[448,128]{1,0:T(8,128)(2,1)S(1)}, bf16[448,128]{1,0:T(8,128)(2,1)S(1)}, u32[]{:S(2)}, u32[]{:S(2)}) collective-permute-start(bf16[448,128]{1,0:T(8,128)(2,1)S(1)} %get-tuple-element.25), channel_id=1, source_target_pairs={{0,2},{1,3},{2,0},{3,1},{4,6},{5,7},{6,4},{7,5},{8,10},{9,11},{10,... | collective-permute-start | bytes 344072 | tf_op jit(solution)/shard_map/ppermute | solution.py:396
  94.8 10.9 %copy-start.6 = (bf16[8,222,888]{2,0,1:T(8,128)(2,1)S(1)}, bf16[8,222,888]{2,0,1:T(8,128)(2,1)}, u32[]{:S(2)}) copy-start(bf16[8,222,888]{2,0,1:T(8,128)(2,1)} %param.9) | copy-start | bytes 9462532
  103.6 6.6 %collective-permute-start.16 = (bf16[2,222,512]{2,1,0:T(8,128)(2,1)}, bf16[2,222,512]{2,1,0:T(8,128)(2,1)}, u32[]{:S(2)}, u32[]{:S(2)}) collective-permute-start(bf16[2,222,512]{2,1,0:T(8,128)(2,1)} %get-tuple-element.24), channel_id=1, source_target_pairs={{0,1},{1,0},{2,3},{3,2},{4,5},{5,4},{6,7},{7,6},{8,9},{9,8},{10,11... | collective-permute-start | bytes 1363976 | tf_op jit(solution)/shard_map/ppermute | solution.py:382
  104.1 1.6 %collective-permute-start.19 = (bf16[448,128]{1,0:T(8,128)(2,1)S(1)}, bf16[448,128]{1,0:T(8,128)(2,1)S(1)}, u32[]{:S(2)}, u32[]{:S(2)}) collective-permute-start(bf16[448,128]{1,0:T(8,128)(2,1)S(1)} %add_convert_fusion.mine), channel_id=1, source_target_pairs={{0,1},{1,0},{2,3},{3,2},{4,5},{5,4},{6,7},{7,6},{8,9},{9,8},{10,11... | collective-permute-start | bytes 344072 | tf_op jit(solution)/shard_map/ppermute | solution.py:397
  104.4 4.2 %copy-start.17 = (bf16[222,512]{1,0:T(8,128)(2,1)S(1)}, bf16[222,512]{1,0:T(8,128)(2,1)}, u32[]{:S(2)}) copy-start(bf16[222,512]{1,0:T(8,128)(2,1)} %fusion.1) | copy-start | bytes 681988
  104.4 5.7 %copy-start.12 = (f32[2,222,512]{2,1,0:T(8,128)S(1)}, f32[2,222,512]{2,1,0:T(8,128)}, u32[]{:S(2)}) copy-start(f32[2,222,512]{2,1,0:T(8,128)} %copy-done.11) | copy-start | bytes 2727940
  105.7 9.9 %copy-start.16 = (f32[2,222,512]{2,1,0:T(8,128)S(1)}, f32[2,222,512]{2,1,0:T(8,128)}, u32[]{:S(2)}) copy-start(f32[2,222,512]{2,1,0:T(8,128)} %copy-done.15) | copy-start | bytes 2727940
  108.6 7.0 %collective-permute-start.10 = (bf16[222,512]{1,0:T(8,128)(2,1)S(1)}, bf16[222,512]{1,0:T(8,128)(2,1)S(1)}, u32[]{:S(2)}, u32[]{:S(2)}) collective-permute-start(bf16[222,512]{1,0:T(8,128)(2,1)S(1)} %copy-done.17), channel_id=1, source_target_pairs={{0,2},{1,3},{2,0},{3,1},{4,6},{5,7},{6,4},{7,5},{8,10},{9,11},{10,... | collective-permute-start | bytes 681992 | tf_op jit(solution)/shard_map/ppermute | solution.py:385
  111.4 9.1 %collective-permute-start.17 = (bf16[222,512]{1,0:T(8,128)(2,1)S(1)}, bf16[222,512]{1,0:T(8,128)(2,1)S(1)}, u32[]{:S(2)}, u32[]{:S(2)}) collective-permute-start(bf16[222,512]{1,0:T(8,128)(2,1)S(1)} %fusion.2), channel_id=1, source_target_pairs={{0,2},{1,3},{2,0},{3,1},{4,6},{5,7},{6,4},{7,5},{8,10},{9,11},{10,... | collective-permute-start | bytes 681992 | tf_op jit(solution)/shard_map/ppermute | solution.py:385
  (10 other events, 14.3 us)

commit v3 on v2

--- a/solution.py
+++ b/solution.py
@@ -17,7 +17,6 @@
 chunks = 2
 chunk = half // chunks
 early = 6 * half - 2 * chunk
-vmem = pltpu.CompilerParams(vmem_limit_bytes=24 << 20)
 
 
 def one_hop(groups):
@@ -29,7 +28,7 @@
     return [(4 * s + r, 4 * s + (r ^ flip)) for s in range(groups) for r in range(4)]
 
 
-def call(kernel, scalars, args, in_specs, out_specs, out_shape, grid=(1,), scratch=()):
+def call(kernel, scalars, args, in_specs, out_specs, out_shape, limit, grid=(1,), scratch=()):
     return pl.pallas_call(
         kernel,
         grid_spec=pltpu.PrefetchScalarGridSpec(
@@ -40,31 +39,63 @@
             scratch_shapes=scratch,
         ),
         out_shape=out_shape,
-        compiler_params=vmem,
+        compiler_params=pltpu.CompilerParams(vmem_limit_bytes=limit << 20),
         cost_estimate=pl.CostEstimate(flops=0, bytes_accessed=0, transcendentals=0),
     )(scalars, *args)
 
 
-def whole(a):
+def whole(a=None):
     return pl.BlockSpec(memory_space=pltpu.VMEM)
 
 
-def turn_kernel(first, x_ref, o_ref):
-    width = x_ref.shape[1]
-    tall = jnp.concatenate([x_ref[...].astype(f32), jnp.zeros((wide - rows, width), f32)], 0)
-    o_ref[...] = tall.T.astype(bf16)
-
-
-def turned(x, first, count, width):
-    return call(
-        turn_kernel,
-        first,
-        (x,),
-        [pl.BlockSpec((rows, width), lambda i, s: (0, s[0] + i))],
-        pl.BlockSpec((width, wide), lambda i, s: (i, 0)),
-        jax.ShapeDtypeStruct((count * width, wide), bf16),
-        grid=(count,),
-    )
+def turn_kernel(firsts, x_ref, *outs):
+    for n, o_ref in enumerate(outs):
+        for i in range(o_ref.shape[0] // 128):
+            part = x_ref[:, pl.ds(pl.multiple_of(firsts[n] + i * 128, 128), 128)].astype(f32)
+            tall = jnp.concatenate([part, jnp.zeros((wide - rows, 128), f32)], 0)
+            o_ref[pl.ds(i * 128, 128), :] = tall.T.astype(bf16)
+
+
+def turned(x, firsts, counts):
+    shapes = [jax.ShapeDtypeStruct((n, wide), bf16) for n in counts]
+    return call(turn_kernel, firsts, (x,), [whole()], [whole() for _ in counts], shapes, 8)
+
+
+def small(kernel, sc, args, shapes, limit=6):
+    shapes = [jax.ShapeDtypeStruct(*s) for s in shapes]
+    return call(kernel, sc, args, [whole() for _ in args], [whole() for _ in shapes], shapes, limit)
+
+
+def join_kernel(sc, *refs):
+    at = 0
+    for part in refs[:-1]:
+        refs[-1][:, at : at + part.shape[1]] = part[...]
+        at += part.shape[1]
+
+
+def joined(sc, *parts):
+    width = sum(p.shape[1] for p in parts)
+    return small(join_kernel, sc, parts, [((parts[0].shape[0], width), bf16)])[0]
+
+
+def split_kernel(sc, keep, got, here, away):
+    l = sc[1]
+    here[...] = keep[l] + got[l].astype(f32)
+    away[...] = (keep[1 - l] + got[1 - l].astype(f32)).astype(bf16)
+
+
+def add_kernel(sc, one, two, *outs):
+    total = one[...] + two[...].astype(f32)
+    for o_ref in outs:
+        o_ref[...] = total.astype(o_ref.dtype)
+
+
+def last_kernel(sc, spread, *refs):
+    o_ref, at = refs[-1], 0
+    for here, there in zip(refs[:-1:2], refs[1:-1:2]):
+        lanes = slice(at, at + here.shape[1])
+        o_ref[:, lanes] = (here[...] + there[...].astype(f32) + spread[:, lanes]).astype(bf16)
+        at += here.shape[1]
 
 
 def to_planes(src, dst, height):
@@ -107,8 +138,9 @@
         sc,
         args,
         [whole(a) for a in args],
-        pl.BlockSpec((share, parents), lambda *_: (0, 0)),
+        whole(),
         jax.ShapeDtypeStruct((share, parents), bf16),
+        14,
         scratch=[
             pltpu.VMEM((tiles * 8 * share, 128), f32),
             pltpu.VMEM((tiles * boxes, 128), f32),
@@ -118,7 +150,7 @@
 
 def coarse_kernel(sc, lists, far, own, a, b, own_o, ab_o, send, keep, picked, result):
     c, l = sc[0], sc[1]
-    wanted = lists[...]
+    wanted = jnp.concatenate([lists[k : k + 1, :] for k in range(3)], 1)
     count = wanted.shape[1]
     spot = lax.broadcasted_iota(jnp.int32, (parents, count), 0)
     hot = jnp.concatenate(
@@ -160,14 +192,14 @@
 def coarse_partial(sc, lists, far, own, a, b, own_o, ab_o):
     args = (lists, far, own, a, b, own_o, ab_o)
     shape = (wide // 2, parents)
-    spec = pl.BlockSpec(shape, lambda *_: (0, 0))
     return call(
         coarse_kernel,
         sc,
         args,
         [whole(x) for x in args],
-        [spec, spec],
+        [whole(), whole()],
         [jax.ShapeDtypeStruct(shape, bf16), jax.ShapeDtypeStruct(shape, f32)],
+        8,
         scratch=[pltpu.VMEM((rows, 3 * parents), f32), pltpu.VMEM((wide, parents), f32)],
     )
 
@@ -197,8 +229,9 @@
         sc,
         args,
         [whole(x) for x in args],
-        pl.BlockSpec((share, boxes), lambda *_: (0, 0)),
+        whole(),
         jax.ShapeDtypeStruct((share, boxes), f32),
+        12,
         scratch=[
             pltpu.VMEM((tiles * 8 * share, 128), f32),
             pltpu.VMEM((wide, parents), bf16),
@@ -214,6 +247,8 @@
     pieces, o_ref, planes, got = refs[:-3], refs[-3], refs[-2], refs[-1]
     step = pl.program_id(0)
     depth = step_boxes + 8
+    entry = step // (boxes // step_boxes)
+    first = (step % (boxes // step_boxes)) * step_boxes
 
     @pl.when(step == 0)
     def _():
@@ -230,7 +265,7 @@
 
     def body(i, carry):
         found = [
-            planes[pl.ds(spots[step * step_boxes + i * unroll + u], 8, stride=pitch), :]
+            planes[pl.ds(spots[entry, first + i * unroll + u], 8, stride=pitch), :]
             for u in range(unroll)
         ]
         for u in range(unroll):
@@ -239,19 +274,20 @@
 
     lax.fori_loop(0, step_boxes // unroll, body, 0)
     for s in range(tiles):
-        o_ref[0, :, s * 128 : (s + 1) * 128] = got[pl.ds(s * depth, step_boxes), :].astype(bf16)
+        spot = pl.ds(pl.multiple_of(step * step_boxes, step_boxes), step_boxes)
+        o_ref[spot, s * 128 : (s + 1) * 128] = got[pl.ds(s * depth, step_boxes), :].astype(bf16)
 
 
 def gathered(spots, pieces):
-    steps = boxes // step_boxes
     return call(
         gather_kernel,
         spots,
         tuple(pieces),
         [whole(p) for p in pieces],
-        pl.BlockSpec((1, step_boxes, wide), lambda i, s: (i // steps, i % steps, 0)),
-        jax.ShapeDtypeStruct((3, boxes, wide), bf16),
-        grid=(3 * steps,),
+        whole(),
+        jax.ShapeDtypeStruct((3 * boxes, wide), bf16),
+        16,
+        grid=(3 * boxes // step_boxes,),
         scratch=[
             pltpu.VMEM((8 * pitch, 128), f32),
             pltpu.VMEM((8 * (step_boxes + 8), 128), f32),
@@ -259,55 +295,55 @@
     )
 
 
-def far_kernel(sc, far, sources, lists, late, late_o, send, keep, result):
+def far_kernel(start, width, sc, far, sources, lists, late, late_o, send, keep, result):
     c = sc[0]
-    width = sources.shape[1]
     spot = lax.broadcasted_iota(jnp.int32, (width, 128), 1).astype(f32)
     late_boxes = jnp.concatenate([late[...], late_o[...]], 0)
-    total = None
-    for k in range(3):
-        wanted = jnp.broadcast_to(lists[k].astype(f32), (128, width)).T
-        hot = jnp.concatenate(
-            [
-                (wanted == spot + float(base)).astype(f32).astype(bf16)
-                for base in range(0, 2 * chunk, 128)
-            ],
-            1,
-        )
-        found = jnp.dot(hot, late_boxes, preferred_element_type=f32) + sources[k].astype(f32)
-        term = lax.dot_general(
-            far[k],
-            found.astype(bf16)[:, :rows],
-            (((1,), (1,)), ((), ())),
-            preferred_element_type=f32,
-        )
-        total = term if total is None else total + term
-    result[...] = total
-    for x in (0, 1):
-        first = result[pl.ds(share * 2 * x, share), :]
-        second = result[pl.ds(share * (2 * x + 1), share), :]
-        keep[x] = jnp.where(c == 0, first, second)
-        send[x] = jnp.where(c == 0, second, first).astype(bf16)
+
+    def tile(i):
+        total = None
+        for k in range(3):
+            at = k * boxes + start + i * width
+            wanted = jnp.broadcast_to(lists[k : k + 1, pl.ds(start + i * width, width)].astype(f32), (128, width)).T
+            hot = jnp.concatenate(
+                [
+                    (wanted == spot + float(base)).astype(f32).astype(bf16)
+                    for base in range(0, 2 * chunk, 128)
+                ],
+                1,
+            )
+            found = jnp.dot(hot, late_boxes, preferred_element_type=f32)
+            found = found + sources[pl.ds(at, width), :].astype(f32)
+            term = lax.dot_general(
+                far[k],
+                found.astype(bf16)[:, :rows],
+                (((1,), (1,)), ((), ())),
+                preferred_element_type=f32,
+            )
+            total = term if total is None else total + term
+        result[...] = total
+        lanes = pl.ds(i * width, width)
+        for x in (0, 1):
+            first = result[pl.ds(share * 2 * x, share), :]
+            second = result[pl.ds(share * (2 * x + 1), share), :]
+            keep[x, :, lanes] = jnp.where(c == 0, first, second)
+            send[x, :, lanes] = jnp.where(c == 0, second, first).astype(bf16)
+
+    for i in range(send.shape[2] // width):
+        tile(i)
 
 
 def far_partial(sc, far, sources, lists, late, late_o, start, count, width=256):
     shape = (2, share, count)
-    spec = pl.BlockSpec((2, share, width), lambda i, s: (0, 0, i))
-    skip = start // width
+    args = (far, sources, lists, late, late_o)
     return call(
-        far_kernel,
+        functools.partial(far_kernel, start, width),
         sc,
-        (far, sources, lists, late, late_o),
-        [
-            whole(far),
-            pl.BlockSpec((3, width, wide), lambda i, s: (0, skip + i, 0)),
-            pl.BlockSpec((3, 1, width), lambda i, s: (0, 0, skip + i)),
-            whole(late),
-            whole(late_o),
-        ],
-        [spec, spec],
+        args,
+        [whole(x) for x in args],
+        [whole(), whole()],
         [jax.ShapeDtypeStruct(shape, bf16), jax.ShapeDtypeStruct(shape, f32)],
-        grid=(count // width,),
+        12,
         scratch=[pltpu.VMEM((rows, width), f32)],
     )
 
@@ -342,23 +378,6 @@
     up_ops = jnp.transpose(upward_ops, (1, 0, 2)).reshape(8 * share, rows)
     down_ops = jnp.transpose(downward_ops, (1, 0, 2)).reshape(8 * share, rows)
 
-    mine = [turned(leaf_density, at(c * chunks + i), 1, chunk) for i in range(chunks)]
-    a = [hop(m) for m in mine]
-    other = turned(leaf_density, at((1 - c) * 2), 2, 256)
-    up = parent_rows(sc, up_ops, mine, other)
-    first = after(a[0], up)
-    b = [zswap(first)]
-    a_o = [cswap(first)]
-    own = jnp.concatenate([up, zswap(up)], 1)
-    ca = hop(own)
-    own_o = cswap(own)
-    second = after(a[1], own)
-    b.append(zswap(second))
-    a_o.append(cswap(second))
-    cb = zswap(ca)
-    b_o = [cswap(x) for x in b]
-    cab_o = cswap(jnp.concatenate([ca, cb], 1))
-
     which, side, offset = fine_lists >> 10, (fine_lists >> 9) & 1, fine_lists & (half - 1)
     outside = ((which == 0) & no_previous) | ((which == 2) & no_next)
     direct = (which == 0) == (l == 0)
@@ -375,29 +394,47 @@
     )
     spots = jnp.where(outside | is_late, early, spots)
     late_lists = jnp.where(is_late & ~outside, theirs * chunk + offset - (half - chunk), -1)
-    late_lists = late_lists.reshape(3, 1, boxes)
-    picked = gathered(spots.reshape(-1), [*mine, other, *a, *a_o, b[0], b_o[0]])
+
+    head = turned(leaf_density, at(c * half), [chunk])[0]
+    rest = jnp.stack([c * half + chunk, (1 - c) * half]).astype(jnp.int32)
+    tail, other = turned(leaf_density, after(rest, head), [half - chunk, half])
+    up = parent_rows(after(sc, spots, late_lists), up_ops, [head, tail], other)
+    mine = [head, after(tail, up)]
+    a = [hop(m) for m in mine]
+    own = joined(sc, up, zswap(up))
+    early_a = after(a[0], up)
+    b = [zswap(early_a)]
+    a_o = [cswap(early_a)]
+    ca = hop(own)
+    own_o = cswap(own)
+    second = after(a[1], early_a, ca, own_o)
+    b.append(zswap(second))
+    a_o.append(cswap(second))
+    cb = zswap(ca)
+    b_o = [cswap(b[0])]
+    picked = gathered(spots, [*mine, other, *a, *a_o, b[0], b_o[0]])
+    b_o.append(cswap(after(b[1], picked)))
+    cab_o = cswap(joined(sc, ca, cb))
 
     def summed(send, keep):
-        part = keep + cswap(send).astype(f32)
-        away = lax.dynamic_index_in_dim(part, 1 - l, 0, keepdims=False).astype(bf16)
-        here = lax.dynamic_index_in_dim(part, l, 0, keepdims=False)
+        shape = (share, send.shape[2])
+        here, away = small(split_kernel, sc, (keep, cswap(send)), [(shape, f32), (shape, bf16)])
         return here, zswap(away), away
 
     late = (b[1], b_o[1])
     send, keep = far_partial(sc, far_ops, picked, late_lists, *late, 0, half)
-    left = summed(send, keep)
-    send, keep = coarse_partial(
-        after(sc, send), coarse_lists.reshape(1, 3 * parents), far_ops, own, ca, cb, own_o, cab_o
-    )
-    part = keep + cswap(send).astype(f32)
-    send, keep = far_partial(after(sc, part, left[2]), far_ops, picked, late_lists, *late, half, half)
-    right = summed(send, keep)
-    check = (part + zswap(part.astype(bf16)).astype(f32)).astype(bf16)
-    spread = downward(sc, down_ops, check, cswap(check))
-
-    fine = jnp.concatenate([here + there.astype(f32) for here, there, _ in (left, right)], 1)
-    return (fine + spread).astype(bf16)
+    left = summed(after(send, cb), keep)
+    send, keep = coarse_partial(after(sc, send), coarse_lists, far_ops, own, ca, cb, own_o, cab_o)
+    shape = (wide // 2, parents)
+    part, part_sent = small(add_kernel, sc, (keep, cswap(send)), [(shape, f32), (shape, bf16)])
+    send, keep = far_partial(
+        after(sc, part, left[2]), far_ops, picked, late_lists, *late, half, half
+    )
+    part_got = zswap(part_sent)
+    right = summed(after(send, left[1], part_got), keep)
+    check = small(add_kernel, sc, (part, part_got), [(shape, bf16)])[0]
+    spread = downward(after(sc, right[2]), down_ops, check, cswap(check))
+    return small(last_kernel, sc, (spread, *left[:2], *right[:2]), [((share, boxes), bf16)])[0]
 
 
 def solution(mesh):

time: 122 us -> 97.7 us (0.80)
  waiting for transfers between devices: 35.3 us -> 23.8 us
  local copies, waits for them, and re-layouts: 14.4 us -> 3.41 us
  Pallas kernels: 36.4 us -> 39.1 us
  other arithmetic: 3.3 us -> 0.92 us
  starting transfers between devices: 31.9 us -> 30.2 us
    ppermute x11, waiting for transfers between devices: 6.53 us -> 16.9 us  [the longest x1 10.1 us: local(): own = joined(sc, up, zswap(up))]
    unnamed x45 -> x14, local copies, waits for them, and re-layouts: 13.5 us -> 3.41 us
    ppermute x2, waiting for transfers between devices: 8.92 us -> 1.37 us  [summed(): return (here, zswap(away), away)]
    ppermute x2, waiting for transfers between devices: 9.18 us -> 3.19 us  [local(): a = [hop(m) for m in mine]]
    ppermute x1, waiting for transfers between devices: 5.93 us -> 0.01 us  [local(): b.append(zswap(second))]
    ppermute x1, waiting for transfers between devices: 4.69 us -> 0.01 us  [local(): cb = zswap(ca)]
    ppermute x1, starting transfers between devices: 0.87 us -> 3.89 us  [local(): own_o = cswap(own)]
    pallas_call x9 -> x15, Pallas kernels: 36.4 us -> 39.1 us  [call(): pl.pallas_call(kernel, grid_spec=pltpu.PrefetchScalarGridSpec(num_scalar_...]
  transfers between devices with their start and end apart: 20 -> 20, of which waited for: 9 -> 12; matrix products, arithmetic and copies ran while one was open for 3% -> 1% of each run, Pallas kernels for 30% -> 38%
where the time goes in v3:
time: 97.7 us; the launch traced here: 97.5 us
  Pallas kernels  39.1 us (40%)
  starting transfers between devices  30.2 us (31%)
  waiting for transfers between devices  23.8 us (24%)
  local copies, waits for them, and re-layouts  3.41 us (3%)
    pallas_call x15, Pallas kernels, call(): pl.pallas_call(kernel, grid_spec=pltpu.PrefetchScalarGridSpec(num_scalar_...  39.1 us
    ppermute x2, starting transfers between devices, local(): a = [hop(m) for m in mine]  11.5 us
    ppermute x1, waiting for transfers between devices, local(): own = joined(sc, up, zswap(up))  10.1 us
    ppermute x1, starting transfers between devices, local(): ca = hop(own)  5.6 us
    ppermute x1, starting transfers between devices, local(): own_o = cswap(own)  3.89 us
    unnamed x14, local copies, waits for them, and re-layouts  3.41 us
    ppermute x2, waiting for transfers between devices, local(): a = [hop(m) for m in mine]  3.19 us
    ppermute x1, starting transfers between devices, local(): a_o.append(cswap(second))  2.41 us
  transfers between devices with their start and end apart: 20, of which 12 were waited for; matrix products, arithmetic and copies ran while one was open for 1% of the time, Pallas kernels for 38%

profile of v3, /device:TPU:1, one launch (start us, length us, event | category | flops | bytes accessed | tf_op | source)
XLA Modules:
  0.0 97.5 jit_solution(4667003296661838267)
XLA Ops:
  0.0 1.5 %copy-done = bf16[888,1024]{1,0:T(8,128)(2,1)S(1)} copy-done((bf16[888,1024]{1,0:T(8,128)(2,1)S(1)}, bf16[888,1024]{1,0:T(8,128)(2,1)}, u32[]{:S(2)}) %copy-start) | copy-done | bytes 1818648
  1.7 11.1 %collective-permute-start = (bf16[256,896]{1,0:T(8,128)(2,1)S(1)}, bf16[256,896]{1,0:T(8,128)(2,1)S(1)}, u32[]{:S(2)}, u32[]{:S(2)}) collective-permute-start(bf16[256,896]{1,0:T(8,128)(2,1)S(1)} %shard_map.64.refs_0_), channel_id=1, source_target_pairs={{2,4},{3,5},{6,8},{7,9},{10,12},{11,13},{14,16},{15,17},{18,20},{1... | collective-permute-start | bytes 1376264 | tf_op jit(solution)/shard_map/ppermute | solution.py:403
  12.9 0.8 fusion.6
  13.8 1.0 %shard_map.65 = (bf16[256,896]{1,0:T(8,128)(2,1)S(1)}, bf16[512,896]{1,0:T(8,128)(2,1)S(1)}) custom-call(s32[2]{0:T(128)S(1)} %pad_add_fusion.1.firsts, bf16[888,1024]{1,0:T(8,128)(2,1)S(1)} %copy-done.1), custom_call_target="tpu_custom_call" | custom-call | tf_op jit(solution)/shard_map/pallas_call | solution.py:32
  14.8 1.9 %copy-done.2 = bf16[8,222,888]{2,0,1:T(8,128)(2,1)S(1)} copy-done((bf16[8,222,888]{2,0,1:T(8,128)(2,1)S(1)}, bf16[8,222,888]{2,0,1:T(8,128)(2,1)}, u32[]{:S(2)}) %copy-start.2) | copy-done | bytes 3154200
  16.7 2.9 %shard_map.66.refs_0_ = bf16[222,128]{1,0:T(8,128)(2,1)S(1)} custom-call(s32[4]{0:T(128)S(1)} %pad_add_fusion.sc, bf16[1776,888]{1,0:T(8,128)(2,1)S(1)} %bitcast.15, bf16[512,896]{1,0:T(8,128)(2,1)S(1)} %get-tuple-element.33.other.refs_2_, bf16[256,896]{1,0:T(8,128)(2,1)S(1)} %shard_map.64.refs_0_, bf16[256,896]{1,0:T(8,128)(2,1)S(1)} %get-tuple-element.34.refs_1_), custom_call_target="tpu_custom_call" | custom-call | tf_op jit(solution)/shard_map/pallas_call | solution.py:32
  19.9 3.2 %collective-permute-done.refs_3_ = bf16[256,896]{1,0:T(8,128)(2,1)S(1)} collective-permute-done((bf16[256,896]{1,0:T(8,128)(2,1)S(1)}, bf16[256,896]{1,0:T(8,128)(2,1)S(1)}, u32[]{:S(2)}, u32[]{:S(2)}) %collective-permute-start) | collective-permute-done | bytes 458784 | tf_op jit(solution)/shard_map/ppermute | solution.py:403
  23.1 1.5 %collective-permute-start.3 = (bf16[222,128]{1,0:T(8,128)(2,1)S(1)}, bf16[222,128]{1,0:T(8,128)(2,1)S(1)}, u32[]{:S(2)}, u32[]{:S(2)}) collective-permute-start(bf16[222,128]{1,0:T(8,128)(2,1)S(1)} %shard_map.66.refs_0_), channel_id=1, source_target_pairs={{0,2},{1,3},{2,0},{3,1},{4,6},{5,7},{6,4},{7,5},{8,10},{9,11},{10,... | collective-permute-start | bytes 170504 | tf_op jit(solution)/shard_map/ppermute | solution.py:404
  24.6 10.1 %collective-permute-done.3.refs_1_ = bf16[222,128]{1,0:T(8,128)(2,1)S(1)} collective-permute-done((bf16[222,128]{1,0:T(8,128)(2,1)S(1)}, bf16[222,128]{1,0:T(8,128)(2,1)S(1)}, u32[]{:S(2)}, u32[]{:S(2)}) %collective-permute-start.3) | collective-permute-done | bytes 56864 | tf_op jit(solution)/shard_map/ppermute | solution.py:404
  35.3 5.6 %collective-permute-start.4 = (bf16[222,256]{1,0:T(8,128)(2,1)S(1)}, bf16[222,256]{1,0:T(8,128)(2,1)S(1)}, u32[]{:S(2)}, u32[]{:S(2)}) collective-permute-start(bf16[222,256]{1,0:T(8,128)(2,1)S(1)} %shard_map.67.own), channel_id=1, source_target_pairs={{2,4},{3,5},{6,8},{7,9},{10,12},{11,13},{14,16},{15,17},{18,20},{1... | collective-permute-start | bytes 341000 | tf_op jit(solution)/shard_map/ppermute | solution.py:408
  40.9 3.9 %collective-permute-start.5 = (bf16[222,256]{1,0:T(8,128)(2,1)S(1)}, bf16[222,256]{1,0:T(8,128)(2,1)S(1)}, u32[]{:S(2)}, u32[]{:S(2)}) collective-permute-start(bf16[222,256]{1,0:T(8,128)(2,1)S(1)} %shard_map.67.own), channel_id=1, source_target_pairs={{0,1},{1,0},{2,3},{3,2},{4,5},{5,4},{6,7},{7,6},{8,9},{9,8},{10,11... | collective-permute-start | bytes 341000 | tf_op jit(solution)/shard_map/ppermute | solution.py:409
  44.8 1.0 collective-permute-done.5.own_o
  45.7 2.4 %collective-permute-start.6 = (bf16[256,896]{1,0:T(8,128)(2,1)S(1)}, bf16[256,896]{1,0:T(8,128)(2,1)S(1)}, u32[]{:S(2)}, u32[]{:S(2)}) collective-permute-start(bf16[256,896]{1,0:T(8,128)(2,1)S(1)} %collective-permute-done.1.refs_4_), channel_id=1, source_target_pairs={{0,1},{1,0},{2,3},{3,2},{4,5},{5,4},{6,7},{7,6},{8,9},{9,8},{10,11... | collective-permute-start | bytes 1376264 | tf_op jit(solution)/shard_map/ppermute | solution.py:412
  48.3 1.3 %collective-permute-done.6.refs_6_ = bf16[256,896]{1,0:T(8,128)(2,1)S(1)} collective-permute-done((bf16[256,896]{1,0:T(8,128)(2,1)S(1)}, bf16[256,896]{1,0:T(8,128)(2,1)S(1)}, u32[]{:S(2)}, u32[]{:S(2)}) %collective-permute-start.6) | collective-permute-done | bytes 458784 | tf_op jit(solution)/shard_map/ppermute | solution.py:412
  49.6 0.7 collective-permute-done.8.refs_8_
  50.3 11.9 %shard_map.68.sources = bf16[3072,896]{1,0:T(8,128)(2,1)S(1)} custom-call(s32[3,1024]{1,0:T(4,128)S(1)} %get-tuple-element.56.spots, bf16[256,896]{1,0:T(8,128)(2,1)S(1)} %shard_map.64.refs_0_, bf16[256,896]{1,0:T(8,128)(2,1)S(1)} %get-tuple-element.34.refs_1_, bf16[512,896]{1,0:T(8,128)(2,1)S(1)} %get-tuple-element.33.other.refs_2_, ...), custom_call_target="tpu_custom_call" | custom-call | tf_op jit(solution)/shard_map/pallas_call | solution.py:32
  62.6 1.4 %collective-permute-done.10.late_o = bf16[256,896]{1,0:T(8,128)(2,1)S(1)} collective-permute-done((bf16[256,896]{1,0:T(8,128)(2,1)S(1)}, bf16[256,896]{1,0:T(8,128)(2,1)S(1)}, u32[]{:S(2)}, u32[]{:S(2)}) %collective-permute-start.10) | collective-permute-done | bytes 458784 | tf_op jit(solution)/shard_map/ppermute | solution.py:416
  64.1 6.2 %shard_map.69 = (bf16[2,222,512]{2,1,0:T(8,128)(2,1)S(1)}, f32[2,222,512]{2,1,0:T(8,128)S(1)}) custom-call(s32[4]{0:T(128)S(1)} %pad_add_fusion.sc, bf16[3,888,888]{2,1,0:T(8,128)(2,1)S(1)} %bitcast.14, bf16[3072,896]{1,0:T(8,128)(2,1)S(1)} %shard_map.68.sources, s32[3,1024]{1,0:T(4,128)S(1)} %get-tuple-element.55.lists, ...), custom_call_target="tpu_custom_call" | custom-call | tf_op jit(solution)/shard_map/pallas_call | solution.py:32
  71.6 1.3 %collective-permute-done.12.ab_o = bf16[222,512]{1,0:T(8,128)(2,1)S(1)} collective-permute-done((bf16[222,512]{1,0:T(8,128)(2,1)S(1)}, bf16[222,512]{1,0:T(8,128)(2,1)S(1)}, u32[]{:S(2)}, u32[]{:S(2)}) %collective-permute-start.12) | collective-permute-done | bytes 227360 | tf_op jit(solution)/shard_map/ppermute | solution.py:417
  73.0 2.7 %shard_map.71 = (bf16[448,128]{1,0:T(8,128)(2,1)S(1)}, f32[448,128]{1,0:T(8,128)S(1)}) custom-call(s32[4]{0:T(128)S(1)} %pad_add_fusion.sc, s32[3,128]{1,0:T(4,128)S(1)} %copy-done.4, bf16[3,888,888]{2,1,0:T(8,128)(2,1)S(1)} %bitcast.14, bf16[222,256]{1,0:T(8,128)(2,1)S(1)} %shard_map.67.own, bf16[222,256]{1,0:T(8,128)(2,1)S(1)} %collective-permute-done.4.refs_0_.a, ...), custom_call_target="tpu_custom_call" | custom-call | tf_op jit(solution)/shard_map/pallas_call | solution.py:32
  75.9 0.6 shard_map.73
  77.6 1.3 %collective-permute-start.16 = (bf16[448,128]{1,0:T(8,128)(2,1)S(1)}, bf16[448,128]{1,0:T(8,128)(2,1)S(1)}, u32[]{:S(2)}, u32[]{:S(2)}) collective-permute-start(bf16[448,128]{1,0:T(8,128)(2,1)S(1)} %get-tuple-element.49), channel_id=1, source_target_pairs={{0,2},{1,3},{2,0},{3,1},{4,6},{5,7},{6,4},{7,5},{8,10},{9,11},{10,... | collective-permute-start | bytes 344072 | tf_op jit(solution)/shard_map/ppermute | solution.py:433
  78.9 6.2 %shard_map.74 = (bf16[2,222,512]{2,1,0:T(8,128)(2,1)S(1)}, f32[2,222,512]{2,1,0:T(8,128)S(1)}) custom-call(s32[4]{0:T(128)S(1)} %pad_add_fusion.sc, bf16[3,888,888]{2,1,0:T(8,128)(2,1)S(1)} %bitcast.14, bf16[3072,896]{1,0:T(8,128)(2,1)S(1)} %shard_map.68.sources, s32[3,1024]{1,0:T(4,128)S(1)} %get-tuple-element.55.lists, ...), custom_call_target="tpu_custom_call" | custom-call | tf_op jit(solution)/shard_map/pallas_call | solution.py:32
  85.2 0.7 collective-permute-done.16.two
  85.9 1.2 %collective-permute-start.17 = (bf16[2,222,512]{2,1,0:T(8,128)(2,1)S(1)}, bf16[2,222,512]{2,1,0:T(8,128)(2,1)S(1)}, u32[]{:S(2)}, u32[]{:S(2)}) collective-permute-start(bf16[2,222,512]{2,1,0:T(8,128)(2,1)S(1)} %get-tuple-element.50), channel_id=1, source_target_pairs={{0,1},{1,0},{2,3},{3,2},{4,5},{5,4},{6,7},{7,6},{8,9},{9,8},{10,11... | collective-permute-start | bytes 1363976 | tf_op jit(solution)/shard_map/ppermute | solution.py:421
  87.1 1.4 %collective-permute-done.17.got = bf16[2,222,512]{2,1,0:T(8,128)(2,1)S(1)} collective-permute-done((bf16[2,222,512]{2,1,0:T(8,128)(2,1)S(1)}, bf16[2,222,512]{2,1,0:T(8,128)(2,1)S(1)}, u32[]{:S(2)}, u32[]{:S(2)}) %collective-permute-start.17) | collective-permute-done | bytes 454688 | tf_op jit(solution)/shard_map/ppermute | solution.py:421
  88.5 0.7 shard_map.75
  90.1 0.7 collective-permute-start.18
  90.8 1.0 collective-permute-done.18.other
  91.8 2.9 %shard_map.77.spread = f32[222,1024]{1,0:T(8,128)S(1)} custom-call(s32[4]{0:T(128)S(1)} %pad_add_fusion.sc, bf16[1776,888]{1,0:T(8,128)(2,1)S(1)} %bitcast.16, bf16[448,128]{1,0:T(8,128)(2,1)S(1)} %shard_map.76.mine, bf16[448,128]{1,0:T(8,128)(2,1)S(1)} %collective-permute-done.18.other), custom_call_target="tpu_custom_call" | custom-call | tf_op jit(solution)/shard_map/pallas_call | solution.py:32
  94.7 1.4 %collective-permute-done.19.refs_3_ = bf16[222,512]{1,0:T(8,128)(2,1)S(1)} collective-permute-done((bf16[222,512]{1,0:T(8,128)(2,1)S(1)}, bf16[222,512]{1,0:T(8,128)(2,1)S(1)}, u32[]{:S(2)}, u32[]{:S(2)}) %collective-permute-start.19) | collective-permute-done | bytes 227360 | tf_op jit(solution)/shard_map/ppermute | solution.py:422
  96.1 1.5 %shard_map.78 = bf16[222,1024]{1,0:T(8,128)(2,1)} custom-call(s32[4]{0:T(128)S(1)} %pad_add_fusion.sc, f32[222,1024]{1,0:T(8,128)S(1)} %shard_map.77.spread, f32[222,512]{1,0:T(8,128)S(1)} %get-tuple-element.53.refs_0_, bf16[222,512]{1,0:T(8,128)(2,1)S(1)} %collective-permute-done.15.refs_1_, f32[222,512]{1,0:T(8,128)S(1)} %get-tuple-element.54.refs_2_, ...), custom_call_target="tpu_custom_call" | custom-call | tf_op jit(solution)/shard_map/pallas_call | solution.py:32
  (41 shorter events, 5.4 us)
Async XLA Ops:
  0.0 1.5 %copy-start = (bf16[888,1024]{1,0:T(8,128)(2,1)S(1)}, bf16[888,1024]{1,0:T(8,128)(2,1)}, u32[]{:S(2)}) copy-start(bf16[888,1024]{1,0:T(8,128)(2,1)} %x_ref.3) | copy-start | bytes 5455876
  1.5 12.3 %copy-start.1 = (bf16[888,1024]{1,0:T(8,128)(2,1)S(1)}, bf16[888,1024]{1,0:T(8,128)(2,1)}, u32[]{:S(2)}) copy-start(bf16[888,1024]{1,0:T(8,128)(2,1)} %x_ref.3) | copy-start | bytes 5455876
  1.7 21.4 %collective-permute-start = (bf16[256,896]{1,0:T(8,128)(2,1)S(1)}, bf16[256,896]{1,0:T(8,128)(2,1)S(1)}, u32[]{:S(2)}, u32[]{:S(2)}) collective-permute-start(bf16[256,896]{1,0:T(8,128)(2,1)S(1)} %shard_map.64.refs_0_), channel_id=1, source_target_pairs={{2,4},{3,5},{6,8},{7,9},{10,12},{11,13},{14,16},{15,17},{18,20},{1... | collective-permute-start | bytes 1376264 | tf_op jit(solution)/shard_map/ppermute | solution.py:403
  14.8 1.9 %copy-start.2 = (bf16[8,222,888]{2,0,1:T(8,128)(2,1)S(1)}, bf16[8,222,888]{2,0,1:T(8,128)(2,1)}, u32[]{:S(2)}) copy-start(bf16[8,222,888]{2,0,1:T(8,128)(2,1)} %param.7) | copy-start | bytes 9462532
  19.5 26.2 %collective-permute-start.1 = (bf16[256,896]{1,0:T(8,128)(2,1)S(1)}, bf16[256,896]{1,0:T(8,128)(2,1)S(1)}, u32[]{:S(2)}, u32[]{:S(2)}) collective-permute-start(bf16[256,896]{1,0:T(8,128)(2,1)S(1)} %get-tuple-element.34.refs_1_), channel_id=1, source_target_pairs={{2,4},{3,5},{6,8},{7,9},{10,12},{11,13},{14,16},{15,17},{18,20},{1... | collective-permute-start | bytes 1376264 | tf_op jit(solution)/shard_map/ppermute | solution.py:403
  23.1 25.1 %collective-permute-start.7 = (bf16[256,896]{1,0:T(8,128)(2,1)S(1)}, bf16[256,896]{1,0:T(8,128)(2,1)S(1)}, u32[]{:S(2)}, u32[]{:S(2)}) collective-permute-start(bf16[256,896]{1,0:T(8,128)(2,1)S(1)} %collective-permute-done.refs_3_), channel_id=1, source_target_pairs={{0,2},{1,3},{2,0},{3,1},{4,6},{5,7},{6,4},{7,5},{8,10},{9,11},{10,... | collective-permute-start | bytes 1376264 | tf_op jit(solution)/shard_map/ppermute | solution.py:406
  23.1 11.6 %collective-permute-start.3 = (bf16[222,128]{1,0:T(8,128)(2,1)S(1)}, bf16[222,128]{1,0:T(8,128)(2,1)S(1)}, u32[]{:S(2)}, u32[]{:S(2)}) collective-permute-start(bf16[222,128]{1,0:T(8,128)(2,1)S(1)} %shard_map.66.refs_0_), channel_id=1, source_target_pairs={{0,2},{1,3},{2,0},{3,1},{4,6},{5,7},{6,4},{7,5},{8,10},{9,11},{10,... | collective-permute-start | bytes 170504 | tf_op jit(solution)/shard_map/ppermute | solution.py:404
  34.7 29.4 %slice-start = ((s8[4773888]{0:T(1024)(128)(4,1)}), s8[4194304]{0:T(1024)(128)(4,1)S(1)}, s32[]{:S(2)}) async-start(s8[4773888]{0:T(1024)(128)(4,1)} %bitcast.13), calls=%async_computation | async-start | bytes 8388608
  35.3 28.8 %slice-start.1 = ((s8[4773888]{0:T(1024)(128)(4,1)}), s8[579584]{0:T(1024)(128)(4,1)S(1)}, s32[]{:S(2)}) async-start(s8[4773888]{0:T(1024)(128)(4,1)} %bitcast.13), calls=%async_computation.1 | async-start | bytes 1159168
  35.3 9.5 %collective-permute-start.4 = (bf16[222,256]{1,0:T(8,128)(2,1)S(1)}, bf16[222,256]{1,0:T(8,128)(2,1)S(1)}, u32[]{:S(2)}, u32[]{:S(2)}) collective-permute-start(bf16[222,256]{1,0:T(8,128)(2,1)S(1)} %shard_map.67.own), channel_id=1, source_target_pairs={{2,4},{3,5},{6,8},{7,9},{10,12},{11,13},{14,16},{15,17},{18,20},{1... | collective-permute-start | bytes 341000 | tf_op jit(solution)/shard_map/ppermute | solution.py:408
  40.9 4.9 %collective-permute-start.5 = (bf16[222,256]{1,0:T(8,128)(2,1)S(1)}, bf16[222,256]{1,0:T(8,128)(2,1)S(1)}, u32[]{:S(2)}, u32[]{:S(2)}) collective-permute-start(bf16[222,256]{1,0:T(8,128)(2,1)S(1)} %shard_map.67.own), channel_id=1, source_target_pairs={{0,1},{1,0},{2,3},{3,2},{4,5},{5,4},{6,7},{7,6},{8,9},{9,8},{10,11... | collective-permute-start | bytes 341000 | tf_op jit(solution)/shard_map/ppermute | solution.py:409
  44.8 4.8 %collective-permute-start.2 = (bf16[256,896]{1,0:T(8,128)(2,1)S(1)}, bf16[256,896]{1,0:T(8,128)(2,1)S(1)}, u32[]{:S(2)}, u32[]{:S(2)}) collective-permute-start(bf16[256,896]{1,0:T(8,128)(2,1)S(1)} %collective-permute-done.refs_3_), channel_id=1, source_target_pairs={{0,1},{1,0},{2,3},{3,2},{4,5},{5,4},{6,7},{7,6},{8,9},{9,8},{10,11... | collective-permute-start | bytes 1376264 | tf_op jit(solution)/shard_map/ppermute | solution.py:407
  45.7 3.9 %collective-permute-start.6 = (bf16[256,896]{1,0:T(8,128)(2,1)S(1)}, bf16[256,896]{1,0:T(8,128)(2,1)S(1)}, u32[]{:S(2)}, u32[]{:S(2)}) collective-permute-start(bf16[256,896]{1,0:T(8,128)(2,1)S(1)} %collective-permute-done.1.refs_4_), channel_id=1, source_target_pairs={{0,1},{1,0},{2,3},{3,2},{4,5},{5,4},{6,7},{7,6},{8,9},{9,8},{10,11... | collective-permute-start | bytes 1376264 | tf_op jit(solution)/shard_map/ppermute | solution.py:412
  48.2 2.1 %collective-permute-start.8 = (bf16[256,896]{1,0:T(8,128)(2,1)S(1)}, bf16[256,896]{1,0:T(8,128)(2,1)S(1)}, u32[]{:S(2)}, u32[]{:S(2)}) collective-permute-start(bf16[256,896]{1,0:T(8,128)(2,1)S(1)} %collective-permute-done.7.refs_7_), channel_id=1, source_target_pairs={{0,1},{1,0},{2,3},{3,2},{4,5},{5,4},{6,7},{7,6},{8,9},{9,8},{10,11... | collective-permute-start | bytes 1376264 | tf_op jit(solution)/shard_map/ppermute | solution.py:414
  48.3 13.9 %collective-permute-start.9 = (bf16[256,896]{1,0:T(8,128)(2,1)S(1)}, bf16[256,896]{1,0:T(8,128)(2,1)S(1)}, u32[]{:S(2)}, u32[]{:S(2)}) collective-permute-start(bf16[256,896]{1,0:T(8,128)(2,1)S(1)} %collective-permute-done.1.refs_4_), channel_id=1, source_target_pairs={{0,2},{1,3},{2,0},{3,1},{4,6},{5,7},{6,4},{7,5},{8,10},{9,11},{10,... | collective-permute-start | bytes 1376264 | tf_op jit(solution)/shard_map/ppermute | solution.py:411
  62.2 10.8 %copy-start.4 = (s32[3,128]{1,0:T(4,128)S(1)}, s32[3,128]{1,0:T(4,128)}, u32[]{:S(2)}) copy-start(s32[3,128]{1,0:T(4,128)} %lists.1) | copy-start | bytes 4612
  62.2 1.9 %collective-permute-start.10 = (bf16[256,896]{1,0:T(8,128)(2,1)S(1)}, bf16[256,896]{1,0:T(8,128)(2,1)S(1)}, u32[]{:S(2)}, u32[]{:S(2)}) collective-permute-start(bf16[256,896]{1,0:T(8,128)(2,1)S(1)} %collective-permute-done.9.late), channel_id=1, source_target_pairs={{0,1},{1,0},{2,3},{3,2},{4,5},{5,4},{6,7},{7,6},{8,9},{9,8},{10,11... | collective-permute-start | bytes 1376264 | tf_op jit(solution)/shard_map/ppermute | solution.py:416
  62.6 7.7 %collective-permute-start.11 = (bf16[222,256]{1,0:T(8,128)(2,1)S(1)}, bf16[222,256]{1,0:T(8,128)(2,1)S(1)}, u32[]{:S(2)}, u32[]{:S(2)}) collective-permute-start(bf16[222,256]{1,0:T(8,128)(2,1)S(1)} %collective-permute-done.4.refs_0_.a), channel_id=1, source_target_pairs={{0,2},{1,3},{2,0},{3,1},{4,6},{5,7},{6,4},{7,5},{8,10},{9,11},{10,... | collective-permute-start | bytes 341000 | tf_op jit(solution)/shard_map/ppermute | solution.py:413
  70.4 5.5 %collective-permute-start.14 = (bf16[2,222,512]{2,1,0:T(8,128)(2,1)S(1)}, bf16[2,222,512]{2,1,0:T(8,128)(2,1)S(1)}, u32[]{:S(2)}, u32[]{:S(2)}) collective-permute-start(bf16[2,222,512]{2,1,0:T(8,128)(2,1)S(1)} %get-tuple-element.44), channel_id=1, source_target_pairs={{0,1},{1,0},{2,3},{3,2},{4,5},{5,4},{6,7},{7,6},{8,9},{9,8},{10,11... | collective-permute-start | bytes 1363976 | tf_op jit(solution)/shard_map/ppermute | solution.py:421
  71.4 1.6 %collective-permute-start.12 = (bf16[222,512]{1,0:T(8,128)(2,1)S(1)}, bf16[222,512]{1,0:T(8,128)(2,1)S(1)}, u32[]{:S(2)}, u32[]{:S(2)}) collective-permute-start(bf16[222,512]{1,0:T(8,128)(2,1)S(1)} %shard_map.70), channel_id=1, source_target_pairs={{0,1},{1,0},{2,3},{3,2},{4,5},{5,4},{6,7},{7,6},{8,9},{9,8},{10,11... | collective-permute-start | bytes 681992 | tf_op jit(solution)/shard_map/ppermute | solution.py:417
  75.6 1.4 %collective-permute-start.13 = (bf16[448,128]{1,0:T(8,128)(2,1)S(1)}, bf16[448,128]{1,0:T(8,128)(2,1)S(1)}, u32[]{:S(2)}, u32[]{:S(2)}) collective-permute-start(bf16[448,128]{1,0:T(8,128)(2,1)S(1)} %get-tuple-element.41), channel_id=1, source_target_pairs={{0,1},{1,0},{2,3},{3,2},{4,5},{5,4},{6,7},{7,6},{8,9},{9,8},{10,11... | collective-permute-start | bytes 344072 | tf_op jit(solution)/shard_map/ppermute | solution.py:429
  76.5 9.4 %collective-permute-start.15 = (bf16[222,512]{1,0:T(8,128)(2,1)S(1)}, bf16[222,512]{1,0:T(8,128)(2,1)S(1)}, u32[]{:S(2)}, u32[]{:S(2)}) collective-permute-start(bf16[222,512]{1,0:T(8,128)(2,1)S(1)} %get-tuple-element.45), channel_id=1, source_target_pairs={{0,2},{1,3},{2,0},{3,1},{4,6},{5,7},{6,4},{7,5},{8,10},{9,11},{10,... | collective-permute-start | bytes 681992 | tf_op jit(solution)/shard_map/ppermute | solution.py:422
  77.6 8.2 %collective-permute-start.16 = (bf16[448,128]{1,0:T(8,128)(2,1)S(1)}, bf16[448,128]{1,0:T(8,128)(2,1)S(1)}, u32[]{:S(2)}, u32[]{:S(2)}) collective-permute-start(bf16[448,128]{1,0:T(8,128)(2,1)S(1)} %get-tuple-element.49), channel_id=1, source_target_pairs={{0,2},{1,3},{2,0},{3,1},{4,6},{5,7},{6,4},{7,5},{8,10},{9,11},{10,... | collective-permute-start | bytes 344072 | tf_op jit(solution)/shard_map/ppermute | solution.py:433
  78.9 12.8 %copy-start.3 = (bf16[8,222,888]{2,0,1:T(8,128)(2,1)S(1)}, bf16[8,222,888]{2,0,1:T(8,128)(2,1)}, u32[]{:S(2)}) copy-start(bf16[8,222,888]{2,0,1:T(8,128)(2,1)} %param.9) | copy-start | bytes 9462532
  85.9 2.7 %collective-permute-start.17 = (bf16[2,222,512]{2,1,0:T(8,128)(2,1)S(1)}, bf16[2,222,512]{2,1,0:T(8,128)(2,1)S(1)}, u32[]{:S(2)}, u32[]{:S(2)}) collective-permute-start(bf16[2,222,512]{2,1,0:T(8,128)(2,1)S(1)} %get-tuple-element.50), channel_id=1, source_target_pairs={{0,1},{1,0},{2,3},{3,2},{4,5},{5,4},{6,7},{7,6},{8,9},{9,8},{10,11... | collective-permute-start | bytes 1363976 | tf_op jit(solution)/shard_map/ppermute | solution.py:421
  89.2 6.9 %collective-permute-start.19 = (bf16[222,512]{1,0:T(8,128)(2,1)S(1)}, bf16[222,512]{1,0:T(8,128)(2,1)S(1)}, u32[]{:S(2)}, u32[]{:S(2)}) collective-permute-start(bf16[222,512]{1,0:T(8,128)(2,1)S(1)} %get-tuple-element.51), channel_id=1, source_target_pairs={{0,2},{1,3},{2,0},{3,1},{4,6},{5,7},{6,4},{7,5},{8,10},{9,11},{10,... | collective-permute-start | bytes 681992 | tf_op jit(solution)/shard_map/ppermute | solution.py:422
  90.1 1.7 %collective-permute-start.18 = (bf16[448,128]{1,0:T(8,128)(2,1)S(1)}, bf16[448,128]{1,0:T(8,128)(2,1)S(1)}, u32[]{:S(2)}, u32[]{:S(2)}) collective-permute-start(bf16[448,128]{1,0:T(8,128)(2,1)S(1)} %shard_map.76.mine), channel_id=1, source_target_pairs={{0,1},{1,0},{2,3},{3,2},{4,5},{5,4},{6,7},{7,6},{8,9},{9,8},{10,11... | collective-permute-start | bytes 344072 | tf_op jit(solution)/shard_map/ppermute | solution.py:436

commit v4 on v3

--- a/solution.py
+++ b/solution.py
@@ -20,8 +20,9 @@
 
 
 def one_hop(groups):
-    up = [(4 * s + 2 + c, 4 * ((s + 1) % groups) + c) for s in range(groups) for c in (0, 1)]
-    return up + [(j, i) for i, j in up]
+    up = [(4 * s + 2 + c, 4 * (s + 1) + c) for s in range(groups - 1) for c in (0, 1)]
+    ends = [(i, i) for i in (0, 1, 4 * groups - 2, 4 * groups - 1)]
+    return up + [(j, i) for i, j in up] + ends
 
 
 def across(groups, flip):
@@ -247,8 +248,6 @@
     pieces, o_ref, planes, got = refs[:-3], refs[-3], refs[-2], refs[-1]
     step = pl.program_id(0)
     depth = step_boxes + 8
-    entry = step // (boxes // step_boxes)
-    first = (step % (boxes // step_boxes)) * step_boxes
 
     @pl.when(step == 0)
     def _():
@@ -265,7 +264,7 @@
 
     def body(i, carry):
         found = [
-            planes[pl.ds(spots[entry, first + i * unroll + u], 8, stride=pitch), :]
+            planes[pl.ds(spots[step * step_boxes + i * unroll + u], 8, stride=pitch), :]
             for u in range(unroll)
         ]
         for u in range(unroll):
@@ -392,7 +391,7 @@
             4 * half + theirs * (half - chunk) + offset,
         ),
     )
-    spots = jnp.where(outside | is_late, early, spots)
+    spots = jnp.where(outside | is_late, early, spots).reshape(-1)
     late_lists = jnp.where(is_late & ~outside, theirs * chunk + offset - (half - chunk), -1)
 
     head = turned(leaf_density, at(c * half), [chunk])[0]
@@ -402,7 +401,7 @@
     mine = [head, after(tail, up)]
     a = [hop(m) for m in mine]
     own = joined(sc, up, zswap(up))
-    early_a = after(a[0], up)
+    early_a = after(a[0], own)
     b = [zswap(early_a)]
     a_o = [cswap(early_a)]
     ca = hop(own)

time: 97.7 us -> 88.7 us (0.908)
  the two profiles are of different devices: /device:TPU:1 before, /device:TPU:24 now
where the time goes in v4:
time: 88.7 us; the launch traced here: 88.5 us
  Pallas kernels  34.4 us (39%)
  starting transfers between devices  26.4 us (30%)
  waiting for transfers between devices  23 us (26%)
  local copies, waits for them, and re-layouts  3.43 us (4%)
  other arithmetic  0.92 us (1%)
    pallas_call x15, Pallas kernels, call(): pl.pallas_call(kernel, grid_spec=pltpu.PrefetchScalarGridSpec(num_scalar_...  34.4 us
    ppermute x2, starting transfers between devices, local(): a = [hop(m) for m in mine]  14.2 us
    ppermute x1, waiting for transfers between devices, local(): ca = hop(own)  8.43 us
    ppermute x1, starting transfers between devices, local(): ca = hop(own)  6.65 us
    unnamed x14, local copies, waits for them, and re-layouts  3.41 us
    ppermute x1, waiting for transfers between devices, local(): b.append(zswap(second))  3.23 us
    ppermute x2, waiting for transfers between devices, summed(): return (here, zswap(away), away)  2.4 us
    ppermute x1, starting transfers between devices, local(): part_got = zswap(part_sent)  2.05 us
  transfers between devices with their start and end apart: 20, of which 11 were waited for; matrix products, arithmetic and copies ran while one was open for 1% of the time, Pallas kernels for 36%

profile of v4, /device:TPU:24, one launch (start us, length us, event | category | flops | bytes accessed | tf_op | source)
XLA Modules:
  0.0 88.5 jit_solution(5526027914568922454)
XLA Ops:
  0.0 1.5 %copy-done = bf16[888,1024]{1,0:T(8,128)(2,1)S(1)} copy-done((bf16[888,1024]{1,0:T(8,128)(2,1)S(1)}, bf16[888,1024]{1,0:T(8,128)(2,1)}, u32[]{:S(2)}) %copy-start) | copy-done | bytes 1818648
  1.7 10.3 %collective-permute-start = (bf16[256,896]{1,0:T(8,128)(2,1)S(1)}, bf16[256,896]{1,0:T(8,128)(2,1)S(1)}, u32[]{:S(2)}, u32[]{:S(2)}) collective-permute-start(bf16[256,896]{1,0:T(8,128)(2,1)S(1)} %shard_map.64.refs_0_), channel_id=1, source_target_pairs={{2,4},{3,5},{6,8},{7,9},{10,12},{11,13},{14,16},{15,17},{18,20},{1... | collective-permute-start | bytes 1376264 | tf_op jit(solution)/shard_map/ppermute | solution.py:402
  12.0 0.8 fusion.6
  13.0 1.0 %shard_map.65 = (bf16[256,896]{1,0:T(8,128)(2,1)S(1)}, bf16[512,896]{1,0:T(8,128)(2,1)S(1)}) custom-call(s32[2]{0:T(128)S(1)} %pad_add_fusion.1.firsts, bf16[888,1024]{1,0:T(8,128)(2,1)S(1)} %copy-done.1), custom_call_target="tpu_custom_call" | custom-call | tf_op jit(solution)/shard_map/pallas_call | solution.py:33
  14.0 1.9 %copy-done.2 = bf16[8,222,888]{2,0,1:T(8,128)(2,1)S(1)} copy-done((bf16[8,222,888]{2,0,1:T(8,128)(2,1)S(1)}, bf16[8,222,888]{2,0,1:T(8,128)(2,1)}, u32[]{:S(2)}) %copy-start.2) | copy-done | bytes 3154200
  15.9 2.9 %shard_map.66.refs_0_ = bf16[222,128]{1,0:T(8,128)(2,1)S(1)} custom-call(s32[4]{0:T(128)S(1)} %pad_add_fusion.sc, bf16[1776,888]{1,0:T(8,128)(2,1)S(1)} %bitcast.15, bf16[512,896]{1,0:T(8,128)(2,1)S(1)} %get-tuple-element.33.other.refs_2_, bf16[256,896]{1,0:T(8,128)(2,1)S(1)} %shard_map.64.refs_0_, bf16[256,896]{1,0:T(8,128)(2,1)S(1)} %get-tuple-element.34.refs_1_), custom_call_target="tpu_custom_call" | custom-call | tf_op jit(solution)/shard_map/pallas_call | solution.py:33
  18.8 3.9 %collective-permute-start.1 = (bf16[256,896]{1,0:T(8,128)(2,1)S(1)}, bf16[256,896]{1,0:T(8,128)(2,1)S(1)}, u32[]{:S(2)}, u32[]{:S(2)}) collective-permute-start(bf16[256,896]{1,0:T(8,128)(2,1)S(1)} %get-tuple-element.34.refs_1_), channel_id=1, source_target_pairs={{2,4},{3,5},{6,8},{7,9},{10,12},{11,13},{14,16},{15,17},{18,20},{1... | collective-permute-start | bytes 1376264 | tf_op jit(solution)/shard_map/ppermute | solution.py:402
  23.0 0.6 shard_map.67.own
  23.7 6.6 %collective-permute-start.4 = (bf16[222,256]{1,0:T(8,128)(2,1)S(1)}, bf16[222,256]{1,0:T(8,128)(2,1)S(1)}, u32[]{:S(2)}, u32[]{:S(2)}) collective-permute-start(bf16[222,256]{1,0:T(8,128)(2,1)S(1)} %shard_map.67.own), channel_id=1, source_target_pairs={{2,4},{3,5},{6,8},{7,9},{10,12},{11,13},{14,16},{15,17},{18,20},{1... | collective-permute-start | bytes 341000 | tf_op jit(solution)/shard_map/ppermute | solution.py:407
  30.4 0.5 collective-permute-start.3
  30.9 8.4 %collective-permute-done.4.refs_0_.a = bf16[222,256]{1,0:T(8,128)(2,1)S(1)} collective-permute-done((bf16[222,256]{1,0:T(8,128)(2,1)S(1)}, bf16[222,256]{1,0:T(8,128)(2,1)S(1)}, u32[]{:S(2)}, u32[]{:S(2)}) %collective-permute-start.4) | collective-permute-done | bytes 113696 | tf_op jit(solution)/shard_map/ppermute | solution.py:407
  39.9 1.3 %collective-permute-done.6.refs_6_ = bf16[256,896]{1,0:T(8,128)(2,1)S(1)} collective-permute-done((bf16[256,896]{1,0:T(8,128)(2,1)S(1)}, bf16[256,896]{1,0:T(8,128)(2,1)S(1)}, u32[]{:S(2)}, u32[]{:S(2)}) %collective-permute-start.6) | collective-permute-done | bytes 458784 | tf_op jit(solution)/shard_map/ppermute | solution.py:411
  41.2 0.7 collective-permute-done.8.refs_8_
  41.9 7.3 %shard_map.68.sources = bf16[3072,896]{1,0:T(8,128)(2,1)S(1)} custom-call(s32[3072]{0:T(1024)S(1)} %reshape.12.spots, bf16[256,896]{1,0:T(8,128)(2,1)S(1)} %shard_map.64.refs_0_, bf16[256,896]{1,0:T(8,128)(2,1)S(1)} %get-tuple-element.34.refs_1_, bf16[512,896]{1,0:T(8,128)(2,1)S(1)} %get-tuple-element.33.other.refs_2_, ...), custom_call_target="tpu_custom_call" | custom-call | tf_op jit(solution)/shard_map/pallas_call | solution.py:33
  49.2 3.2 %collective-permute-done.9.late = bf16[256,896]{1,0:T(8,128)(2,1)S(1)} collective-permute-done((bf16[256,896]{1,0:T(8,128)(2,1)S(1)}, bf16[256,896]{1,0:T(8,128)(2,1)S(1)}, u32[]{:S(2)}, u32[]{:S(2)}) %collective-permute-start.9) | collective-permute-done | bytes 458784 | tf_op jit(solution)/shard_map/ppermute | solution.py:410
  52.7 1.5 %collective-permute-done.10.late_o = bf16[256,896]{1,0:T(8,128)(2,1)S(1)} collective-permute-done((bf16[256,896]{1,0:T(8,128)(2,1)S(1)}, bf16[256,896]{1,0:T(8,128)(2,1)S(1)}, u32[]{:S(2)}, u32[]{:S(2)}) %collective-permute-start.10) | collective-permute-done | bytes 458784 | tf_op jit(solution)/shard_map/ppermute | solution.py:415
  54.3 6.2 %shard_map.69 = (bf16[2,222,512]{2,1,0:T(8,128)(2,1)S(1)}, f32[2,222,512]{2,1,0:T(8,128)S(1)}) custom-call(s32[4]{0:T(128)S(1)} %pad_add_fusion.sc, bf16[3,888,888]{2,1,0:T(8,128)(2,1)S(1)} %bitcast.14, bf16[3072,896]{1,0:T(8,128)(2,1)S(1)} %shard_map.68.sources, s32[3,1024]{1,0:T(4,128)S(1)} %get-tuple-element.55.lists, ...), custom_call_target="tpu_custom_call" | custom-call | tf_op jit(solution)/shard_map/pallas_call | solution.py:33
  60.7 0.6 shard_map.70
  61.7 1.1 %collective-permute-done.12.ab_o = bf16[222,512]{1,0:T(8,128)(2,1)S(1)} collective-permute-done((bf16[222,512]{1,0:T(8,128)(2,1)S(1)}, bf16[222,512]{1,0:T(8,128)(2,1)S(1)}, u32[]{:S(2)}, u32[]{:S(2)}) %collective-permute-start.12) | collective-permute-done | bytes 227360 | tf_op jit(solution)/shard_map/ppermute | solution.py:416
  62.9 2.7 %shard_map.71 = (bf16[448,128]{1,0:T(8,128)(2,1)S(1)}, f32[448,128]{1,0:T(8,128)S(1)}) custom-call(s32[4]{0:T(128)S(1)} %pad_add_fusion.sc, s32[3,128]{1,0:T(4,128)S(1)} %copy-done.4, bf16[3,888,888]{2,1,0:T(8,128)(2,1)S(1)} %bitcast.14, bf16[222,256]{1,0:T(8,128)(2,1)S(1)} %shard_map.67.own, bf16[222,256]{1,0:T(8,128)(2,1)S(1)} %collective-permute-done.4.refs_0_.a, ...), custom_call_target="tpu_custom_call" | custom-call | tf_op jit(solution)/shard_map/pallas_call | solution.py:33
  66.0 0.6 shard_map.73
  67.0 0.6 shard_map.72
  67.6 2.1 %collective-permute-start.16 = (bf16[448,128]{1,0:T(8,128)(2,1)S(1)}, bf16[448,128]{1,0:T(8,128)(2,1)S(1)}, u32[]{:S(2)}, u32[]{:S(2)}) collective-permute-start(bf16[448,128]{1,0:T(8,128)(2,1)S(1)} %get-tuple-element.49), channel_id=1, source_target_pairs={{0,2},{1,3},{2,0},{3,1},{4,6},{5,7},{6,4},{7,5},{8,10},{9,11},{10,... | collective-permute-start | bytes 344072 | tf_op jit(solution)/shard_map/ppermute | solution.py:432
  69.7 6.2 %shard_map.74 = (bf16[2,222,512]{2,1,0:T(8,128)(2,1)S(1)}, f32[2,222,512]{2,1,0:T(8,128)S(1)}) custom-call(s32[4]{0:T(128)S(1)} %pad_add_fusion.sc, bf16[3,888,888]{2,1,0:T(8,128)(2,1)S(1)} %bitcast.14, bf16[3072,896]{1,0:T(8,128)(2,1)S(1)} %shard_map.68.sources, s32[3,1024]{1,0:T(4,128)S(1)} %get-tuple-element.55.lists, ...), custom_call_target="tpu_custom_call" | custom-call | tf_op jit(solution)/shard_map/pallas_call | solution.py:33
  75.9 1.0 %collective-permute-done.16.two = bf16[448,128]{1,0:T(8,128)(2,1)S(1)} collective-permute-done((bf16[448,128]{1,0:T(8,128)(2,1)S(1)}, bf16[448,128]{1,0:T(8,128)(2,1)S(1)}, u32[]{:S(2)}, u32[]{:S(2)}) %collective-permute-start.16) | collective-permute-done | bytes 114720 | tf_op jit(solution)/shard_map/ppermute | solution.py:432
  76.8 1.8 %collective-permute-done.17.got = bf16[2,222,512]{2,1,0:T(8,128)(2,1)S(1)} collective-permute-done((bf16[2,222,512]{2,1,0:T(8,128)(2,1)S(1)}, bf16[2,222,512]{2,1,0:T(8,128)(2,1)S(1)}, u32[]{:S(2)}, u32[]{:S(2)}) %collective-permute-start.17) | collective-permute-done | bytes 454688 | tf_op jit(solution)/shard_map/ppermute | solution.py:420
  78.7 0.7 shard_map.75
  79.7 0.6 shard_map.76.mine
  80.4 1.3 %collective-permute-done.18.other = bf16[448,128]{1,0:T(8,128)(2,1)S(1)} collective-permute-done((bf16[448,128]{1,0:T(8,128)(2,1)S(1)}, bf16[448,128]{1,0:T(8,128)(2,1)S(1)}, u32[]{:S(2)}, u32[]{:S(2)}) %collective-permute-start.18) | collective-permute-done | bytes 114720 | tf_op jit(solution)/shard_map/ppermute | solution.py:435
  81.7 2.9 %shard_map.77.spread = f32[222,1024]{1,0:T(8,128)S(1)} custom-call(s32[4]{0:T(128)S(1)} %pad_add_fusion.sc, bf16[1776,888]{1,0:T(8,128)(2,1)S(1)} %bitcast.16, bf16[448,128]{1,0:T(8,128)(2,1)S(1)} %shard_map.76.mine, bf16[448,128]{1,0:T(8,128)(2,1)S(1)} %collective-permute-done.18.other), custom_call_target="tpu_custom_call" | custom-call | tf_op jit(solution)/shard_map/pallas_call | solution.py:33
  84.6 2.4 %collective-permute-done.19.refs_3_ = bf16[222,512]{1,0:T(8,128)(2,1)S(1)} collective-permute-done((bf16[222,512]{1,0:T(8,128)(2,1)S(1)}, bf16[222,512]{1,0:T(8,128)(2,1)S(1)}, u32[]{:S(2)}, u32[]{:S(2)}) %collective-permute-start.19) | collective-permute-done | bytes 227360 | tf_op jit(solution)/shard_map/ppermute | solution.py:421
  87.0 1.4 %shard_map.78 = bf16[222,1024]{1,0:T(8,128)(2,1)} custom-call(s32[4]{0:T(128)S(1)} %pad_add_fusion.sc, f32[222,1024]{1,0:T(8,128)S(1)} %shard_map.77.spread, f32[222,512]{1,0:T(8,128)S(1)} %get-tuple-element.53.refs_0_, bf16[222,512]{1,0:T(8,128)(2,1)S(1)} %collective-permute-done.15.refs_1_, f32[222,512]{1,0:T(8,128)S(1)} %get-tuple-element.54.refs_2_, ...), custom_call_target="tpu_custom_call" | custom-call | tf_op jit(solution)/shard_map/pallas_call | solution.py:33
  (42 shorter events, 3.8 us)
Async XLA Ops:
  0.0 1.5 %copy-start = (bf16[888,1024]{1,0:T(8,128)(2,1)S(1)}, bf16[888,1024]{1,0:T(8,128)(2,1)}, u32[]{:S(2)}) copy-start(bf16[888,1024]{1,0:T(8,128)(2,1)} %x_ref.3) | copy-start | bytes 5455876
  1.5 11.5 %copy-start.1 = (bf16[888,1024]{1,0:T(8,128)(2,1)S(1)}, bf16[888,1024]{1,0:T(8,128)(2,1)}, u32[]{:S(2)}) copy-start(bf16[888,1024]{1,0:T(8,128)(2,1)} %x_ref.3) | copy-start | bytes 5455876
  1.7 21.9 %collective-permute-start = (bf16[256,896]{1,0:T(8,128)(2,1)S(1)}, bf16[256,896]{1,0:T(8,128)(2,1)S(1)}, u32[]{:S(2)}, u32[]{:S(2)}) collective-permute-start(bf16[256,896]{1,0:T(8,128)(2,1)S(1)} %shard_map.64.refs_0_), channel_id=1, source_target_pairs={{2,4},{3,5},{6,8},{7,9},{10,12},{11,13},{14,16},{15,17},{18,20},{1... | collective-permute-start | bytes 1376264 | tf_op jit(solution)/shard_map/ppermute | solution.py:402
  14.0 1.9 %copy-start.2 = (bf16[8,222,888]{2,0,1:T(8,128)(2,1)S(1)}, bf16[8,222,888]{2,0,1:T(8,128)(2,1)}, u32[]{:S(2)}) copy-start(bf16[8,222,888]{2,0,1:T(8,128)(2,1)} %param.7) | copy-start | bytes 9462532
  18.7 4.3 %collective-permute-start.2 = (bf16[222,128]{1,0:T(8,128)(2,1)S(1)}, bf16[222,128]{1,0:T(8,128)(2,1)S(1)}, u32[]{:S(2)}, u32[]{:S(2)}) collective-permute-start(bf16[222,128]{1,0:T(8,128)(2,1)S(1)} %shard_map.66.refs_0_), channel_id=1, source_target_pairs={{0,2},{1,3},{2,0},{3,1},{4,6},{5,7},{6,4},{7,5},{8,10},{9,11},{10,... | collective-permute-start | bytes 170504 | tf_op jit(solution)/shard_map/ppermute | solution.py:403
  18.8 20.6 %collective-permute-start.1 = (bf16[256,896]{1,0:T(8,128)(2,1)S(1)}, bf16[256,896]{1,0:T(8,128)(2,1)S(1)}, u32[]{:S(2)}, u32[]{:S(2)}) collective-permute-start(bf16[256,896]{1,0:T(8,128)(2,1)S(1)} %get-tuple-element.34.refs_1_), channel_id=1, source_target_pairs={{2,4},{3,5},{6,8},{7,9},{10,12},{11,13},{14,16},{15,17},{18,20},{1... | collective-permute-start | bytes 1376264 | tf_op jit(solution)/shard_map/ppermute | solution.py:402
  23.0 31.3 %slice-start = ((s8[4773888]{0:T(1024)(128)(4,1)}), s8[4194304]{0:T(1024)(128)(4,1)S(1)}, s32[]{:S(2)}) async-start(s8[4773888]{0:T(1024)(128)(4,1)} %bitcast.13), calls=%async_computation | async-start | bytes 8388608
  23.6 30.7 %slice-start.1 = ((s8[4773888]{0:T(1024)(128)(4,1)}), s8[579584]{0:T(1024)(128)(4,1)S(1)}, s32[]{:S(2)}) async-start(s8[4773888]{0:T(1024)(128)(4,1)} %bitcast.13), calls=%async_computation.1 | async-start | bytes 1159168
  23.6 15.8 %collective-permute-start.7 = (bf16[256,896]{1,0:T(8,128)(2,1)S(1)}, bf16[256,896]{1,0:T(8,128)(2,1)S(1)}, u32[]{:S(2)}, u32[]{:S(2)}) collective-permute-start(bf16[256,896]{1,0:T(8,128)(2,1)S(1)} %collective-permute-done.refs_3_), channel_id=1, source_target_pairs={{0,2},{1,3},{2,0},{3,1},{4,6},{5,7},{6,4},{7,5},{8,10},{9,11},{10,... | collective-permute-start | bytes 1376264 | tf_op jit(solution)/shard_map/ppermute | solution.py:405
  23.7 15.7 %collective-permute-start.4 = (bf16[222,256]{1,0:T(8,128)(2,1)S(1)}, bf16[222,256]{1,0:T(8,128)(2,1)S(1)}, u32[]{:S(2)}, u32[]{:S(2)}) collective-permute-start(bf16[222,256]{1,0:T(8,128)(2,1)S(1)} %shard_map.67.own), channel_id=1, source_target_pairs={{2,4},{3,5},{6,8},{7,9},{10,12},{11,13},{14,16},{15,17},{18,20},{1... | collective-permute-start | bytes 341000 | tf_op jit(solution)/shard_map/ppermute | solution.py:407
  30.3 9.0 %collective-permute-start.5 = (bf16[222,256]{1,0:T(8,128)(2,1)S(1)}, bf16[222,256]{1,0:T(8,128)(2,1)S(1)}, u32[]{:S(2)}, u32[]{:S(2)}) collective-permute-start(bf16[222,256]{1,0:T(8,128)(2,1)S(1)} %shard_map.67.own), channel_id=1, source_target_pairs={{0,1},{1,0},{2,3},{3,2},{4,5},{5,4},{6,7},{7,6},{8,9},{9,8},{10,11... | collective-permute-start | bytes 341000 | tf_op jit(solution)/shard_map/ppermute | solution.py:408
  30.4 10.8 %collective-permute-start.3 = (bf16[256,896]{1,0:T(8,128)(2,1)S(1)}, bf16[256,896]{1,0:T(8,128)(2,1)S(1)}, u32[]{:S(2)}, u32[]{:S(2)}) collective-permute-start(bf16[256,896]{1,0:T(8,128)(2,1)S(1)} %collective-permute-done.refs_3_), channel_id=1, source_target_pairs={{0,1},{1,0},{2,3},{3,2},{4,5},{5,4},{6,7},{7,6},{8,9},{9,8},{10,11... | collective-permute-start | bytes 1376264 | tf_op jit(solution)/shard_map/ppermute | solution.py:406
  39.4 1.8 %collective-permute-start.6 = (bf16[256,896]{1,0:T(8,128)(2,1)S(1)}, bf16[256,896]{1,0:T(8,128)(2,1)S(1)}, u32[]{:S(2)}, u32[]{:S(2)}) collective-permute-start(bf16[256,896]{1,0:T(8,128)(2,1)S(1)} %collective-permute-done.1.refs_4_), channel_id=1, source_target_pairs={{0,1},{1,0},{2,3},{3,2},{4,5},{5,4},{6,7},{7,6},{8,9},{9,8},{10,11... | collective-permute-start | bytes 1376264 | tf_op jit(solution)/shard_map/ppermute | solution.py:411
  39.4 2.5 %collective-permute-start.8 = (bf16[256,896]{1,0:T(8,128)(2,1)S(1)}, bf16[256,896]{1,0:T(8,128)(2,1)S(1)}, u32[]{:S(2)}, u32[]{:S(2)}) collective-permute-start(bf16[256,896]{1,0:T(8,128)(2,1)S(1)} %collective-permute-done.7.refs_7_), channel_id=1, source_target_pairs={{0,1},{1,0},{2,3},{3,2},{4,5},{5,4},{6,7},{7,6},{8,9},{9,8},{10,11... | collective-permute-start | bytes 1376264 | tf_op jit(solution)/shard_map/ppermute | solution.py:413
  39.9 12.5 %collective-permute-start.9 = (bf16[256,896]{1,0:T(8,128)(2,1)S(1)}, bf16[256,896]{1,0:T(8,128)(2,1)S(1)}, u32[]{:S(2)}, u32[]{:S(2)}) collective-permute-start(bf16[256,896]{1,0:T(8,128)(2,1)S(1)} %collective-permute-done.1.refs_4_), channel_id=1, source_target_pairs={{0,2},{1,3},{2,0},{3,1},{4,6},{5,7},{6,4},{7,5},{8,10},{9,11},{10,... | collective-permute-start | bytes 1376264 | tf_op jit(solution)/shard_map/ppermute | solution.py:410
  49.2 13.7 %copy-start.4 = (s32[3,128]{1,0:T(4,128)S(1)}, s32[3,128]{1,0:T(4,128)}, u32[]{:S(2)}) copy-start(s32[3,128]{1,0:T(4,128)} %lists.1) | copy-start | bytes 4612
  52.4 1.8 %collective-permute-start.10 = (bf16[256,896]{1,0:T(8,128)(2,1)S(1)}, bf16[256,896]{1,0:T(8,128)(2,1)S(1)}, u32[]{:S(2)}, u32[]{:S(2)}) collective-permute-start(bf16[256,896]{1,0:T(8,128)(2,1)S(1)} %collective-permute-done.9.late), channel_id=1, source_target_pairs={{0,1},{1,0},{2,3},{3,2},{4,5},{5,4},{6,7},{7,6},{8,9},{9,8},{10,11... | collective-permute-start | bytes 1376264 | tf_op jit(solution)/shard_map/ppermute | solution.py:415
  52.4 8.1 %collective-permute-start.11 = (bf16[222,256]{1,0:T(8,128)(2,1)S(1)}, bf16[222,256]{1,0:T(8,128)(2,1)S(1)}, u32[]{:S(2)}, u32[]{:S(2)}) collective-permute-start(bf16[222,256]{1,0:T(8,128)(2,1)S(1)} %collective-permute-done.4.refs_0_.a), channel_id=1, source_target_pairs={{0,2},{1,3},{2,0},{3,1},{4,6},{5,7},{6,4},{7,5},{8,10},{9,11},{10,... | collective-permute-start | bytes 341000 | tf_op jit(solution)/shard_map/ppermute | solution.py:412
  60.5 5.5 %collective-permute-start.14 = (bf16[2,222,512]{2,1,0:T(8,128)(2,1)S(1)}, bf16[2,222,512]{2,1,0:T(8,128)(2,1)S(1)}, u32[]{:S(2)}, u32[]{:S(2)}) collective-permute-start(bf16[2,222,512]{2,1,0:T(8,128)(2,1)S(1)} %get-tuple-element.44), channel_id=1, source_target_pairs={{0,1},{1,0},{2,3},{3,2},{4,5},{5,4},{6,7},{7,6},{8,9},{9,8},{10,11... | collective-permute-start | bytes 1363976 | tf_op jit(solution)/shard_map/ppermute | solution.py:420
  61.3 1.6 %collective-permute-start.12 = (bf16[222,512]{1,0:T(8,128)(2,1)S(1)}, bf16[222,512]{1,0:T(8,128)(2,1)S(1)}, u32[]{:S(2)}, u32[]{:S(2)}) collective-permute-start(bf16[222,512]{1,0:T(8,128)(2,1)S(1)} %shard_map.70), channel_id=1, source_target_pairs={{0,1},{1,0},{2,3},{3,2},{4,5},{5,4},{6,7},{7,6},{8,9},{9,8},{10,11... | collective-permute-start | bytes 681992 | tf_op jit(solution)/shard_map/ppermute | solution.py:416
  65.5 1.5 %collective-permute-start.13 = (bf16[448,128]{1,0:T(8,128)(2,1)S(1)}, bf16[448,128]{1,0:T(8,128)(2,1)S(1)}, u32[]{:S(2)}, u32[]{:S(2)}) collective-permute-start(bf16[448,128]{1,0:T(8,128)(2,1)S(1)} %get-tuple-element.41), channel_id=1, source_target_pairs={{0,1},{1,0},{2,3},{3,2},{4,5},{5,4},{6,7},{7,6},{8,9},{9,8},{10,11... | collective-permute-start | bytes 344072 | tf_op jit(solution)/shard_map/ppermute | solution.py:428
  66.6 10.2 %collective-permute-start.15 = (bf16[222,512]{1,0:T(8,128)(2,1)S(1)}, bf16[222,512]{1,0:T(8,128)(2,1)S(1)}, u32[]{:S(2)}, u32[]{:S(2)}) collective-permute-start(bf16[222,512]{1,0:T(8,128)(2,1)S(1)} %get-tuple-element.45), channel_id=1, source_target_pairs={{0,2},{1,3},{2,0},{3,1},{4,6},{5,7},{6,4},{7,5},{8,10},{9,11},{10,... | collective-permute-start | bytes 681992 | tf_op jit(solution)/shard_map/ppermute | solution.py:421
  67.6 9.2 %collective-permute-start.16 = (bf16[448,128]{1,0:T(8,128)(2,1)S(1)}, bf16[448,128]{1,0:T(8,128)(2,1)S(1)}, u32[]{:S(2)}, u32[]{:S(2)}) collective-permute-start(bf16[448,128]{1,0:T(8,128)(2,1)S(1)} %get-tuple-element.49), channel_id=1, source_target_pairs={{0,2},{1,3},{2,0},{3,1},{4,6},{5,7},{6,4},{7,5},{8,10},{9,11},{10,... | collective-permute-start | bytes 344072 | tf_op jit(solution)/shard_map/ppermute | solution.py:432
  69.7 12.1 %copy-start.3 = (bf16[8,222,888]{2,0,1:T(8,128)(2,1)S(1)}, bf16[8,222,888]{2,0,1:T(8,128)(2,1)}, u32[]{:S(2)}) copy-start(bf16[8,222,888]{2,0,1:T(8,128)(2,1)} %param.9) | copy-start | bytes 9462532
  76.8 1.8 %collective-permute-start.17 = (bf16[2,222,512]{2,1,0:T(8,128)(2,1)S(1)}, bf16[2,222,512]{2,1,0:T(8,128)(2,1)S(1)}, u32[]{:S(2)}, u32[]{:S(2)}) collective-permute-start(bf16[2,222,512]{2,1,0:T(8,128)(2,1)S(1)} %get-tuple-element.50), channel_id=1, source_target_pairs={{0,1},{1,0},{2,3},{3,2},{4,5},{5,4},{6,7},{7,6},{8,9},{9,8},{10,11... | collective-permute-start | bytes 1363976 | tf_op jit(solution)/shard_map/ppermute | solution.py:420
  79.3 7.7 %collective-permute-start.19 = (bf16[222,512]{1,0:T(8,128)(2,1)S(1)}, bf16[222,512]{1,0:T(8,128)(2,1)S(1)}, u32[]{:S(2)}, u32[]{:S(2)}) collective-permute-start(bf16[222,512]{1,0:T(8,128)(2,1)S(1)} %get-tuple-element.51), channel_id=1, source_target_pairs={{0,2},{1,3},{2,0},{3,1},{4,6},{5,7},{6,4},{7,5},{8,10},{9,11},{10,... | collective-permute-start | bytes 681992 | tf_op jit(solution)/shard_map/ppermute | solution.py:421
  80.3 1.4 %collective-permute-start.18 = (bf16[448,128]{1,0:T(8,128)(2,1)S(1)}, bf16[448,128]{1,0:T(8,128)(2,1)S(1)}, u32[]{:S(2)}, u32[]{:S(2)}) collective-permute-start(bf16[448,128]{1,0:T(8,128)(2,1)S(1)} %shard_map.76.mine), channel_id=1, source_target_pairs={{0,1},{1,0},{2,3},{3,2},{4,5},{5,4},{6,7},{7,6},{8,9},{9,8},{10,11... | collective-permute-start | bytes 344072 | tf_op jit(solution)/shard_map/ppermute | solution.py:435

commit v5 on v4

--- a/solution.py
+++ b/solution.py
@@ -17,12 +17,13 @@
 chunks = 2
 chunk = half // chunks
 early = 6 * half - 2 * chunk
+ahead = 640
 
 
 def one_hop(groups):
     up = [(4 * s + 2 + c, 4 * (s + 1) + c) for s in range(groups - 1) for c in (0, 1)]
-    ends = [(i, i) for i in (0, 1, 4 * groups - 2, 4 * groups - 1)]
-    return up + [(j, i) for i, j in up] + ends
+    up += [(0, 1), (4 * groups - 2, 4 * groups - 1)]
+    return up + [(j, i) for i, j in up]
 
 
 def across(groups, flip):
@@ -294,16 +295,17 @@
     )
 
 
-def far_kernel(start, width, sc, far, sources, lists, late, late_o, send, keep, result):
+def far_kernel(start, sc, far, sources, lists, late, late_o, send, keep, result):
     c = sc[0]
-    spot = lax.broadcasted_iota(jnp.int32, (width, 128), 1).astype(f32)
+    count, most = send.shape[2], result.shape[1]
     late_boxes = jnp.concatenate([late[...], late_o[...]], 0)
 
-    def tile(i):
+    def tile(at, width):
+        spot = lax.broadcasted_iota(jnp.int32, (width, 128), 1).astype(f32)
         total = None
         for k in range(3):
-            at = k * boxes + start + i * width
-            wanted = jnp.broadcast_to(lists[k : k + 1, pl.ds(start + i * width, width)].astype(f32), (128, width)).T
+            listed = lists[k : k + 1, start + at : start + at + width].astype(f32)
+            wanted = jnp.broadcast_to(listed, (128, width)).T
             hot = jnp.concatenate(
                 [
                     (wanted == spot + float(base)).astype(f32).astype(bf16)
@@ -312,7 +314,7 @@
                 1,
             )
             found = jnp.dot(hot, late_boxes, preferred_element_type=f32)
-            found = found + sources[pl.ds(at, width), :].astype(f32)
+            found = found + sources[pl.ds(k * boxes + start + at, width), :].astype(f32)
             term = lax.dot_general(
                 far[k],
                 found.astype(bf16)[:, :rows],
@@ -320,30 +322,30 @@
                 preferred_element_type=f32,
             )
             total = term if total is None else total + term
-        result[...] = total
-        lanes = pl.ds(i * width, width)
+        result[:, :width] = total
+        lanes = slice(at, at + width)
         for x in (0, 1):
-            first = result[pl.ds(share * 2 * x, share), :]
-            second = result[pl.ds(share * (2 * x + 1), share), :]
+            first = result[pl.ds(share * 2 * x, share), :width]
+            second = result[pl.ds(share * (2 * x + 1), share), :width]
             keep[x, :, lanes] = jnp.where(c == 0, first, second)
             send[x, :, lanes] = jnp.where(c == 0, second, first).astype(bf16)
 
-    for i in range(send.shape[2] // width):
-        tile(i)
-
-
-def far_partial(sc, far, sources, lists, late, late_o, start, count, width=256):
+    for at in range(0, count, most):
+        tile(at, min(most, count - at))
+
+
+def far_partial(sc, far, sources, lists, late, late_o, start, count):
     shape = (2, share, count)
     args = (far, sources, lists, late, late_o)
     return call(
-        functools.partial(far_kernel, start, width),
+        functools.partial(far_kernel, start),
         sc,
         args,
         [whole(x) for x in args],
         [whole(), whole()],
         [jax.ShapeDtypeStruct(shape, bf16), jax.ShapeDtypeStruct(shape, f32)],
         12,
-        scratch=[pltpu.VMEM((rows, width), f32)],
+        scratch=[pltpu.VMEM((rows, 256), f32)],
     )
 
 
@@ -398,22 +400,27 @@
     rest = jnp.stack([c * half + chunk, (1 - c) * half]).astype(jnp.int32)
     tail, other = turned(leaf_density, after(rest, head), [half - chunk, half])
     up = parent_rows(after(sc, spots, late_lists), up_ops, [head, tail], other)
-    mine = [head, after(tail, up)]
+    own = joined(sc, up, zswap(up))
+    ca = hop(own)
+    own_o = cswap(own)
+    mine = [head, after(tail, own_o)]
     a = [hop(m) for m in mine]
-    own = joined(sc, up, zswap(up))
-    early_a = after(a[0], own)
+    early_a = after(a[0], ca)
     b = [zswap(early_a)]
     a_o = [cswap(early_a)]
-    ca = hop(own)
-    own_o = cswap(own)
-    second = after(a[1], early_a, ca, own_o)
+    cb = zswap(ca)
+    cab_o = cswap(joined(sc, ca, cb))
+    second = after(a[1], early_a, cb, own_o)
     b.append(zswap(second))
     a_o.append(cswap(second))
-    cb = zswap(ca)
     b_o = [cswap(b[0])]
-    picked = gathered(spots, [*mine, other, *a, *a_o, b[0], b_o[0]])
-    b_o.append(cswap(after(b[1], picked)))
-    cab_o = cswap(joined(sc, ca, cb))
+
+    send, keep = coarse_partial(sc, coarse_lists, far_ops, own, ca, cb, own_o, cab_o)
+    picked = gathered(after(spots, keep), [*mine, other, *a, *a_o, b[0], b_o[0]])
+    shape = (wide // 2, parents)
+    part, part_sent = small(add_kernel, sc, (keep, cswap(send)), [(shape, f32), (shape, bf16)])
+    b_o.append(cswap(after(b[1], picked, part)))
+    part_got = zswap(part_sent)
 
     def summed(send, keep):
         shape = (share, send.shape[2])
@@ -421,18 +428,15 @@
         return here, zswap(away), away
 
     late = (b[1], b_o[1])
-    send, keep = far_partial(sc, far_ops, picked, late_lists, *late, 0, half)
-    left = summed(after(send, cb), keep)
-    send, keep = coarse_partial(after(sc, send), coarse_lists, far_ops, own, ca, cb, own_o, cab_o)
-    shape = (wide // 2, parents)
-    part, part_sent = small(add_kernel, sc, (keep, cswap(send)), [(shape, f32), (shape, bf16)])
+    send, keep = far_partial(after(sc, part), far_ops, picked, late_lists, *late, 0, ahead)
+    left = summed(after(send, part_got), keep)
+    check = small(add_kernel, sc, (part, part_got), [(shape, bf16)])[0]
+    check_o = cswap(check)
     send, keep = far_partial(
-        after(sc, part, left[2]), far_ops, picked, late_lists, *late, half, half
-    )
-    part_got = zswap(part_sent)
-    right = summed(after(send, left[1], part_got), keep)
-    check = small(add_kernel, sc, (part, part_got), [(shape, bf16)])[0]
-    spread = downward(after(sc, right[2]), down_ops, check, cswap(check))
+        after(sc, check, left[2]), far_ops, picked, late_lists, *late, ahead, boxes - ahead
+    )
+    right = summed(after(send, left[1], check_o), keep)
+    spread = downward(after(sc, right[2]), down_ops, check, check_o)
     return small(last_kernel, sc, (spread, *left[:2], *right[:2]), [((share, boxes), bf16)])[0]
 
 

time: 88.7 us -> 93.3 us (1.052)
  waiting for transfers between devices: 23 us -> 30.3 us
  starting transfers between devices: 26.4 us -> 23.1 us
    ppermute x1, waiting for transfers between devices: 0.01 us -> 12 us  [local(): cb = zswap(ca)]
    ppermute x1, starting transfers between devices: 6.65 us -> 0.33 us  [local(): ca = hop(own)]
    ppermute x1, waiting for transfers between devices: 8.43 us -> 3.92 us  [local(): ca = hop(own)]
    ppermute x1, waiting for transfers between devices: 0.26 us -> 4.16 us  [local(): own = joined(sc, up, zswap(up))]
    ppermute x1, waiting for transfers between devices: 3.23 us -> 0.01 us  [local(): b.append(zswap(second))]
    ppermute x2, waiting for transfers between devices: 2.84 us -> 0.01 us  [the longest x1 0.01 us: local(): b_o.append(cswap(after(b[1], picked, part)))]
    ppermute x2, starting transfers between devices: 0.77 us -> 3.48 us  [summed(): return (here, zswap(away), away)]
    ppermute x2, waiting for transfers between devices: 1.82 us -> 3.57 us  [summed(): cswap(send)]
  transfers between devices with their start and end apart: 20 -> 20, of which waited for: 11 -> 10; matrix products, arithmetic and copies ran while one was open for 1% -> 1% of each run, Pallas kernels for 36% -> 34%
where the time goes in v5:
time: 93.3 us; the launch traced here: 93.2 us
  Pallas kernels  34.5 us (37%)
  waiting for transfers between devices  30.3 us (32%)
  starting transfers between devices  23.1 us (25%)
  local copies, waits for them, and re-layouts  4.07 us (4%)
    pallas_call x15, Pallas kernels, call(): pl.pallas_call(kernel, grid_spec=pltpu.PrefetchScalarGridSpec(num_scalar_...  34.5 us
    ppermute x2, starting transfers between devices, local(): a = [hop(m) for m in mine]  13.3 us
    ppermute x1, waiting for transfers between devices, local(): cb = zswap(ca)  12 us
    ppermute x1, waiting for transfers between devices, local(): own = joined(sc, up, zswap(up))  4.16 us
    ppermute x1, waiting for transfers between devices, local(): ca = hop(own)  3.92 us
    ppermute x2, waiting for transfers between devices, summed(): cswap(send)  3.57 us
    unnamed x12, local copies, waits for them, and re-layouts  3.56 us
    ppermute x2, starting transfers between devices, summed(): return (here, zswap(away), away)  3.48 us
  transfers between devices with their start and end apart: 20, of which 10 were waited for; matrix products, arithmetic and copies ran while one was open for 1% of the time, Pallas kernels for 34%

profile of v5, /device:TPU:24, one launch (start us, length us, event | category | flops | bytes accessed | tf_op | source)
XLA Modules:
  0.0 93.2 jit_solution(8629705397823055731)
XLA Ops:
  0.0 1.5 %copy-done.1 = bf16[888,1024]{1,0:T(8,128)(2,1)S(1)} copy-done((bf16[888,1024]{1,0:T(8,128)(2,1)S(1)}, bf16[888,1024]{1,0:T(8,128)(2,1)}, u32[]{:S(2)}) %copy-start.1) | copy-done | bytes 1818648
  1.7 8.3 %collective-permute-start.7 = (bf16[256,896]{1,0:T(8,128)(2,1)S(1)}, bf16[256,896]{1,0:T(8,128)(2,1)S(1)}, u32[]{:S(2)}, u32[]{:S(2)}) collective-permute-start(bf16[256,896]{1,0:T(8,128)(2,1)S(1)} %shard_map.64.refs_0_), channel_id=1, source_target_pairs={{2,4},{3,5},{6,8},{7,9},{10,12},{11,13},{14,16},{15,17},{18,20},{1... | collective-permute-start | bytes 1376264 | tf_op jit(solution)/shard_map/ppermute | solution.py:407
  10.0 0.8 fusion.6
  11.0 1.0 %shard_map.65 = (bf16[256,896]{1,0:T(8,128)(2,1)S(1)}, bf16[512,896]{1,0:T(8,128)(2,1)S(1)}) custom-call(s32[2]{0:T(128)S(1)} %pad_add_fusion.1.firsts, bf16[888,1024]{1,0:T(8,128)(2,1)S(1)} %copy-done.2), custom_call_target="tpu_custom_call" | custom-call | tf_op jit(solution)/shard_map/pallas_call | solution.py:34
  12.0 2.0 %copy-done.3 = bf16[8,222,888]{2,0,1:T(8,128)(2,1)S(1)} copy-done((bf16[8,222,888]{2,0,1:T(8,128)(2,1)S(1)}, bf16[8,222,888]{2,0,1:T(8,128)(2,1)}, u32[]{:S(2)}) %copy-start.3) | copy-done | bytes 3154200
  14.1 2.9 %shard_map.66.refs_0_ = bf16[222,128]{1,0:T(8,128)(2,1)S(1)} custom-call(s32[4]{0:T(128)S(1)} %pad_add_fusion.sc, bf16[1776,888]{1,0:T(8,128)(2,1)S(1)} %bitcast.13, bf16[512,896]{1,0:T(8,128)(2,1)S(1)} %get-tuple-element.33.other.refs_2_, bf16[256,896]{1,0:T(8,128)(2,1)S(1)} %shard_map.64.refs_0_, bf16[256,896]{1,0:T(8,128)(2,1)S(1)} %get-tuple-element.41.refs_1_), custom_call_target="tpu_custom_call" | custom-call | tf_op jit(solution)/shard_map/pallas_call | solution.py:34
  17.0 4.2 %collective-permute-done.refs_1_ = bf16[222,128]{1,0:T(8,128)(2,1)S(1)} collective-permute-done((bf16[222,128]{1,0:T(8,128)(2,1)S(1)}, bf16[222,128]{1,0:T(8,128)(2,1)S(1)}, u32[]{:S(2)}, u32[]{:S(2)}) %collective-permute-start) | collective-permute-done | bytes 56864 | tf_op jit(solution)/shard_map/ppermute | solution.py:403
  21.2 0.6 shard_map.67.own
  22.2 1.0 %collective-permute-done.3.own_o = bf16[222,256]{1,0:T(8,128)(2,1)S(1)} collective-permute-done((bf16[222,256]{1,0:T(8,128)(2,1)S(1)}, bf16[222,256]{1,0:T(8,128)(2,1)S(1)}, u32[]{:S(2)}, u32[]{:S(2)}) %collective-permute-start.3) | collective-permute-done | bytes 113696 | tf_op jit(solution)/shard_map/ppermute | solution.py:405
  23.2 5.0 %collective-permute-start.8 = (bf16[256,896]{1,0:T(8,128)(2,1)S(1)}, bf16[256,896]{1,0:T(8,128)(2,1)S(1)}, u32[]{:S(2)}, u32[]{:S(2)}) collective-permute-start(bf16[256,896]{1,0:T(8,128)(2,1)S(1)} %get-tuple-element.41.refs_1_), channel_id=1, source_target_pairs={{2,4},{3,5},{6,8},{7,9},{10,12},{11,13},{14,16},{15,17},{18,20},{1... | collective-permute-start | bytes 1376264 | tf_op jit(solution)/shard_map/ppermute | solution.py:407
  28.2 3.9 %collective-permute-done.1.refs_0_.a = bf16[222,256]{1,0:T(8,128)(2,1)S(1)} collective-permute-done((bf16[222,256]{1,0:T(8,128)(2,1)S(1)}, bf16[222,256]{1,0:T(8,128)(2,1)S(1)}, u32[]{:S(2)}, u32[]{:S(2)}) %collective-permute-start.1) | collective-permute-done | bytes 113696 | tf_op jit(solution)/shard_map/ppermute | solution.py:404
  32.1 2.0 %collective-permute-start.2 = (bf16[222,256]{1,0:T(8,128)(2,1)S(1)}, bf16[222,256]{1,0:T(8,128)(2,1)S(1)}, u32[]{:S(2)}, u32[]{:S(2)}) collective-permute-start(bf16[222,256]{1,0:T(8,128)(2,1)S(1)} %collective-permute-done.1.refs_0_.a), channel_id=1, source_target_pairs={{0,2},{1,3},{2,0},{3,1},{4,6},{5,7},{6,4},{7,5},{8,10},{9,11},{10,... | collective-permute-start | bytes 341000 | tf_op jit(solution)/shard_map/ppermute | solution.py:411
  34.2 12.0 %collective-permute-done.2.refs_1_.b = bf16[222,256]{1,0:T(8,128)(2,1)S(1)} collective-permute-done((bf16[222,256]{1,0:T(8,128)(2,1)S(1)}, bf16[222,256]{1,0:T(8,128)(2,1)S(1)}, u32[]{:S(2)}, u32[]{:S(2)}) %collective-permute-start.2) | collective-permute-done | bytes 113696 | tf_op jit(solution)/shard_map/ppermute | solution.py:411
  47.6 1.5 %collective-permute-done.4.ab_o = bf16[222,512]{1,0:T(8,128)(2,1)S(1)} collective-permute-done((bf16[222,512]{1,0:T(8,128)(2,1)S(1)}, bf16[222,512]{1,0:T(8,128)(2,1)S(1)}, u32[]{:S(2)}, u32[]{:S(2)}) %collective-permute-start.4) | collective-permute-done | bytes 227360 | tf_op jit(solution)/shard_map/ppermute | solution.py:412
  49.1 2.7 %shard_map.69 = (bf16[448,128]{1,0:T(8,128)(2,1)S(1)}, f32[448,128]{1,0:T(8,128)S(1)}) custom-call(s32[4]{0:T(128)S(1)} %pad_add_fusion.sc, s32[3,128]{1,0:T(4,128)S(1)} %copy-done.5, bf16[3,888,888]{2,1,0:T(8,128)(2,1)S(1)} %copy-done, bf16[222,256]{1,0:T(8,128)(2,1)S(1)} %shard_map.67.own, bf16[222,256]{1,0:T(8,128)(2,1)S(1)} %collective-permute-done.1.refs_0_.a, ...), custom_call_target="tpu_custom_call" | custom-call | tf_op jit(solution)/shard_map/pallas_call | solution.py:34
  52.2 1.2 %collective-permute-done.5.two = bf16[448,128]{1,0:T(8,128)(2,1)S(1)} collective-permute-done((bf16[448,128]{1,0:T(8,128)(2,1)S(1)}, bf16[448,128]{1,0:T(8,128)(2,1)S(1)}, u32[]{:S(2)}, u32[]{:S(2)}) %collective-permute-start.5) | collective-permute-done | bytes 114720 | tf_op jit(solution)/shard_map/ppermute | solution.py:421
  53.4 0.6 shard_map.70
  54.0 7.3 %shard_map.72.sources = bf16[3072,896]{1,0:T(8,128)(2,1)S(1)} custom-call(s32[3072]{0:T(1024)S(1)} %reshape.12.spots, bf16[256,896]{1,0:T(8,128)(2,1)S(1)} %shard_map.64.refs_0_, bf16[256,896]{1,0:T(8,128)(2,1)S(1)} %get-tuple-element.41.refs_1_, bf16[512,896]{1,0:T(8,128)(2,1)S(1)} %get-tuple-element.33.other.refs_2_, ...), custom_call_target="tpu_custom_call" | custom-call | tf_op jit(solution)/shard_map/pallas_call | solution.py:34
  61.6 1.8 %collective-permute-start.6 = (bf16[448,128]{1,0:T(8,128)(2,1)S(1)}, bf16[448,128]{1,0:T(8,128)(2,1)S(1)}, u32[]{:S(2)}, u32[]{:S(2)}) collective-permute-start(bf16[448,128]{1,0:T(8,128)(2,1)S(1)} %get-tuple-element.38), channel_id=1, source_target_pairs={{0,2},{1,3},{2,0},{3,1},{4,6},{5,7},{6,4},{7,5},{8,10},{9,11},{10,... | collective-permute-start | bytes 344072 | tf_op jit(solution)/shard_map/ppermute | solution.py:423
  63.3 7.3 %shard_map.73 = (bf16[2,222,640]{2,1,0:T(8,128)(2,1)S(1)}, f32[2,222,640]{2,1,0:T(8,128)S(1)}) custom-call(s32[4]{0:T(128)S(1)} %pad_add_fusion.sc, bf16[3,888,888]{2,1,0:T(8,128)(2,1)S(1)} %copy-done, bf16[3072,896]{1,0:T(8,128)(2,1)S(1)} %shard_map.72.sources, s32[3,1024]{1,0:T(4,128)S(1)} %get-tuple-element.57.lists, ...), custom_call_target="tpu_custom_call" | custom-call | tf_op jit(solution)/shard_map/pallas_call | solution.py:34
  71.3 1.9 %collective-permute-done.15 = bf16[2,222,640]{2,0,1:T(2,128)(2,1)S(1)} collective-permute-done((bf16[2,222,640]{2,0,1:T(2,128)(2,1)S(1)}, bf16[2,222,640]{2,0,1:T(2,128)(2,1)S(1)}, u32[]{:S(2)}, u32[]{:S(2)}) %collective-permute-start.15) | collective-permute-done | bytes 568352 | tf_op jit(solution)/shard_map/ppermute | solution.py:427
  73.3 0.7 shard_map.74
  74.0 1.7 %collective-permute-start.16 = (bf16[222,640]{1,0:T(8,128)(2,1)S(1)}, bf16[222,640]{1,0:T(8,128)(2,1)S(1)}, u32[]{:S(2)}, u32[]{:S(2)}) collective-permute-start(bf16[222,640]{1,0:T(8,128)(2,1)S(1)} %get-tuple-element.48), channel_id=1, source_target_pairs={{0,2},{1,3},{2,0},{3,1},{4,6},{5,7},{6,4},{7,5},{8,10},{9,11},{10,... | collective-permute-start | bytes 852488 | tf_op jit(solution)/shard_map/ppermute | solution.py:428
  75.7 0.6 shard_map.71.mine
  76.6 5.1 %shard_map.75 = (bf16[2,222,384]{2,1,0:T(8,128)(2,1)S(1)}, f32[2,222,384]{2,1,0:T(8,128)S(1)}) custom-call(s32[4]{0:T(128)S(1)} %pad_add_fusion.sc, bf16[3,888,888]{2,1,0:T(8,128)(2,1)S(1)} %copy-done, bf16[3072,896]{1,0:T(8,128)(2,1)S(1)} %shard_map.72.sources, s32[3,1024]{1,0:T(4,128)S(1)} %get-tuple-element.57.lists, ...), custom_call_target="tpu_custom_call" | custom-call | tf_op jit(solution)/shard_map/pallas_call | solution.py:34
  81.7 1.2 %collective-permute-done.16.refs_1_ = bf16[222,640]{1,0:T(8,128)(2,1)S(1)} collective-permute-done((bf16[222,640]{1,0:T(8,128)(2,1)S(1)}, bf16[222,640]{1,0:T(8,128)(2,1)S(1)}, u32[]{:S(2)}, u32[]{:S(2)}) %collective-permute-start.16) | collective-permute-done | bytes 284192 | tf_op jit(solution)/shard_map/ppermute | solution.py:428
  82.9 1.6 %collective-permute-done.18.got = bf16[2,222,384]{2,1,0:T(8,128)(2,1)S(1)} collective-permute-done((bf16[2,222,384]{2,1,0:T(8,128)(2,1)S(1)}, bf16[2,222,384]{2,1,0:T(8,128)(2,1)S(1)}, u32[]{:S(2)}, u32[]{:S(2)}) %collective-permute-start.18) | collective-permute-done | bytes 341024 | tf_op jit(solution)/shard_map/ppermute | solution.py:427
  84.6 0.6 shard_map.76
  85.2 1.7 %collective-permute-start.19 = (bf16[222,384]{1,0:T(8,128)(2,1)S(1)}, bf16[222,384]{1,0:T(8,128)(2,1)S(1)}, u32[]{:S(2)}, u32[]{:S(2)}) collective-permute-start(bf16[222,384]{1,0:T(8,128)(2,1)S(1)} %get-tuple-element.53), channel_id=1, source_target_pairs={{0,2},{1,3},{2,0},{3,1},{4,6},{5,7},{6,4},{7,5},{8,10},{9,11},{10,... | collective-permute-start | bytes 511496 | tf_op jit(solution)/shard_map/ppermute | solution.py:428
  86.9 3.0 %shard_map.77.spread = f32[222,1024]{1,0:T(8,128)S(1)} custom-call(s32[4]{0:T(128)S(1)} %pad_add_fusion.sc, bf16[1776,888]{1,0:T(8,128)(2,1)S(1)} %bitcast.14, bf16[448,128]{1,0:T(8,128)(2,1)S(1)} %shard_map.71.mine, bf16[448,128]{1,0:T(8,128)(2,1)S(1)} %collective-permute-done.17.other), custom_call_target="tpu_custom_call" | custom-call | tf_op jit(solution)/shard_map/pallas_call | solution.py:34
  89.9 1.8 %collective-permute-done.19.refs_3_ = bf16[222,384]{1,0:T(8,128)(2,1)S(1)} collective-permute-done((bf16[222,384]{1,0:T(8,128)(2,1)S(1)}, bf16[222,384]{1,0:T(8,128)(2,1)S(1)}, u32[]{:S(2)}, u32[]{:S(2)}) %collective-permute-start.19) | collective-permute-done | bytes 170528 | tf_op jit(solution)/shard_map/ppermute | solution.py:428
  91.7 1.5 %shard_map.78 = bf16[222,1024]{1,0:T(8,128)(2,1)} custom-call(s32[4]{0:T(128)S(1)} %pad_add_fusion.sc, f32[222,1024]{1,0:T(8,128)S(1)} %shard_map.77.spread, f32[222,640]{1,0:T(8,128)S(1)} %get-tuple-element.55.refs_0_, bf16[222,640]{1,0:T(8,128)(2,1)S(1)} %collective-permute-done.16.refs_1_, f32[222,384]{1,0:T(8,128)S(1)} %get-tuple-element.56.refs_2_, ...), custom_call_target="tpu_custom_call" | custom-call | tf_op jit(solution)/shard_map/pallas_call | solution.py:34
  (41 shorter events, 4.0 us)
Async XLA Ops:
  0.0 1.5 %copy-start.1 = (bf16[888,1024]{1,0:T(8,128)(2,1)S(1)}, bf16[888,1024]{1,0:T(8,128)(2,1)}, u32[]{:S(2)}) copy-start(bf16[888,1024]{1,0:T(8,128)(2,1)} %x_ref.3) | copy-start | bytes 5455876
  1.5 9.5 %copy-start.2 = (bf16[888,1024]{1,0:T(8,128)(2,1)S(1)}, bf16[888,1024]{1,0:T(8,128)(2,1)}, u32[]{:S(2)}) copy-start(bf16[888,1024]{1,0:T(8,128)(2,1)} %x_ref.3) | copy-start | bytes 5455876
  1.7 30.4 %collective-permute-start.7 = (bf16[256,896]{1,0:T(8,128)(2,1)S(1)}, bf16[256,896]{1,0:T(8,128)(2,1)S(1)}, u32[]{:S(2)}, u32[]{:S(2)}) collective-permute-start(bf16[256,896]{1,0:T(8,128)(2,1)S(1)} %shard_map.64.refs_0_), channel_id=1, source_target_pairs={{2,4},{3,5},{6,8},{7,9},{10,12},{11,13},{14,16},{15,17},{18,20},{1... | collective-permute-start | bytes 1376264 | tf_op jit(solution)/shard_map/ppermute | solution.py:407
  11.0 38.1 %copy-start.5 = (s32[3,128]{1,0:T(4,128)S(1)}, s32[3,128]{1,0:T(4,128)}, u32[]{:S(2)}) copy-start(s32[3,128]{1,0:T(4,128)} %lists.1) | copy-start | bytes 4612
  12.0 37.1 %copy-start = (bf16[3,888,888]{2,1,0:T(8,128)(2,1)S(1)}, bf16[3,888,888]{2,1,0:T(8,128)(2,1)}, u32[]{:S(2)}) copy-start(bf16[3,888,888]{2,1,0:T(8,128)(2,1)} %far.5) | copy-start | bytes 14193796
  12.0 2.1 %copy-start.3 = (bf16[8,222,888]{2,0,1:T(8,128)(2,1)S(1)}, bf16[8,222,888]{2,0,1:T(8,128)(2,1)}, u32[]{:S(2)}) copy-start(bf16[8,222,888]{2,0,1:T(8,128)(2,1)} %param.7) | copy-start | bytes 9462532
  16.9 4.3 %collective-permute-start = (bf16[222,128]{1,0:T(8,128)(2,1)S(1)}, bf16[222,128]{1,0:T(8,128)(2,1)S(1)}, u32[]{:S(2)}, u32[]{:S(2)}) collective-permute-start(bf16[222,128]{1,0:T(8,128)(2,1)S(1)} %shard_map.66.refs_0_), channel_id=1, source_target_pairs={{0,2},{1,3},{2,0},{3,1},{4,6},{5,7},{6,4},{7,5},{8,10},{9,11},{10,... | collective-permute-start | bytes 170504 | tf_op jit(solution)/shard_map/ppermute | solution.py:403
  21.8 1.4 %collective-permute-start.3 = (bf16[222,256]{1,0:T(8,128)(2,1)S(1)}, bf16[222,256]{1,0:T(8,128)(2,1)S(1)}, u32[]{:S(2)}, u32[]{:S(2)}) collective-permute-start(bf16[222,256]{1,0:T(8,128)(2,1)S(1)} %shard_map.67.own), channel_id=1, source_target_pairs={{0,1},{1,0},{2,3},{3,2},{4,5},{5,4},{6,7},{7,6},{8,9},{9,8},{10,11... | collective-permute-start | bytes 341000 | tf_op jit(solution)/shard_map/ppermute | solution.py:405
  21.9 10.3 %collective-permute-start.1 = (bf16[222,256]{1,0:T(8,128)(2,1)S(1)}, bf16[222,256]{1,0:T(8,128)(2,1)S(1)}, u32[]{:S(2)}, u32[]{:S(2)}) collective-permute-start(bf16[222,256]{1,0:T(8,128)(2,1)S(1)} %shard_map.67.own), channel_id=1, source_target_pairs={{2,4},{3,5},{6,8},{7,9},{10,12},{11,13},{14,16},{15,17},{18,20},{1... | collective-permute-start | bytes 341000 | tf_op jit(solution)/shard_map/ppermute | solution.py:404
  23.2 23.0 %collective-permute-start.8 = (bf16[256,896]{1,0:T(8,128)(2,1)S(1)}, bf16[256,896]{1,0:T(8,128)(2,1)S(1)}, u32[]{:S(2)}, u32[]{:S(2)}) collective-permute-start(bf16[256,896]{1,0:T(8,128)(2,1)S(1)} %get-tuple-element.41.refs_1_), channel_id=1, source_target_pairs={{2,4},{3,5},{6,8},{7,9},{10,12},{11,13},{14,16},{15,17},{18,20},{1... | collective-permute-start | bytes 1376264 | tf_op jit(solution)/shard_map/ppermute | solution.py:407
  32.1 14.1 %collective-permute-start.11 = (bf16[256,896]{1,0:T(8,128)(2,1)S(1)}, bf16[256,896]{1,0:T(8,128)(2,1)S(1)}, u32[]{:S(2)}, u32[]{:S(2)}) collective-permute-start(bf16[256,896]{1,0:T(8,128)(2,1)S(1)} %collective-permute-done.7.refs_3_), channel_id=1, source_target_pairs={{0,2},{1,3},{2,0},{3,1},{4,6},{5,7},{6,4},{7,5},{8,10},{9,11},{10,... | collective-permute-start | bytes 1376264 | tf_op jit(solution)/shard_map/ppermute | solution.py:409
  32.1 14.0 %collective-permute-start.2 = (bf16[222,256]{1,0:T(8,128)(2,1)S(1)}, bf16[222,256]{1,0:T(8,128)(2,1)S(1)}, u32[]{:S(2)}, u32[]{:S(2)}) collective-permute-start(bf16[222,256]{1,0:T(8,128)(2,1)S(1)} %collective-permute-done.1.refs_0_.a), channel_id=1, source_target_pairs={{0,2},{1,3},{2,0},{3,1},{4,6},{5,7},{6,4},{7,5},{8,10},{9,11},{10,... | collective-permute-start | bytes 341000 | tf_op jit(solution)/shard_map/ppermute | solution.py:411
  34.2 19.8 %collective-permute-start.9 = (bf16[256,896]{1,0:T(8,128)(2,1)S(1)}, bf16[256,896]{1,0:T(8,128)(2,1)S(1)}, u32[]{:S(2)}, u32[]{:S(2)}) collective-permute-start(bf16[256,896]{1,0:T(8,128)(2,1)S(1)} %collective-permute-done.7.refs_3_), channel_id=1, source_target_pairs={{0,1},{1,0},{2,3},{3,2},{4,5},{5,4},{6,7},{7,6},{8,9},{9,8},{10,11... | collective-permute-start | bytes 1376264 | tf_op jit(solution)/shard_map/ppermute | solution.py:410
  46.2 7.8 %collective-permute-start.10 = (bf16[256,896]{1,0:T(8,128)(2,1)S(1)}, bf16[256,896]{1,0:T(8,128)(2,1)S(1)}, u32[]{:S(2)}, u32[]{:S(2)}) collective-permute-start(bf16[256,896]{1,0:T(8,128)(2,1)S(1)} %collective-permute-done.8.refs_4_), channel_id=1, source_target_pairs={{0,1},{1,0},{2,3},{3,2},{4,5},{5,4},{6,7},{7,6},{8,9},{9,8},{10,11... | collective-permute-start | bytes 1376264 | tf_op jit(solution)/shard_map/ppermute | solution.py:415
  46.2 7.8 %collective-permute-start.12 = (bf16[256,896]{1,0:T(8,128)(2,1)S(1)}, bf16[256,896]{1,0:T(8,128)(2,1)S(1)}, u32[]{:S(2)}, u32[]{:S(2)}) collective-permute-start(bf16[256,896]{1,0:T(8,128)(2,1)S(1)} %collective-permute-done.11.refs_7_), channel_id=1, source_target_pairs={{0,1},{1,0},{2,3},{3,2},{4,5},{5,4},{6,7},{7,6},{8,9},{9,8},{10,11... | collective-permute-start | bytes 1376264 | tf_op jit(solution)/shard_map/ppermute | solution.py:416
  46.7 14.6 %collective-permute-start.13 = (bf16[256,896]{1,0:T(8,128)(2,1)S(1)}, bf16[256,896]{1,0:T(8,128)(2,1)S(1)}, u32[]{:S(2)}, u32[]{:S(2)}) collective-permute-start(bf16[256,896]{1,0:T(8,128)(2,1)S(1)} %collective-permute-done.8.refs_4_), channel_id=1, source_target_pairs={{0,2},{1,3},{2,0},{3,1},{4,6},{5,7},{6,4},{7,5},{8,10},{9,11},{10,... | collective-permute-start | bytes 1376264 | tf_op jit(solution)/shard_map/ppermute | solution.py:414
  47.5 1.6 %collective-permute-start.4 = (bf16[222,512]{1,0:T(8,128)(2,1)S(1)}, bf16[222,512]{1,0:T(8,128)(2,1)S(1)}, u32[]{:S(2)}, u32[]{:S(2)}) collective-permute-start(bf16[222,512]{1,0:T(8,128)(2,1)S(1)} %shard_map.68), channel_id=1, source_target_pairs={{0,1},{1,0},{2,3},{3,2},{4,5},{5,4},{6,7},{7,6},{8,9},{9,8},{10,11... | collective-permute-start | bytes 681992 | tf_op jit(solution)/shard_map/ppermute | solution.py:412
  51.8 1.6 %collective-permute-start.5 = (bf16[448,128]{1,0:T(8,128)(2,1)S(1)}, bf16[448,128]{1,0:T(8,128)(2,1)S(1)}, u32[]{:S(2)}, u32[]{:S(2)}) collective-permute-start(bf16[448,128]{1,0:T(8,128)(2,1)S(1)} %get-tuple-element.36), channel_id=1, source_target_pairs={{0,1},{1,0},{2,3},{3,2},{4,5},{5,4},{6,7},{7,6},{8,9},{9,8},{10,11... | collective-permute-start | bytes 344072 | tf_op jit(solution)/shard_map/ppermute | solution.py:421
  61.3 2.0 %collective-permute-start.14 = (bf16[256,896]{1,0:T(8,128)(2,1)S(1)}, bf16[256,896]{1,0:T(8,128)(2,1)S(1)}, u32[]{:S(2)}, u32[]{:S(2)}) collective-permute-start(bf16[256,896]{1,0:T(8,128)(2,1)S(1)} %collective-permute-done.13.late), channel_id=1, source_target_pairs={{0,1},{1,0},{2,3},{3,2},{4,5},{5,4},{6,7},{7,6},{8,9},{9,8},{10,11... | collective-permute-start | bytes 1376264 | tf_op jit(solution)/shard_map/ppermute | solution.py:422
  61.6 9.1 %collective-permute-start.6 = (bf16[448,128]{1,0:T(8,128)(2,1)S(1)}, bf16[448,128]{1,0:T(8,128)(2,1)S(1)}, u32[]{:S(2)}, u32[]{:S(2)}) collective-permute-start(bf16[448,128]{1,0:T(8,128)(2,1)S(1)} %get-tuple-element.38), channel_id=1, source_target_pairs={{0,2},{1,3},{2,0},{3,1},{4,6},{5,7},{6,4},{7,5},{8,10},{9,11},{10,... | collective-permute-start | bytes 344072 | tf_op jit(solution)/shard_map/ppermute | solution.py:423
  71.1 2.1 %collective-permute-start.15 = (bf16[2,222,640]{2,0,1:T(2,128)(2,1)S(1)}, bf16[2,222,640]{2,0,1:T(2,128)(2,1)S(1)}, u32[]{:S(2)}, u32[]{:S(2)}) collective-permute-start(bf16[2,222,640]{2,0,1:T(2,128)(2,1)S(1)} %copy.7), channel_id=1, source_target_pairs={{0,1},{1,0},{2,3},{3,2},{4,5},{5,4},{6,7},{7,6},{8,9},{9,8},{10,11... | collective-permute-start | bytes 1704968 | tf_op jit(solution)/shard_map/ppermute | solution.py:427
  74.0 9.0 %collective-permute-start.16 = (bf16[222,640]{1,0:T(8,128)(2,1)S(1)}, bf16[222,640]{1,0:T(8,128)(2,1)S(1)}, u32[]{:S(2)}, u32[]{:S(2)}) collective-permute-start(bf16[222,640]{1,0:T(8,128)(2,1)S(1)} %get-tuple-element.48), channel_id=1, source_target_pairs={{0,2},{1,3},{2,0},{3,1},{4,6},{5,7},{6,4},{7,5},{8,10},{9,11},{10,... | collective-permute-start | bytes 852488 | tf_op jit(solution)/shard_map/ppermute | solution.py:428
  76.2 5.5 %collective-permute-start.17 = (bf16[448,128]{1,0:T(8,128)(2,1)S(1)}, bf16[448,128]{1,0:T(8,128)(2,1)S(1)}, u32[]{:S(2)}, u32[]{:S(2)}) collective-permute-start(bf16[448,128]{1,0:T(8,128)(2,1)S(1)} %shard_map.71.mine), channel_id=1, source_target_pairs={{0,1},{1,0},{2,3},{3,2},{4,5},{5,4},{6,7},{7,6},{8,9},{9,8},{10,11... | collective-permute-start | bytes 344072 | tf_op jit(solution)/shard_map/ppermute | solution.py:434
  76.6 10.4 %copy-start.4 = (bf16[8,222,888]{2,0,1:T(8,128)(2,1)S(1)}, bf16[8,222,888]{2,0,1:T(8,128)(2,1)}, u32[]{:S(2)}) copy-start(bf16[8,222,888]{2,0,1:T(8,128)(2,1)} %param.9) | copy-start | bytes 9462532
  82.9 1.7 %collective-permute-start.18 = (bf16[2,222,384]{2,1,0:T(8,128)(2,1)S(1)}, bf16[2,222,384]{2,1,0:T(8,128)(2,1)S(1)}, u32[]{:S(2)}, u32[]{:S(2)}) collective-permute-start(bf16[2,222,384]{2,1,0:T(8,128)(2,1)S(1)} %get-tuple-element.52), channel_id=1, source_target_pairs={{0,1},{1,0},{2,3},{3,2},{4,5},{5,4},{6,7},{7,6},{8,9},{9,8},{10,11... | collective-permute-start | bytes 1022984 | tf_op jit(solution)/shard_map/ppermute | solution.py:427
  85.2 6.5 %collective-permute-start.19 = (bf16[222,384]{1,0:T(8,128)(2,1)S(1)}, bf16[222,384]{1,0:T(8,128)(2,1)S(1)}, u32[]{:S(2)}, u32[]{:S(2)}) collective-permute-start(bf16[222,384]{1,0:T(8,128)(2,1)S(1)} %get-tuple-element.53), channel_id=1, source_target_pairs={{0,2},{1,3},{2,0},{3,1},{4,6},{5,7},{6,4},{7,5},{8,10},{9,11},{10,... | collective-permute-start | bytes 511496 | tf_op jit(solution)/shard_map/ppermute | solution.py:428

commit v6 on v5

--- a/solution.py
+++ b/solution.py
@@ -17,7 +17,7 @@
 chunks = 2
 chunk = half // chunks
 early = 6 * half - 2 * chunk
-ahead = 640
+ahead = 512
 
 
 def one_hop(groups):
@@ -150,7 +150,7 @@
     )
 
 
-def coarse_kernel(sc, lists, far, own, a, b, own_o, ab_o, send, keep, picked, result):
+def coarse_kernel(sc, lists, far, own, a, b, own_o, a_o, b_o, send, keep, picked, result):
     c, l = sc[0], sc[1]
     wanted = jnp.concatenate([lists[k : k + 1, :] for k in range(3)], 1)
     count = wanted.shape[1]
@@ -167,7 +167,6 @@
         return jnp.dot(jnp.concatenate(parts, 1), hot, preferred_element_type=f32)
 
     lo, hi = slice(0, parents), slice(parents, 2 * parents)
-    a_o, b_o = ab_o[:, : 2 * parents], ab_o[:, 2 * parents :]
     found = (
         (pick(own[:, lo], a[:, hi], b[:, lo]), pick(own[:, hi], a[:, lo], b[:, hi])),
         (pick(own_o[:, lo], a_o[:, hi], b_o[:, lo]), pick(own_o[:, hi], a_o[:, lo], b_o[:, hi])),
@@ -191,8 +190,8 @@
     send[...] = result[pl.ds(pl.multiple_of((1 - c) * part, part), part), :].astype(bf16)
 
 
-def coarse_partial(sc, lists, far, own, a, b, own_o, ab_o):
-    args = (lists, far, own, a, b, own_o, ab_o)
+def coarse_partial(sc, lists, far, own, a, b, own_o, a_o, b_o):
+    args = (lists, far, own, a, b, own_o, a_o, b_o)
     shape = (wide // 2, parents)
     return call(
         coarse_kernel,
@@ -403,24 +402,17 @@
     own = joined(sc, up, zswap(up))
     ca = hop(own)
     own_o = cswap(own)
-    mine = [head, after(tail, own_o)]
+    mine = [head, after(tail, up)]
     a = [hop(m) for m in mine]
-    early_a = after(a[0], ca)
-    b = [zswap(early_a)]
-    a_o = [cswap(early_a)]
-    cb = zswap(ca)
-    cab_o = cswap(joined(sc, ca, cb))
-    second = after(a[1], early_a, cb, own_o)
-    b.append(zswap(second))
-    a_o.append(cswap(second))
+    early_a = after(a[0], own)
+    second = after(a[1], early_a, own_o)
+    b = [zswap(early_a), zswap(second)]
+    a_o = [cswap(early_a), cswap(after(second, ca))]
+    cb, ca_o = zswap(ca), cswap(ca)
     b_o = [cswap(b[0])]
-
-    send, keep = coarse_partial(sc, coarse_lists, far_ops, own, ca, cb, own_o, cab_o)
-    picked = gathered(after(spots, keep), [*mine, other, *a, *a_o, b[0], b_o[0]])
-    shape = (wide // 2, parents)
-    part, part_sent = small(add_kernel, sc, (keep, cswap(send)), [(shape, f32), (shape, bf16)])
-    b_o.append(cswap(after(b[1], picked, part)))
-    part_got = zswap(part_sent)
+    picked = gathered(spots, [*mine, other, *a, *a_o, b[0], b_o[0]])
+    b_o.append(cswap(after(b[1], picked, cb)))
+    cb_o = cswap(cb)
 
     def summed(send, keep):
         shape = (share, send.shape[2])
@@ -428,14 +420,22 @@
         return here, zswap(away), away
 
     late = (b[1], b_o[1])
-    send, keep = far_partial(after(sc, part), far_ops, picked, late_lists, *late, 0, ahead)
-    left = summed(after(send, part_got), keep)
+    send, keep = far_partial(sc, far_ops, picked, late_lists, *late, 0, ahead)
+    left = summed(after(send, cb_o, ca_o), keep)
+    send, keep = coarse_partial(
+        after(sc, send), coarse_lists, far_ops, own, ca, cb, own_o, ca_o, cb_o
+    )
+    shape = (wide // 2, parents)
+    part, part_sent = small(
+        add_kernel, after(sc, left[2]), (keep, cswap(send)), [(shape, f32), (shape, bf16)]
+    )
+    send, keep = far_partial(
+        after(sc, part), far_ops, picked, late_lists, *late, ahead, boxes - ahead
+    )
+    part_got = zswap(part_sent)
+    right = summed(after(send, left[1], part_got), keep)
     check = small(add_kernel, sc, (part, part_got), [(shape, bf16)])[0]
     check_o = cswap(check)
-    send, keep = far_partial(
-        after(sc, check, left[2]), far_ops, picked, late_lists, *late, ahead, boxes - ahead
-    )
-    right = summed(after(send, left[1], check_o), keep)
     spread = downward(after(sc, right[2]), down_ops, check, check_o)
     return small(last_kernel, sc, (spread, *left[:2], *right[:2]), [((share, boxes), bf16)])[0]
 

time: 93.3 us -> 85.1 us (0.912)
  waiting for transfers between devices: 30.3 us -> 23.2 us
    ppermute x7 -> x8, waiting for transfers between devices: 13.5 us -> 6.83 us  [the longest x2 5.51 us: local(): cb, ca_o = (zswap(ca), cswap(ca))]
    ppermute x2, waiting for transfers between devices: 0.01 us -> 6.47 us  [local(): a = [hop(m) for m in mine]]
    ppermute x1, starting transfers between devices: 0.33 us -> 5.85 us  [local(): ca = hop(own)]
    ppermute x2, starting transfers between devices: 13.3 us -> 10.3 us  [local(): a = [hop(m) for m in mine]]
    ppermute x2, starting transfers between devices: 3.48 us -> 0.75 us  [summed(): return (here, zswap(away), away)]
    ppermute x1, waiting for transfers between devices: 3.92 us -> 1.23 us  [local(): ca = hop(own)]
    ppermute x1, waiting for transfers between devices: 4.16 us -> 2.16 us  [local(): own = joined(sc, up, zswap(up))]
    ppermute x2, waiting for transfers between devices: 3.57 us -> 1.82 us  [summed(): cswap(send)]
  transfers between devices with their start and end apart: 20 -> 21, of which waited for: 10 -> 9; matrix products, arithmetic and copies ran while one was open for 1% -> 1% of each run, Pallas kernels for 34% -> 37%
where the time goes in v6:
time: 85.1 us; the launch traced here: 84.9 us
  Pallas kernels  33.8 us (40%)
  starting transfers between devices  23.3 us (27%)
  waiting for transfers between devices  23.2 us (27%)
  local copies, waits for them, and re-layouts  3.43 us (4%)
  other arithmetic  0.92 us (1%)
    pallas_call x14, Pallas kernels, call(): pl.pallas_call(kernel, grid_spec=pltpu.PrefetchScalarGridSpec(num_scalar_...  33.8 us
    ppermute x2, starting transfers between devices, local(): a = [hop(m) for m in mine]  10.3 us
    ppermute x2, waiting for transfers between devices, local(): a = [hop(m) for m in mine]  6.47 us
    ppermute x1, starting transfers between devices, local(): ca = hop(own)  5.85 us
    ppermute x2, waiting for transfers between devices, local(): cb, ca_o = (zswap(ca), cswap(ca))  5.51 us
    unnamed x14, local copies, waits for them, and re-layouts  3.41 us
    ppermute x2, starting transfers between devices, local(): cb, ca_o = (zswap(ca), cswap(ca))  2.53 us
    ppermute x2, waiting for transfers between devices, summed(): return (here, zswap(away), away)  2.43 us
  transfers between devices with their start and end apart: 21, of which 9 were waited for; matrix products, arithmetic and copies ran while one was open for 1% of the time, Pallas kernels for 37%

profile of v6, /device:TPU:24, one launch (start us, length us, event | category | flops | bytes accessed | tf_op | source)
XLA Modules:
  0.0 84.9 jit_solution(8452823663783295052)
XLA Ops:
  0.0 1.5 %copy-done = bf16[888,1024]{1,0:T(8,128)(2,1)S(1)} copy-done((bf16[888,1024]{1,0:T(8,128)(2,1)S(1)}, bf16[888,1024]{1,0:T(8,128)(2,1)}, u32[]{:S(2)}) %copy-start) | copy-done | bytes 1818648
  1.7 8.3 %collective-permute-start = (bf16[256,896]{1,0:T(8,128)(2,1)S(1)}, bf16[256,896]{1,0:T(8,128)(2,1)S(1)}, u32[]{:S(2)}, u32[]{:S(2)}) collective-permute-start(bf16[256,896]{1,0:T(8,128)(2,1)S(1)} %shard_map.64.refs_0_), channel_id=1, source_target_pairs={{2,4},{3,5},{6,8},{7,9},{10,12},{11,13},{14,16},{15,17},{18,20},{1... | collective-permute-start | bytes 1376264 | tf_op jit(solution)/shard_map/ppermute | solution.py:406
  10.0 0.8 fusion.6
  11.0 1.0 %shard_map.65 = (bf16[256,896]{1,0:T(8,128)(2,1)S(1)}, bf16[512,896]{1,0:T(8,128)(2,1)S(1)}) custom-call(s32[2]{0:T(128)S(1)} %pad_add_fusion.1.firsts, bf16[888,1024]{1,0:T(8,128)(2,1)S(1)} %copy-done.1), custom_call_target="tpu_custom_call" | custom-call | tf_op jit(solution)/shard_map/pallas_call | solution.py:34
  12.0 1.9 %copy-done.2 = bf16[8,222,888]{2,0,1:T(8,128)(2,1)S(1)} copy-done((bf16[8,222,888]{2,0,1:T(8,128)(2,1)S(1)}, bf16[8,222,888]{2,0,1:T(8,128)(2,1)}, u32[]{:S(2)}) %copy-start.2) | copy-done | bytes 3154200
  13.9 2.9 %shard_map.66.refs_0_ = bf16[222,128]{1,0:T(8,128)(2,1)S(1)} custom-call(s32[4]{0:T(128)S(1)} %pad_add_fusion.sc, bf16[1776,888]{1,0:T(8,128)(2,1)S(1)} %bitcast.15, bf16[512,896]{1,0:T(8,128)(2,1)S(1)} %get-tuple-element.35.other.refs_2_, bf16[256,896]{1,0:T(8,128)(2,1)S(1)} %shard_map.64.refs_0_, bf16[256,896]{1,0:T(8,128)(2,1)S(1)} %get-tuple-element.36.refs_1_), custom_call_target="tpu_custom_call" | custom-call | tf_op jit(solution)/shard_map/pallas_call | solution.py:34
  16.8 2.0 %collective-permute-start.1 = (bf16[256,896]{1,0:T(8,128)(2,1)S(1)}, bf16[256,896]{1,0:T(8,128)(2,1)S(1)}, u32[]{:S(2)}, u32[]{:S(2)}) collective-permute-start(bf16[256,896]{1,0:T(8,128)(2,1)S(1)} %get-tuple-element.36.refs_1_), channel_id=1, source_target_pairs={{2,4},{3,5},{6,8},{7,9},{10,12},{11,13},{14,16},{15,17},{18,20},{1... | collective-permute-start | bytes 1376264 | tf_op jit(solution)/shard_map/ppermute | solution.py:406
  18.8 2.2 %collective-permute-done.2.refs_1_ = bf16[222,128]{1,0:T(8,128)(2,1)S(1)} collective-permute-done((bf16[222,128]{1,0:T(8,128)(2,1)S(1)}, bf16[222,128]{1,0:T(8,128)(2,1)S(1)}, u32[]{:S(2)}, u32[]{:S(2)}) %collective-permute-start.2) | collective-permute-done | bytes 56864 | tf_op jit(solution)/shard_map/ppermute | solution.py:402
  21.0 0.6 shard_map.67.own
  21.8 5.9 %collective-permute-start.5 = (bf16[222,256]{1,0:T(8,128)(2,1)S(1)}, bf16[222,256]{1,0:T(8,128)(2,1)S(1)}, u32[]{:S(2)}, u32[]{:S(2)}) collective-permute-start(bf16[222,256]{1,0:T(8,128)(2,1)S(1)} %shard_map.67.own), channel_id=1, source_target_pairs={{2,4},{3,5},{6,8},{7,9},{10,12},{11,13},{14,16},{15,17},{18,20},{1... | collective-permute-start | bytes 341000 | tf_op jit(solution)/shard_map/ppermute | solution.py:403
  27.9 6.5 %collective-permute-done.1.refs_4_ = bf16[256,896]{1,0:T(8,128)(2,1)S(1)} collective-permute-done((bf16[256,896]{1,0:T(8,128)(2,1)S(1)}, bf16[256,896]{1,0:T(8,128)(2,1)S(1)}, u32[]{:S(2)}, u32[]{:S(2)}) %collective-permute-start.1) | collective-permute-done | bytes 458784 | tf_op jit(solution)/shard_map/ppermute | solution.py:406
  34.4 1.2 %collective-permute-done.5.a = bf16[222,256]{1,0:T(8,128)(2,1)S(1)} collective-permute-done((bf16[222,256]{1,0:T(8,128)(2,1)S(1)}, bf16[222,256]{1,0:T(8,128)(2,1)S(1)}, u32[]{:S(2)}, u32[]{:S(2)}) %collective-permute-start.5) | collective-permute-done | bytes 113696 | tf_op jit(solution)/shard_map/ppermute | solution.py:403
  35.6 0.5 collective-permute-start.8
  36.1 2.0 %collective-permute-start.10 = (bf16[222,256]{1,0:T(8,128)(2,1)S(1)}, bf16[222,256]{1,0:T(8,128)(2,1)S(1)}, u32[]{:S(2)}, u32[]{:S(2)}) collective-permute-start(bf16[222,256]{1,0:T(8,128)(2,1)S(1)} %collective-permute-done.5.a), channel_id=1, source_target_pairs={{0,2},{1,3},{2,0},{3,1},{4,6},{5,7},{6,4},{7,5},{8,10},{9,11},{10,... | collective-permute-start | bytes 341000 | tf_op jit(solution)/shard_map/ppermute | solution.py:411
  38.1 7.3 %shard_map.68.sources = bf16[3072,896]{1,0:T(8,128)(2,1)S(1)} custom-call(s32[3072]{0:T(1024)S(1)} %reshape.12.spots, bf16[256,896]{1,0:T(8,128)(2,1)S(1)} %shard_map.64.refs_0_, bf16[256,896]{1,0:T(8,128)(2,1)S(1)} %get-tuple-element.36.refs_1_, bf16[512,896]{1,0:T(8,128)(2,1)S(1)} %get-tuple-element.35.other.refs_2_, ...), custom_call_target="tpu_custom_call" | custom-call | tf_op jit(solution)/shard_map/pallas_call | solution.py:34
  45.5 5.5 %collective-permute-done.10.b = bf16[222,256]{1,0:T(8,128)(2,1)S(1)} collective-permute-done((bf16[222,256]{1,0:T(8,128)(2,1)S(1)}, bf16[222,256]{1,0:T(8,128)(2,1)S(1)}, u32[]{:S(2)}, u32[]{:S(2)}) %collective-permute-start.10) | collective-permute-done | bytes 113696 | tf_op jit(solution)/shard_map/ppermute | solution.py:411
  51.0 0.5 collective-permute-start.13
  51.5 1.3 %collective-permute-done.11.late_o = bf16[256,896]{1,0:T(8,128)(2,1)S(1)} collective-permute-done((bf16[256,896]{1,0:T(8,128)(2,1)S(1)}, bf16[256,896]{1,0:T(8,128)(2,1)S(1)}, u32[]{:S(2)}, u32[]{:S(2)}) %collective-permute-start.11) | collective-permute-done | bytes 458784 | tf_op jit(solution)/shard_map/ppermute | solution.py:414
  52.8 6.2 %shard_map.69 = (bf16[2,222,512]{2,1,0:T(8,128)(2,1)S(1)}, f32[2,222,512]{2,1,0:T(8,128)S(1)}) custom-call(s32[4]{0:T(128)S(1)} %pad_add_fusion.sc, bf16[3,888,888]{2,1,0:T(8,128)(2,1)S(1)} %bitcast.14, bf16[3072,896]{1,0:T(8,128)(2,1)S(1)} %shard_map.68.sources, s32[3,1024]{1,0:T(4,128)S(1)} %get-tuple-element.59.lists, ...), custom_call_target="tpu_custom_call" | custom-call | tf_op jit(solution)/shard_map/pallas_call | solution.py:34
  59.3 2.7 %shard_map.71 = (bf16[448,128]{1,0:T(8,128)(2,1)S(1)}, f32[448,128]{1,0:T(8,128)S(1)}) custom-call(s32[4]{0:T(128)S(1)} %pad_add_fusion.sc, s32[3,128]{1,0:T(4,128)S(1)} %copy-done.4, bf16[3,888,888]{2,1,0:T(8,128)(2,1)S(1)} %bitcast.14, bf16[222,256]{1,0:T(8,128)(2,1)S(1)} %shard_map.67.own, bf16[222,256]{1,0:T(8,128)(2,1)S(1)} %collective-permute-done.5.a, ...), custom_call_target="tpu_custom_call" | custom-call | tf_op jit(solution)/shard_map/pallas_call | solution.py:34
  62.4 0.6 shard_map.70
  63.5 0.6 shard_map.72
  64.0 2.0 %collective-permute-start.17 = (bf16[448,128]{1,0:T(8,128)(2,1)S(1)}, bf16[448,128]{1,0:T(8,128)(2,1)S(1)}, u32[]{:S(2)}, u32[]{:S(2)}) collective-permute-start(bf16[448,128]{1,0:T(8,128)(2,1)S(1)} %get-tuple-element.53), channel_id=1, source_target_pairs={{0,2},{1,3},{2,0},{3,1},{4,6},{5,7},{6,4},{7,5},{8,10},{9,11},{10,... | collective-permute-start | bytes 344072 | tf_op jit(solution)/shard_map/ppermute | solution.py:435
  66.1 6.2 %shard_map.73 = (bf16[2,222,512]{2,1,0:T(8,128)(2,1)S(1)}, f32[2,222,512]{2,1,0:T(8,128)S(1)}) custom-call(s32[4]{0:T(128)S(1)} %pad_add_fusion.sc, bf16[3,888,888]{2,1,0:T(8,128)(2,1)S(1)} %bitcast.14, bf16[3072,896]{1,0:T(8,128)(2,1)S(1)} %shard_map.68.sources, s32[3,1024]{1,0:T(4,128)S(1)} %get-tuple-element.59.lists, ...), custom_call_target="tpu_custom_call" | custom-call | tf_op jit(solution)/shard_map/pallas_call | solution.py:34
  72.3 1.0 %collective-permute-done.17.two = bf16[448,128]{1,0:T(8,128)(2,1)S(1)} collective-permute-done((bf16[448,128]{1,0:T(8,128)(2,1)S(1)}, bf16[448,128]{1,0:T(8,128)(2,1)S(1)}, u32[]{:S(2)}, u32[]{:S(2)}) %collective-permute-start.17) | collective-permute-done | bytes 114720 | tf_op jit(solution)/shard_map/ppermute | solution.py:435
  73.3 1.8 %collective-permute-done.18.got = bf16[2,222,512]{2,1,0:T(8,128)(2,1)S(1)} collective-permute-done((bf16[2,222,512]{2,1,0:T(8,128)(2,1)S(1)}, bf16[2,222,512]{2,1,0:T(8,128)(2,1)S(1)}, u32[]{:S(2)}, u32[]{:S(2)}) %collective-permute-start.18) | collective-permute-done | bytes 454688 | tf_op jit(solution)/shard_map/ppermute | solution.py:419
  75.1 0.7 shard_map.74
  76.1 0.6 shard_map.75.mine
  76.8 1.3 %collective-permute-done.19.other = bf16[448,128]{1,0:T(8,128)(2,1)S(1)} collective-permute-done((bf16[448,128]{1,0:T(8,128)(2,1)S(1)}, bf16[448,128]{1,0:T(8,128)(2,1)S(1)}, u32[]{:S(2)}, u32[]{:S(2)}) %collective-permute-start.19) | collective-permute-done | bytes 114720 | tf_op jit(solution)/shard_map/ppermute | solution.py:438
  78.1 2.9 %shard_map.76.spread = f32[222,1024]{1,0:T(8,128)S(1)} custom-call(s32[4]{0:T(128)S(1)} %pad_add_fusion.sc, bf16[1776,888]{1,0:T(8,128)(2,1)S(1)} %bitcast.16, bf16[448,128]{1,0:T(8,128)(2,1)S(1)} %shard_map.75.mine, bf16[448,128]{1,0:T(8,128)(2,1)S(1)} %collective-permute-done.19.other), custom_call_target="tpu_custom_call" | custom-call | tf_op jit(solution)/shard_map/pallas_call | solution.py:34
  81.0 2.4 %collective-permute-done.20.refs_3_ = bf16[222,512]{1,0:T(8,128)(2,1)S(1)} collective-permute-done((bf16[222,512]{1,0:T(8,128)(2,1)S(1)}, bf16[222,512]{1,0:T(8,128)(2,1)S(1)}, u32[]{:S(2)}, u32[]{:S(2)}) %collective-permute-start.20) | collective-permute-done | bytes 227360 | tf_op jit(solution)/shard_map/ppermute | solution.py:420
  83.5 1.4 %shard_map.77 = bf16[222,1024]{1,0:T(8,128)(2,1)} custom-call(s32[4]{0:T(128)S(1)} %pad_add_fusion.sc, f32[222,1024]{1,0:T(8,128)S(1)} %shard_map.76.spread, f32[222,512]{1,0:T(8,128)S(1)} %get-tuple-element.57.refs_0_, bf16[222,512]{1,0:T(8,128)(2,1)S(1)} %collective-permute-done.16.refs_1_, f32[222,512]{1,0:T(8,128)S(1)} %get-tuple-element.58.refs_2_, ...), custom_call_target="tpu_custom_call" | custom-call | tf_op jit(solution)/shard_map/pallas_call | solution.py:34
  (43 shorter events, 2.5 us)
Async XLA Ops:
  0.0 1.5 %copy-start = (bf16[888,1024]{1,0:T(8,128)(2,1)S(1)}, bf16[888,1024]{1,0:T(8,128)(2,1)}, u32[]{:S(2)}) copy-start(bf16[888,1024]{1,0:T(8,128)(2,1)} %x_ref.3) | copy-start | bytes 5455876
  1.5 9.5 %copy-start.1 = (bf16[888,1024]{1,0:T(8,128)(2,1)S(1)}, bf16[888,1024]{1,0:T(8,128)(2,1)}, u32[]{:S(2)}) copy-start(bf16[888,1024]{1,0:T(8,128)(2,1)} %x_ref.3) | copy-start | bytes 5455876
  1.7 19.9 %collective-permute-start = (bf16[256,896]{1,0:T(8,128)(2,1)S(1)}, bf16[256,896]{1,0:T(8,128)(2,1)S(1)}, u32[]{:S(2)}, u32[]{:S(2)}) collective-permute-start(bf16[256,896]{1,0:T(8,128)(2,1)S(1)} %shard_map.64.refs_0_), channel_id=1, source_target_pairs={{2,4},{3,5},{6,8},{7,9},{10,12},{11,13},{14,16},{15,17},{18,20},{1... | collective-permute-start | bytes 1376264 | tf_op jit(solution)/shard_map/ppermute | solution.py:406
  12.0 1.9 %copy-start.2 = (bf16[8,222,888]{2,0,1:T(8,128)(2,1)S(1)}, bf16[8,222,888]{2,0,1:T(8,128)(2,1)}, u32[]{:S(2)}) copy-start(bf16[8,222,888]{2,0,1:T(8,128)(2,1)} %param.7) | copy-start | bytes 9462532
  16.7 4.3 %collective-permute-start.2 = (bf16[222,128]{1,0:T(8,128)(2,1)S(1)}, bf16[222,128]{1,0:T(8,128)(2,1)S(1)}, u32[]{:S(2)}, u32[]{:S(2)}) collective-permute-start(bf16[222,128]{1,0:T(8,128)(2,1)S(1)} %shard_map.66.refs_0_), channel_id=1, source_target_pairs={{0,2},{1,3},{2,0},{3,1},{4,6},{5,7},{6,4},{7,5},{8,10},{9,11},{10,... | collective-permute-start | bytes 170504 | tf_op jit(solution)/shard_map/ppermute | solution.py:402
  16.8 17.5 %collective-permute-start.1 = (bf16[256,896]{1,0:T(8,128)(2,1)S(1)}, bf16[256,896]{1,0:T(8,128)(2,1)S(1)}, u32[]{:S(2)}, u32[]{:S(2)}) collective-permute-start(bf16[256,896]{1,0:T(8,128)(2,1)S(1)} %get-tuple-element.36.refs_1_), channel_id=1, source_target_pairs={{2,4},{3,5},{6,8},{7,9},{10,12},{11,13},{14,16},{15,17},{18,20},{1... | collective-permute-start | bytes 1376264 | tf_op jit(solution)/shard_map/ppermute | solution.py:406
  21.0 31.8 %slice-start = ((s8[4773888]{0:T(1024)(128)(4,1)}), s8[4194304]{0:T(1024)(128)(4,1)S(1)}, s32[]{:S(2)}) async-start(s8[4773888]{0:T(1024)(128)(4,1)} %bitcast.13), calls=%async_computation | async-start | bytes 8388608
  21.6 31.2 %slice-start.1 = ((s8[4773888]{0:T(1024)(128)(4,1)}), s8[579584]{0:T(1024)(128)(4,1)S(1)}, s32[]{:S(2)}) async-start(s8[4773888]{0:T(1024)(128)(4,1)} %bitcast.13), calls=%async_computation.1 | async-start | bytes 1159168
  21.6 14.0 %collective-permute-start.7 = (bf16[256,896]{1,0:T(8,128)(2,1)S(1)}, bf16[256,896]{1,0:T(8,128)(2,1)S(1)}, u32[]{:S(2)}, u32[]{:S(2)}) collective-permute-start(bf16[256,896]{1,0:T(8,128)(2,1)S(1)} %collective-permute-done.refs_3_), channel_id=1, source_target_pairs={{0,2},{1,3},{2,0},{3,1},{4,6},{5,7},{6,4},{7,5},{8,10},{9,11},{10,... | collective-permute-start | bytes 1376264 | tf_op jit(solution)/shard_map/ppermute | solution.py:409
  21.7 6.2 %collective-permute-start.4 = (bf16[222,256]{1,0:T(8,128)(2,1)S(1)}, bf16[222,256]{1,0:T(8,128)(2,1)S(1)}, u32[]{:S(2)}, u32[]{:S(2)}) collective-permute-start(bf16[222,256]{1,0:T(8,128)(2,1)S(1)} %shard_map.67.own), channel_id=1, source_target_pairs={{0,1},{1,0},{2,3},{3,2},{4,5},{5,4},{6,7},{7,6},{8,9},{9,8},{10,11... | collective-permute-start | bytes 341000 | tf_op jit(solution)/shard_map/ppermute | solution.py:404
  21.8 13.8 %collective-permute-start.5 = (bf16[222,256]{1,0:T(8,128)(2,1)S(1)}, bf16[222,256]{1,0:T(8,128)(2,1)S(1)}, u32[]{:S(2)}, u32[]{:S(2)}) collective-permute-start(bf16[222,256]{1,0:T(8,128)(2,1)S(1)} %shard_map.67.own), channel_id=1, source_target_pairs={{2,4},{3,5},{6,8},{7,9},{10,12},{11,13},{14,16},{15,17},{18,20},{1... | collective-permute-start | bytes 341000 | tf_op jit(solution)/shard_map/ppermute | solution.py:403
  27.7 10.5 %collective-permute-start.3 = (bf16[256,896]{1,0:T(8,128)(2,1)S(1)}, bf16[256,896]{1,0:T(8,128)(2,1)S(1)}, u32[]{:S(2)}, u32[]{:S(2)}) collective-permute-start(bf16[256,896]{1,0:T(8,128)(2,1)S(1)} %collective-permute-done.refs_3_), channel_id=1, source_target_pairs={{0,1},{1,0},{2,3},{3,2},{4,5},{5,4},{6,7},{7,6},{8,9},{9,8},{10,11... | collective-permute-start | bytes 1376264 | tf_op jit(solution)/shard_map/ppermute | solution.py:410
  35.6 2.5 %collective-permute-start.6 = (bf16[256,896]{1,0:T(8,128)(2,1)S(1)}, bf16[256,896]{1,0:T(8,128)(2,1)S(1)}, u32[]{:S(2)}, u32[]{:S(2)}) collective-permute-start(bf16[256,896]{1,0:T(8,128)(2,1)S(1)} %collective-permute-done.1.refs_4_), channel_id=1, source_target_pairs={{0,1},{1,0},{2,3},{3,2},{4,5},{5,4},{6,7},{7,6},{8,9},{9,8},{10,11... | collective-permute-start | bytes 1376264 | tf_op jit(solution)/shard_map/ppermute | solution.py:410
  35.6 2.5 %collective-permute-start.8 = (bf16[256,896]{1,0:T(8,128)(2,1)S(1)}, bf16[256,896]{1,0:T(8,128)(2,1)S(1)}, u32[]{:S(2)}, u32[]{:S(2)}) collective-permute-start(bf16[256,896]{1,0:T(8,128)(2,1)S(1)} %collective-permute-done.7.refs_7_), channel_id=1, source_target_pairs={{0,1},{1,0},{2,3},{3,2},{4,5},{5,4},{6,7},{7,6},{8,9},{9,8},{10,11... | collective-permute-start | bytes 1376264 | tf_op jit(solution)/shard_map/ppermute | solution.py:412
  36.1 14.9 %collective-permute-start.9 = (bf16[256,896]{1,0:T(8,128)(2,1)S(1)}, bf16[256,896]{1,0:T(8,128)(2,1)S(1)}, u32[]{:S(2)}, u32[]{:S(2)}) collective-permute-start(bf16[256,896]{1,0:T(8,128)(2,1)S(1)} %collective-permute-done.1.refs_4_), channel_id=1, source_target_pairs={{0,2},{1,3},{2,0},{3,1},{4,6},{5,7},{6,4},{7,5},{8,10},{9,11},{10,... | collective-permute-start | bytes 1376264 | tf_op jit(solution)/shard_map/ppermute | solution.py:409
  36.1 14.9 %collective-permute-start.10 = (bf16[222,256]{1,0:T(8,128)(2,1)S(1)}, bf16[222,256]{1,0:T(8,128)(2,1)S(1)}, u32[]{:S(2)}, u32[]{:S(2)}) collective-permute-start(bf16[222,256]{1,0:T(8,128)(2,1)S(1)} %collective-permute-done.5.a), channel_id=1, source_target_pairs={{0,2},{1,3},{2,0},{3,1},{4,6},{5,7},{6,4},{7,5},{8,10},{9,11},{10,... | collective-permute-start | bytes 341000 | tf_op jit(solution)/shard_map/ppermute | solution.py:411
  45.5 13.8 %copy-start.4 = (s32[3,128]{1,0:T(4,128)S(1)}, s32[3,128]{1,0:T(4,128)}, u32[]{:S(2)}) copy-start(s32[3,128]{1,0:T(4,128)} %lists.1) | copy-start | bytes 4612
  51.0 1.8 %collective-permute-start.11 = (bf16[256,896]{1,0:T(8,128)(2,1)S(1)}, bf16[256,896]{1,0:T(8,128)(2,1)S(1)}, u32[]{:S(2)}, u32[]{:S(2)}) collective-permute-start(bf16[256,896]{1,0:T(8,128)(2,1)S(1)} %collective-permute-done.9.late), channel_id=1, source_target_pairs={{0,1},{1,0},{2,3},{3,2},{4,5},{5,4},{6,7},{7,6},{8,9},{9,8},{10,11... | collective-permute-start | bytes 1376264 | tf_op jit(solution)/shard_map/ppermute | solution.py:414
  51.0 8.1 %collective-permute-start.13 = (bf16[222,256]{1,0:T(8,128)(2,1)S(1)}, bf16[222,256]{1,0:T(8,128)(2,1)S(1)}, u32[]{:S(2)}, u32[]{:S(2)}) collective-permute-start(bf16[222,256]{1,0:T(8,128)(2,1)S(1)} %collective-permute-done.5.a), channel_id=1, source_target_pairs={{0,1},{1,0},{2,3},{3,2},{4,5},{5,4},{6,7},{7,6},{8,9},{9,8},{10,11... | collective-permute-start | bytes 341000 | tf_op jit(solution)/shard_map/ppermute | solution.py:411
  51.5 7.6 %collective-permute-start.12 = (bf16[222,256]{1,0:T(8,128)(2,1)S(1)}, bf16[222,256]{1,0:T(8,128)(2,1)S(1)}, u32[]{:S(2)}, u32[]{:S(2)}) collective-permute-start(bf16[222,256]{1,0:T(8,128)(2,1)S(1)} %collective-permute-done.10.b), channel_id=1, source_target_pairs={{0,1},{1,0},{2,3},{3,2},{4,5},{5,4},{6,7},{7,6},{8,9},{9,8},{10,11... | collective-permute-start | bytes 341000 | tf_op jit(solution)/shard_map/ppermute | solution.py:415
  59.1 3.4 %collective-permute-start.14 = (bf16[2,222,512]{2,1,0:T(8,128)(2,1)S(1)}, bf16[2,222,512]{2,1,0:T(8,128)(2,1)S(1)}, u32[]{:S(2)}, u32[]{:S(2)}) collective-permute-start(bf16[2,222,512]{2,1,0:T(8,128)(2,1)S(1)} %get-tuple-element.43), channel_id=1, source_target_pairs={{0,1},{1,0},{2,3},{3,2},{4,5},{5,4},{6,7},{7,6},{8,9},{9,8},{10,11... | collective-permute-start | bytes 1363976 | tf_op jit(solution)/shard_map/ppermute | solution.py:419
  62.0 1.5 %collective-permute-start.15 = (bf16[448,128]{1,0:T(8,128)(2,1)S(1)}, bf16[448,128]{1,0:T(8,128)(2,1)S(1)}, u32[]{:S(2)}, u32[]{:S(2)}) collective-permute-start(bf16[448,128]{1,0:T(8,128)(2,1)S(1)} %get-tuple-element.48), channel_id=1, source_target_pairs={{0,1},{1,0},{2,3},{3,2},{4,5},{5,4},{6,7},{7,6},{8,9},{9,8},{10,11... | collective-permute-start | bytes 344072 | tf_op jit(solution)/shard_map/ppermute | solution.py:430
  63.1 10.2 %collective-permute-start.16 = (bf16[222,512]{1,0:T(8,128)(2,1)S(1)}, bf16[222,512]{1,0:T(8,128)(2,1)S(1)}, u32[]{:S(2)}, u32[]{:S(2)}) collective-permute-start(bf16[222,512]{1,0:T(8,128)(2,1)S(1)} %get-tuple-element.44), channel_id=1, source_target_pairs={{0,2},{1,3},{2,0},{3,1},{4,6},{5,7},{6,4},{7,5},{8,10},{9,11},{10,... | collective-permute-start | bytes 681992 | tf_op jit(solution)/shard_map/ppermute | solution.py:420
  64.0 9.2 %collective-permute-start.17 = (bf16[448,128]{1,0:T(8,128)(2,1)S(1)}, bf16[448,128]{1,0:T(8,128)(2,1)S(1)}, u32[]{:S(2)}, u32[]{:S(2)}) collective-permute-start(bf16[448,128]{1,0:T(8,128)(2,1)S(1)} %get-tuple-element.53), channel_id=1, source_target_pairs={{0,2},{1,3},{2,0},{3,1},{4,6},{5,7},{6,4},{7,5},{8,10},{9,11},{10,... | collective-permute-start | bytes 344072 | tf_op jit(solution)/shard_map/ppermute | solution.py:435
  66.1 12.0 %copy-start.3 = (bf16[8,222,888]{2,0,1:T(8,128)(2,1)S(1)}, bf16[8,222,888]{2,0,1:T(8,128)(2,1)}, u32[]{:S(2)}) copy-start(bf16[8,222,888]{2,0,1:T(8,128)(2,1)} %param.9) | copy-start | bytes 9462532
  73.3 1.8 %collective-permute-start.18 = (bf16[2,222,512]{2,1,0:T(8,128)(2,1)S(1)}, bf16[2,222,512]{2,1,0:T(8,128)(2,1)S(1)}, u32[]{:S(2)}, u32[]{:S(2)}) collective-permute-start(bf16[2,222,512]{2,1,0:T(8,128)(2,1)S(1)} %get-tuple-element.54), channel_id=1, source_target_pairs={{0,1},{1,0},{2,3},{3,2},{4,5},{5,4},{6,7},{7,6},{8,9},{9,8},{10,11... | collective-permute-start | bytes 1363976 | tf_op jit(solution)/shard_map/ppermute | solution.py:419
  75.7 7.7 %collective-permute-start.20 = (bf16[222,512]{1,0:T(8,128)(2,1)S(1)}, bf16[222,512]{1,0:T(8,128)(2,1)S(1)}, u32[]{:S(2)}, u32[]{:S(2)}) collective-permute-start(bf16[222,512]{1,0:T(8,128)(2,1)S(1)} %get-tuple-element.55), channel_id=1, source_target_pairs={{0,2},{1,3},{2,0},{3,1},{4,6},{5,7},{6,4},{7,5},{8,10},{9,11},{10,... | collective-permute-start | bytes 681992 | tf_op jit(solution)/shard_map/ppermute | solution.py:420
  76.7 1.4 %collective-permute-start.19 = (bf16[448,128]{1,0:T(8,128)(2,1)S(1)}, bf16[448,128]{1,0:T(8,128)(2,1)S(1)}, u32[]{:S(2)}, u32[]{:S(2)}) collective-permute-start(bf16[448,128]{1,0:T(8,128)(2,1)S(1)} %shard_map.75.mine), channel_id=1, source_target_pairs={{0,1},{1,0},{2,3},{3,2},{4,5},{5,4},{6,7},{7,6},{8,9},{9,8},{10,11... | collective-permute-start | bytes 344072 | tf_op jit(solution)/shard_map/ppermute | solution.py:438

commit v7 on v5

--- a/solution.py
+++ b/solution.py
@@ -17,7 +17,7 @@
 chunks = 2
 chunk = half // chunks
 early = 6 * half - 2 * chunk
-ahead = 640
+ahead = 512
 
 
 def one_hop(groups):
@@ -150,7 +150,7 @@
     )
 
 
-def coarse_kernel(sc, lists, far, own, a, b, own_o, ab_o, send, keep, picked, result):
+def coarse_kernel(sc, lists, far, own, a, b, own_o, a_o, b_o, send, keep, picked, result):
     c, l = sc[0], sc[1]
     wanted = jnp.concatenate([lists[k : k + 1, :] for k in range(3)], 1)
     count = wanted.shape[1]
@@ -167,7 +167,6 @@
         return jnp.dot(jnp.concatenate(parts, 1), hot, preferred_element_type=f32)
 
     lo, hi = slice(0, parents), slice(parents, 2 * parents)
-    a_o, b_o = ab_o[:, : 2 * parents], ab_o[:, 2 * parents :]
     found = (
         (pick(own[:, lo], a[:, hi], b[:, lo]), pick(own[:, hi], a[:, lo], b[:, hi])),
         (pick(own_o[:, lo], a_o[:, hi], b_o[:, lo]), pick(own_o[:, hi], a_o[:, lo], b_o[:, hi])),
@@ -191,8 +190,8 @@
     send[...] = result[pl.ds(pl.multiple_of((1 - c) * part, part), part), :].astype(bf16)
 
 
-def coarse_partial(sc, lists, far, own, a, b, own_o, ab_o):
-    args = (lists, far, own, a, b, own_o, ab_o)
+def coarse_partial(sc, lists, far, own, a, b, own_o, a_o, b_o):
+    args = (lists, far, own, a, b, own_o, a_o, b_o)
     shape = (wide // 2, parents)
     return call(
         coarse_kernel,
@@ -403,23 +402,23 @@
     own = joined(sc, up, zswap(up))
     ca = hop(own)
     own_o = cswap(own)
-    mine = [head, after(tail, own_o)]
+    mine = [head, after(tail, up)]
     a = [hop(m) for m in mine]
-    early_a = after(a[0], ca)
-    b = [zswap(early_a)]
-    a_o = [cswap(early_a)]
-    cb = zswap(ca)
-    cab_o = cswap(joined(sc, ca, cb))
-    second = after(a[1], early_a, cb, own_o)
-    b.append(zswap(second))
-    a_o.append(cswap(second))
+    early_a = after(a[0], own)
+    cb, ca_o = zswap(ca), cswap(ca)
+    second = after(a[1], early_a, own_o, cb)
+    b = [zswap(early_a), zswap(second)]
+    a_o = [cswap(early_a), cswap(second)]
+    cb_o = cswap(cb)
     b_o = [cswap(b[0])]
-
-    send, keep = coarse_partial(sc, coarse_lists, far_ops, own, ca, cb, own_o, cab_o)
-    picked = gathered(after(spots, keep), [*mine, other, *a, *a_o, b[0], b_o[0]])
+    picked = gathered(spots, [*mine, other, *a, *a_o, b[0], b_o[0]])
+
+    send, keep = coarse_partial(
+        after(sc, picked), coarse_lists, far_ops, own, ca, cb, own_o, ca_o, cb_o
+    )
+    b_o.append(cswap(after(b[1], keep)))
     shape = (wide // 2, parents)
     part, part_sent = small(add_kernel, sc, (keep, cswap(send)), [(shape, f32), (shape, bf16)])
-    b_o.append(cswap(after(b[1], picked, part)))
     part_got = zswap(part_sent)
 
     def summed(send, keep):

time: 93.3 us -> 86.7 us (0.929)
  starting transfers between devices: 23.1 us -> 20.1 us
  waiting for transfers between devices: 30.3 us -> 28 us
    ppermute x7 -> x8, waiting for transfers between devices: 13.5 us -> 6.35 us  [the longest x2 4.79 us: local(): cb, ca_o = (zswap(ca), cswap(ca))]
    ppermute x1, starting transfers between devices: 0.33 us -> 6.07 us  [local(): ca = hop(own)]
    ppermute x2, starting transfers between devices: 13.3 us -> 8.67 us  [local(): a = [hop(m) for m in mine]]
    ppermute x1, waiting for transfers between devices: 3.92 us -> 7.44 us  [local(): ca = hop(own)]
    ppermute x2, waiting for transfers between devices: 3 us -> 4.6 us  [summed(): return (here, zswap(away), away)]
    ppermute x7 -> x8, starting transfers between devices: 2.65 us -> 1.25 us  [the longest x2 0.51 us: local(): a_o = [cswap(early_a), cswap(second)]]
    ppermute x1, starting transfers between devices: 1.76 us -> 0.37 us  [local(): part_got = zswap(part_sent)]
    ppermute x2, starting transfers between devices: 3.48 us -> 2.22 us  [summed(): return (here, zswap(away), away)]
  transfers between devices with their start and end apart: 20 -> 21, of which waited for: 10 -> 11; matrix products, arithmetic and copies ran while one was open for 1% -> 1% of each run, Pallas kernels for 34% -> 36%
where the time goes in v7:
time: 86.7 us; the launch traced here: 86.6 us
  Pallas kernels  33.9 us (39%)
  waiting for transfers between devices  28 us (32%)
  starting transfers between devices  20.1 us (23%)
  local copies, waits for them, and re-layouts  3.43 us (4%)
  other arithmetic  0.92 us (1%)
    pallas_call x14, Pallas kernels, call(): pl.pallas_call(kernel, grid_spec=pltpu.PrefetchScalarGridSpec(num_scalar_...  33.9 us
    ppermute x2, starting transfers between devices, local(): a = [hop(m) for m in mine]  8.67 us
    ppermute x1, waiting for transfers between devices, local(): ca = hop(own)  7.44 us
    ppermute x1, starting transfers between devices, local(): ca = hop(own)  6.07 us
    ppermute x2, waiting for transfers between devices, local(): cb, ca_o = (zswap(ca), cswap(ca))  4.79 us
    ppermute x2, waiting for transfers between devices, summed(): return (here, zswap(away), away)  4.6 us
    ppermute x1, waiting for transfers between devices, local(): own = joined(sc, up, zswap(up))  4.17 us
    unnamed x14, local copies, waits for them, and re-layouts  3.42 us
  transfers between devices with their start and end apart: 21, of which 11 were waited for; matrix products, arithmetic and copies ran while one was open for 1% of the time, Pallas kernels for 36%

profile of v7, /device:TPU:24, one launch (start us, length us, event | category | flops | bytes accessed | tf_op | source)
XLA Modules:
  0.0 86.6 jit_solution(17857337128600528525)
XLA Ops:
  0.0 1.5 %copy-done = bf16[888,1024]{1,0:T(8,128)(2,1)S(1)} copy-done((bf16[888,1024]{1,0:T(8,128)(2,1)S(1)}, bf16[888,1024]{1,0:T(8,128)(2,1)}, u32[]{:S(2)}) %copy-start) | copy-done | bytes 1818648
  1.7 8.3 %collective-permute-start = (bf16[256,896]{1,0:T(8,128)(2,1)S(1)}, bf16[256,896]{1,0:T(8,128)(2,1)S(1)}, u32[]{:S(2)}, u32[]{:S(2)}) collective-permute-start(bf16[256,896]{1,0:T(8,128)(2,1)S(1)} %shard_map.64.refs_0_), channel_id=1, source_target_pairs={{2,4},{3,5},{6,8},{7,9},{10,12},{11,13},{14,16},{15,17},{18,20},{1... | collective-permute-start | bytes 1376264 | tf_op jit(solution)/shard_map/ppermute | solution.py:406
  10.0 0.8 fusion.6
  11.0 1.0 %shard_map.65 = (bf16[256,896]{1,0:T(8,128)(2,1)S(1)}, bf16[512,896]{1,0:T(8,128)(2,1)S(1)}) custom-call(s32[2]{0:T(128)S(1)} %pad_add_fusion.1.firsts, bf16[888,1024]{1,0:T(8,128)(2,1)S(1)} %copy-done.1), custom_call_target="tpu_custom_call" | custom-call | tf_op jit(solution)/shard_map/pallas_call | solution.py:34
  12.0 1.9 %copy-done.2 = bf16[8,222,888]{2,0,1:T(8,128)(2,1)S(1)} copy-done((bf16[8,222,888]{2,0,1:T(8,128)(2,1)S(1)}, bf16[8,222,888]{2,0,1:T(8,128)(2,1)}, u32[]{:S(2)}) %copy-start.2) | copy-done | bytes 3154200
  13.9 2.9 %shard_map.66.refs_0_ = bf16[222,128]{1,0:T(8,128)(2,1)S(1)} custom-call(s32[4]{0:T(128)S(1)} %pad_add_fusion.sc, bf16[1776,888]{1,0:T(8,128)(2,1)S(1)} %bitcast.15, bf16[512,896]{1,0:T(8,128)(2,1)S(1)} %get-tuple-element.34.other.refs_2_, bf16[256,896]{1,0:T(8,128)(2,1)S(1)} %shard_map.64.refs_0_, bf16[256,896]{1,0:T(8,128)(2,1)S(1)} %get-tuple-element.35.refs_1_), custom_call_target="tpu_custom_call" | custom-call | tf_op jit(solution)/shard_map/pallas_call | solution.py:34
  17.1 4.2 %collective-permute-done.2.refs_1_ = bf16[222,128]{1,0:T(8,128)(2,1)S(1)} collective-permute-done((bf16[222,128]{1,0:T(8,128)(2,1)S(1)}, bf16[222,128]{1,0:T(8,128)(2,1)S(1)}, u32[]{:S(2)}, u32[]{:S(2)}) %collective-permute-start.2) | collective-permute-done | bytes 56864 | tf_op jit(solution)/shard_map/ppermute | solution.py:402
  21.3 0.6 shard_map.67.own
  22.0 6.1 %collective-permute-start.5 = (bf16[222,256]{1,0:T(8,128)(2,1)S(1)}, bf16[222,256]{1,0:T(8,128)(2,1)S(1)}, u32[]{:S(2)}, u32[]{:S(2)}) collective-permute-start(bf16[222,256]{1,0:T(8,128)(2,1)S(1)} %shard_map.67.own), channel_id=1, source_target_pairs={{2,4},{3,5},{6,8},{7,9},{10,12},{11,13},{14,16},{15,17},{18,20},{1... | collective-permute-start | bytes 341000 | tf_op jit(solution)/shard_map/ppermute | solution.py:403
  28.0 7.4 %collective-permute-done.5.a = bf16[222,256]{1,0:T(8,128)(2,1)S(1)} collective-permute-done((bf16[222,256]{1,0:T(8,128)(2,1)S(1)}, bf16[222,256]{1,0:T(8,128)(2,1)S(1)}, u32[]{:S(2)}, u32[]{:S(2)}) %collective-permute-start.5) | collective-permute-done | bytes 113696 | tf_op jit(solution)/shard_map/ppermute | solution.py:403
  35.5 4.8 %collective-permute-done.6.b = bf16[222,256]{1,0:T(8,128)(2,1)S(1)} collective-permute-done((bf16[222,256]{1,0:T(8,128)(2,1)S(1)}, bf16[222,256]{1,0:T(8,128)(2,1)S(1)}, u32[]{:S(2)}, u32[]{:S(2)}) %collective-permute-start.6) | collective-permute-done | bytes 113696 | tf_op jit(solution)/shard_map/ppermute | solution.py:408
  40.3 0.5 collective-permute-start.3
  41.3 0.8 collective-permute-done.7.refs_6_
  42.2 0.5 collective-permute-done.3.refs_5_
  42.8 0.7 collective-permute-done.9.refs_8_
  43.4 7.3 %shard_map.68.sources = bf16[3072,896]{1,0:T(8,128)(2,1)S(1)} custom-call(s32[3072]{0:T(1024)S(1)} %reshape.12.spots, bf16[256,896]{1,0:T(8,128)(2,1)S(1)} %shard_map.64.refs_0_, bf16[256,896]{1,0:T(8,128)(2,1)S(1)} %get-tuple-element.35.refs_1_, bf16[512,896]{1,0:T(8,128)(2,1)S(1)} %get-tuple-element.34.other.refs_2_, ...), custom_call_target="tpu_custom_call" | custom-call | tf_op jit(solution)/shard_map/pallas_call | solution.py:34
  50.8 2.7 %shard_map.69 = (bf16[448,128]{1,0:T(8,128)(2,1)S(1)}, f32[448,128]{1,0:T(8,128)S(1)}) custom-call(s32[4]{0:T(128)S(1)} %pad_add_fusion.sc, s32[3,128]{1,0:T(4,128)S(1)} %copy-done.4, bf16[3,888,888]{2,1,0:T(8,128)(2,1)S(1)} %bitcast.14, bf16[222,256]{1,0:T(8,128)(2,1)S(1)} %shard_map.67.own, bf16[222,256]{1,0:T(8,128)(2,1)S(1)} %collective-permute-done.5.a, ...), custom_call_target="tpu_custom_call" | custom-call | tf_op jit(solution)/shard_map/pallas_call | solution.py:34
  53.7 0.5 collective-permute-start.12
  54.2 1.5 %collective-permute-done.12.two = bf16[448,128]{1,0:T(8,128)(2,1)S(1)} collective-permute-done((bf16[448,128]{1,0:T(8,128)(2,1)S(1)}, bf16[448,128]{1,0:T(8,128)(2,1)S(1)}, u32[]{:S(2)}, u32[]{:S(2)}) %collective-permute-start.12) | collective-permute-done | bytes 114720 | tf_op jit(solution)/shard_map/ppermute | solution.py:421
  55.7 0.6 shard_map.70
  56.7 6.2 %shard_map.72 = (bf16[2,222,512]{2,1,0:T(8,128)(2,1)S(1)}, f32[2,222,512]{2,1,0:T(8,128)S(1)}) custom-call(s32[4]{0:T(128)S(1)} %pad_add_fusion.sc, bf16[3,888,888]{2,1,0:T(8,128)(2,1)S(1)} %bitcast.14, bf16[3072,896]{1,0:T(8,128)(2,1)S(1)} %shard_map.68.sources, s32[3,1024]{1,0:T(4,128)S(1)} %get-tuple-element.57.lists, ...), custom_call_target="tpu_custom_call" | custom-call | tf_op jit(solution)/shard_map/pallas_call | solution.py:34
  63.0 1.8 %collective-permute-done.16.got = bf16[2,222,512]{2,1,0:T(8,128)(2,1)S(1)} collective-permute-done((bf16[2,222,512]{2,1,0:T(8,128)(2,1)S(1)}, bf16[2,222,512]{2,1,0:T(8,128)(2,1)S(1)}, u32[]{:S(2)}, u32[]{:S(2)}) %collective-permute-start.16) | collective-permute-done | bytes 454688 | tf_op jit(solution)/shard_map/ppermute | solution.py:426
  64.8 0.7 shard_map.73
  65.5 1.8 %collective-permute-start.17 = (bf16[222,512]{1,0:T(8,128)(2,1)S(1)}, bf16[222,512]{1,0:T(8,128)(2,1)S(1)}, u32[]{:S(2)}, u32[]{:S(2)}) collective-permute-start(bf16[222,512]{1,0:T(8,128)(2,1)S(1)} %get-tuple-element.48), channel_id=1, source_target_pairs={{0,2},{1,3},{2,0},{3,1},{4,6},{5,7},{6,4},{7,5},{8,10},{9,11},{10,... | collective-permute-start | bytes 681992 | tf_op jit(solution)/shard_map/ppermute | solution.py:427
  67.3 0.6 shard_map.71.mine
  68.2 6.2 %shard_map.74 = (bf16[2,222,512]{2,1,0:T(8,128)(2,1)S(1)}, f32[2,222,512]{2,1,0:T(8,128)S(1)}) custom-call(s32[4]{0:T(128)S(1)} %pad_add_fusion.sc, bf16[3,888,888]{2,1,0:T(8,128)(2,1)S(1)} %bitcast.14, bf16[3072,896]{1,0:T(8,128)(2,1)S(1)} %shard_map.68.sources, s32[3,1024]{1,0:T(4,128)S(1)} %get-tuple-element.57.lists, ...), custom_call_target="tpu_custom_call" | custom-call | tf_op jit(solution)/shard_map/pallas_call | solution.py:34
  74.5 0.6 collective-permute-start.19
  75.0 1.4 %collective-permute-done.19.got = bf16[2,222,512]{2,1,0:T(8,128)(2,1)S(1)} collective-permute-done((bf16[2,222,512]{2,1,0:T(8,128)(2,1)S(1)}, bf16[2,222,512]{2,1,0:T(8,128)(2,1)S(1)}, u32[]{:S(2)}, u32[]{:S(2)}) %collective-permute-start.19) | collective-permute-done | bytes 454688 | tf_op jit(solution)/shard_map/ppermute | solution.py:426
  76.5 0.7 shard_map.75
  77.5 3.0 %shard_map.76.spread = f32[222,1024]{1,0:T(8,128)S(1)} custom-call(s32[4]{0:T(128)S(1)} %pad_add_fusion.sc, bf16[1776,888]{1,0:T(8,128)(2,1)S(1)} %bitcast.16, bf16[448,128]{1,0:T(8,128)(2,1)S(1)} %shard_map.71.mine, bf16[448,128]{1,0:T(8,128)(2,1)S(1)} %collective-permute-done.18.other), custom_call_target="tpu_custom_call" | custom-call | tf_op jit(solution)/shard_map/pallas_call | solution.py:34
  80.5 4.6 %collective-permute-done.20.refs_3_ = bf16[222,512]{1,0:T(8,128)(2,1)S(1)} collective-permute-done((bf16[222,512]{1,0:T(8,128)(2,1)S(1)}, bf16[222,512]{1,0:T(8,128)(2,1)S(1)}, u32[]{:S(2)}, u32[]{:S(2)}) %collective-permute-start.20) | collective-permute-done | bytes 227360 | tf_op jit(solution)/shard_map/ppermute | solution.py:427
  85.1 1.5 %shard_map.77 = bf16[222,1024]{1,0:T(8,128)(2,1)} custom-call(s32[4]{0:T(128)S(1)} %pad_add_fusion.sc, f32[222,1024]{1,0:T(8,128)S(1)} %shard_map.76.spread, f32[222,512]{1,0:T(8,128)S(1)} %get-tuple-element.55.refs_0_, bf16[222,512]{1,0:T(8,128)(2,1)S(1)} %collective-permute-done.17.refs_1_, f32[222,512]{1,0:T(8,128)S(1)} %get-tuple-element.56.refs_2_, ...), custom_call_target="tpu_custom_call" | custom-call | tf_op jit(solution)/shard_map/pallas_call | solution.py:34
  (43 shorter events, 3.0 us)
Async XLA Ops:
  0.0 1.5 %copy-start = (bf16[888,1024]{1,0:T(8,128)(2,1)S(1)}, bf16[888,1024]{1,0:T(8,128)(2,1)}, u32[]{:S(2)}) copy-start(bf16[888,1024]{1,0:T(8,128)(2,1)} %x_ref.3) | copy-start | bytes 5455876
  1.5 9.5 %copy-start.1 = (bf16[888,1024]{1,0:T(8,128)(2,1)S(1)}, bf16[888,1024]{1,0:T(8,128)(2,1)}, u32[]{:S(2)}) copy-start(bf16[888,1024]{1,0:T(8,128)(2,1)} %x_ref.3) | copy-start | bytes 5455876
  1.7 20.2 %collective-permute-start = (bf16[256,896]{1,0:T(8,128)(2,1)S(1)}, bf16[256,896]{1,0:T(8,128)(2,1)S(1)}, u32[]{:S(2)}, u32[]{:S(2)}) collective-permute-start(bf16[256,896]{1,0:T(8,128)(2,1)S(1)} %shard_map.64.refs_0_), channel_id=1, source_target_pairs={{2,4},{3,5},{6,8},{7,9},{10,12},{11,13},{14,16},{15,17},{18,20},{1... | collective-permute-start | bytes 1376264 | tf_op jit(solution)/shard_map/ppermute | solution.py:406
  12.0 1.9 %copy-start.2 = (bf16[8,222,888]{2,0,1:T(8,128)(2,1)S(1)}, bf16[8,222,888]{2,0,1:T(8,128)(2,1)}, u32[]{:S(2)}) copy-start(bf16[8,222,888]{2,0,1:T(8,128)(2,1)} %param.7) | copy-start | bytes 9462532
  16.7 23.5 %collective-permute-start.1 = (bf16[256,896]{1,0:T(8,128)(2,1)S(1)}, bf16[256,896]{1,0:T(8,128)(2,1)S(1)}, u32[]{:S(2)}, u32[]{:S(2)}) collective-permute-start(bf16[256,896]{1,0:T(8,128)(2,1)S(1)} %get-tuple-element.35.refs_1_), channel_id=1, source_target_pairs={{2,4},{3,5},{6,8},{7,9},{10,12},{11,13},{14,16},{15,17},{18,20},{1... | collective-permute-start | bytes 1376264 | tf_op jit(solution)/shard_map/ppermute | solution.py:406
  17.1 4.2 %collective-permute-start.2 = (bf16[222,128]{1,0:T(8,128)(2,1)S(1)}, bf16[222,128]{1,0:T(8,128)(2,1)S(1)}, u32[]{:S(2)}, u32[]{:S(2)}) collective-permute-start(bf16[222,128]{1,0:T(8,128)(2,1)S(1)} %shard_map.66.refs_0_), channel_id=1, source_target_pairs={{0,2},{1,3},{2,0},{3,1},{4,6},{5,7},{6,4},{7,5},{8,10},{9,11},{10,... | collective-permute-start | bytes 170504 | tf_op jit(solution)/shard_map/ppermute | solution.py:402
  21.3 29.5 %slice-start = ((s8[4773888]{0:T(1024)(128)(4,1)}), s8[4194304]{0:T(1024)(128)(4,1)S(1)}, s32[]{:S(2)}) async-start(s8[4773888]{0:T(1024)(128)(4,1)} %bitcast.13), calls=%async_computation | async-start | bytes 8388608
  21.8 28.9 %slice-start.1 = ((s8[4773888]{0:T(1024)(128)(4,1)}), s8[579584]{0:T(1024)(128)(4,1)S(1)}, s32[]{:S(2)}) async-start(s8[4773888]{0:T(1024)(128)(4,1)} %bitcast.13), calls=%async_computation.1 | async-start | bytes 1159168
  21.9 28.9 %copy-start.4 = (s32[3,128]{1,0:T(4,128)S(1)}, s32[3,128]{1,0:T(4,128)}, u32[]{:S(2)}) copy-start(s32[3,128]{1,0:T(4,128)} %lists.1) | copy-start | bytes 4612
  21.9 18.9 %collective-permute-start.8 = (bf16[256,896]{1,0:T(8,128)(2,1)S(1)}, bf16[256,896]{1,0:T(8,128)(2,1)S(1)}, u32[]{:S(2)}, u32[]{:S(2)}) collective-permute-start(bf16[256,896]{1,0:T(8,128)(2,1)S(1)} %collective-permute-done.refs_3_), channel_id=1, source_target_pairs={{0,2},{1,3},{2,0},{3,1},{4,6},{5,7},{6,4},{7,5},{8,10},{9,11},{10,... | collective-permute-start | bytes 1376264 | tf_op jit(solution)/shard_map/ppermute | solution.py:410
  22.0 13.5 %collective-permute-start.5 = (bf16[222,256]{1,0:T(8,128)(2,1)S(1)}, bf16[222,256]{1,0:T(8,128)(2,1)S(1)}, u32[]{:S(2)}, u32[]{:S(2)}) collective-permute-start(bf16[222,256]{1,0:T(8,128)(2,1)S(1)} %shard_map.67.own), channel_id=1, source_target_pairs={{2,4},{3,5},{6,8},{7,9},{10,12},{11,13},{14,16},{15,17},{18,20},{1... | collective-permute-start | bytes 341000 | tf_op jit(solution)/shard_map/ppermute | solution.py:403
  28.0 7.4 %collective-permute-start.4 = (bf16[222,256]{1,0:T(8,128)(2,1)S(1)}, bf16[222,256]{1,0:T(8,128)(2,1)S(1)}, u32[]{:S(2)}, u32[]{:S(2)}) collective-permute-start(bf16[222,256]{1,0:T(8,128)(2,1)S(1)} %shard_map.67.own), channel_id=1, source_target_pairs={{0,1},{1,0},{2,3},{3,2},{4,5},{5,4},{6,7},{7,6},{8,9},{9,8},{10,11... | collective-permute-start | bytes 341000 | tf_op jit(solution)/shard_map/ppermute | solution.py:404
  35.5 4.8 %collective-permute-start.6 = (bf16[222,256]{1,0:T(8,128)(2,1)S(1)}, bf16[222,256]{1,0:T(8,128)(2,1)S(1)}, u32[]{:S(2)}, u32[]{:S(2)}) collective-permute-start(bf16[222,256]{1,0:T(8,128)(2,1)S(1)} %collective-permute-done.5.a), channel_id=1, source_target_pairs={{0,2},{1,3},{2,0},{3,1},{4,6},{5,7},{6,4},{7,5},{8,10},{9,11},{10,... | collective-permute-start | bytes 341000 | tf_op jit(solution)/shard_map/ppermute | solution.py:408
  40.3 1.8 %collective-permute-start.7 = (bf16[256,896]{1,0:T(8,128)(2,1)S(1)}, bf16[256,896]{1,0:T(8,128)(2,1)S(1)}, u32[]{:S(2)}, u32[]{:S(2)}) collective-permute-start(bf16[256,896]{1,0:T(8,128)(2,1)S(1)} %collective-permute-done.1.refs_4_), channel_id=1, source_target_pairs={{0,1},{1,0},{2,3},{3,2},{4,5},{5,4},{6,7},{7,6},{8,9},{9,8},{10,11... | collective-permute-start | bytes 1376264 | tf_op jit(solution)/shard_map/ppermute | solution.py:411
  40.3 2.5 %collective-permute-start.3 = (bf16[256,896]{1,0:T(8,128)(2,1)S(1)}, bf16[256,896]{1,0:T(8,128)(2,1)S(1)}, u32[]{:S(2)}, u32[]{:S(2)}) collective-permute-start(bf16[256,896]{1,0:T(8,128)(2,1)S(1)} %collective-permute-done.refs_3_), channel_id=1, source_target_pairs={{0,1},{1,0},{2,3},{3,2},{4,5},{5,4},{6,7},{7,6},{8,9},{9,8},{10,11... | collective-permute-start | bytes 1376264 | tf_op jit(solution)/shard_map/ppermute | solution.py:411
  40.8 2.6 %collective-permute-start.9 = (bf16[256,896]{1,0:T(8,128)(2,1)S(1)}, bf16[256,896]{1,0:T(8,128)(2,1)S(1)}, u32[]{:S(2)}, u32[]{:S(2)}) collective-permute-start(bf16[256,896]{1,0:T(8,128)(2,1)S(1)} %collective-permute-done.8.refs_7_), channel_id=1, source_target_pairs={{0,1},{1,0},{2,3},{3,2},{4,5},{5,4},{6,7},{7,6},{8,9},{9,8},{10,11... | collective-permute-start | bytes 1376264 | tf_op jit(solution)/shard_map/ppermute | solution.py:413
  40.8 12.9 %collective-permute-start.14 = (bf16[256,896]{1,0:T(8,128)(2,1)S(1)}, bf16[256,896]{1,0:T(8,128)(2,1)S(1)}, u32[]{:S(2)}, u32[]{:S(2)}) collective-permute-start(bf16[256,896]{1,0:T(8,128)(2,1)S(1)} %collective-permute-done.1.refs_4_), channel_id=1, source_target_pairs={{0,2},{1,3},{2,0},{3,1},{4,6},{5,7},{6,4},{7,5},{8,10},{9,11},{10,... | collective-permute-start | bytes 1376264 | tf_op jit(solution)/shard_map/ppermute | solution.py:410
  40.8 9.9 %collective-permute-start.10 = (bf16[222,256]{1,0:T(8,128)(2,1)S(1)}, bf16[222,256]{1,0:T(8,128)(2,1)S(1)}, u32[]{:S(2)}, u32[]{:S(2)}) collective-permute-start(bf16[222,256]{1,0:T(8,128)(2,1)S(1)} %collective-permute-done.5.a), channel_id=1, source_target_pairs={{0,1},{1,0},{2,3},{3,2},{4,5},{5,4},{6,7},{7,6},{8,9},{9,8},{10,11... | collective-permute-start | bytes 341000 | tf_op jit(solution)/shard_map/ppermute | solution.py:408
  42.1 8.6 %collective-permute-start.11 = (bf16[222,256]{1,0:T(8,128)(2,1)S(1)}, bf16[222,256]{1,0:T(8,128)(2,1)S(1)}, u32[]{:S(2)}, u32[]{:S(2)}) collective-permute-start(bf16[222,256]{1,0:T(8,128)(2,1)S(1)} %collective-permute-done.6.b), channel_id=1, source_target_pairs={{0,1},{1,0},{2,3},{3,2},{4,5},{5,4},{6,7},{7,6},{8,9},{9,8},{10,11... | collective-permute-start | bytes 341000 | tf_op jit(solution)/shard_map/ppermute | solution.py:412
  53.7 2.9 %collective-permute-start.15 = (bf16[256,896]{1,0:T(8,128)(2,1)S(1)}, bf16[256,896]{1,0:T(8,128)(2,1)S(1)}, u32[]{:S(2)}, u32[]{:S(2)}) collective-permute-start(bf16[256,896]{1,0:T(8,128)(2,1)S(1)} %collective-permute-done.14.late), channel_id=1, source_target_pairs={{0,1},{1,0},{2,3},{3,2},{4,5},{5,4},{6,7},{7,6},{8,9},{9,8},{10,11... | collective-permute-start | bytes 1376264 | tf_op jit(solution)/shard_map/ppermute | solution.py:419
  53.7 2.0 %collective-permute-start.12 = (bf16[448,128]{1,0:T(8,128)(2,1)S(1)}, bf16[448,128]{1,0:T(8,128)(2,1)S(1)}, u32[]{:S(2)}, u32[]{:S(2)}) collective-permute-start(bf16[448,128]{1,0:T(8,128)(2,1)S(1)} %get-tuple-element.40), channel_id=1, source_target_pairs={{0,1},{1,0},{2,3},{3,2},{4,5},{5,4},{6,7},{7,6},{8,9},{9,8},{10,11... | collective-permute-start | bytes 344072 | tf_op jit(solution)/shard_map/ppermute | solution.py:421
  56.3 6.6 %collective-permute-start.13 = (bf16[448,128]{1,0:T(8,128)(2,1)S(1)}, bf16[448,128]{1,0:T(8,128)(2,1)S(1)}, u32[]{:S(2)}, u32[]{:S(2)}) collective-permute-start(bf16[448,128]{1,0:T(8,128)(2,1)S(1)} %get-tuple-element.42), channel_id=1, source_target_pairs={{0,2},{1,3},{2,0},{3,1},{4,6},{5,7},{6,4},{7,5},{8,10},{9,11},{10,... | collective-permute-start | bytes 344072 | tf_op jit(solution)/shard_map/ppermute | solution.py:422
  62.9 1.9 %collective-permute-start.16 = (bf16[2,222,512]{2,1,0:T(8,128)(2,1)S(1)}, bf16[2,222,512]{2,1,0:T(8,128)(2,1)S(1)}, u32[]{:S(2)}, u32[]{:S(2)}) collective-permute-start(bf16[2,222,512]{2,1,0:T(8,128)(2,1)S(1)} %get-tuple-element.47), channel_id=1, source_target_pairs={{0,1},{1,0},{2,3},{3,2},{4,5},{5,4},{6,7},{7,6},{8,9},{9,8},{10,11... | collective-permute-start | bytes 1363976 | tf_op jit(solution)/shard_map/ppermute | solution.py:426
  65.5 9.0 %collective-permute-start.17 = (bf16[222,512]{1,0:T(8,128)(2,1)S(1)}, bf16[222,512]{1,0:T(8,128)(2,1)S(1)}, u32[]{:S(2)}, u32[]{:S(2)}) collective-permute-start(bf16[222,512]{1,0:T(8,128)(2,1)S(1)} %get-tuple-element.48), channel_id=1, source_target_pairs={{0,2},{1,3},{2,0},{3,1},{4,6},{5,7},{6,4},{7,5},{8,10},{9,11},{10,... | collective-permute-start | bytes 681992 | tf_op jit(solution)/shard_map/ppermute | solution.py:427
  67.9 6.6 %collective-permute-start.18 = (bf16[448,128]{1,0:T(8,128)(2,1)S(1)}, bf16[448,128]{1,0:T(8,128)(2,1)S(1)}, u32[]{:S(2)}, u32[]{:S(2)}) collective-permute-start(bf16[448,128]{1,0:T(8,128)(2,1)S(1)} %shard_map.71.mine), channel_id=1, source_target_pairs={{0,1},{1,0},{2,3},{3,2},{4,5},{5,4},{6,7},{7,6},{8,9},{9,8},{10,11... | collective-permute-start | bytes 344072 | tf_op jit(solution)/shard_map/ppermute | solution.py:433
  68.2 9.3 %copy-start.3 = (bf16[8,222,888]{2,0,1:T(8,128)(2,1)S(1)}, bf16[8,222,888]{2,0,1:T(8,128)(2,1)}, u32[]{:S(2)}) copy-start(bf16[8,222,888]{2,0,1:T(8,128)(2,1)} %param.9) | copy-start | bytes 9462532
  74.5 2.0 %collective-permute-start.19 = (bf16[2,222,512]{2,1,0:T(8,128)(2,1)S(1)}, bf16[2,222,512]{2,1,0:T(8,128)(2,1)S(1)}, u32[]{:S(2)}, u32[]{:S(2)}) collective-permute-start(bf16[2,222,512]{2,1,0:T(8,128)(2,1)S(1)} %get-tuple-element.52), channel_id=1, source_target_pairs={{0,1},{1,0},{2,3},{3,2},{4,5},{5,4},{6,7},{7,6},{8,9},{9,8},{10,11... | collective-permute-start | bytes 1363976 | tf_op jit(solution)/shard_map/ppermute | solution.py:426
  77.1 8.0 %collective-permute-start.20 = (bf16[222,512]{1,0:T(8,128)(2,1)S(1)}, bf16[222,512]{1,0:T(8,128)(2,1)S(1)}, u32[]{:S(2)}, u32[]{:S(2)}) collective-permute-start(bf16[222,512]{1,0:T(8,128)(2,1)S(1)} %get-tuple-element.53), channel_id=1, source_target_pairs={{0,2},{1,3},{2,0},{3,1},{4,6},{5,7},{6,4},{7,5},{8,10},{9,11},{10,... | collective-permute-start | bytes 681992 | tf_op jit(solution)/shard_map/ppermute | solution.py:427

commit v8 on v6

--- a/solution.py
+++ b/solution.py
@@ -14,10 +14,10 @@
 boxes, half = 1024, 512
 parents = 128
 share = 222
-chunks = 2
+chunks = 4
 chunk = half // chunks
 early = 6 * half - 2 * chunk
-ahead = 512
+ahead = 640
 
 
 def one_hop(groups):
@@ -396,22 +396,26 @@
     late_lists = jnp.where(is_late & ~outside, theirs * chunk + offset - (half - chunk), -1)
 
     head = turned(leaf_density, at(c * half), [chunk])[0]
-    rest = jnp.stack([c * half + chunk, (1 - c) * half]).astype(jnp.int32)
-    tail, other = turned(leaf_density, after(rest, head), [half - chunk, half])
-    up = parent_rows(after(sc, spots, late_lists), up_ops, [head, tail], other)
+    rest = [c * half + i * chunk for i in range(1, chunks)] + [(1 - c) * half]
+    rest = jnp.stack(rest).astype(jnp.int32)
+    *tails, other = turned(leaf_density, after(rest, head), [chunk] * (chunks - 1) + [half])
+    up = parent_rows(after(sc, spots, late_lists), up_ops, [head, *tails], other)
     own = joined(sc, up, zswap(up))
     ca = hop(own)
     own_o = cswap(own)
-    mine = [head, after(tail, up)]
+    mine = [head, tails[0], after(tails[1], up), after(tails[2], own)]
     a = [hop(m) for m in mine]
-    early_a = after(a[0], own)
-    second = after(a[1], early_a, own_o)
-    b = [zswap(early_a), zswap(second)]
-    a_o = [cswap(early_a), cswap(after(second, ca))]
+    came, b = [], []
+    for i, x in enumerate(a):
+        earlier = (up, own, own_o)[: i + 1] + tuple(came[-1:]) + tuple(b[i - 2 : i - 1] if i > 1 else ())
+        came.append(after(x, *earlier))
+        b.append(zswap(came[-1]))
+    came[-1] = after(came[-1], ca, b[-2])
+    a_o = [cswap(x) for x in came]
     cb, ca_o = zswap(ca), cswap(ca)
-    b_o = [cswap(b[0])]
-    picked = gathered(spots, [*mine, other, *a, *a_o, b[0], b_o[0]])
-    b_o.append(cswap(after(b[1], picked, cb)))
+    b_o = [cswap(x) for x in b[:-1]]
+    picked = gathered(spots, [*mine, other, *a, *a_o, *b[:-1], *b_o])
+    b_o.append(cswap(after(b[-1], picked, cb)))
     cb_o = cswap(cb)
 
     def summed(send, keep):
@@ -419,7 +423,7 @@
         here, away = small(split_kernel, sc, (keep, cswap(send)), [(shape, f32), (shape, bf16)])
         return here, zswap(away), away
 
-    late = (b[1], b_o[1])
+    late = (b[-1], b_o[-1])
     send, keep = far_partial(sc, far_ops, picked, late_lists, *late, 0, ahead)
     left = summed(after(send, cb_o, ca_o), keep)
     send, keep = coarse_partial(

time: 85.1 us -> 88.1 us (1.035)
  starting transfers between devices: 23.3 us -> 30.6 us
  waiting for transfers between devices: 23.2 us -> 18.2 us
  local copies, waits for them, and re-layouts: 3.43 us -> 5.57 us
    ppermute x2 -> x4, starting transfers between devices: 10.3 us -> 19.4 us  [local(): a = [hop(m) for m in mine]]
    ppermute x2 -> x4, waiting for transfers between devices: 6.47 us -> 0.01 us  [local(): a = [hop(m) for m in mine]]
    ppermute x2, waiting for transfers between devices: 5.51 us -> 0.01 us  [local(): cb, ca_o = (zswap(ca), cswap(ca))]
    ppermute x1, waiting for transfers between devices: 1.23 us -> 6.15 us  [local(): ca = hop(own)]
    ppermute x1, starting transfers between devices: 5.85 us -> 1.58 us  [local(): ca = hop(own)]
    ppermute x6 -> x12, waiting for transfers between devices: 1.31 us -> 4.75 us  [the longest x4 3.86 us: local(): b.append(zswap(came[-1]))]
    ppermute x6 -> x12, starting transfers between devices: 0.84 us -> 3.6 us  [the longest x4 2.3 us: local(): b.append(zswap(came[-1]))]
    ppermute x1, waiting for transfers between devices: 2.16 us -> 0.01 us  [local(): own = joined(sc, up, zswap(up))]
  transfers between devices with their start and end apart: 21 -> 29, of which waited for: 9 -> 9; matrix products, arithmetic and copies ran while one was open for 1% -> 0% of each run, Pallas kernels for 37% -> 34%
where the time goes in v8:
time: 88.1 us; the launch traced here: 87.9 us
  Pallas kernels  33 us (37%)
  starting transfers between devices  30.6 us (35%)
  waiting for transfers between devices  18.2 us (21%)
  local copies, waits for them, and re-layouts  5.57 us (6%)
    pallas_call x14, Pallas kernels, call(): pl.pallas_call(kernel, grid_spec=pltpu.PrefetchScalarGridSpec(num_scalar_...  33 us
    ppermute x4, starting transfers between devices, local(): a = [hop(m) for m in mine]  19.4 us
    ppermute x1, waiting for transfers between devices, local(): ca = hop(own)  6.15 us
    unnamed x22, local copies, waits for them, and re-layouts  5.05 us
    ppermute x4, waiting for transfers between devices, local(): b.append(zswap(came[-1]))  3.86 us
    ppermute x2, waiting for transfers between devices, summed(): cswap(send)  3.49 us
    ppermute x4, starting transfers between devices, local(): b.append(zswap(came[-1]))  2.3 us
    ppermute x2, starting transfers between devices, local(): cb, ca_o = (zswap(ca), cswap(ca))  2.24 us
  transfers between devices with their start and end apart: 29, of which 9 were waited for; matrix products, arithmetic and copies ran while one was open for 0% of the time, Pallas kernels for 34%

profile of v8, /device:TPU:24, one launch (start us, length us, event | category | flops | bytes accessed | tf_op | source)
XLA Modules:
  0.0 87.9 jit_solution(4034992427453977475)
XLA Ops:
  0.0 1.5 %copy-done = bf16[888,1024]{1,0:T(8,128)(2,1)S(1)} copy-done((bf16[888,1024]{1,0:T(8,128)(2,1)S(1)}, bf16[888,1024]{1,0:T(8,128)(2,1)}, u32[]{:S(2)}) %copy-start) | copy-done | bytes 1818648
  1.6 8.3 %collective-permute-start.1 = (bf16[128,896]{1,0:T(8,128)(2,1)S(1)}, bf16[128,896]{1,0:T(8,128)(2,1)}, u32[]{:S(2)}, u32[]{:S(2)}) collective-permute-start(bf16[128,896]{1,0:T(8,128)(2,1)S(1)} %shard_map.64.refs_0_), channel_id=1, source_target_pairs={{2,4},{3,5},{6,8},{7,9},{10,12},{11,13},{14,16},{15,17},{18,20},{1... | collective-permute-start | bytes 688136 | tf_op jit(solution)/shard_map/ppermute | solution.py:407
  10.0 1.1 %shard_map.65 = (bf16[128,896]{1,0:T(8,128)(2,1)S(1)}, bf16[128,896]{1,0:T(8,128)(2,1)S(1)}, bf16[128,896]{1,0:T(8,128)(2,1)S(1)}, bf16[512,896]{1,0:T(8,128)(2,1)S(1)}) custom-call(s32[4]{0:T(128)S(1)} %pad_add_fusion.1.firsts, bf16[888,1024]{1,0:T(8,128)(2,1)S(1)} %copy-done.1), custom_call_target="tpu_custom_call" | custom-call | tf_op jit(solution)/shard_map/pallas_call | solution.py:34
  11.1 0.7 copy-done.4
  11.8 1.2 %collective-permute-start.2 = (bf16[128,896]{1,0:T(8,128)(2,1)S(1)}, bf16[128,896]{1,0:T(8,128)(2,1)S(1)}, u32[]{:S(2)}, u32[]{:S(2)}) collective-permute-start(bf16[128,896]{1,0:T(8,128)(2,1)S(1)} %get-tuple-element.38.refs_1_), channel_id=1, source_target_pairs={{2,4},{3,5},{6,8},{7,9},{10,12},{11,13},{14,16},{15,17},{18,20},{1... | collective-permute-start | bytes 688136 | tf_op jit(solution)/shard_map/ppermute | solution.py:407
  13.2 1.9 %copy-done.2 = bf16[8,222,888]{2,0,1:T(8,128)(2,1)S(1)} copy-done((bf16[8,222,888]{2,0,1:T(8,128)(2,1)S(1)}, bf16[8,222,888]{2,0,1:T(8,128)(2,1)}, u32[]{:S(2)}) %copy-start.2) | copy-done | bytes 3154200
  15.1 0.9 %copy-done.5 = bf16[128,896]{1,0:T(8,128)(2,1)S(1)} copy-done((bf16[128,896]{1,0:T(8,128)(2,1)S(1)}, bf16[128,896]{1,0:T(8,128)(2,1)}, u32[]{:S(2)}) %copy-start.5) | copy-done | bytes 229400
  16.0 2.9 %shard_map.66.refs_0_ = bf16[222,128]{1,0:T(8,128)(2,1)S(1)} custom-call(s32[4]{0:T(128)S(1)} %pad_add_fusion.sc, bf16[1776,888]{1,0:T(8,128)(2,1)S(1)} %bitcast.17, bf16[512,896]{1,0:T(8,128)(2,1)S(1)} %get-tuple-element.41.other.refs_4_, bf16[128,896]{1,0:T(8,128)(2,1)S(1)} %shard_map.64.refs_0_, bf16[128,896]{1,0:T(8,128)(2,1)S(1)} %get-tuple-element.38.refs_1_, ...), custom_call_target="tpu_custom_call" | custom-call | tf_op jit(solution)/shard_map/pallas_call | solution.py:34
  19.0 5.1 %collective-permute-start.3 = (bf16[128,896]{1,0:T(8,128)(2,1)S(1)}, bf16[128,896]{1,0:T(8,128)(2,1)S(1)}, u32[]{:S(2)}, u32[]{:S(2)}) collective-permute-start(bf16[128,896]{1,0:T(8,128)(2,1)S(1)} %get-tuple-element.43.refs_2_), channel_id=1, source_target_pairs={{2,4},{3,5},{6,8},{7,9},{10,12},{11,13},{14,16},{15,17},{18,20},{1... | collective-permute-start | bytes 688136 | tf_op jit(solution)/shard_map/ppermute | solution.py:407
  24.7 4.7 %collective-permute-start.4 = (bf16[128,896]{1,0:T(8,128)(2,1)S(1)}, bf16[128,896]{1,0:T(8,128)(2,1)S(1)}, u32[]{:S(2)}, u32[]{:S(2)}) collective-permute-start(bf16[128,896]{1,0:T(8,128)(2,1)S(1)} %copy-done.5), channel_id=1, source_target_pairs={{2,4},{3,5},{6,8},{7,9},{10,12},{11,13},{14,16},{15,17},{18,20},{1... | collective-permute-start | bytes 688136 | tf_op jit(solution)/shard_map/ppermute | solution.py:407
  29.5 1.6 %collective-permute-start.11 = (bf16[222,256]{1,0:T(8,128)(2,1)S(1)}, bf16[222,256]{1,0:T(8,128)(2,1)S(1)}, u32[]{:S(2)}, u32[]{:S(2)}) collective-permute-start(bf16[222,256]{1,0:T(8,128)(2,1)S(1)} %shard_map.67.own), channel_id=1, source_target_pairs={{2,4},{3,5},{6,8},{7,9},{10,12},{11,13},{14,16},{15,17},{18,20},{1... | collective-permute-start | bytes 341000 | tf_op jit(solution)/shard_map/ppermute | solution.py:404
  31.1 2.0 %collective-permute-start.12 = (bf16[128,896]{1,0:T(8,128)(2,1)S(1)}, bf16[128,896]{1,0:T(8,128)(2,1)S(1)}, u32[]{:S(2)}, u32[]{:S(2)}) collective-permute-start(bf16[128,896]{1,0:T(8,128)(2,1)S(1)} %collective-permute-done.3.refs_7_), channel_id=1, source_target_pairs={{0,2},{1,3},{2,0},{3,1},{4,6},{5,7},{6,4},{7,5},{8,10},{9,11},{10,... | collective-permute-start | bytes 688136 | tf_op jit(solution)/shard_map/ppermute | solution.py:412
  33.1 6.2 %collective-permute-done.11.a = bf16[222,256]{1,0:T(8,128)(2,1)S(1)} collective-permute-done((bf16[222,256]{1,0:T(8,128)(2,1)S(1)}, bf16[222,256]{1,0:T(8,128)(2,1)S(1)}, u32[]{:S(2)}, u32[]{:S(2)}) %collective-permute-start.11) | collective-permute-done | bytes 113696 | tf_op jit(solution)/shard_map/ppermute | solution.py:404
  39.9 3.9 %collective-permute-done.12.refs_15_ = bf16[128,896]{1,0:T(8,128)(2,1)S(1)} collective-permute-done((bf16[128,896]{1,0:T(8,128)(2,1)S(1)}, bf16[128,896]{1,0:T(8,128)(2,1)S(1)}, u32[]{:S(2)}, u32[]{:S(2)}) %collective-permute-start.12) | collective-permute-done | bytes 229408 | tf_op jit(solution)/shard_map/ppermute | solution.py:412
  44.6 1.7 %collective-permute-start.18 = (bf16[222,256]{1,0:T(8,128)(2,1)S(1)}, bf16[222,256]{1,0:T(8,128)(2,1)S(1)}, u32[]{:S(2)}, u32[]{:S(2)}) collective-permute-start(bf16[222,256]{1,0:T(8,128)(2,1)S(1)} %collective-permute-done.11.a), channel_id=1, source_target_pairs={{0,2},{1,3},{2,0},{3,1},{4,6},{5,7},{6,4},{7,5},{8,10},{9,11},{10,... | collective-permute-start | bytes 341000 | tf_op jit(solution)/shard_map/ppermute | solution.py:415
  46.4 8.3 %shard_map.68.sources = bf16[3072,896]{1,0:T(8,128)(2,1)S(1)} custom-call(s32[3072]{0:T(1024)S(1)} %reshape.12.spots, bf16[128,896]{1,0:T(8,128)(2,1)S(1)} %shard_map.64.refs_0_, bf16[128,896]{1,0:T(8,128)(2,1)S(1)} %get-tuple-element.38.refs_1_, bf16[128,896]{1,0:T(8,128)(2,1)S(1)} %get-tuple-element.43.refs_2_, bf16[128,896]{1,0:T(8,128)(2,1)S(1)} %copy-done.6, ...), custom_call_target="tpu_custom_call" | custom-call | tf_op jit(solution)/shard_map/pallas_call | solution.py:34
  55.5 0.9 collective-permute-done.19.late_o
  56.3 6.3 %shard_map.69 = (bf16[2,222,640]{2,1,0:T(8,128)(2,1)S(1)}, f32[2,222,640]{2,1,0:T(8,128)S(1)}) custom-call(s32[4]{0:T(128)S(1)} %pad_add_fusion.sc, bf16[3,888,888]{2,1,0:T(8,128)(2,1)S(1)} %bitcast.16, bf16[3072,896]{1,0:T(8,128)(2,1)S(1)} %shard_map.68.sources, s32[3,1024]{1,0:T(4,128)S(1)} %get-tuple-element.69.lists, ...), custom_call_target="tpu_custom_call" | custom-call | tf_op jit(solution)/shard_map/pallas_call | solution.py:34
  63.4 1.8 %collective-permute-done.22 = bf16[2,222,640]{2,0,1:T(2,128)(2,1)S(1)} collective-permute-done((bf16[2,222,640]{2,0,1:T(2,128)(2,1)S(1)}, bf16[2,222,640]{2,0,1:T(2,128)(2,1)S(1)}, u32[]{:S(2)}, u32[]{:S(2)}) %collective-permute-start.22) | collective-permute-done | bytes 568352 | tf_op jit(solution)/shard_map/ppermute | solution.py:423
  65.3 0.7 shard_map.70
  66.0 0.6 collective-permute-start.24
  66.6 2.7 %shard_map.71 = (bf16[448,128]{1,0:T(8,128)(2,1)S(1)}, f32[448,128]{1,0:T(8,128)S(1)}) custom-call(s32[4]{0:T(128)S(1)} %pad_add_fusion.sc, s32[3,128]{1,0:T(4,128)S(1)} %copy-done.7, bf16[3,888,888]{2,1,0:T(8,128)(2,1)S(1)} %bitcast.16, bf16[222,256]{1,0:T(8,128)(2,1)S(1)} %shard_map.67.own, bf16[222,256]{1,0:T(8,128)(2,1)S(1)} %collective-permute-done.11.a, ...), custom_call_target="tpu_custom_call" | custom-call | tf_op jit(solution)/shard_map/pallas_call | solution.py:34
  69.4 1.3 %collective-permute-done.23.two = bf16[448,128]{1,0:T(8,128)(2,1)S(1)} collective-permute-done((bf16[448,128]{1,0:T(8,128)(2,1)S(1)}, bf16[448,128]{1,0:T(8,128)(2,1)S(1)}, u32[]{:S(2)}, u32[]{:S(2)}) %collective-permute-start.23) | collective-permute-done | bytes 114720 | tf_op jit(solution)/shard_map/ppermute | solution.py:434
  71.3 1.8 %collective-permute-start.25 = (bf16[448,128]{1,0:T(8,128)(2,1)S(1)}, bf16[448,128]{1,0:T(8,128)(2,1)S(1)}, u32[]{:S(2)}, u32[]{:S(2)}) collective-permute-start(bf16[448,128]{1,0:T(8,128)(2,1)S(1)} %get-tuple-element.63), channel_id=1, source_target_pairs={{0,2},{1,3},{2,0},{3,1},{4,6},{5,7},{6,4},{7,5},{8,10},{9,11},{10,... | collective-permute-start | bytes 344072 | tf_op jit(solution)/shard_map/ppermute | solution.py:439
  73.1 4.2 %shard_map.73 = (bf16[2,222,384]{2,1,0:T(8,128)(2,1)S(1)}, f32[2,222,384]{2,1,0:T(8,128)S(1)}) custom-call(s32[4]{0:T(128)S(1)} %pad_add_fusion.sc, bf16[3,888,888]{2,1,0:T(8,128)(2,1)S(1)} %bitcast.16, bf16[3072,896]{1,0:T(8,128)(2,1)S(1)} %shard_map.68.sources, s32[3,1024]{1,0:T(4,128)S(1)} %get-tuple-element.69.lists, ...), custom_call_target="tpu_custom_call" | custom-call | tf_op jit(solution)/shard_map/pallas_call | solution.py:34
  77.6 1.7 %collective-permute-done.26.got = bf16[2,222,384]{2,1,0:T(8,128)(2,1)S(1)} collective-permute-done((bf16[2,222,384]{2,1,0:T(8,128)(2,1)S(1)}, bf16[2,222,384]{2,1,0:T(8,128)(2,1)S(1)}, u32[]{:S(2)}, u32[]{:S(2)}) %collective-permute-start.26) | collective-permute-done | bytes 341024 | tf_op jit(solution)/shard_map/ppermute | solution.py:423
  79.3 0.6 shard_map.74
  79.9 0.7 collective-permute-start.28
  81.3 1.3 %collective-permute-done.27.other = bf16[448,128]{1,0:T(8,128)(2,1)S(1)} collective-permute-done((bf16[448,128]{1,0:T(8,128)(2,1)S(1)}, bf16[448,128]{1,0:T(8,128)(2,1)S(1)}, u32[]{:S(2)}, u32[]{:S(2)}) %collective-permute-start.27) | collective-permute-done | bytes 114720 | tf_op jit(solution)/shard_map/ppermute | solution.py:442
  82.6 2.9 %shard_map.76.spread = f32[222,1024]{1,0:T(8,128)S(1)} custom-call(s32[4]{0:T(128)S(1)} %pad_add_fusion.sc, bf16[1776,888]{1,0:T(8,128)(2,1)S(1)} %bitcast.18, bf16[448,128]{1,0:T(8,128)(2,1)S(1)} %shard_map.75.mine, bf16[448,128]{1,0:T(8,128)(2,1)S(1)} %collective-permute-done.27.other), custom_call_target="tpu_custom_call" | custom-call | tf_op jit(solution)/shard_map/pallas_call | solution.py:34
  85.6 0.8 collective-permute-done.28.refs_3_
  86.4 1.5 %shard_map.77 = bf16[222,1024]{1,0:T(8,128)(2,1)} custom-call(s32[4]{0:T(128)S(1)} %pad_add_fusion.sc, f32[222,1024]{1,0:T(8,128)S(1)} %shard_map.76.spread, f32[222,640]{1,0:T(8,128)S(1)} %get-tuple-element.67.refs_0_, bf16[222,640]{1,0:T(8,128)(2,1)S(1)} %collective-permute-done.24.refs_1_, f32[222,384]{1,0:T(8,128)S(1)} %get-tuple-element.68.refs_2_, ...), custom_call_target="tpu_custom_call" | custom-call | tf_op jit(solution)/shard_map/pallas_call | solution.py:34
  (69 shorter events, 5.7 us)
Async XLA Ops:
  1.6 22.5 %collective-permute-start.1 = (bf16[128,896]{1,0:T(8,128)(2,1)S(1)}, bf16[128,896]{1,0:T(8,128)(2,1)}, u32[]{:S(2)}, u32[]{:S(2)}) collective-permute-start(bf16[128,896]{1,0:T(8,128)(2,1)S(1)} %shard_map.64.refs_0_), channel_id=1, source_target_pairs={{2,4},{3,5},{6,8},{7,9},{10,12},{11,13},{14,16},{15,17},{18,20},{1... | collective-permute-start | bytes 688136 | tf_op jit(solution)/shard_map/ppermute | solution.py:407
  11.8 17.7 %collective-permute-start.2 = (bf16[128,896]{1,0:T(8,128)(2,1)S(1)}, bf16[128,896]{1,0:T(8,128)(2,1)S(1)}, u32[]{:S(2)}, u32[]{:S(2)}) collective-permute-start(bf16[128,896]{1,0:T(8,128)(2,1)S(1)} %get-tuple-element.38.refs_1_), channel_id=1, source_target_pairs={{2,4},{3,5},{6,8},{7,9},{10,12},{11,13},{14,16},{15,17},{18,20},{1... | collective-permute-start | bytes 688136 | tf_op jit(solution)/shard_map/ppermute | solution.py:407
  16.0 30.4 %copy-start.6 = (bf16[128,896]{1,0:T(8,128)(2,1)S(1)}, bf16[128,896]{1,0:T(8,128)(2,1)}, u32[]{:S(2)}) copy-start(bf16[128,896]{1,0:T(8,128)(2,1)} %copy-done.4) | copy-start | bytes 688132
  18.9 5.3 %collective-permute-start = (bf16[222,128]{1,0:T(8,128)(2,1)S(1)}, bf16[222,128]{1,0:T(8,128)(2,1)S(1)}, u32[]{:S(2)}, u32[]{:S(2)}) collective-permute-start(bf16[222,128]{1,0:T(8,128)(2,1)S(1)} %shard_map.66.refs_0_), channel_id=1, source_target_pairs={{0,2},{1,3},{2,0},{3,1},{4,6},{5,7},{6,4},{7,5},{8,10},{9,11},{10,... | collective-permute-start | bytes 170504 | tf_op jit(solution)/shard_map/ppermute | solution.py:403
  19.0 12.1 %collective-permute-start.3 = (bf16[128,896]{1,0:T(8,128)(2,1)S(1)}, bf16[128,896]{1,0:T(8,128)(2,1)S(1)}, u32[]{:S(2)}, u32[]{:S(2)}) collective-permute-start(bf16[128,896]{1,0:T(8,128)(2,1)S(1)} %get-tuple-element.43.refs_2_), channel_id=1, source_target_pairs={{2,4},{3,5},{6,8},{7,9},{10,12},{11,13},{14,16},{15,17},{18,20},{1... | collective-permute-start | bytes 688136 | tf_op jit(solution)/shard_map/ppermute | solution.py:407
  24.1 7.0 %collective-permute-start.8 = (bf16[128,896]{1,0:T(8,128)(2,1)}, bf16[128,896]{1,0:T(8,128)(2,1)S(1)}, u32[]{:S(2)}, u32[]{:S(2)}) collective-permute-start(bf16[128,896]{1,0:T(8,128)(2,1)} %collective-permute-done.1.refs_5_), channel_id=1, source_target_pairs={{0,2},{1,3},{2,0},{3,1},{4,6},{5,7},{6,4},{7,5},{8,10},{9,11},{10,... | collective-permute-start | bytes 688136 | tf_op jit(solution)/shard_map/ppermute | solution.py:412
  24.1 32.2 %slice-start = ((s8[4773888]{0:T(1024)(128)(4,1)}), s8[4194304]{0:T(1024)(128)(4,1)S(1)}, s32[]{:S(2)}) async-start(s8[4773888]{0:T(1024)(128)(4,1)} %bitcast.15), calls=%async_computation | async-start | bytes 8388608
  24.7 31.6 %slice-start.1 = ((s8[4773888]{0:T(1024)(128)(4,1)}), s8[579584]{0:T(1024)(128)(4,1)S(1)}, s32[]{:S(2)}) async-start(s8[4773888]{0:T(1024)(128)(4,1)} %bitcast.15), calls=%async_computation.1 | async-start | bytes 1159168
  24.7 14.5 %collective-permute-start.4 = (bf16[128,896]{1,0:T(8,128)(2,1)S(1)}, bf16[128,896]{1,0:T(8,128)(2,1)S(1)}, u32[]{:S(2)}, u32[]{:S(2)}) collective-permute-start(bf16[128,896]{1,0:T(8,128)(2,1)S(1)} %copy-done.5), channel_id=1, source_target_pairs={{2,4},{3,5},{6,8},{7,9},{10,12},{11,13},{14,16},{15,17},{18,20},{1... | collective-permute-start | bytes 688136 | tf_op jit(solution)/shard_map/ppermute | solution.py:407
  29.5 1.6 %collective-permute-start.7 = (bf16[222,256]{1,0:T(8,128)(2,1)S(1)}, bf16[222,256]{1,0:T(8,128)(2,1)S(1)}, u32[]{:S(2)}, u32[]{:S(2)}) collective-permute-start(bf16[222,256]{1,0:T(8,128)(2,1)S(1)} %shard_map.67.own), channel_id=1, source_target_pairs={{0,1},{1,0},{2,3},{3,2},{4,5},{5,4},{6,7},{7,6},{8,9},{9,8},{10,11... | collective-permute-start | bytes 341000 | tf_op jit(solution)/shard_map/ppermute | solution.py:405
  29.5 9.8 %collective-permute-start.11 = (bf16[222,256]{1,0:T(8,128)(2,1)S(1)}, bf16[222,256]{1,0:T(8,128)(2,1)S(1)}, u32[]{:S(2)}, u32[]{:S(2)}) collective-permute-start(bf16[222,256]{1,0:T(8,128)(2,1)S(1)} %shard_map.67.own), channel_id=1, source_target_pairs={{2,4},{3,5},{6,8},{7,9},{10,12},{11,13},{14,16},{15,17},{18,20},{1... | collective-permute-start | bytes 341000 | tf_op jit(solution)/shard_map/ppermute | solution.py:404
  31.1 8.7 %collective-permute-start.10 = (bf16[128,896]{1,0:T(8,128)(2,1)S(1)}, bf16[128,896]{1,0:T(8,128)(2,1)S(1)}, u32[]{:S(2)}, u32[]{:S(2)}) collective-permute-start(bf16[128,896]{1,0:T(8,128)(2,1)S(1)} %collective-permute-done.2.refs_6_), channel_id=1, source_target_pairs={{0,2},{1,3},{2,0},{3,1},{4,6},{5,7},{6,4},{7,5},{8,10},{9,11},{10,... | collective-permute-start | bytes 688136 | tf_op jit(solution)/shard_map/ppermute | solution.py:412
  31.1 12.6 %collective-permute-start.12 = (bf16[128,896]{1,0:T(8,128)(2,1)S(1)}, bf16[128,896]{1,0:T(8,128)(2,1)S(1)}, u32[]{:S(2)}, u32[]{:S(2)}) collective-permute-start(bf16[128,896]{1,0:T(8,128)(2,1)S(1)} %collective-permute-done.3.refs_7_), channel_id=1, source_target_pairs={{0,2},{1,3},{2,0},{3,1},{4,6},{5,7},{6,4},{7,5},{8,10},{9,11},{10,... | collective-permute-start | bytes 688136 | tf_op jit(solution)/shard_map/ppermute | solution.py:412
  33.1 10.6 %collective-permute-start.6 = (bf16[128,896]{1,0:T(8,128)(2,1)S(1)}, bf16[128,896]{1,0:T(8,128)(2,1)S(1)}, u32[]{:S(2)}, u32[]{:S(2)}) collective-permute-start(bf16[128,896]{1,0:T(8,128)(2,1)S(1)} %collective-permute-done.2.refs_6_), channel_id=1, source_target_pairs={{0,1},{1,0},{2,3},{3,2},{4,5},{5,4},{6,7},{7,6},{8,9},{9,8},{10,11... | collective-permute-start | bytes 688136 | tf_op jit(solution)/shard_map/ppermute | solution.py:414
  39.3 5.0 %collective-permute-start.5 = (bf16[128,896]{1,0:T(8,128)(2,1)}, bf16[128,896]{1,0:T(8,128)(2,1)S(1)}, u32[]{:S(2)}, u32[]{:S(2)}) collective-permute-start(bf16[128,896]{1,0:T(8,128)(2,1)} %collective-permute-done.1.refs_5_), channel_id=1, source_target_pairs={{0,1},{1,0},{2,3},{3,2},{4,5},{5,4},{6,7},{7,6},{8,9},{9,8},{10,11... | collective-permute-start | bytes 688136 | tf_op jit(solution)/shard_map/ppermute | solution.py:414
  39.3 5.1 %collective-permute-start.9 = (bf16[128,896]{1,0:T(8,128)(2,1)S(1)}, bf16[128,896]{1,0:T(8,128)(2,1)S(1)}, u32[]{:S(2)}, u32[]{:S(2)}) collective-permute-start(bf16[128,896]{1,0:T(8,128)(2,1)S(1)} %collective-permute-done.3.refs_7_), channel_id=1, source_target_pairs={{0,1},{1,0},{2,3},{3,2},{4,5},{5,4},{6,7},{7,6},{8,9},{9,8},{10,11... | collective-permute-start | bytes 688136 | tf_op jit(solution)/shard_map/ppermute | solution.py:414
  39.8 4.8 %collective-permute-start.15 = (bf16[128,896]{1,0:T(8,128)(2,1)S(1)}, bf16[128,896]{1,0:T(8,128)(2,1)S(1)}, u32[]{:S(2)}, u32[]{:S(2)}) collective-permute-start(bf16[128,896]{1,0:T(8,128)(2,1)S(1)} %collective-permute-done.10.refs_14_), channel_id=1, source_target_pairs={{0,1},{1,0},{2,3},{3,2},{4,5},{5,4},{6,7},{7,6},{8,9},{9,8},{10,11... | collective-permute-start | bytes 688136 | tf_op jit(solution)/shard_map/ppermute | solution.py:416
  43.7 2.6 %collective-permute-start.14 = (bf16[128,896]{1,0:T(8,128)(2,1)S(1)}, bf16[128,896]{1,0:T(8,128)(2,1)S(1)}, u32[]{:S(2)}, u32[]{:S(2)}) collective-permute-start(bf16[128,896]{1,0:T(8,128)(2,1)S(1)} %collective-permute-done.8.refs_13_), channel_id=1, source_target_pairs={{0,1},{1,0},{2,3},{3,2},{4,5},{5,4},{6,7},{7,6},{8,9},{9,8},{10,11... | collective-permute-start | bytes 688136 | tf_op jit(solution)/shard_map/ppermute | solution.py:416
  43.7 2.6 %collective-permute-start.13 = (bf16[128,896]{1,0:T(8,128)(2,1)S(1)}, bf16[128,896]{1,0:T(8,128)(2,1)S(1)}, u32[]{:S(2)}, u32[]{:S(2)}) collective-permute-start(bf16[128,896]{1,0:T(8,128)(2,1)S(1)} %collective-permute-done.4.refs_8_), channel_id=1, source_target_pairs={{0,1},{1,0},{2,3},{3,2},{4,5},{5,4},{6,7},{7,6},{8,9},{9,8},{10,11... | collective-permute-start | bytes 688136 | tf_op jit(solution)/shard_map/ppermute | solution.py:414
  44.2 2.1 %collective-permute-start.16 = (bf16[128,896]{1,0:T(8,128)(2,1)S(1)}, bf16[128,896]{1,0:T(8,128)(2,1)S(1)}, u32[]{:S(2)}, u32[]{:S(2)}) collective-permute-start(bf16[128,896]{1,0:T(8,128)(2,1)S(1)} %collective-permute-done.12.refs_15_), channel_id=1, source_target_pairs={{0,1},{1,0},{2,3},{3,2},{4,5},{5,4},{6,7},{7,6},{8,9},{9,8},{10,11... | collective-permute-start | bytes 688136 | tf_op jit(solution)/shard_map/ppermute | solution.py:416
  44.3 10.4 %collective-permute-start.17 = (bf16[128,896]{1,0:T(8,128)(2,1)S(1)}, bf16[128,896]{1,0:T(8,128)(2,1)S(1)}, u32[]{:S(2)}, u32[]{:S(2)}) collective-permute-start(bf16[128,896]{1,0:T(8,128)(2,1)S(1)} %collective-permute-done.4.refs_8_), channel_id=1, source_target_pairs={{0,2},{1,3},{2,0},{3,1},{4,6},{5,7},{6,4},{7,5},{8,10},{9,11},{10,... | collective-permute-start | bytes 688136 | tf_op jit(solution)/shard_map/ppermute | solution.py:412
  44.6 10.1 %collective-permute-start.18 = (bf16[222,256]{1,0:T(8,128)(2,1)S(1)}, bf16[222,256]{1,0:T(8,128)(2,1)S(1)}, u32[]{:S(2)}, u32[]{:S(2)}) collective-permute-start(bf16[222,256]{1,0:T(8,128)(2,1)S(1)} %collective-permute-done.11.a), channel_id=1, source_target_pairs={{0,2},{1,3},{2,0},{3,1},{4,6},{5,7},{6,4},{7,5},{8,10},{9,11},{10,... | collective-permute-start | bytes 341000 | tf_op jit(solution)/shard_map/ppermute | solution.py:415
  54.8 1.6 %collective-permute-start.19 = (bf16[128,896]{1,0:T(8,128)(2,1)S(1)}, bf16[128,896]{1,0:T(8,128)(2,1)S(1)}, u32[]{:S(2)}, u32[]{:S(2)}) collective-permute-start(bf16[128,896]{1,0:T(8,128)(2,1)S(1)} %collective-permute-done.17.late), channel_id=1, source_target_pairs={{0,1},{1,0},{2,3},{3,2},{4,5},{5,4},{6,7},{7,6},{8,9},{9,8},{10,11... | collective-permute-start | bytes 688136 | tf_op jit(solution)/shard_map/ppermute | solution.py:418
  54.9 7.8 %collective-permute-start.21 = (bf16[222,256]{1,0:T(8,128)(2,1)S(1)}, bf16[222,256]{1,0:T(8,128)(2,1)S(1)}, u32[]{:S(2)}, u32[]{:S(2)}) collective-permute-start(bf16[222,256]{1,0:T(8,128)(2,1)S(1)} %collective-permute-done.11.a), channel_id=1, source_target_pairs={{0,1},{1,0},{2,3},{3,2},{4,5},{5,4},{6,7},{7,6},{8,9},{9,8},{10,11... | collective-permute-start | bytes 341000 | tf_op jit(solution)/shard_map/ppermute | solution.py:415
  55.4 7.4 %collective-permute-start.20 = (bf16[222,256]{1,0:T(8,128)(2,1)S(1)}, bf16[222,256]{1,0:T(8,128)(2,1)S(1)}, u32[]{:S(2)}, u32[]{:S(2)}) collective-permute-start(bf16[222,256]{1,0:T(8,128)(2,1)S(1)} %collective-permute-done.18.b), channel_id=1, source_target_pairs={{0,1},{1,0},{2,3},{3,2},{4,5},{5,4},{6,7},{7,6},{8,9},{9,8},{10,11... | collective-permute-start | bytes 341000 | tf_op jit(solution)/shard_map/ppermute | solution.py:419
  63.2 2.1 %collective-permute-start.22 = (bf16[2,222,640]{2,0,1:T(2,128)(2,1)S(1)}, bf16[2,222,640]{2,0,1:T(2,128)(2,1)S(1)}, u32[]{:S(2)}, u32[]{:S(2)}) collective-permute-start(bf16[2,222,640]{2,0,1:T(2,128)(2,1)S(1)} %copy.7), channel_id=1, source_target_pairs={{0,1},{1,0},{2,3},{3,2},{4,5},{5,4},{6,7},{7,6},{8,9},{9,8},{10,11... | collective-permute-start | bytes 1704968 | tf_op jit(solution)/shard_map/ppermute | solution.py:423
  66.0 11.6 %collective-permute-start.24 = (bf16[222,640]{1,0:T(8,128)(2,1)S(1)}, bf16[222,640]{1,0:T(8,128)(2,1)S(1)}, u32[]{:S(2)}, u32[]{:S(2)}) collective-permute-start(bf16[222,640]{1,0:T(8,128)(2,1)S(1)} %get-tuple-element.54), channel_id=1, source_target_pairs={{0,2},{1,3},{2,0},{3,1},{4,6},{5,7},{6,4},{7,5},{8,10},{9,11},{10,... | collective-permute-start | bytes 852488 | tf_op jit(solution)/shard_map/ppermute | solution.py:424
  69.3 1.4 %collective-permute-start.23 = (bf16[448,128]{1,0:T(8,128)(2,1)S(1)}, bf16[448,128]{1,0:T(8,128)(2,1)S(1)}, u32[]{:S(2)}, u32[]{:S(2)}) collective-permute-start(bf16[448,128]{1,0:T(8,128)(2,1)S(1)} %get-tuple-element.58), channel_id=1, source_target_pairs={{0,1},{1,0},{2,3},{3,2},{4,5},{5,4},{6,7},{7,6},{8,9},{9,8},{10,11... | collective-permute-start | bytes 344072 | tf_op jit(solution)/shard_map/ppermute | solution.py:434
  71.3 6.4 %collective-permute-start.25 = (bf16[448,128]{1,0:T(8,128)(2,1)S(1)}, bf16[448,128]{1,0:T(8,128)(2,1)S(1)}, u32[]{:S(2)}, u32[]{:S(2)}) collective-permute-start(bf16[448,128]{1,0:T(8,128)(2,1)S(1)} %get-tuple-element.63), channel_id=1, source_target_pairs={{0,2},{1,3},{2,0},{3,1},{4,6},{5,7},{6,4},{7,5},{8,10},{9,11},{10,... | collective-permute-start | bytes 344072 | tf_op jit(solution)/shard_map/ppermute | solution.py:439
  77.6 1.7 %collective-permute-start.26 = (bf16[2,222,384]{2,1,0:T(8,128)(2,1)S(1)}, bf16[2,222,384]{2,1,0:T(8,128)(2,1)S(1)}, u32[]{:S(2)}, u32[]{:S(2)}) collective-permute-start(bf16[2,222,384]{2,1,0:T(8,128)(2,1)S(1)} %get-tuple-element.64), channel_id=1, source_target_pairs={{0,1},{1,0},{2,3},{3,2},{4,5},{5,4},{6,7},{7,6},{8,9},{9,8},{10,11... | collective-permute-start | bytes 1022984 | tf_op jit(solution)/shard_map/ppermute | solution.py:423
  79.9 6.5 %collective-permute-start.28 = (bf16[222,384]{1,0:T(8,128)(2,1)S(1)}, bf16[222,384]{1,0:T(8,128)(2,1)S(1)}, u32[]{:S(2)}, u32[]{:S(2)}) collective-permute-start(bf16[222,384]{1,0:T(8,128)(2,1)S(1)} %get-tuple-element.65), channel_id=1, source_target_pairs={{0,2},{1,3},{2,0},{3,1},{4,6},{5,7},{6,4},{7,5},{8,10},{9,11},{10,... | collective-permute-start | bytes 511496 | tf_op jit(solution)/shard_map/ppermute | solution.py:424
  81.2 1.4 %collective-permute-start.27 = (bf16[448,128]{1,0:T(8,128)(2,1)S(1)}, bf16[448,128]{1,0:T(8,128)(2,1)S(1)}, u32[]{:S(2)}, u32[]{:S(2)}) collective-permute-start(bf16[448,128]{1,0:T(8,128)(2,1)S(1)} %shard_map.75.mine), channel_id=1, source_target_pairs={{0,1},{1,0},{2,3},{3,2},{4,5},{5,4},{6,7},{7,6},{8,9},{9,8},{10,11... | collective-permute-start | bytes 344072 | tf_op jit(solution)/shard_map/ppermute | solution.py:442
  (8 other events, 38.5 us)

commit v9 on v6

--- a/solution.py
+++ b/solution.py
@@ -13,7 +13,8 @@
 rows, wide, tiles = 888, 896, 7
 boxes, half = 1024, 512
 parents = 128
-share = 222
+share, share_pad = 222, 224
+coarse_block = wide // 8
 chunks = 2
 chunk = half // chunks
 early = 6 * half - 2 * chunk
@@ -86,17 +87,31 @@
     away[...] = (keep[1 - l] + got[1 - l].astype(f32)).astype(bf16)
 
 
-def add_kernel(sc, one, two, *outs):
-    total = one[...] + two[...].astype(f32)
-    for o_ref in outs:
-        o_ref[...] = total.astype(o_ref.dtype)
+def split_both_kernel(sc, keep, got, coarse_keep, coarse_got, here, away, part):
+    l = sc[1]
+    here[...] = keep[l] + got[l].astype(f32)
+    theirs = keep[1 - l] + got[1 - l].astype(f32)
+    theirs = jnp.concatenate([theirs, jnp.zeros((share_pad - share, theirs.shape[1]), f32)], 0)
+    away[:share_pad, :] = theirs.astype(bf16)
+    total = coarse_keep[...] + coarse_got[...].astype(f32)
+    part[...] = total
+    for i in range(4):
+        block = total[i * coarse_block : (i + 1) * coarse_block]
+        away[share_pad:, i * parents : (i + 1) * parents] = block.astype(bf16)
+
+
+def check_kernel(sc, part, got, o_ref):
+    for i in range(4):
+        lines = slice(i * coarse_block, (i + 1) * coarse_block)
+        theirs = got[share_pad:, i * parents : (i + 1) * parents].astype(f32)
+        o_ref[lines, :] = (part[lines, :] + theirs).astype(bf16)
 
 
 def last_kernel(sc, spread, *refs):
     o_ref, at = refs[-1], 0
     for here, there in zip(refs[:-1:2], refs[1:-1:2]):
         lanes = slice(at, at + here.shape[1])
-        o_ref[:, lanes] = (here[...] + there[...].astype(f32) + spread[:, lanes]).astype(bf16)
+        o_ref[:, lanes] = (here[...] + there[:share, :].astype(f32) + spread[:, lanes]).astype(bf16)
         at += here.shape[1]
 
 
@@ -411,33 +426,38 @@
     cb, ca_o = zswap(ca), cswap(ca)
     b_o = [cswap(b[0])]
     picked = gathered(spots, [*mine, other, *a, *a_o, b[0], b_o[0]])
-    b_o.append(cswap(after(b[1], picked, cb)))
+    b_o.append(cswap(after(b[1], picked)))
     cb_o = cswap(cb)
-
-    def summed(send, keep):
-        shape = (share, send.shape[2])
-        here, away = small(split_kernel, sc, (keep, cswap(send)), [(shape, f32), (shape, bf16)])
-        return here, zswap(away), away
 
     late = (b[1], b_o[1])
     send, keep = far_partial(sc, far_ops, picked, late_lists, *late, 0, ahead)
-    left = summed(after(send, cb_o, ca_o), keep)
-    send, keep = coarse_partial(
+    got = cswap(after(send, cb, ca_o))
+    coarse_send, coarse_keep = coarse_partial(
         after(sc, send), coarse_lists, far_ops, own, ca, cb, own_o, ca_o, cb_o
     )
-    shape = (wide // 2, parents)
-    part, part_sent = small(
-        add_kernel, after(sc, left[2]), (keep, cswap(send)), [(shape, f32), (shape, bf16)]
-    )
+    here, away, part = small(
+        split_both_kernel,
+        sc,
+        (keep, got, coarse_keep, cswap(coarse_send)),
+        [
+            ((share, ahead), f32),
+            ((share_pad + coarse_block, ahead), bf16),
+            ((wide // 2, parents), f32),
+        ],
+    )
+    left = here, zswap(away)
     send, keep = far_partial(
         after(sc, part), far_ops, picked, late_lists, *late, ahead, boxes - ahead
     )
-    part_got = zswap(part_sent)
-    right = summed(after(send, left[1], part_got), keep)
-    check = small(add_kernel, sc, (part, part_got), [(shape, bf16)])[0]
+    shape = (share, boxes - ahead)
+    here, away = small(
+        split_kernel, sc, (keep, cswap(after(send, left[1]))), [(shape, f32), (shape, bf16)]
+    )
+    right = here, zswap(away)
+    check = small(check_kernel, sc, (part, left[1]), [((wide // 2, parents), bf16)])[0]
     check_o = cswap(check)
-    spread = downward(after(sc, right[2]), down_ops, check, check_o)
-    return small(last_kernel, sc, (spread, *left[:2], *right[:2]), [((share, boxes), bf16)])[0]
+    spread = downward(after(sc, away), down_ops, check, check_o)
+    return small(last_kernel, sc, (spread, *left, *right), [((share, boxes), bf16)])[0]
 
 
 def solution(mesh):

time: 85.1 us -> 85.7 us (level)
  waiting for transfers between devices: 23.2 us -> 27.6 us
  starting transfers between devices: 23.3 us -> 20.1 us
    ppermute x2, waiting for transfers between devices: 5.51 us -> 0.01 us  [local(): cb, ca_o = (zswap(ca), cswap(ca))]
    ppermute x7 -> x6, waiting for transfers between devices: 6.51 us -> 9.85 us  [the longest x1 3.42 us: local(): left = (here, zswap(away))]
    ppermute x2, waiting for transfers between devices: 0.01 us -> 3.14 us  [local(): b = [zswap(early_a), zswap(second)]]
    ppermute x2, starting transfers between devices: 2.53 us -> 0.51 us  [local(): cb, ca_o = (zswap(ca), cswap(ca))]
    ppermute x7 -> x6, starting transfers between devices: 3.48 us -> 1.89 us  [the longest x1 0.76 us: local(): left = (here, zswap(away))]
    ppermute x1, waiting for transfers between devices: 0.01 us -> 1.47 us  [local(): cb_o = cswap(cb)]
    ppermute x2, waiting for transfers between devices: 0.01 us -> 1.3 us  [local(): a_o = [cswap(early_a), cswap(after(second, ca))]]
    pallas_call x14 -> x13, Pallas kernels: 33.8 us -> 33.4 us  [call(): pl.pallas_call(kernel, grid_spec=pltpu.PrefetchScalarGridSpec(num_scalar_...]
  transfers between devices with their start and end apart: 21 -> 20, of which waited for: 9 -> 13; matrix products, arithmetic and copies ran while one was open for 1% -> 1% of each run, Pallas kernels for 37% -> 35%
where the time goes in v9:
time: 85.7 us; the launch traced here: 85.6 us
  Pallas kernels  33.4 us (39%)
  waiting for transfers between devices  27.6 us (32%)
  starting transfers between devices  20.1 us (23%)
  local copies, waits for them, and re-layouts  3.43 us (4%)
  other arithmetic  0.92 us (1%)
    pallas_call x13, Pallas kernels, call(): pl.pallas_call(kernel, grid_spec=pltpu.PrefetchScalarGridSpec(num_scalar_...  33.4 us
    ppermute x2, starting transfers between devices, local(): a = [hop(m) for m in mine]  10.3 us
    ppermute x2, waiting for transfers between devices, local(): a = [hop(m) for m in mine]  6.47 us
    ppermute x1, starting transfers between devices, local(): ca = hop(own)  5.85 us
    ppermute x1, waiting for transfers between devices, local(): left = (here, zswap(away))  3.42 us
    unnamed x14, local copies, waits for them, and re-layouts  3.41 us
    ppermute x2, waiting for transfers between devices, local(): b = [zswap(early_a), zswap(second)]  3.14 us
    ppermute x1, waiting for transfers between devices, local(): own = joined(sc, up, zswap(up))  2.16 us
  transfers between devices with their start and end apart: 20, of which 13 were waited for; matrix products, arithmetic and copies ran while one was open for 1% of the time, Pallas kernels for 35%

profile of v9, /device:TPU:24, one launch (start us, length us, event | category | flops | bytes accessed | tf_op | source)
XLA Modules:
  0.0 85.6 jit_solution(18205706486308116522)
XLA Ops:
  0.0 1.5 %copy-done = bf16[888,1024]{1,0:T(8,128)(2,1)S(1)} copy-done((bf16[888,1024]{1,0:T(8,128)(2,1)S(1)}, bf16[888,1024]{1,0:T(8,128)(2,1)}, u32[]{:S(2)}) %copy-start) | copy-done | bytes 1818648
  1.7 8.3 %collective-permute-start = (bf16[256,896]{1,0:T(8,128)(2,1)S(1)}, bf16[256,896]{1,0:T(8,128)(2,1)S(1)}, u32[]{:S(2)}, u32[]{:S(2)}) collective-permute-start(bf16[256,896]{1,0:T(8,128)(2,1)S(1)} %shard_map.64.refs_0_), channel_id=1, source_target_pairs={{2,4},{3,5},{6,8},{7,9},{10,12},{11,13},{14,16},{15,17},{18,20},{1... | collective-permute-start | bytes 1376264 | tf_op jit(solution)/shard_map/ppermute | solution.py:421
  10.0 0.8 fusion.6
  11.0 1.0 %shard_map.65 = (bf16[256,896]{1,0:T(8,128)(2,1)S(1)}, bf16[512,896]{1,0:T(8,128)(2,1)S(1)}) custom-call(s32[2]{0:T(128)S(1)} %pad_add_fusion.1.firsts, bf16[888,1024]{1,0:T(8,128)(2,1)S(1)} %copy-done.1), custom_call_target="tpu_custom_call" | custom-call | tf_op jit(solution)/shard_map/pallas_call | solution.py:35
  12.0 1.9 %copy-done.2 = bf16[8,222,888]{2,0,1:T(8,128)(2,1)S(1)} copy-done((bf16[8,222,888]{2,0,1:T(8,128)(2,1)S(1)}, bf16[8,222,888]{2,0,1:T(8,128)(2,1)}, u32[]{:S(2)}) %copy-start.2) | copy-done | bytes 3154200
  13.9 2.9 %shard_map.66.refs_0_ = bf16[222,128]{1,0:T(8,128)(2,1)S(1)} custom-call(s32[4]{0:T(128)S(1)} %pad_add_fusion.sc, bf16[1776,888]{1,0:T(8,128)(2,1)S(1)} %bitcast.15, bf16[512,896]{1,0:T(8,128)(2,1)S(1)} %get-tuple-element.33.other.refs_2_, bf16[256,896]{1,0:T(8,128)(2,1)S(1)} %shard_map.64.refs_0_, bf16[256,896]{1,0:T(8,128)(2,1)S(1)} %get-tuple-element.34.refs_1_), custom_call_target="tpu_custom_call" | custom-call | tf_op jit(solution)/shard_map/pallas_call | solution.py:35
  16.8 2.0 %collective-permute-start.1 = (bf16[256,896]{1,0:T(8,128)(2,1)S(1)}, bf16[256,896]{1,0:T(8,128)(2,1)S(1)}, u32[]{:S(2)}, u32[]{:S(2)}) collective-permute-start(bf16[256,896]{1,0:T(8,128)(2,1)S(1)} %get-tuple-element.34.refs_1_), channel_id=1, source_target_pairs={{2,4},{3,5},{6,8},{7,9},{10,12},{11,13},{14,16},{15,17},{18,20},{1... | collective-permute-start | bytes 1376264 | tf_op jit(solution)/shard_map/ppermute | solution.py:421
  18.8 2.2 %collective-permute-done.2.refs_1_ = bf16[222,128]{1,0:T(8,128)(2,1)S(1)} collective-permute-done((bf16[222,128]{1,0:T(8,128)(2,1)S(1)}, bf16[222,128]{1,0:T(8,128)(2,1)S(1)}, u32[]{:S(2)}, u32[]{:S(2)}) %collective-permute-start.2) | collective-permute-done | bytes 56864 | tf_op jit(solution)/shard_map/ppermute | solution.py:417
  21.8 5.9 %collective-permute-start.5 = (bf16[222,256]{1,0:T(8,128)(2,1)S(1)}, bf16[222,256]{1,0:T(8,128)(2,1)S(1)}, u32[]{:S(2)}, u32[]{:S(2)}) collective-permute-start(bf16[222,256]{1,0:T(8,128)(2,1)S(1)} %shard_map.67.own), channel_id=1, source_target_pairs={{2,4},{3,5},{6,8},{7,9},{10,12},{11,13},{14,16},{15,17},{18,20},{1... | collective-permute-start | bytes 341000 | tf_op jit(solution)/shard_map/ppermute | solution.py:418
  27.9 6.5 %collective-permute-done.1.refs_4_ = bf16[256,896]{1,0:T(8,128)(2,1)S(1)} collective-permute-done((bf16[256,896]{1,0:T(8,128)(2,1)S(1)}, bf16[256,896]{1,0:T(8,128)(2,1)S(1)}, u32[]{:S(2)}, u32[]{:S(2)}) %collective-permute-start.1) | collective-permute-done | bytes 458784 | tf_op jit(solution)/shard_map/ppermute | solution.py:421
  34.4 1.2 %collective-permute-done.5.a = bf16[222,256]{1,0:T(8,128)(2,1)S(1)} collective-permute-done((bf16[222,256]{1,0:T(8,128)(2,1)S(1)}, bf16[222,256]{1,0:T(8,128)(2,1)S(1)}, u32[]{:S(2)}, u32[]{:S(2)}) %collective-permute-start.5) | collective-permute-done | bytes 113696 | tf_op jit(solution)/shard_map/ppermute | solution.py:418
  36.1 1.3 %collective-permute-done.6.refs_6_ = bf16[256,896]{1,0:T(8,128)(2,1)S(1)} collective-permute-done((bf16[256,896]{1,0:T(8,128)(2,1)S(1)}, bf16[256,896]{1,0:T(8,128)(2,1)S(1)}, u32[]{:S(2)}, u32[]{:S(2)}) %collective-permute-start.6) | collective-permute-done | bytes 458784 | tf_op jit(solution)/shard_map/ppermute | solution.py:425
  37.4 0.7 collective-permute-done.8.refs_8_
  38.1 7.3 %shard_map.68.sources = bf16[3072,896]{1,0:T(8,128)(2,1)S(1)} custom-call(s32[3072]{0:T(1024)S(1)} %reshape.12.spots, bf16[256,896]{1,0:T(8,128)(2,1)S(1)} %shard_map.64.refs_0_, bf16[256,896]{1,0:T(8,128)(2,1)S(1)} %get-tuple-element.34.refs_1_, bf16[512,896]{1,0:T(8,128)(2,1)S(1)} %get-tuple-element.33.other.refs_2_, ...), custom_call_target="tpu_custom_call" | custom-call | tf_op jit(solution)/shard_map/pallas_call | solution.py:35
  45.4 3.1 %collective-permute-done.9.late = bf16[256,896]{1,0:T(8,128)(2,1)S(1)} collective-permute-done((bf16[256,896]{1,0:T(8,128)(2,1)S(1)}, bf16[256,896]{1,0:T(8,128)(2,1)S(1)}, u32[]{:S(2)}, u32[]{:S(2)}) %collective-permute-start.9) | collective-permute-done | bytes 458784 | tf_op jit(solution)/shard_map/ppermute | solution.py:424
  49.0 1.3 %collective-permute-done.10.late_o = bf16[256,896]{1,0:T(8,128)(2,1)S(1)} collective-permute-done((bf16[256,896]{1,0:T(8,128)(2,1)S(1)}, bf16[256,896]{1,0:T(8,128)(2,1)S(1)}, u32[]{:S(2)}, u32[]{:S(2)}) %collective-permute-start.10) | collective-permute-done | bytes 458784 | tf_op jit(solution)/shard_map/ppermute | solution.py:429
  50.4 6.2 %shard_map.69 = (bf16[2,222,512]{2,1,0:T(8,128)(2,1)S(1)}, f32[2,222,512]{2,1,0:T(8,128)S(1)}) custom-call(s32[4]{0:T(128)S(1)} %pad_add_fusion.sc, bf16[3,888,888]{2,1,0:T(8,128)(2,1)S(1)} %bitcast.14, bf16[3072,896]{1,0:T(8,128)(2,1)S(1)} %shard_map.68.sources, s32[3,1024]{1,0:T(4,128)S(1)} %get-tuple-element.55.lists, ...), custom_call_target="tpu_custom_call" | custom-call | tf_op jit(solution)/shard_map/pallas_call | solution.py:35
  57.2 1.5 %collective-permute-done.14.b_o = bf16[222,256]{1,0:T(8,128)(2,1)S(1)} collective-permute-done((bf16[222,256]{1,0:T(8,128)(2,1)S(1)}, bf16[222,256]{1,0:T(8,128)(2,1)S(1)}, u32[]{:S(2)}, u32[]{:S(2)}) %collective-permute-start.14) | collective-permute-done | bytes 113696 | tf_op jit(solution)/shard_map/ppermute | solution.py:430
  58.7 2.7 %shard_map.70 = (bf16[448,128]{1,0:T(8,128)(2,1)S(1)}, f32[448,128]{1,0:T(8,128)S(1)}) custom-call(s32[4]{0:T(128)S(1)} %pad_add_fusion.sc, s32[3,128]{1,0:T(4,128)S(1)} %copy-done.4, bf16[3,888,888]{2,1,0:T(8,128)(2,1)S(1)} %bitcast.14, bf16[222,256]{1,0:T(8,128)(2,1)S(1)} %shard_map.67.own, bf16[222,256]{1,0:T(8,128)(2,1)S(1)} %collective-permute-done.5.a, ...), custom_call_target="tpu_custom_call" | custom-call | tf_op jit(solution)/shard_map/pallas_call | solution.py:35
  61.6 1.2 %collective-permute-done.15.coarse_got = bf16[448,128]{1,0:T(8,128)(2,1)S(1)} collective-permute-done((bf16[448,128]{1,0:T(8,128)(2,1)S(1)}, bf16[448,128]{1,0:T(8,128)(2,1)S(1)}, u32[]{:S(2)}, u32[]{:S(2)}) %collective-permute-start.15) | collective-permute-done | bytes 114720 | tf_op jit(solution)/shard_map/ppermute | solution.py:441
  62.8 0.7 shard_map.71
  63.4 0.8 collective-permute-start.16
  64.2 6.2 %shard_map.72 = (bf16[2,222,512]{2,1,0:T(8,128)(2,1)S(1)}, f32[2,222,512]{2,1,0:T(8,128)S(1)}) custom-call(s32[4]{0:T(128)S(1)} %pad_add_fusion.sc, bf16[3,888,888]{2,1,0:T(8,128)(2,1)S(1)} %bitcast.14, bf16[3072,896]{1,0:T(8,128)(2,1)S(1)} %shard_map.68.sources, s32[3,1024]{1,0:T(4,128)S(1)} %get-tuple-element.55.lists, ...), custom_call_target="tpu_custom_call" | custom-call | tf_op jit(solution)/shard_map/pallas_call | solution.py:35
  70.5 3.4 %collective-permute-done.16.got.refs_1_ = bf16[336,512]{1,0:T(8,128)(2,1)S(1)} collective-permute-done((bf16[336,512]{1,0:T(8,128)(2,1)S(1)}, bf16[336,512]{1,0:T(8,128)(2,1)S(1)}, u32[]{:S(2)}, u32[]{:S(2)}) %collective-permute-start.16) | collective-permute-done | bytes 344096 | tf_op jit(solution)/shard_map/ppermute | solution.py:448
  73.9 1.8 %collective-permute-done.17.got = bf16[2,222,512]{2,1,0:T(8,128)(2,1)S(1)} collective-permute-done((bf16[2,222,512]{2,1,0:T(8,128)(2,1)S(1)}, bf16[2,222,512]{2,1,0:T(8,128)(2,1)S(1)}, u32[]{:S(2)}, u32[]{:S(2)}) %collective-permute-start.17) | collective-permute-done | bytes 454688 | tf_op jit(solution)/shard_map/ppermute | solution.py:454
  75.7 0.7 shard_map.73
  76.3 0.7 collective-permute-start.19
  77.0 0.6 shard_map.74.mine
  77.7 1.3 %collective-permute-done.18.other = bf16[448,128]{1,0:T(8,128)(2,1)S(1)} collective-permute-done((bf16[448,128]{1,0:T(8,128)(2,1)S(1)}, bf16[448,128]{1,0:T(8,128)(2,1)S(1)}, u32[]{:S(2)}, u32[]{:S(2)}) %collective-permute-start.18) | collective-permute-done | bytes 114720 | tf_op jit(solution)/shard_map/ppermute | solution.py:458
  79.0 2.9 %shard_map.75.spread = f32[222,1024]{1,0:T(8,128)S(1)} custom-call(s32[4]{0:T(128)S(1)} %pad_add_fusion.sc, bf16[1776,888]{1,0:T(8,128)(2,1)S(1)} %bitcast.16, bf16[448,128]{1,0:T(8,128)(2,1)S(1)} %shard_map.74.mine, bf16[448,128]{1,0:T(8,128)(2,1)S(1)} %collective-permute-done.18.other), custom_call_target="tpu_custom_call" | custom-call | tf_op jit(solution)/shard_map/pallas_call | solution.py:35
  82.0 2.1 %collective-permute-done.19.refs_3_ = bf16[222,512]{1,0:T(8,128)(2,1)S(1)} collective-permute-done((bf16[222,512]{1,0:T(8,128)(2,1)S(1)}, bf16[222,512]{1,0:T(8,128)(2,1)S(1)}, u32[]{:S(2)}, u32[]{:S(2)}) %collective-permute-start.19) | collective-permute-done | bytes 227360 | tf_op jit(solution)/shard_map/ppermute | solution.py:456
  84.1 1.5 %shard_map.76 = bf16[222,1024]{1,0:T(8,128)(2,1)} custom-call(s32[4]{0:T(128)S(1)} %pad_add_fusion.sc, f32[222,1024]{1,0:T(8,128)S(1)} %shard_map.75.spread, f32[222,512]{1,0:T(8,128)S(1)} %get-tuple-element.53.refs_0_, bf16[336,512]{1,0:T(8,128)(2,1)S(1)} %collective-permute-done.16.got.refs_1_, f32[222,512]{1,0:T(8,128)S(1)} %get-tuple-element.54.refs_2_, ...), custom_call_target="tpu_custom_call" | custom-call | tf_op jit(solution)/shard_map/pallas_call | solution.py:35
  (40 shorter events, 3.4 us)
Async XLA Ops:
  0.0 1.5 %copy-start = (bf16[888,1024]{1,0:T(8,128)(2,1)S(1)}, bf16[888,1024]{1,0:T(8,128)(2,1)}, u32[]{:S(2)}) copy-start(bf16[888,1024]{1,0:T(8,128)(2,1)} %x_ref.3) | copy-start | bytes 5455876
  1.5 9.5 %copy-start.1 = (bf16[888,1024]{1,0:T(8,128)(2,1)S(1)}, bf16[888,1024]{1,0:T(8,128)(2,1)}, u32[]{:S(2)}) copy-start(bf16[888,1024]{1,0:T(8,128)(2,1)} %x_ref.3) | copy-start | bytes 5455876
  1.7 19.9 %collective-permute-start = (bf16[256,896]{1,0:T(8,128)(2,1)S(1)}, bf16[256,896]{1,0:T(8,128)(2,1)S(1)}, u32[]{:S(2)}, u32[]{:S(2)}) collective-permute-start(bf16[256,896]{1,0:T(8,128)(2,1)S(1)} %shard_map.64.refs_0_), channel_id=1, source_target_pairs={{2,4},{3,5},{6,8},{7,9},{10,12},{11,13},{14,16},{15,17},{18,20},{1... | collective-permute-start | bytes 1376264 | tf_op jit(solution)/shard_map/ppermute | solution.py:421
  12.0 1.9 %copy-start.2 = (bf16[8,222,888]{2,0,1:T(8,128)(2,1)S(1)}, bf16[8,222,888]{2,0,1:T(8,128)(2,1)}, u32[]{:S(2)}) copy-start(bf16[8,222,888]{2,0,1:T(8,128)(2,1)} %param.7) | copy-start | bytes 9462532
  16.7 4.3 %collective-permute-start.2 = (bf16[222,128]{1,0:T(8,128)(2,1)S(1)}, bf16[222,128]{1,0:T(8,128)(2,1)S(1)}, u32[]{:S(2)}, u32[]{:S(2)}) collective-permute-start(bf16[222,128]{1,0:T(8,128)(2,1)S(1)} %shard_map.66.refs_0_), channel_id=1, source_target_pairs={{0,2},{1,3},{2,0},{3,1},{4,6},{5,7},{6,4},{7,5},{8,10},{9,11},{10,... | collective-permute-start | bytes 170504 | tf_op jit(solution)/shard_map/ppermute | solution.py:417
  16.8 17.5 %collective-permute-start.1 = (bf16[256,896]{1,0:T(8,128)(2,1)S(1)}, bf16[256,896]{1,0:T(8,128)(2,1)S(1)}, u32[]{:S(2)}, u32[]{:S(2)}) collective-permute-start(bf16[256,896]{1,0:T(8,128)(2,1)S(1)} %get-tuple-element.34.refs_1_), channel_id=1, source_target_pairs={{2,4},{3,5},{6,8},{7,9},{10,12},{11,13},{14,16},{15,17},{18,20},{1... | collective-permute-start | bytes 1376264 | tf_op jit(solution)/shard_map/ppermute | solution.py:421
  21.0 29.3 %slice-start = ((s8[4773888]{0:T(1024)(128)(4,1)}), s8[4194304]{0:T(1024)(128)(4,1)S(1)}, s32[]{:S(2)}) async-start(s8[4773888]{0:T(1024)(128)(4,1)} %bitcast.13), calls=%async_computation | async-start | bytes 8388608
  21.6 28.8 %slice-start.1 = ((s8[4773888]{0:T(1024)(128)(4,1)}), s8[579584]{0:T(1024)(128)(4,1)S(1)}, s32[]{:S(2)}) async-start(s8[4773888]{0:T(1024)(128)(4,1)} %bitcast.13), calls=%async_computation.1 | async-start | bytes 1159168
  21.6 14.0 %collective-permute-start.7 = (bf16[256,896]{1,0:T(8,128)(2,1)S(1)}, bf16[256,896]{1,0:T(8,128)(2,1)S(1)}, u32[]{:S(2)}, u32[]{:S(2)}) collective-permute-start(bf16[256,896]{1,0:T(8,128)(2,1)S(1)} %collective-permute-done.refs_3_), channel_id=1, source_target_pairs={{0,2},{1,3},{2,0},{3,1},{4,6},{5,7},{6,4},{7,5},{8,10},{9,11},{10,... | collective-permute-start | bytes 1376264 | tf_op jit(solution)/shard_map/ppermute | solution.py:424
  21.7 6.2 %collective-permute-start.4 = (bf16[222,256]{1,0:T(8,128)(2,1)S(1)}, bf16[222,256]{1,0:T(8,128)(2,1)S(1)}, u32[]{:S(2)}, u32[]{:S(2)}) collective-permute-start(bf16[222,256]{1,0:T(8,128)(2,1)S(1)} %shard_map.67.own), channel_id=1, source_target_pairs={{0,1},{1,0},{2,3},{3,2},{4,5},{5,4},{6,7},{7,6},{8,9},{9,8},{10,11... | collective-permute-start | bytes 341000 | tf_op jit(solution)/shard_map/ppermute | solution.py:419
  21.8 13.8 %collective-permute-start.5 = (bf16[222,256]{1,0:T(8,128)(2,1)S(1)}, bf16[222,256]{1,0:T(8,128)(2,1)S(1)}, u32[]{:S(2)}, u32[]{:S(2)}) collective-permute-start(bf16[222,256]{1,0:T(8,128)(2,1)S(1)} %shard_map.67.own), channel_id=1, source_target_pairs={{2,4},{3,5},{6,8},{7,9},{10,12},{11,13},{14,16},{15,17},{18,20},{1... | collective-permute-start | bytes 341000 | tf_op jit(solution)/shard_map/ppermute | solution.py:418
  27.7 9.8 %collective-permute-start.3 = (bf16[256,896]{1,0:T(8,128)(2,1)S(1)}, bf16[256,896]{1,0:T(8,128)(2,1)S(1)}, u32[]{:S(2)}, u32[]{:S(2)}) collective-permute-start(bf16[256,896]{1,0:T(8,128)(2,1)S(1)} %collective-permute-done.refs_3_), channel_id=1, source_target_pairs={{0,1},{1,0},{2,3},{3,2},{4,5},{5,4},{6,7},{7,6},{8,9},{9,8},{10,11... | collective-permute-start | bytes 1376264 | tf_op jit(solution)/shard_map/ppermute | solution.py:425
  35.6 1.8 %collective-permute-start.6 = (bf16[256,896]{1,0:T(8,128)(2,1)S(1)}, bf16[256,896]{1,0:T(8,128)(2,1)S(1)}, u32[]{:S(2)}, u32[]{:S(2)}) collective-permute-start(bf16[256,896]{1,0:T(8,128)(2,1)S(1)} %collective-permute-done.1.refs_4_), channel_id=1, source_target_pairs={{0,1},{1,0},{2,3},{3,2},{4,5},{5,4},{6,7},{7,6},{8,9},{9,8},{10,11... | collective-permute-start | bytes 1376264 | tf_op jit(solution)/shard_map/ppermute | solution.py:425
  35.6 2.5 %collective-permute-start.8 = (bf16[256,896]{1,0:T(8,128)(2,1)S(1)}, bf16[256,896]{1,0:T(8,128)(2,1)S(1)}, u32[]{:S(2)}, u32[]{:S(2)}) collective-permute-start(bf16[256,896]{1,0:T(8,128)(2,1)S(1)} %collective-permute-done.7.refs_7_), channel_id=1, source_target_pairs={{0,1},{1,0},{2,3},{3,2},{4,5},{5,4},{6,7},{7,6},{8,9},{9,8},{10,11... | collective-permute-start | bytes 1376264 | tf_op jit(solution)/shard_map/ppermute | solution.py:427
  36.1 12.4 %collective-permute-start.9 = (bf16[256,896]{1,0:T(8,128)(2,1)S(1)}, bf16[256,896]{1,0:T(8,128)(2,1)S(1)}, u32[]{:S(2)}, u32[]{:S(2)}) collective-permute-start(bf16[256,896]{1,0:T(8,128)(2,1)S(1)} %collective-permute-done.1.refs_4_), channel_id=1, source_target_pairs={{0,2},{1,3},{2,0},{3,1},{4,6},{5,7},{6,4},{7,5},{8,10},{9,11},{10,... | collective-permute-start | bytes 1376264 | tf_op jit(solution)/shard_map/ppermute | solution.py:424
  45.4 13.3 %copy-start.4 = (s32[3,128]{1,0:T(4,128)S(1)}, s32[3,128]{1,0:T(4,128)}, u32[]{:S(2)}) copy-start(s32[3,128]{1,0:T(4,128)} %lists.1) | copy-start | bytes 4612
  48.5 1.8 %collective-permute-start.10 = (bf16[256,896]{1,0:T(8,128)(2,1)S(1)}, bf16[256,896]{1,0:T(8,128)(2,1)S(1)}, u32[]{:S(2)}, u32[]{:S(2)}) collective-permute-start(bf16[256,896]{1,0:T(8,128)(2,1)S(1)} %collective-permute-done.9.late), channel_id=1, source_target_pairs={{0,1},{1,0},{2,3},{3,2},{4,5},{5,4},{6,7},{7,6},{8,9},{9,8},{10,11... | collective-permute-start | bytes 1376264 | tf_op jit(solution)/shard_map/ppermute | solution.py:429
  48.5 8.1 %collective-permute-start.11 = (bf16[222,256]{1,0:T(8,128)(2,1)S(1)}, bf16[222,256]{1,0:T(8,128)(2,1)S(1)}, u32[]{:S(2)}, u32[]{:S(2)}) collective-permute-start(bf16[222,256]{1,0:T(8,128)(2,1)S(1)} %collective-permute-done.5.a), channel_id=1, source_target_pairs={{0,2},{1,3},{2,0},{3,1},{4,6},{5,7},{6,4},{7,5},{8,10},{9,11},{10,... | collective-permute-start | bytes 341000 | tf_op jit(solution)/shard_map/ppermute | solution.py:426
  48.8 7.8 %collective-permute-start.12 = (bf16[222,256]{1,0:T(8,128)(2,1)S(1)}, bf16[222,256]{1,0:T(8,128)(2,1)S(1)}, u32[]{:S(2)}, u32[]{:S(2)}) collective-permute-start(bf16[222,256]{1,0:T(8,128)(2,1)S(1)} %collective-permute-done.5.a), channel_id=1, source_target_pairs={{0,1},{1,0},{2,3},{3,2},{4,5},{5,4},{6,7},{7,6},{8,9},{9,8},{10,11... | collective-permute-start | bytes 341000 | tf_op jit(solution)/shard_map/ppermute | solution.py:426
  56.6 6.2 %collective-permute-start.13 = (bf16[2,222,512]{2,1,0:T(8,128)(2,1)S(1)}, bf16[2,222,512]{2,1,0:T(8,128)(2,1)S(1)}, u32[]{:S(2)}, u32[]{:S(2)}) collective-permute-start(bf16[2,222,512]{2,1,0:T(8,128)(2,1)S(1)} %get-tuple-element.41), channel_id=1, source_target_pairs={{0,1},{1,0},{2,3},{3,2},{4,5},{5,4},{6,7},{7,6},{8,9},{9,8},{10,11... | collective-permute-start | bytes 1363976 | tf_op jit(solution)/shard_map/ppermute | solution.py:434
  56.8 1.8 %collective-permute-start.14 = (bf16[222,256]{1,0:T(8,128)(2,1)S(1)}, bf16[222,256]{1,0:T(8,128)(2,1)S(1)}, u32[]{:S(2)}, u32[]{:S(2)}) collective-permute-start(bf16[222,256]{1,0:T(8,128)(2,1)S(1)} %collective-permute-done.11.b), channel_id=1, source_target_pairs={{0,1},{1,0},{2,3},{3,2},{4,5},{5,4},{6,7},{7,6},{8,9},{9,8},{10,11... | collective-permute-start | bytes 341000 | tf_op jit(solution)/shard_map/ppermute | solution.py:430
  61.4 1.4 %collective-permute-start.15 = (bf16[448,128]{1,0:T(8,128)(2,1)S(1)}, bf16[448,128]{1,0:T(8,128)(2,1)S(1)}, u32[]{:S(2)}, u32[]{:S(2)}) collective-permute-start(bf16[448,128]{1,0:T(8,128)(2,1)S(1)} %get-tuple-element.44), channel_id=1, source_target_pairs={{0,1},{1,0},{2,3},{3,2},{4,5},{5,4},{6,7},{7,6},{8,9},{9,8},{10,11... | collective-permute-start | bytes 344072 | tf_op jit(solution)/shard_map/ppermute | solution.py:441
  63.4 10.4 %collective-permute-start.16 = (bf16[336,512]{1,0:T(8,128)(2,1)S(1)}, bf16[336,512]{1,0:T(8,128)(2,1)S(1)}, u32[]{:S(2)}, u32[]{:S(2)}) collective-permute-start(bf16[336,512]{1,0:T(8,128)(2,1)S(1)} %get-tuple-element.49), channel_id=1, source_target_pairs={{0,2},{1,3},{2,0},{3,1},{4,6},{5,7},{6,4},{7,5},{8,10},{9,11},{10,... | collective-permute-start | bytes 1032200 | tf_op jit(solution)/shard_map/ppermute | solution.py:448
  64.2 14.8 %copy-start.3 = (bf16[8,222,888]{2,0,1:T(8,128)(2,1)S(1)}, bf16[8,222,888]{2,0,1:T(8,128)(2,1)}, u32[]{:S(2)}) copy-start(bf16[8,222,888]{2,0,1:T(8,128)(2,1)} %param.9) | copy-start | bytes 9462532
  73.9 1.8 %collective-permute-start.17 = (bf16[2,222,512]{2,1,0:T(8,128)(2,1)S(1)}, bf16[2,222,512]{2,1,0:T(8,128)(2,1)S(1)}, u32[]{:S(2)}, u32[]{:S(2)}) collective-permute-start(bf16[2,222,512]{2,1,0:T(8,128)(2,1)S(1)} %get-tuple-element.50), channel_id=1, source_target_pairs={{0,1},{1,0},{2,3},{3,2},{4,5},{5,4},{6,7},{7,6},{8,9},{9,8},{10,11... | collective-permute-start | bytes 1363976 | tf_op jit(solution)/shard_map/ppermute | solution.py:454
  76.3 7.7 %collective-permute-start.19 = (bf16[222,512]{1,0:T(8,128)(2,1)S(1)}, bf16[222,512]{1,0:T(8,128)(2,1)S(1)}, u32[]{:S(2)}, u32[]{:S(2)}) collective-permute-start(bf16[222,512]{1,0:T(8,128)(2,1)S(1)} %get-tuple-element.51), channel_id=1, source_target_pairs={{0,2},{1,3},{2,0},{3,1},{4,6},{5,7},{6,4},{7,5},{8,10},{9,11},{10,... | collective-permute-start | bytes 681992 | tf_op jit(solution)/shard_map/ppermute | solution.py:456
  77.6 1.4 %collective-permute-start.18 = (bf16[448,128]{1,0:T(8,128)(2,1)S(1)}, bf16[448,128]{1,0:T(8,128)(2,1)S(1)}, u32[]{:S(2)}, u32[]{:S(2)}) collective-permute-start(bf16[448,128]{1,0:T(8,128)(2,1)S(1)} %shard_map.74.mine), channel_id=1, source_target_pairs={{0,1},{1,0},{2,3},{3,2},{4,5},{5,4},{6,7},{7,6},{8,9},{9,8},{10,11... | collective-permute-start | bytes 344072 | tf_op jit(solution)/shard_map/ppermute | solution.py:458

commit v10 on v6

--- a/solution.py
+++ b/solution.py
@@ -411,7 +411,7 @@
     cb, ca_o = zswap(ca), cswap(ca)
     b_o = [cswap(b[0])]
     picked = gathered(spots, [*mine, other, *a, *a_o, b[0], b_o[0]])
-    b_o.append(cswap(after(b[1], picked, cb)))
+    b_o.append(cswap(after(b[1], picked)))
     cb_o = cswap(cb)
 
     def summed(send, keep):

time: 85.1 us -> 86.8 us (1.020)
  waiting for transfers between devices: 23.2 us -> 27.2 us
  starting transfers between devices: 23.3 us -> 21 us
    ppermute x2, waiting for transfers between devices: 0.01 us -> 3.14 us  [local(): b = [zswap(early_a), zswap(second)]]
    ppermute x2, starting transfers between devices: 2.53 us -> 0.51 us  [local(): cb, ca_o = (zswap(ca), cswap(ca))]
    ppermute x1, waiting for transfers between devices: 1.3 us -> 0.01 us  [local(): b_o.append(cswap(after(b[1], picked)))]
    ppermute x2, waiting for transfers between devices: 0.01 us -> 1.3 us  [local(): a_o = [cswap(early_a), cswap(after(second, ca))]]
  transfers between devices with their start and end apart: 21 -> 21, of which waited for: 9 -> 12; matrix products, arithmetic and copies ran while one was open for 1% -> 1% of each run, Pallas kernels for 37% -> 36%
where the time goes in v10:
time: 86.8 us; the launch traced here: 86.6 us
  Pallas kernels  33.8 us (39%)
  waiting for transfers between devices  27.2 us (31%)
  starting transfers between devices  21 us (24%)
  local copies, waits for them, and re-layouts  3.43 us (4%)
  other arithmetic  0.92 us (1%)
    pallas_call x14, Pallas kernels, call(): pl.pallas_call(kernel, grid_spec=pltpu.PrefetchScalarGridSpec(num_scalar_...  33.8 us
    ppermute x2, starting transfers between devices, local(): a = [hop(m) for m in mine]  10.3 us
    ppermute x2, waiting for transfers between devices, local(): a = [hop(m) for m in mine]  6.47 us
    ppermute x1, starting transfers between devices, local(): ca = hop(own)  5.85 us
    ppermute x2, waiting for transfers between devices, local(): cb, ca_o = (zswap(ca), cswap(ca))  5.05 us
    unnamed x14, local copies, waits for them, and re-layouts  3.41 us
    ppermute x2, waiting for transfers between devices, local(): b = [zswap(early_a), zswap(second)]  3.14 us
    ppermute x2, waiting for transfers between devices, summed(): return (here, zswap(away), away)  2.43 us
  transfers between devices with their start and end apart: 21, of which 12 were waited for; matrix products, arithmetic and copies ran while one was open for 1% of the time, Pallas kernels for 36%

profile of v10, /device:TPU:24, one launch (start us, length us, event | category | flops | bytes accessed | tf_op | source)
XLA Modules:
  0.0 86.6 jit_solution(7834937811822751683)
XLA Ops:
  0.0 1.5 %copy-done = bf16[888,1024]{1,0:T(8,128)(2,1)S(1)} copy-done((bf16[888,1024]{1,0:T(8,128)(2,1)S(1)}, bf16[888,1024]{1,0:T(8,128)(2,1)}, u32[]{:S(2)}) %copy-start) | copy-done | bytes 1818648
  1.7 8.3 %collective-permute-start = (bf16[256,896]{1,0:T(8,128)(2,1)S(1)}, bf16[256,896]{1,0:T(8,128)(2,1)S(1)}, u32[]{:S(2)}, u32[]{:S(2)}) collective-permute-start(bf16[256,896]{1,0:T(8,128)(2,1)S(1)} %shard_map.64.refs_0_), channel_id=1, source_target_pairs={{2,4},{3,5},{6,8},{7,9},{10,12},{11,13},{14,16},{15,17},{18,20},{1... | collective-permute-start | bytes 1376264 | tf_op jit(solution)/shard_map/ppermute | solution.py:406
  10.0 0.8 fusion.6
  11.0 1.0 %shard_map.65 = (bf16[256,896]{1,0:T(8,128)(2,1)S(1)}, bf16[512,896]{1,0:T(8,128)(2,1)S(1)}) custom-call(s32[2]{0:T(128)S(1)} %pad_add_fusion.1.firsts, bf16[888,1024]{1,0:T(8,128)(2,1)S(1)} %copy-done.1), custom_call_target="tpu_custom_call" | custom-call | tf_op jit(solution)/shard_map/pallas_call | solution.py:34
  12.0 1.9 %copy-done.2 = bf16[8,222,888]{2,0,1:T(8,128)(2,1)S(1)} copy-done((bf16[8,222,888]{2,0,1:T(8,128)(2,1)S(1)}, bf16[8,222,888]{2,0,1:T(8,128)(2,1)}, u32[]{:S(2)}) %copy-start.2) | copy-done | bytes 3154200
  13.9 2.9 %shard_map.66.refs_0_ = bf16[222,128]{1,0:T(8,128)(2,1)S(1)} custom-call(s32[4]{0:T(128)S(1)} %pad_add_fusion.sc, bf16[1776,888]{1,0:T(8,128)(2,1)S(1)} %bitcast.15, bf16[512,896]{1,0:T(8,128)(2,1)S(1)} %get-tuple-element.35.other.refs_2_, bf16[256,896]{1,0:T(8,128)(2,1)S(1)} %shard_map.64.refs_0_, bf16[256,896]{1,0:T(8,128)(2,1)S(1)} %get-tuple-element.36.refs_1_), custom_call_target="tpu_custom_call" | custom-call | tf_op jit(solution)/shard_map/pallas_call | solution.py:34
  16.8 2.0 %collective-permute-start.1 = (bf16[256,896]{1,0:T(8,128)(2,1)S(1)}, bf16[256,896]{1,0:T(8,128)(2,1)S(1)}, u32[]{:S(2)}, u32[]{:S(2)}) collective-permute-start(bf16[256,896]{1,0:T(8,128)(2,1)S(1)} %get-tuple-element.36.refs_1_), channel_id=1, source_target_pairs={{2,4},{3,5},{6,8},{7,9},{10,12},{11,13},{14,16},{15,17},{18,20},{1... | collective-permute-start | bytes 1376264 | tf_op jit(solution)/shard_map/ppermute | solution.py:406
  18.8 2.2 %collective-permute-done.2.refs_1_ = bf16[222,128]{1,0:T(8,128)(2,1)S(1)} collective-permute-done((bf16[222,128]{1,0:T(8,128)(2,1)S(1)}, bf16[222,128]{1,0:T(8,128)(2,1)S(1)}, u32[]{:S(2)}, u32[]{:S(2)}) %collective-permute-start.2) | collective-permute-done | bytes 56864 | tf_op jit(solution)/shard_map/ppermute | solution.py:402
  21.0 0.6 shard_map.67.own
  21.8 5.9 %collective-permute-start.5 = (bf16[222,256]{1,0:T(8,128)(2,1)S(1)}, bf16[222,256]{1,0:T(8,128)(2,1)S(1)}, u32[]{:S(2)}, u32[]{:S(2)}) collective-permute-start(bf16[222,256]{1,0:T(8,128)(2,1)S(1)} %shard_map.67.own), channel_id=1, source_target_pairs={{2,4},{3,5},{6,8},{7,9},{10,12},{11,13},{14,16},{15,17},{18,20},{1... | collective-permute-start | bytes 341000 | tf_op jit(solution)/shard_map/ppermute | solution.py:403
  27.9 6.5 %collective-permute-done.1.refs_4_ = bf16[256,896]{1,0:T(8,128)(2,1)S(1)} collective-permute-done((bf16[256,896]{1,0:T(8,128)(2,1)S(1)}, bf16[256,896]{1,0:T(8,128)(2,1)S(1)}, u32[]{:S(2)}, u32[]{:S(2)}) %collective-permute-start.1) | collective-permute-done | bytes 458784 | tf_op jit(solution)/shard_map/ppermute | solution.py:406
  34.4 1.2 %collective-permute-done.5.a = bf16[222,256]{1,0:T(8,128)(2,1)S(1)} collective-permute-done((bf16[222,256]{1,0:T(8,128)(2,1)S(1)}, bf16[222,256]{1,0:T(8,128)(2,1)S(1)}, u32[]{:S(2)}, u32[]{:S(2)}) %collective-permute-start.5) | collective-permute-done | bytes 113696 | tf_op jit(solution)/shard_map/ppermute | solution.py:403
  36.1 1.3 %collective-permute-done.6.refs_6_ = bf16[256,896]{1,0:T(8,128)(2,1)S(1)} collective-permute-done((bf16[256,896]{1,0:T(8,128)(2,1)S(1)}, bf16[256,896]{1,0:T(8,128)(2,1)S(1)}, u32[]{:S(2)}, u32[]{:S(2)}) %collective-permute-start.6) | collective-permute-done | bytes 458784 | tf_op jit(solution)/shard_map/ppermute | solution.py:410
  37.4 0.7 collective-permute-done.8.refs_8_
  38.1 7.3 %shard_map.68.sources = bf16[3072,896]{1,0:T(8,128)(2,1)S(1)} custom-call(s32[3072]{0:T(1024)S(1)} %reshape.12.spots, bf16[256,896]{1,0:T(8,128)(2,1)S(1)} %shard_map.64.refs_0_, bf16[256,896]{1,0:T(8,128)(2,1)S(1)} %get-tuple-element.36.refs_1_, bf16[512,896]{1,0:T(8,128)(2,1)S(1)} %get-tuple-element.35.other.refs_2_, ...), custom_call_target="tpu_custom_call" | custom-call | tf_op jit(solution)/shard_map/pallas_call | solution.py:34
  45.4 3.1 %collective-permute-done.9.late = bf16[256,896]{1,0:T(8,128)(2,1)S(1)} collective-permute-done((bf16[256,896]{1,0:T(8,128)(2,1)S(1)}, bf16[256,896]{1,0:T(8,128)(2,1)S(1)}, u32[]{:S(2)}, u32[]{:S(2)}) %collective-permute-start.9) | collective-permute-done | bytes 458784 | tf_op jit(solution)/shard_map/ppermute | solution.py:409
  49.0 5.0 %collective-permute-done.11.b = bf16[222,256]{1,0:T(8,128)(2,1)S(1)} collective-permute-done((bf16[222,256]{1,0:T(8,128)(2,1)S(1)}, bf16[222,256]{1,0:T(8,128)(2,1)S(1)}, u32[]{:S(2)}, u32[]{:S(2)}) %collective-permute-start.11) | collective-permute-done | bytes 113696 | tf_op jit(solution)/shard_map/ppermute | solution.py:411
  54.1 6.2 %shard_map.69 = (bf16[2,222,512]{2,1,0:T(8,128)(2,1)S(1)}, f32[2,222,512]{2,1,0:T(8,128)S(1)}) custom-call(s32[4]{0:T(128)S(1)} %pad_add_fusion.sc, bf16[3,888,888]{2,1,0:T(8,128)(2,1)S(1)} %bitcast.14, bf16[3072,896]{1,0:T(8,128)(2,1)S(1)} %shard_map.68.sources, s32[3,1024]{1,0:T(4,128)S(1)} %get-tuple-element.59.lists, ...), custom_call_target="tpu_custom_call" | custom-call | tf_op jit(solution)/shard_map/pallas_call | solution.py:34
  60.4 0.6 collective-permute-start.14
  61.0 2.7 %shard_map.71 = (bf16[448,128]{1,0:T(8,128)(2,1)S(1)}, f32[448,128]{1,0:T(8,128)S(1)}) custom-call(s32[4]{0:T(128)S(1)} %pad_add_fusion.sc, s32[3,128]{1,0:T(4,128)S(1)} %copy-done.4, bf16[3,888,888]{2,1,0:T(8,128)(2,1)S(1)} %bitcast.14, bf16[222,256]{1,0:T(8,128)(2,1)S(1)} %shard_map.67.own, bf16[222,256]{1,0:T(8,128)(2,1)S(1)} %collective-permute-done.5.a, ...), custom_call_target="tpu_custom_call" | custom-call | tf_op jit(solution)/shard_map/pallas_call | solution.py:34
  63.8 0.6 shard_map.70
  65.1 0.6 shard_map.72
  65.6 1.8 %collective-permute-start.17 = (bf16[448,128]{1,0:T(8,128)(2,1)S(1)}, bf16[448,128]{1,0:T(8,128)(2,1)S(1)}, u32[]{:S(2)}, u32[]{:S(2)}) collective-permute-start(bf16[448,128]{1,0:T(8,128)(2,1)S(1)} %get-tuple-element.53), channel_id=1, source_target_pairs={{0,2},{1,3},{2,0},{3,1},{4,6},{5,7},{6,4},{7,5},{8,10},{9,11},{10,... | collective-permute-start | bytes 344072 | tf_op jit(solution)/shard_map/ppermute | solution.py:435
  67.4 6.2 %shard_map.73 = (bf16[2,222,512]{2,1,0:T(8,128)(2,1)S(1)}, f32[2,222,512]{2,1,0:T(8,128)S(1)}) custom-call(s32[4]{0:T(128)S(1)} %pad_add_fusion.sc, bf16[3,888,888]{2,1,0:T(8,128)(2,1)S(1)} %bitcast.14, bf16[3072,896]{1,0:T(8,128)(2,1)S(1)} %shard_map.68.sources, s32[3,1024]{1,0:T(4,128)S(1)} %get-tuple-element.59.lists, ...), custom_call_target="tpu_custom_call" | custom-call | tf_op jit(solution)/shard_map/pallas_call | solution.py:34
  73.6 1.3 %collective-permute-done.17.two = bf16[448,128]{1,0:T(8,128)(2,1)S(1)} collective-permute-done((bf16[448,128]{1,0:T(8,128)(2,1)S(1)}, bf16[448,128]{1,0:T(8,128)(2,1)S(1)}, u32[]{:S(2)}, u32[]{:S(2)}) %collective-permute-start.17) | collective-permute-done | bytes 114720 | tf_op jit(solution)/shard_map/ppermute | solution.py:435
  74.9 1.8 %collective-permute-done.18.got = bf16[2,222,512]{2,1,0:T(8,128)(2,1)S(1)} collective-permute-done((bf16[2,222,512]{2,1,0:T(8,128)(2,1)S(1)}, bf16[2,222,512]{2,1,0:T(8,128)(2,1)S(1)}, u32[]{:S(2)}, u32[]{:S(2)}) %collective-permute-start.18) | collective-permute-done | bytes 454688 | tf_op jit(solution)/shard_map/ppermute | solution.py:419
  76.8 0.7 shard_map.74
  77.8 0.6 shard_map.75.mine
  78.5 1.3 %collective-permute-done.19.other = bf16[448,128]{1,0:T(8,128)(2,1)S(1)} collective-permute-done((bf16[448,128]{1,0:T(8,128)(2,1)S(1)}, bf16[448,128]{1,0:T(8,128)(2,1)S(1)}, u32[]{:S(2)}, u32[]{:S(2)}) %collective-permute-start.19) | collective-permute-done | bytes 114720 | tf_op jit(solution)/shard_map/ppermute | solution.py:438
  79.8 2.9 %shard_map.76.spread = f32[222,1024]{1,0:T(8,128)S(1)} custom-call(s32[4]{0:T(128)S(1)} %pad_add_fusion.sc, bf16[1776,888]{1,0:T(8,128)(2,1)S(1)} %bitcast.16, bf16[448,128]{1,0:T(8,128)(2,1)S(1)} %shard_map.75.mine, bf16[448,128]{1,0:T(8,128)(2,1)S(1)} %collective-permute-done.19.other), custom_call_target="tpu_custom_call" | custom-call | tf_op jit(solution)/shard_map/pallas_call | solution.py:34
  82.7 2.4 %collective-permute-done.20.refs_3_ = bf16[222,512]{1,0:T(8,128)(2,1)S(1)} collective-permute-done((bf16[222,512]{1,0:T(8,128)(2,1)S(1)}, bf16[222,512]{1,0:T(8,128)(2,1)S(1)}, u32[]{:S(2)}, u32[]{:S(2)}) %collective-permute-start.20) | collective-permute-done | bytes 227360 | tf_op jit(solution)/shard_map/ppermute | solution.py:420
  85.1 1.4 %shard_map.77 = bf16[222,1024]{1,0:T(8,128)(2,1)} custom-call(s32[4]{0:T(128)S(1)} %pad_add_fusion.sc, f32[222,1024]{1,0:T(8,128)S(1)} %shard_map.76.spread, f32[222,512]{1,0:T(8,128)S(1)} %get-tuple-element.57.refs_0_, bf16[222,512]{1,0:T(8,128)(2,1)S(1)} %collective-permute-done.16.refs_1_, f32[222,512]{1,0:T(8,128)S(1)} %get-tuple-element.58.refs_2_, ...), custom_call_target="tpu_custom_call" | custom-call | tf_op jit(solution)/shard_map/pallas_call | solution.py:34
  (43 shorter events, 3.2 us)
Async XLA Ops:
  0.0 1.5 %copy-start = (bf16[888,1024]{1,0:T(8,128)(2,1)S(1)}, bf16[888,1024]{1,0:T(8,128)(2,1)}, u32[]{:S(2)}) copy-start(bf16[888,1024]{1,0:T(8,128)(2,1)} %x_ref.3) | copy-start | bytes 5455876
  1.5 9.5 %copy-start.1 = (bf16[888,1024]{1,0:T(8,128)(2,1)S(1)}, bf16[888,1024]{1,0:T(8,128)(2,1)}, u32[]{:S(2)}) copy-start(bf16[888,1024]{1,0:T(8,128)(2,1)} %x_ref.3) | copy-start | bytes 5455876
  1.7 19.9 %collective-permute-start = (bf16[256,896]{1,0:T(8,128)(2,1)S(1)}, bf16[256,896]{1,0:T(8,128)(2,1)S(1)}, u32[]{:S(2)}, u32[]{:S(2)}) collective-permute-start(bf16[256,896]{1,0:T(8,128)(2,1)S(1)} %shard_map.64.refs_0_), channel_id=1, source_target_pairs={{2,4},{3,5},{6,8},{7,9},{10,12},{11,13},{14,16},{15,17},{18,20},{1... | collective-permute-start | bytes 1376264 | tf_op jit(solution)/shard_map/ppermute | solution.py:406
  12.0 1.9 %copy-start.2 = (bf16[8,222,888]{2,0,1:T(8,128)(2,1)S(1)}, bf16[8,222,888]{2,0,1:T(8,128)(2,1)}, u32[]{:S(2)}) copy-start(bf16[8,222,888]{2,0,1:T(8,128)(2,1)} %param.7) | copy-start | bytes 9462532
  16.7 4.3 %collective-permute-start.2 = (bf16[222,128]{1,0:T(8,128)(2,1)S(1)}, bf16[222,128]{1,0:T(8,128)(2,1)S(1)}, u32[]{:S(2)}, u32[]{:S(2)}) collective-permute-start(bf16[222,128]{1,0:T(8,128)(2,1)S(1)} %shard_map.66.refs_0_), channel_id=1, source_target_pairs={{0,2},{1,3},{2,0},{3,1},{4,6},{5,7},{6,4},{7,5},{8,10},{9,11},{10,... | collective-permute-start | bytes 170504 | tf_op jit(solution)/shard_map/ppermute | solution.py:402
  16.8 17.5 %collective-permute-start.1 = (bf16[256,896]{1,0:T(8,128)(2,1)S(1)}, bf16[256,896]{1,0:T(8,128)(2,1)S(1)}, u32[]{:S(2)}, u32[]{:S(2)}) collective-permute-start(bf16[256,896]{1,0:T(8,128)(2,1)S(1)} %get-tuple-element.36.refs_1_), channel_id=1, source_target_pairs={{2,4},{3,5},{6,8},{7,9},{10,12},{11,13},{14,16},{15,17},{18,20},{1... | collective-permute-start | bytes 1376264 | tf_op jit(solution)/shard_map/ppermute | solution.py:406
  21.0 33.1 %slice-start = ((s8[4773888]{0:T(1024)(128)(4,1)}), s8[4194304]{0:T(1024)(128)(4,1)S(1)}, s32[]{:S(2)}) async-start(s8[4773888]{0:T(1024)(128)(4,1)} %bitcast.13), calls=%async_computation | async-start | bytes 8388608
  21.6 32.5 %slice-start.1 = ((s8[4773888]{0:T(1024)(128)(4,1)}), s8[579584]{0:T(1024)(128)(4,1)S(1)}, s32[]{:S(2)}) async-start(s8[4773888]{0:T(1024)(128)(4,1)} %bitcast.13), calls=%async_computation.1 | async-start | bytes 1159168
  21.6 14.0 %collective-permute-start.7 = (bf16[256,896]{1,0:T(8,128)(2,1)S(1)}, bf16[256,896]{1,0:T(8,128)(2,1)S(1)}, u32[]{:S(2)}, u32[]{:S(2)}) collective-permute-start(bf16[256,896]{1,0:T(8,128)(2,1)S(1)} %collective-permute-done.refs_3_), channel_id=1, source_target_pairs={{0,2},{1,3},{2,0},{3,1},{4,6},{5,7},{6,4},{7,5},{8,10},{9,11},{10,... | collective-permute-start | bytes 1376264 | tf_op jit(solution)/shard_map/ppermute | solution.py:409
  21.7 6.2 %collective-permute-start.4 = (bf16[222,256]{1,0:T(8,128)(2,1)S(1)}, bf16[222,256]{1,0:T(8,128)(2,1)S(1)}, u32[]{:S(2)}, u32[]{:S(2)}) collective-permute-start(bf16[222,256]{1,0:T(8,128)(2,1)S(1)} %shard_map.67.own), channel_id=1, source_target_pairs={{0,1},{1,0},{2,3},{3,2},{4,5},{5,4},{6,7},{7,6},{8,9},{9,8},{10,11... | collective-permute-start | bytes 341000 | tf_op jit(solution)/shard_map/ppermute | solution.py:404
  21.8 13.8 %collective-permute-start.5 = (bf16[222,256]{1,0:T(8,128)(2,1)S(1)}, bf16[222,256]{1,0:T(8,128)(2,1)S(1)}, u32[]{:S(2)}, u32[]{:S(2)}) collective-permute-start(bf16[222,256]{1,0:T(8,128)(2,1)S(1)} %shard_map.67.own), channel_id=1, source_target_pairs={{2,4},{3,5},{6,8},{7,9},{10,12},{11,13},{14,16},{15,17},{18,20},{1... | collective-permute-start | bytes 341000 | tf_op jit(solution)/shard_map/ppermute | solution.py:403
  27.7 9.8 %collective-permute-start.3 = (bf16[256,896]{1,0:T(8,128)(2,1)S(1)}, bf16[256,896]{1,0:T(8,128)(2,1)S(1)}, u32[]{:S(2)}, u32[]{:S(2)}) collective-permute-start(bf16[256,896]{1,0:T(8,128)(2,1)S(1)} %collective-permute-done.refs_3_), channel_id=1, source_target_pairs={{0,1},{1,0},{2,3},{3,2},{4,5},{5,4},{6,7},{7,6},{8,9},{9,8},{10,11... | collective-permute-start | bytes 1376264 | tf_op jit(solution)/shard_map/ppermute | solution.py:410
  35.6 1.8 %collective-permute-start.6 = (bf16[256,896]{1,0:T(8,128)(2,1)S(1)}, bf16[256,896]{1,0:T(8,128)(2,1)S(1)}, u32[]{:S(2)}, u32[]{:S(2)}) collective-permute-start(bf16[256,896]{1,0:T(8,128)(2,1)S(1)} %collective-permute-done.1.refs_4_), channel_id=1, source_target_pairs={{0,1},{1,0},{2,3},{3,2},{4,5},{5,4},{6,7},{7,6},{8,9},{9,8},{10,11... | collective-permute-start | bytes 1376264 | tf_op jit(solution)/shard_map/ppermute | solution.py:410
  35.6 2.5 %collective-permute-start.8 = (bf16[256,896]{1,0:T(8,128)(2,1)S(1)}, bf16[256,896]{1,0:T(8,128)(2,1)S(1)}, u32[]{:S(2)}, u32[]{:S(2)}) collective-permute-start(bf16[256,896]{1,0:T(8,128)(2,1)S(1)} %collective-permute-done.7.refs_7_), channel_id=1, source_target_pairs={{0,1},{1,0},{2,3},{3,2},{4,5},{5,4},{6,7},{7,6},{8,9},{9,8},{10,11... | collective-permute-start | bytes 1376264 | tf_op jit(solution)/shard_map/ppermute | solution.py:412
  36.1 12.4 %collective-permute-start.9 = (bf16[256,896]{1,0:T(8,128)(2,1)S(1)}, bf16[256,896]{1,0:T(8,128)(2,1)S(1)}, u32[]{:S(2)}, u32[]{:S(2)}) collective-permute-start(bf16[256,896]{1,0:T(8,128)(2,1)S(1)} %collective-permute-done.1.refs_4_), channel_id=1, source_target_pairs={{0,2},{1,3},{2,0},{3,1},{4,6},{5,7},{6,4},{7,5},{8,10},{9,11},{10,... | collective-permute-start | bytes 1376264 | tf_op jit(solution)/shard_map/ppermute | solution.py:409
  45.4 15.6 %copy-start.4 = (s32[3,128]{1,0:T(4,128)S(1)}, s32[3,128]{1,0:T(4,128)}, u32[]{:S(2)}) copy-start(s32[3,128]{1,0:T(4,128)} %lists.1) | copy-start | bytes 4612
  48.5 5.6 %collective-permute-start.10 = (bf16[256,896]{1,0:T(8,128)(2,1)S(1)}, bf16[256,896]{1,0:T(8,128)(2,1)S(1)}, u32[]{:S(2)}, u32[]{:S(2)}) collective-permute-start(bf16[256,896]{1,0:T(8,128)(2,1)S(1)} %collective-permute-done.9.late), channel_id=1, source_target_pairs={{0,1},{1,0},{2,3},{3,2},{4,5},{5,4},{6,7},{7,6},{8,9},{9,8},{10,11... | collective-permute-start | bytes 1376264 | tf_op jit(solution)/shard_map/ppermute | solution.py:414
  48.5 5.6 %collective-permute-start.11 = (bf16[222,256]{1,0:T(8,128)(2,1)S(1)}, bf16[222,256]{1,0:T(8,128)(2,1)S(1)}, u32[]{:S(2)}, u32[]{:S(2)}) collective-permute-start(bf16[222,256]{1,0:T(8,128)(2,1)S(1)} %collective-permute-done.5.a), channel_id=1, source_target_pairs={{0,2},{1,3},{2,0},{3,1},{4,6},{5,7},{6,4},{7,5},{8,10},{9,11},{10,... | collective-permute-start | bytes 341000 | tf_op jit(solution)/shard_map/ppermute | solution.py:411
  48.8 11.5 %collective-permute-start.13 = (bf16[222,256]{1,0:T(8,128)(2,1)S(1)}, bf16[222,256]{1,0:T(8,128)(2,1)S(1)}, u32[]{:S(2)}, u32[]{:S(2)}) collective-permute-start(bf16[222,256]{1,0:T(8,128)(2,1)S(1)} %collective-permute-done.5.a), channel_id=1, source_target_pairs={{0,1},{1,0},{2,3},{3,2},{4,5},{5,4},{6,7},{7,6},{8,9},{9,8},{10,11... | collective-permute-start | bytes 341000 | tf_op jit(solution)/shard_map/ppermute | solution.py:411
  54.1 6.3 %collective-permute-start.12 = (bf16[222,256]{1,0:T(8,128)(2,1)S(1)}, bf16[222,256]{1,0:T(8,128)(2,1)S(1)}, u32[]{:S(2)}, u32[]{:S(2)}) collective-permute-start(bf16[222,256]{1,0:T(8,128)(2,1)S(1)} %collective-permute-done.11.b), channel_id=1, source_target_pairs={{0,1},{1,0},{2,3},{3,2},{4,5},{5,4},{6,7},{7,6},{8,9},{9,8},{10,11... | collective-permute-start | bytes 341000 | tf_op jit(solution)/shard_map/ppermute | solution.py:415
  60.4 3.4 %collective-permute-start.14 = (bf16[2,222,512]{2,1,0:T(8,128)(2,1)S(1)}, bf16[2,222,512]{2,1,0:T(8,128)(2,1)S(1)}, u32[]{:S(2)}, u32[]{:S(2)}) collective-permute-start(bf16[2,222,512]{2,1,0:T(8,128)(2,1)S(1)} %get-tuple-element.43), channel_id=1, source_target_pairs={{0,1},{1,0},{2,3},{3,2},{4,5},{5,4},{6,7},{7,6},{8,9},{9,8},{10,11... | collective-permute-start | bytes 1363976 | tf_op jit(solution)/shard_map/ppermute | solution.py:419
  63.7 1.4 %collective-permute-start.15 = (bf16[448,128]{1,0:T(8,128)(2,1)S(1)}, bf16[448,128]{1,0:T(8,128)(2,1)S(1)}, u32[]{:S(2)}, u32[]{:S(2)}) collective-permute-start(bf16[448,128]{1,0:T(8,128)(2,1)S(1)} %get-tuple-element.48), channel_id=1, source_target_pairs={{0,1},{1,0},{2,3},{3,2},{4,5},{5,4},{6,7},{7,6},{8,9},{9,8},{10,11... | collective-permute-start | bytes 344072 | tf_op jit(solution)/shard_map/ppermute | solution.py:430
  64.4 10.5 %collective-permute-start.16 = (bf16[222,512]{1,0:T(8,128)(2,1)S(1)}, bf16[222,512]{1,0:T(8,128)(2,1)S(1)}, u32[]{:S(2)}, u32[]{:S(2)}) collective-permute-start(bf16[222,512]{1,0:T(8,128)(2,1)S(1)} %get-tuple-element.44), channel_id=1, source_target_pairs={{0,2},{1,3},{2,0},{3,1},{4,6},{5,7},{6,4},{7,5},{8,10},{9,11},{10,... | collective-permute-start | bytes 681992 | tf_op jit(solution)/shard_map/ppermute | solution.py:420
  65.6 9.3 %collective-permute-start.17 = (bf16[448,128]{1,0:T(8,128)(2,1)S(1)}, bf16[448,128]{1,0:T(8,128)(2,1)S(1)}, u32[]{:S(2)}, u32[]{:S(2)}) collective-permute-start(bf16[448,128]{1,0:T(8,128)(2,1)S(1)} %get-tuple-element.53), channel_id=1, source_target_pairs={{0,2},{1,3},{2,0},{3,1},{4,6},{5,7},{6,4},{7,5},{8,10},{9,11},{10,... | collective-permute-start | bytes 344072 | tf_op jit(solution)/shard_map/ppermute | solution.py:435
  67.4 12.4 %copy-start.3 = (bf16[8,222,888]{2,0,1:T(8,128)(2,1)S(1)}, bf16[8,222,888]{2,0,1:T(8,128)(2,1)}, u32[]{:S(2)}) copy-start(bf16[8,222,888]{2,0,1:T(8,128)(2,1)} %param.9) | copy-start | bytes 9462532
  74.9 1.8 %collective-permute-start.18 = (bf16[2,222,512]{2,1,0:T(8,128)(2,1)S(1)}, bf16[2,222,512]{2,1,0:T(8,128)(2,1)S(1)}, u32[]{:S(2)}, u32[]{:S(2)}) collective-permute-start(bf16[2,222,512]{2,1,0:T(8,128)(2,1)S(1)} %get-tuple-element.54), channel_id=1, source_target_pairs={{0,1},{1,0},{2,3},{3,2},{4,5},{5,4},{6,7},{7,6},{8,9},{9,8},{10,11... | collective-permute-start | bytes 1363976 | tf_op jit(solution)/shard_map/ppermute | solution.py:419
  77.4 7.7 %collective-permute-start.20 = (bf16[222,512]{1,0:T(8,128)(2,1)S(1)}, bf16[222,512]{1,0:T(8,128)(2,1)S(1)}, u32[]{:S(2)}, u32[]{:S(2)}) collective-permute-start(bf16[222,512]{1,0:T(8,128)(2,1)S(1)} %get-tuple-element.55), channel_id=1, source_target_pairs={{0,2},{1,3},{2,0},{3,1},{4,6},{5,7},{6,4},{7,5},{8,10},{9,11},{10,... | collective-permute-start | bytes 681992 | tf_op jit(solution)/shard_map/ppermute | solution.py:420
  78.4 1.4 %collective-permute-start.19 = (bf16[448,128]{1,0:T(8,128)(2,1)S(1)}, bf16[448,128]{1,0:T(8,128)(2,1)S(1)}, u32[]{:S(2)}, u32[]{:S(2)}) collective-permute-start(bf16[448,128]{1,0:T(8,128)(2,1)S(1)} %shard_map.75.mine), channel_id=1, source_target_pairs={{0,1},{1,0},{2,3},{3,2},{4,5},{5,4},{6,7},{7,6},{8,9},{9,8},{10,11... | collective-permute-start | bytes 344072 | tf_op jit(solution)/shard_map/ppermute | solution.py:438

commit v11 on v6

--- a/solution.py
+++ b/solution.py
@@ -17,7 +17,7 @@
 chunks = 2
 chunk = half // chunks
 early = 6 * half - 2 * chunk
-ahead = 512
+ahead = 640
 
 
 def one_hop(groups):

time: 85.1 us -> 86.2 us (1.013)
    ppermute x2, waiting for transfers between devices: 1.82 us -> 3.46 us  [summed(): cswap(send)]
    ppermute x1, waiting for transfers between devices: 0.01 us -> 1.31 us  [local(): cswap(send)]
    ppermute x2, waiting for transfers between devices: 2.43 us -> 1.2 us  [summed(): return (here, zswap(away), away)]
    ppermute x1, waiting for transfers between devices: 0.96 us -> 0.01 us  [local(): part_got = zswap(part_sent)]
  transfers between devices with their start and end apart: 21 -> 21, of which waited for: 9 -> 10; matrix products, arithmetic and copies ran while one was open for 1% -> 1% of each run, Pallas kernels for 37% -> 36%
where the time goes in v11:
time: 86.2 us; the launch traced here: 86 us
  Pallas kernels  33.9 us (39%)
  waiting for transfers between devices  24 us (28%)
  starting transfers between devices  23 us (27%)
  local copies, waits for them, and re-layouts  3.93 us (5%)
  other arithmetic  0.92 us (1%)
    pallas_call x14, Pallas kernels, call(): pl.pallas_call(kernel, grid_spec=pltpu.PrefetchScalarGridSpec(num_scalar_...  33.9 us
    ppermute x2, starting transfers between devices, local(): a = [hop(m) for m in mine]  10.3 us
    ppermute x2, waiting for transfers between devices, local(): a = [hop(m) for m in mine]  6.47 us
    ppermute x1, starting transfers between devices, local(): ca = hop(own)  5.85 us
    ppermute x2, waiting for transfers between devices, local(): cb, ca_o = (zswap(ca), cswap(ca))  5.53 us
    ppermute x2, waiting for transfers between devices, summed(): cswap(send)  3.46 us
    unnamed x14, local copies, waits for them, and re-layouts  3.41 us
    ppermute x2, starting transfers between devices, local(): cb, ca_o = (zswap(ca), cswap(ca))  2.53 us
  transfers between devices with their start and end apart: 21, of which 10 were waited for; matrix products, arithmetic and copies ran while one was open for 1% of the time, Pallas kernels for 36%

profile of v11, /device:TPU:24, one launch (start us, length us, event | category | flops | bytes accessed | tf_op | source)
XLA Modules:
  0.0 86.0 jit_solution(399547035834934195)
XLA Ops:
  0.0 1.5 %copy-done = bf16[888,1024]{1,0:T(8,128)(2,1)S(1)} copy-done((bf16[888,1024]{1,0:T(8,128)(2,1)S(1)}, bf16[888,1024]{1,0:T(8,128)(2,1)}, u32[]{:S(2)}) %copy-start) | copy-done | bytes 1818648
  1.7 8.3 %collective-permute-start = (bf16[256,896]{1,0:T(8,128)(2,1)S(1)}, bf16[256,896]{1,0:T(8,128)(2,1)S(1)}, u32[]{:S(2)}, u32[]{:S(2)}) collective-permute-start(bf16[256,896]{1,0:T(8,128)(2,1)S(1)} %shard_map.64.refs_0_), channel_id=1, source_target_pairs={{2,4},{3,5},{6,8},{7,9},{10,12},{11,13},{14,16},{15,17},{18,20},{1... | collective-permute-start | bytes 1376264 | tf_op jit(solution)/shard_map/ppermute | solution.py:406
  10.0 0.8 fusion.6
  11.0 1.0 %shard_map.65 = (bf16[256,896]{1,0:T(8,128)(2,1)S(1)}, bf16[512,896]{1,0:T(8,128)(2,1)S(1)}) custom-call(s32[2]{0:T(128)S(1)} %pad_add_fusion.1.firsts, bf16[888,1024]{1,0:T(8,128)(2,1)S(1)} %copy-done.1), custom_call_target="tpu_custom_call" | custom-call | tf_op jit(solution)/shard_map/pallas_call | solution.py:34
  12.0 1.9 %copy-done.2 = bf16[8,222,888]{2,0,1:T(8,128)(2,1)S(1)} copy-done((bf16[8,222,888]{2,0,1:T(8,128)(2,1)S(1)}, bf16[8,222,888]{2,0,1:T(8,128)(2,1)}, u32[]{:S(2)}) %copy-start.2) | copy-done | bytes 3154200
  13.9 2.9 %shard_map.66.refs_0_ = bf16[222,128]{1,0:T(8,128)(2,1)S(1)} custom-call(s32[4]{0:T(128)S(1)} %pad_add_fusion.sc, bf16[1776,888]{1,0:T(8,128)(2,1)S(1)} %bitcast.15, bf16[512,896]{1,0:T(8,128)(2,1)S(1)} %get-tuple-element.35.other.refs_2_, bf16[256,896]{1,0:T(8,128)(2,1)S(1)} %shard_map.64.refs_0_, bf16[256,896]{1,0:T(8,128)(2,1)S(1)} %get-tuple-element.36.refs_1_), custom_call_target="tpu_custom_call" | custom-call | tf_op jit(solution)/shard_map/pallas_call | solution.py:34
  16.8 2.0 %collective-permute-start.1 = (bf16[256,896]{1,0:T(8,128)(2,1)S(1)}, bf16[256,896]{1,0:T(8,128)(2,1)S(1)}, u32[]{:S(2)}, u32[]{:S(2)}) collective-permute-start(bf16[256,896]{1,0:T(8,128)(2,1)S(1)} %get-tuple-element.36.refs_1_), channel_id=1, source_target_pairs={{2,4},{3,5},{6,8},{7,9},{10,12},{11,13},{14,16},{15,17},{18,20},{1... | collective-permute-start | bytes 1376264 | tf_op jit(solution)/shard_map/ppermute | solution.py:406
  18.8 2.2 %collective-permute-done.2.refs_1_ = bf16[222,128]{1,0:T(8,128)(2,1)S(1)} collective-permute-done((bf16[222,128]{1,0:T(8,128)(2,1)S(1)}, bf16[222,128]{1,0:T(8,128)(2,1)S(1)}, u32[]{:S(2)}, u32[]{:S(2)}) %collective-permute-start.2) | collective-permute-done | bytes 56864 | tf_op jit(solution)/shard_map/ppermute | solution.py:402
  21.0 0.6 shard_map.67.own
  21.8 5.9 %collective-permute-start.5 = (bf16[222,256]{1,0:T(8,128)(2,1)S(1)}, bf16[222,256]{1,0:T(8,128)(2,1)S(1)}, u32[]{:S(2)}, u32[]{:S(2)}) collective-permute-start(bf16[222,256]{1,0:T(8,128)(2,1)S(1)} %shard_map.67.own), channel_id=1, source_target_pairs={{2,4},{3,5},{6,8},{7,9},{10,12},{11,13},{14,16},{15,17},{18,20},{1... | collective-permute-start | bytes 341000 | tf_op jit(solution)/shard_map/ppermute | solution.py:403
  27.9 6.5 %collective-permute-done.1.refs_4_ = bf16[256,896]{1,0:T(8,128)(2,1)S(1)} collective-permute-done((bf16[256,896]{1,0:T(8,128)(2,1)S(1)}, bf16[256,896]{1,0:T(8,128)(2,1)S(1)}, u32[]{:S(2)}, u32[]{:S(2)}) %collective-permute-start.1) | collective-permute-done | bytes 458784 | tf_op jit(solution)/shard_map/ppermute | solution.py:406
  34.4 1.2 %collective-permute-done.5.a = bf16[222,256]{1,0:T(8,128)(2,1)S(1)} collective-permute-done((bf16[222,256]{1,0:T(8,128)(2,1)S(1)}, bf16[222,256]{1,0:T(8,128)(2,1)S(1)}, u32[]{:S(2)}, u32[]{:S(2)}) %collective-permute-start.5) | collective-permute-done | bytes 113696 | tf_op jit(solution)/shard_map/ppermute | solution.py:403
  36.1 2.0 %collective-permute-start.10 = (bf16[222,256]{1,0:T(8,128)(2,1)S(1)}, bf16[222,256]{1,0:T(8,128)(2,1)S(1)}, u32[]{:S(2)}, u32[]{:S(2)}) collective-permute-start(bf16[222,256]{1,0:T(8,128)(2,1)S(1)} %collective-permute-done.5.a), channel_id=1, source_target_pairs={{0,2},{1,3},{2,0},{3,1},{4,6},{5,7},{6,4},{7,5},{8,10},{9,11},{10,... | collective-permute-start | bytes 341000 | tf_op jit(solution)/shard_map/ppermute | solution.py:411
  38.1 7.3 %shard_map.68.sources = bf16[3072,896]{1,0:T(8,128)(2,1)S(1)} custom-call(s32[3072]{0:T(1024)S(1)} %reshape.12.spots, bf16[256,896]{1,0:T(8,128)(2,1)S(1)} %shard_map.64.refs_0_, bf16[256,896]{1,0:T(8,128)(2,1)S(1)} %get-tuple-element.36.refs_1_, bf16[512,896]{1,0:T(8,128)(2,1)S(1)} %get-tuple-element.35.other.refs_2_, ...), custom_call_target="tpu_custom_call" | custom-call | tf_op jit(solution)/shard_map/pallas_call | solution.py:34
  45.5 5.5 %collective-permute-done.10.b = bf16[222,256]{1,0:T(8,128)(2,1)S(1)} collective-permute-done((bf16[222,256]{1,0:T(8,128)(2,1)S(1)}, bf16[222,256]{1,0:T(8,128)(2,1)S(1)}, u32[]{:S(2)}, u32[]{:S(2)}) %collective-permute-start.10) | collective-permute-done | bytes 113696 | tf_op jit(solution)/shard_map/ppermute | solution.py:411
  51.0 0.5 collective-permute-start.13
  51.5 1.3 %collective-permute-done.11.late_o = bf16[256,896]{1,0:T(8,128)(2,1)S(1)} collective-permute-done((bf16[256,896]{1,0:T(8,128)(2,1)S(1)}, bf16[256,896]{1,0:T(8,128)(2,1)S(1)}, u32[]{:S(2)}, u32[]{:S(2)}) %collective-permute-start.11) | collective-permute-done | bytes 458784 | tf_op jit(solution)/shard_map/ppermute | solution.py:414
  52.8 7.3 %shard_map.69 = (bf16[2,222,640]{2,1,0:T(8,128)(2,1)S(1)}, f32[2,222,640]{2,1,0:T(8,128)S(1)}) custom-call(s32[4]{0:T(128)S(1)} %pad_add_fusion.sc, bf16[3,888,888]{2,1,0:T(8,128)(2,1)S(1)} %bitcast.14, bf16[3072,896]{1,0:T(8,128)(2,1)S(1)} %shard_map.68.sources, s32[3,1024]{1,0:T(4,128)S(1)} %get-tuple-element.59.lists, ...), custom_call_target="tpu_custom_call" | custom-call | tf_op jit(solution)/shard_map/pallas_call | solution.py:34
  60.9 1.8 %collective-permute-done.14 = bf16[2,222,640]{2,0,1:T(2,128)(2,1)S(1)} collective-permute-done((bf16[2,222,640]{2,0,1:T(2,128)(2,1)S(1)}, bf16[2,222,640]{2,0,1:T(2,128)(2,1)S(1)}, u32[]{:S(2)}, u32[]{:S(2)}) %collective-permute-start.14) | collective-permute-done | bytes 568352 | tf_op jit(solution)/shard_map/ppermute | solution.py:419
  62.8 0.7 shard_map.70
  63.8 2.7 %shard_map.71 = (bf16[448,128]{1,0:T(8,128)(2,1)S(1)}, f32[448,128]{1,0:T(8,128)S(1)}) custom-call(s32[4]{0:T(128)S(1)} %pad_add_fusion.sc, s32[3,128]{1,0:T(4,128)S(1)} %copy-done.4, bf16[3,888,888]{2,1,0:T(8,128)(2,1)S(1)} %bitcast.14, bf16[222,256]{1,0:T(8,128)(2,1)S(1)} %shard_map.67.own, bf16[222,256]{1,0:T(8,128)(2,1)S(1)} %collective-permute-done.5.a, ...), custom_call_target="tpu_custom_call" | custom-call | tf_op jit(solution)/shard_map/pallas_call | solution.py:34
  66.6 1.3 %collective-permute-done.15.two = bf16[448,128]{1,0:T(8,128)(2,1)S(1)} collective-permute-done((bf16[448,128]{1,0:T(8,128)(2,1)S(1)}, bf16[448,128]{1,0:T(8,128)(2,1)S(1)}, u32[]{:S(2)}, u32[]{:S(2)}) %collective-permute-start.15) | collective-permute-done | bytes 114720 | tf_op jit(solution)/shard_map/ppermute | solution.py:430
  67.9 0.6 shard_map.72
  68.5 2.0 %collective-permute-start.17 = (bf16[448,128]{1,0:T(8,128)(2,1)S(1)}, bf16[448,128]{1,0:T(8,128)(2,1)S(1)}, u32[]{:S(2)}, u32[]{:S(2)}) collective-permute-start(bf16[448,128]{1,0:T(8,128)(2,1)S(1)} %get-tuple-element.53), channel_id=1, source_target_pairs={{0,2},{1,3},{2,0},{3,1},{4,6},{5,7},{6,4},{7,5},{8,10},{9,11},{10,... | collective-permute-start | bytes 344072 | tf_op jit(solution)/shard_map/ppermute | solution.py:435
  70.5 5.1 %shard_map.73 = (bf16[2,222,384]{2,1,0:T(8,128)(2,1)S(1)}, f32[2,222,384]{2,1,0:T(8,128)S(1)}) custom-call(s32[4]{0:T(128)S(1)} %pad_add_fusion.sc, bf16[3,888,888]{2,1,0:T(8,128)(2,1)S(1)} %bitcast.14, bf16[3072,896]{1,0:T(8,128)(2,1)S(1)} %shard_map.68.sources, s32[3,1024]{1,0:T(4,128)S(1)} %get-tuple-element.59.lists, ...), custom_call_target="tpu_custom_call" | custom-call | tf_op jit(solution)/shard_map/pallas_call | solution.py:34
  75.8 1.6 %collective-permute-done.18.got = bf16[2,222,384]{2,1,0:T(8,128)(2,1)S(1)} collective-permute-done((bf16[2,222,384]{2,1,0:T(8,128)(2,1)S(1)}, bf16[2,222,384]{2,1,0:T(8,128)(2,1)S(1)}, u32[]{:S(2)}, u32[]{:S(2)}) %collective-permute-start.18) | collective-permute-done | bytes 341024 | tf_op jit(solution)/shard_map/ppermute | solution.py:419
  77.4 0.6 shard_map.74
  78.4 0.6 shard_map.75.mine
  79.1 1.3 %collective-permute-done.19.other = bf16[448,128]{1,0:T(8,128)(2,1)S(1)} collective-permute-done((bf16[448,128]{1,0:T(8,128)(2,1)S(1)}, bf16[448,128]{1,0:T(8,128)(2,1)S(1)}, u32[]{:S(2)}, u32[]{:S(2)}) %collective-permute-start.19) | collective-permute-done | bytes 114720 | tf_op jit(solution)/shard_map/ppermute | solution.py:438
  80.4 2.9 %shard_map.76.spread = f32[222,1024]{1,0:T(8,128)S(1)} custom-call(s32[4]{0:T(128)S(1)} %pad_add_fusion.sc, bf16[1776,888]{1,0:T(8,128)(2,1)S(1)} %bitcast.16, bf16[448,128]{1,0:T(8,128)(2,1)S(1)} %shard_map.75.mine, bf16[448,128]{1,0:T(8,128)(2,1)S(1)} %collective-permute-done.19.other), custom_call_target="tpu_custom_call" | custom-call | tf_op jit(solution)/shard_map/pallas_call | solution.py:34
  83.4 1.2 %collective-permute-done.20.refs_3_ = bf16[222,384]{1,0:T(8,128)(2,1)S(1)} collective-permute-done((bf16[222,384]{1,0:T(8,128)(2,1)S(1)}, bf16[222,384]{1,0:T(8,128)(2,1)S(1)}, u32[]{:S(2)}, u32[]{:S(2)}) %collective-permute-start.20) | collective-permute-done | bytes 170528 | tf_op jit(solution)/shard_map/ppermute | solution.py:420
  84.5 1.5 %shard_map.77 = bf16[222,1024]{1,0:T(8,128)(2,1)} custom-call(s32[4]{0:T(128)S(1)} %pad_add_fusion.sc, f32[222,1024]{1,0:T(8,128)S(1)} %shard_map.76.spread, f32[222,640]{1,0:T(8,128)S(1)} %get-tuple-element.57.refs_0_, bf16[222,640]{1,0:T(8,128)(2,1)S(1)} %collective-permute-done.16.refs_1_, f32[222,384]{1,0:T(8,128)S(1)} %get-tuple-element.58.refs_2_, ...), custom_call_target="tpu_custom_call" | custom-call | tf_op jit(solution)/shard_map/pallas_call | solution.py:34
  (45 shorter events, 3.2 us)
Async XLA Ops:
  0.0 1.5 %copy-start = (bf16[888,1024]{1,0:T(8,128)(2,1)S(1)}, bf16[888,1024]{1,0:T(8,128)(2,1)}, u32[]{:S(2)}) copy-start(bf16[888,1024]{1,0:T(8,128)(2,1)} %x_ref.3) | copy-start | bytes 5455876
  1.5 9.5 %copy-start.1 = (bf16[888,1024]{1,0:T(8,128)(2,1)S(1)}, bf16[888,1024]{1,0:T(8,128)(2,1)}, u32[]{:S(2)}) copy-start(bf16[888,1024]{1,0:T(8,128)(2,1)} %x_ref.3) | copy-start | bytes 5455876
  1.7 19.9 %collective-permute-start = (bf16[256,896]{1,0:T(8,128)(2,1)S(1)}, bf16[256,896]{1,0:T(8,128)(2,1)S(1)}, u32[]{:S(2)}, u32[]{:S(2)}) collective-permute-start(bf16[256,896]{1,0:T(8,128)(2,1)S(1)} %shard_map.64.refs_0_), channel_id=1, source_target_pairs={{2,4},{3,5},{6,8},{7,9},{10,12},{11,13},{14,16},{15,17},{18,20},{1... | collective-permute-start | bytes 1376264 | tf_op jit(solution)/shard_map/ppermute | solution.py:406
  12.0 1.9 %copy-start.2 = (bf16[8,222,888]{2,0,1:T(8,128)(2,1)S(1)}, bf16[8,222,888]{2,0,1:T(8,128)(2,1)}, u32[]{:S(2)}) copy-start(bf16[8,222,888]{2,0,1:T(8,128)(2,1)} %param.7) | copy-start | bytes 9462532
  16.7 4.3 %collective-permute-start.2 = (bf16[222,128]{1,0:T(8,128)(2,1)S(1)}, bf16[222,128]{1,0:T(8,128)(2,1)S(1)}, u32[]{:S(2)}, u32[]{:S(2)}) collective-permute-start(bf16[222,128]{1,0:T(8,128)(2,1)S(1)} %shard_map.66.refs_0_), channel_id=1, source_target_pairs={{0,2},{1,3},{2,0},{3,1},{4,6},{5,7},{6,4},{7,5},{8,10},{9,11},{10,... | collective-permute-start | bytes 170504 | tf_op jit(solution)/shard_map/ppermute | solution.py:402
  16.8 17.5 %collective-permute-start.1 = (bf16[256,896]{1,0:T(8,128)(2,1)S(1)}, bf16[256,896]{1,0:T(8,128)(2,1)S(1)}, u32[]{:S(2)}, u32[]{:S(2)}) collective-permute-start(bf16[256,896]{1,0:T(8,128)(2,1)S(1)} %get-tuple-element.36.refs_1_), channel_id=1, source_target_pairs={{2,4},{3,5},{6,8},{7,9},{10,12},{11,13},{14,16},{15,17},{18,20},{1... | collective-permute-start | bytes 1376264 | tf_op jit(solution)/shard_map/ppermute | solution.py:406
  21.0 31.8 %slice-start = ((s8[4773888]{0:T(1024)(128)(4,1)}), s8[4194304]{0:T(1024)(128)(4,1)S(1)}, s32[]{:S(2)}) async-start(s8[4773888]{0:T(1024)(128)(4,1)} %bitcast.13), calls=%async_computation | async-start | bytes 8388608
  21.6 31.2 %slice-start.1 = ((s8[4773888]{0:T(1024)(128)(4,1)}), s8[579584]{0:T(1024)(128)(4,1)S(1)}, s32[]{:S(2)}) async-start(s8[4773888]{0:T(1024)(128)(4,1)} %bitcast.13), calls=%async_computation.1 | async-start | bytes 1159168
  21.6 14.0 %collective-permute-start.7 = (bf16[256,896]{1,0:T(8,128)(2,1)S(1)}, bf16[256,896]{1,0:T(8,128)(2,1)S(1)}, u32[]{:S(2)}, u32[]{:S(2)}) collective-permute-start(bf16[256,896]{1,0:T(8,128)(2,1)S(1)} %collective-permute-done.refs_3_), channel_id=1, source_target_pairs={{0,2},{1,3},{2,0},{3,1},{4,6},{5,7},{6,4},{7,5},{8,10},{9,11},{10,... | collective-permute-start | bytes 1376264 | tf_op jit(solution)/shard_map/ppermute | solution.py:409
  21.7 6.2 %collective-permute-start.4 = (bf16[222,256]{1,0:T(8,128)(2,1)S(1)}, bf16[222,256]{1,0:T(8,128)(2,1)S(1)}, u32[]{:S(2)}, u32[]{:S(2)}) collective-permute-start(bf16[222,256]{1,0:T(8,128)(2,1)S(1)} %shard_map.67.own), channel_id=1, source_target_pairs={{0,1},{1,0},{2,3},{3,2},{4,5},{5,4},{6,7},{7,6},{8,9},{9,8},{10,11... | collective-permute-start | bytes 341000 | tf_op jit(solution)/shard_map/ppermute | solution.py:404
  21.8 13.8 %collective-permute-start.5 = (bf16[222,256]{1,0:T(8,128)(2,1)S(1)}, bf16[222,256]{1,0:T(8,128)(2,1)S(1)}, u32[]{:S(2)}, u32[]{:S(2)}) collective-permute-start(bf16[222,256]{1,0:T(8,128)(2,1)S(1)} %shard_map.67.own), channel_id=1, source_target_pairs={{2,4},{3,5},{6,8},{7,9},{10,12},{11,13},{14,16},{15,17},{18,20},{1... | collective-permute-start | bytes 341000 | tf_op jit(solution)/shard_map/ppermute | solution.py:403
  27.7 10.5 %collective-permute-start.3 = (bf16[256,896]{1,0:T(8,128)(2,1)S(1)}, bf16[256,896]{1,0:T(8,128)(2,1)S(1)}, u32[]{:S(2)}, u32[]{:S(2)}) collective-permute-start(bf16[256,896]{1,0:T(8,128)(2,1)S(1)} %collective-permute-done.refs_3_), channel_id=1, source_target_pairs={{0,1},{1,0},{2,3},{3,2},{4,5},{5,4},{6,7},{7,6},{8,9},{9,8},{10,11... | collective-permute-start | bytes 1376264 | tf_op jit(solution)/shard_map/ppermute | solution.py:410
  35.6 2.5 %collective-permute-start.6 = (bf16[256,896]{1,0:T(8,128)(2,1)S(1)}, bf16[256,896]{1,0:T(8,128)(2,1)S(1)}, u32[]{:S(2)}, u32[]{:S(2)}) collective-permute-start(bf16[256,896]{1,0:T(8,128)(2,1)S(1)} %collective-permute-done.1.refs_4_), channel_id=1, source_target_pairs={{0,1},{1,0},{2,3},{3,2},{4,5},{5,4},{6,7},{7,6},{8,9},{9,8},{10,11... | collective-permute-start | bytes 1376264 | tf_op jit(solution)/shard_map/ppermute | solution.py:410
  35.6 2.5 %collective-permute-start.8 = (bf16[256,896]{1,0:T(8,128)(2,1)S(1)}, bf16[256,896]{1,0:T(8,128)(2,1)S(1)}, u32[]{:S(2)}, u32[]{:S(2)}) collective-permute-start(bf16[256,896]{1,0:T(8,128)(2,1)S(1)} %collective-permute-done.7.refs_7_), channel_id=1, source_target_pairs={{0,1},{1,0},{2,3},{3,2},{4,5},{5,4},{6,7},{7,6},{8,9},{9,8},{10,11... | collective-permute-start | bytes 1376264 | tf_op jit(solution)/shard_map/ppermute | solution.py:412
  36.1 14.9 %collective-permute-start.9 = (bf16[256,896]{1,0:T(8,128)(2,1)S(1)}, bf16[256,896]{1,0:T(8,128)(2,1)S(1)}, u32[]{:S(2)}, u32[]{:S(2)}) collective-permute-start(bf16[256,896]{1,0:T(8,128)(2,1)S(1)} %collective-permute-done.1.refs_4_), channel_id=1, source_target_pairs={{0,2},{1,3},{2,0},{3,1},{4,6},{5,7},{6,4},{7,5},{8,10},{9,11},{10,... | collective-permute-start | bytes 1376264 | tf_op jit(solution)/shard_map/ppermute | solution.py:409
  36.1 14.9 %collective-permute-start.10 = (bf16[222,256]{1,0:T(8,128)(2,1)S(1)}, bf16[222,256]{1,0:T(8,128)(2,1)S(1)}, u32[]{:S(2)}, u32[]{:S(2)}) collective-permute-start(bf16[222,256]{1,0:T(8,128)(2,1)S(1)} %collective-permute-done.5.a), channel_id=1, source_target_pairs={{0,2},{1,3},{2,0},{3,1},{4,6},{5,7},{6,4},{7,5},{8,10},{9,11},{10,... | collective-permute-start | bytes 341000 | tf_op jit(solution)/shard_map/ppermute | solution.py:411
  51.0 1.8 %collective-permute-start.11 = (bf16[256,896]{1,0:T(8,128)(2,1)S(1)}, bf16[256,896]{1,0:T(8,128)(2,1)S(1)}, u32[]{:S(2)}, u32[]{:S(2)}) collective-permute-start(bf16[256,896]{1,0:T(8,128)(2,1)S(1)} %collective-permute-done.9.late), channel_id=1, source_target_pairs={{0,1},{1,0},{2,3},{3,2},{4,5},{5,4},{6,7},{7,6},{8,9},{9,8},{10,11... | collective-permute-start | bytes 1376264 | tf_op jit(solution)/shard_map/ppermute | solution.py:414
  51.0 9.2 %collective-permute-start.13 = (bf16[222,256]{1,0:T(8,128)(2,1)S(1)}, bf16[222,256]{1,0:T(8,128)(2,1)S(1)}, u32[]{:S(2)}, u32[]{:S(2)}) collective-permute-start(bf16[222,256]{1,0:T(8,128)(2,1)S(1)} %collective-permute-done.5.a), channel_id=1, source_target_pairs={{0,1},{1,0},{2,3},{3,2},{4,5},{5,4},{6,7},{7,6},{8,9},{9,8},{10,11... | collective-permute-start | bytes 341000 | tf_op jit(solution)/shard_map/ppermute | solution.py:411
  51.5 8.7 %collective-permute-start.12 = (bf16[222,256]{1,0:T(8,128)(2,1)S(1)}, bf16[222,256]{1,0:T(8,128)(2,1)S(1)}, u32[]{:S(2)}, u32[]{:S(2)}) collective-permute-start(bf16[222,256]{1,0:T(8,128)(2,1)S(1)} %collective-permute-done.10.b), channel_id=1, source_target_pairs={{0,1},{1,0},{2,3},{3,2},{4,5},{5,4},{6,7},{7,6},{8,9},{9,8},{10,11... | collective-permute-start | bytes 341000 | tf_op jit(solution)/shard_map/ppermute | solution.py:415
  60.2 3.7 %copy-start.4 = (s32[3,128]{1,0:T(4,128)S(1)}, s32[3,128]{1,0:T(4,128)}, u32[]{:S(2)}) copy-start(s32[3,128]{1,0:T(4,128)} %lists.1) | copy-start | bytes 4612
  60.6 2.1 %collective-permute-start.14 = (bf16[2,222,640]{2,0,1:T(2,128)(2,1)S(1)}, bf16[2,222,640]{2,0,1:T(2,128)(2,1)S(1)}, u32[]{:S(2)}, u32[]{:S(2)}) collective-permute-start(bf16[2,222,640]{2,0,1:T(2,128)(2,1)S(1)} %copy.7), channel_id=1, source_target_pairs={{0,1},{1,0},{2,3},{3,2},{4,5},{5,4},{6,7},{7,6},{8,9},{9,8},{10,11... | collective-permute-start | bytes 1704968 | tf_op jit(solution)/shard_map/ppermute | solution.py:419
  63.4 12.2 %collective-permute-start.16 = (bf16[222,640]{1,0:T(8,128)(2,1)S(1)}, bf16[222,640]{1,0:T(8,128)(2,1)S(1)}, u32[]{:S(2)}, u32[]{:S(2)}) collective-permute-start(bf16[222,640]{1,0:T(8,128)(2,1)S(1)} %get-tuple-element.44), channel_id=1, source_target_pairs={{0,2},{1,3},{2,0},{3,1},{4,6},{5,7},{6,4},{7,5},{8,10},{9,11},{10,... | collective-permute-start | bytes 852488 | tf_op jit(solution)/shard_map/ppermute | solution.py:420
  66.5 1.4 %collective-permute-start.15 = (bf16[448,128]{1,0:T(8,128)(2,1)S(1)}, bf16[448,128]{1,0:T(8,128)(2,1)S(1)}, u32[]{:S(2)}, u32[]{:S(2)}) collective-permute-start(bf16[448,128]{1,0:T(8,128)(2,1)S(1)} %get-tuple-element.48), channel_id=1, source_target_pairs={{0,1},{1,0},{2,3},{3,2},{4,5},{5,4},{6,7},{7,6},{8,9},{9,8},{10,11... | collective-permute-start | bytes 344072 | tf_op jit(solution)/shard_map/ppermute | solution.py:430
  68.5 7.2 %collective-permute-start.17 = (bf16[448,128]{1,0:T(8,128)(2,1)S(1)}, bf16[448,128]{1,0:T(8,128)(2,1)S(1)}, u32[]{:S(2)}, u32[]{:S(2)}) collective-permute-start(bf16[448,128]{1,0:T(8,128)(2,1)S(1)} %get-tuple-element.53), channel_id=1, source_target_pairs={{0,2},{1,3},{2,0},{3,1},{4,6},{5,7},{6,4},{7,5},{8,10},{9,11},{10,... | collective-permute-start | bytes 344072 | tf_op jit(solution)/shard_map/ppermute | solution.py:435
  70.5 9.9 %copy-start.3 = (bf16[8,222,888]{2,0,1:T(8,128)(2,1)S(1)}, bf16[8,222,888]{2,0,1:T(8,128)(2,1)}, u32[]{:S(2)}) copy-start(bf16[8,222,888]{2,0,1:T(8,128)(2,1)} %param.9) | copy-start | bytes 9462532
  75.7 1.7 %collective-permute-start.18 = (bf16[2,222,384]{2,1,0:T(8,128)(2,1)S(1)}, bf16[2,222,384]{2,1,0:T(8,128)(2,1)S(1)}, u32[]{:S(2)}, u32[]{:S(2)}) collective-permute-start(bf16[2,222,384]{2,1,0:T(8,128)(2,1)S(1)} %get-tuple-element.54), channel_id=1, source_target_pairs={{0,1},{1,0},{2,3},{3,2},{4,5},{5,4},{6,7},{7,6},{8,9},{9,8},{10,11... | collective-permute-start | bytes 1022984 | tf_op jit(solution)/shard_map/ppermute | solution.py:419
  78.0 6.5 %collective-permute-start.20 = (bf16[222,384]{1,0:T(8,128)(2,1)S(1)}, bf16[222,384]{1,0:T(8,128)(2,1)S(1)}, u32[]{:S(2)}, u32[]{:S(2)}) collective-permute-start(bf16[222,384]{1,0:T(8,128)(2,1)S(1)} %get-tuple-element.55), channel_id=1, source_target_pairs={{0,2},{1,3},{2,0},{3,1},{4,6},{5,7},{6,4},{7,5},{8,10},{9,11},{10,... | collective-permute-start | bytes 511496 | tf_op jit(solution)/shard_map/ppermute | solution.py:420
  79.0 1.4 %collective-permute-start.19 = (bf16[448,128]{1,0:T(8,128)(2,1)S(1)}, bf16[448,128]{1,0:T(8,128)(2,1)S(1)}, u32[]{:S(2)}, u32[]{:S(2)}) collective-permute-start(bf16[448,128]{1,0:T(8,128)(2,1)S(1)} %shard_map.75.mine), channel_id=1, source_target_pairs={{0,1},{1,0},{2,3},{3,2},{4,5},{5,4},{6,7},{7,6},{8,9},{9,8},{10,11... | collective-permute-start | bytes 344072 | tf_op jit(solution)/shard_map/ppermute | solution.py:438
